TPU v7x, 32 devices: a whole 2x2x4 slice. The times are simulated.
32 devices in a mesh: inner: 4 (over y, x), outer: 8 (over z, core).
Axes of the slice: x: 2, y: 2, z: 4, core: 2. Of those that a mesh axis runs over, the one named last changes fastest.
Arguments:
- query: bfloat16 [8192, 2048], P(('outer', 'inner')), may hold values from -12 to 12
- keys: bfloat16 [8192, 2048], P(('outer', 'inner')), may hold values from -12 to 12
- values: bfloat16 [8192, 2048], P(('outer', 'inner')), may hold values from -6 to 6
- middle_head_shift: int32 [16], replicated, may hold values from 0 to 3
- coarse_head_shift: int32 [16], replicated, may hold values from 0 to 255
Outputs:
- attended: bfloat16 [8192, 2048], P(('outer', 'inner'))
All inputs are finite; a program needn't handle non-finite values.
Results may differ from a plain program's by a relative error of at most 0.0045.
Values may be sent and summed in bfloat16 or wider, within the bound.
No kernel may reach another device: no remote copies, remote signals or barrier semaphores. Data moves between devices by JAX's collectives and lax.ppermute only.
A program may use at most 64 MiB of HBM per device.

v0:
```python
import jax
import jax.numpy as jnp
from jax import lax
from jax.sharding import PartitionSpec as P

HEAD_COUNT = 16
HEAD_FEATURES = 128
MIDDLE_DILATION = 4


def partner(value, axis, distance):
    mask = 2**distance
    pairs = [(source, source ^ mask) for source in range(lax.axis_size(axis))]
    return lax.ppermute(value, axis, pairs)


def attend(query_part, key_part, value_part):
    scores = jnp.einsum(
        "qhe,khe->qhk", query_part, key_part, preferred_element_type=jnp.float32
    ) * HEAD_FEATURES ** (-0.5)
    top = jnp.max(scores, axis=-1)
    weights = jnp.exp(scores - top[..., None])
    total = jnp.sum(weights, axis=-1)
    summed = jnp.einsum(
        "qhk,khe->qhe", weights.astype(jnp.bfloat16), value_part, preferred_element_type=jnp.float32
    )
    return (summed / total[..., None], top + jnp.log(total))


def pick_dilated_rows(array, select, group):
    shaped = array.reshape(-1, group, HEAD_COUNT, HEAD_FEATURES)
    kept = jnp.where(select[None, :, :, None], shaped, jnp.zeros_like(shaped))
    return jnp.sum(kept, axis=1)


def on_device(query, keys, values, middle_head_shift, coarse_head_shift):
    count = query.shape[0]
    query_per_head = query.reshape(count, HEAD_COUNT, HEAD_FEATURES)
    key_per_head = keys.reshape(count, HEAD_COUNT, HEAD_FEATURES)
    value_per_head = values.reshape(count, HEAD_COUNT, HEAD_FEATURES)
    other_keys, other_values = partner((key_per_head, value_per_head), "inner", 0)
    out_zero, lse_zero = attend(
        query_per_head,
        jnp.concatenate([key_per_head, other_keys], axis=0),
        jnp.concatenate([value_per_head, other_values], axis=0),
    )
    middle_row_index = jnp.arange(MIDDLE_DILATION)[:, None] == middle_head_shift[None, :]
    middle_query_rows = pick_dilated_rows(query_per_head, middle_row_index, MIDDLE_DILATION)
    middle_key_rows = pick_dilated_rows(key_per_head, middle_row_index, MIDDLE_DILATION)
    middle_value_rows = pick_dilated_rows(value_per_head, middle_row_index, MIDDLE_DILATION)
    partner_key_rows = pick_dilated_rows(other_keys, middle_row_index, MIDDLE_DILATION)
    partner_value_rows = pick_dilated_rows(other_values, middle_row_index, MIDDLE_DILATION)
    picked_rows = middle_query_rows.shape[0]
    cross_keys, cross_values = partner((middle_key_rows, middle_value_rows), "inner", 1)
    diagonal_keys, diagonal_values = partner((cross_keys, cross_values), "inner", 0)
    segment_keys = jnp.concatenate(
        [middle_key_rows, partner_key_rows, cross_keys, diagonal_keys], axis=0
    )
    segment_values = jnp.concatenate(
        [middle_value_rows, partner_value_rows, cross_values, diagonal_values], axis=0
    )
    middle_output_sparse, lse_one = attend(middle_query_rows, segment_keys, segment_values)
    lse_one_full = jnp.where(middle_row_index[None], lse_one[:, None, :], -jnp.inf).reshape(
        count, HEAD_COUNT
    )
    middle_output_dense = jnp.broadcast_to(
        middle_output_sparse[:, None], (picked_rows, MIDDLE_DILATION, HEAD_COUNT, HEAD_FEATURES)
    ).reshape(count, HEAD_COUNT, HEAD_FEATURES)
    coarse_row_index = jnp.arange(count)[:, None] == coarse_head_shift[None, :]
    coarse_query_rows = pick_dilated_rows(query_per_head, coarse_row_index, count)
    coarse_key_rows = pick_dilated_rows(key_per_head, coarse_row_index, count)
    coarse_value_rows = pick_dilated_rows(value_per_head, coarse_row_index, count)
    every_keys, every_values = (
        lax.all_gather(coarse_key_rows, ("inner", "outer"), axis=0, tiled=True),
        lax.all_gather(coarse_value_rows, ("inner", "outer"), axis=0, tiled=True),
    )
    coarse_output_sparse, lse_two = attend(coarse_query_rows, every_keys, every_values)
    lse_two_full = jnp.where(coarse_row_index, lse_two, -jnp.inf)
    top = jnp.maximum(jnp.maximum(lse_zero, lse_one_full), lse_two_full)
    weight_zero = jnp.exp(lse_zero - top)
    weight_one = jnp.exp(lse_one_full - top)
    weight_two = jnp.exp(lse_two_full - top)
    mixed = (
        weight_zero[..., None] * out_zero
        + weight_one[..., None] * middle_output_dense
        + weight_two[..., None] * coarse_output_sparse
    )
    mixed = mixed / (weight_zero + weight_one + weight_two)[..., None]
    return mixed.reshape(count, HEAD_COUNT * HEAD_FEATURES).astype(jnp.bfloat16)


def solution(mesh):
    placed = (
        P(("outer", "inner"), None),
        P(("outer", "inner"), None),
        P(("outer", "inner"), None),
        P(),
        P(),
    )
    return jax.shard_map(
        on_device,
        mesh=mesh,
        in_specs=placed,
        out_specs=P(("outer", "inner"), None),
        check_vma=False,
    )
```

profile of v0, /device:TPU:0, one launch (start us, length us, event | category | flops | bytes accessed | tf_op | source)
XLA Modules:
  0.0 137.3 jit_solution(14739090090948255527)
XLA Ops:
  0.0 1.6 %copy.56 = bf16[256,2048]{0,1:T(8,128)(2,1)S(1)} copy(bf16[256,2048]{1,0:T(8,128)(2,1)} %param.6) | data formatting | bytes 2097152 | tf_op args[1]
  1.6 1.3 copy.58
  2.9 2.9 %collective-permute-start = (bf16[256,16,128]{2,0,1:T(8,128)(2,1)}, bf16[256,16,128]{2,0,1:T(8,128)(2,1)}, u32[]{:S(2)}, u32[]{:S(2)}) collective-permute-start(bf16[256,16,128]{2,0,1:T(8,128)(2,1)} %copy.58), channel_id=1, source_target_pairs={{0,8},{8,0},{16,24},{24,16},{1,9},{9,1},{17,25},{25,17},{2,10},{10... | collective-permute-start | bytes 3145736 | tf_op jit(solution)/shard_map/ppermute | solution.py:14
  5.9 1.3 copy.68
  7.2 1.2 copy.87
  8.4 1.2 copy.89
  9.6 1.2 copy.86
  11.1 1.3 broadcast_in_dim.102
  12.4 0.8 fusion.23
  13.2 43.7 %all_gather.6 = bf16[32,16,128]{2,1,0:T(8,128)(2,1)S(1)} all-gather(bf16[1,16,128]{2,1,0:T(8,128)(2,1)S(1)} %bitcast.90), channel_id=1, replica_groups=mesh['inner'=4,'outer'=8] {'inner','outer'}, dimensions={0}, use_global_device_ids=true | all-gather | bytes 135168 | tf_op jit(solution)/shard_map/all_gather | solution.py:74
  56.9 0.2 fusion.48
  57.1 37.3 %all_gather.7 = bf16[32,16,128]{2,1,0:T(8,128)(2,1)S(1)} all-gather(bf16[1,16,128]{2,1,0:T(8,128)(2,1)S(1)} %bitcast.89), channel_id=1, replica_groups=mesh['inner'=4,'outer'=8] {'inner','outer'}, dimensions={0}, use_global_device_ids=true | all-gather | bytes 135168 | tf_op jit(solution)/shard_map/all_gather | solution.py:75
  94.5 0.2 fusion.55
  95.0 2.7 %copy.71 = bf16[256,16,128]{2,1,0:T(8,128)(2,1)} copy(bf16[256,16,128]{0,2,1:T(8,128)(2,1)} %collective-permute-done.3) | data formatting | bytes 2097152 | tf_op jit(solution)/shard_map/ppermute | solution.py:14
  97.6 4.3 %select_reduce_fusion.2 = (bf16[64,16,128]{2,1,0:T(8,128)(2,1)S(1)}, bf16[64,16,128]{2,1,0:T(8,128)(2,1)S(1)}, bf16[64,16,128]{2,1,0:T(8,128)(2,1)S(1)}, bf16[64...) fusion(bf16[64,4,16,128]{3,2,1,0:T(8,128)(2,1)S(1)} %bitcast.81, pred[4,16]{1,0:T(4,128)(4,1)S(1)} %iota_compare_fusion.1, ...), kind=kLoop, calls=%fused_computation.52 | loop fusion | flops 4587520 | bytes 6553664 | tf_op jit(solution)/shard_map/reduce_sum | solution.py:33
  102.0 0.6 collective-permute-start.4
  102.7 1.6 %collective-permute-start.1 = (bf16[64,16,128]{2,0,1:T(8,128)(2,1)S(1)}, bf16[64,16,128]{2,0,1:T(8,128)(2,1)S(1)}, u32[]{:S(2)}, u32[]{:S(2)}) collective-permute-start(bf16[64,16,128]{2,0,1:T(8,128)(2,1)S(1)} %copy.62), channel_id=1, source_target_pairs={{0,16},{8,24},{16,0},{24,8},{1,17},{9,25},{17,1},{25,9},{2,18},{10... | collective-permute-start | bytes 786440 | tf_op jit(solution)/shard_map/ppermute | solution.py:14
  104.2 2.5 %bitcast_reduce_fusion = (f32[256,16]{0,1:T(8,128)S(1)}, f32[16,512,256]{2,1,0:T(8,128)S(1)}) fusion(bf16[256,16,128]{2,0,1:T(8,128)(2,1)} %collective-permute-done, bf16[256,16,128]{2,0,1:T(8,128)(2,1)S(1)} %copy-done.5, bf16[256,2048]{1,0:T(8,128)(2,1)S(1)} %copy-done.2), kind=kOutput, calls=%fused_computation.1 | convolution fusion | flops 545255424 | bytes 11550720 | tf_op jit(solution)/shard_map/qhe,khe->qhk/dot_general | solution.py:18
  106.8 4.6 %fusion.3 = f32[16,128,256]{2,1,0:T(8,128)} fusion(f32[16,512,256]{2,1,0:T(8,128)S(1)} %get-tuple-element.22, f32[256,16]{0,1:T(8,128)S(1)} %get-tuple-element.21, bf16[256,16,128]{0,2,1:T(8,128)(2,1)} %collective-permute-done.3, bf16[256,16,128]{0,2,1:T(8,128)(2,1)} %bitcast.10), kind=kOutput, calls=%fused_computation.5 | convolution fusion | flops 547356672 | bytes 12599296 | tf_op jit(solution)/shard_map/qhk,khe->qhe/dot_general | solution.py:24
  111.4 4.9 %collective-permute-done.1 = bf16[64,16,128]{2,0,1:T(8,128)(2,1)S(1)} collective-permute-done((bf16[64,16,128]{2,0,1:T(8,128)(2,1)S(1)}, bf16[64,16,128]{2,0,1:T(8,128)(2,1)S(1)}, u32[]{:S(2)}, u32[]{:S(2)}) %collective-permute-start.1) | collective-permute-done | bytes 262176 | tf_op jit(solution)/shard_map/ppermute | solution.py:14
  116.3 1.4 %fusion.2 = f32[256,16]{0,1:T(8,128)S(1)} fusion(f32[16,512,256]{2,1,0:T(8,128)S(1)} %get-tuple-element.22, f32[256,16]{0,1:T(8,128)S(1)} %get-tuple-element.21), kind=kLoop, calls=%fused_computation.4 | loop fusion | flops 6287360 | bytes 8421376 | tf_op jit(solution)/shard_map/reduce_sum | solution.py:23
  117.8 2.1 %collective-permute-start.5 = (bf16[64,16,128]{2,0,1:T(8,128)(2,1)S(1)}, bf16[64,16,128]{2,0,1:T(8,128)(2,1)S(1)}, u32[]{:S(2)}, u32[]{:S(2)}) collective-permute-start(bf16[64,16,128]{2,0,1:T(8,128)(2,1)S(1)} %collective-permute-done.4), channel_id=1, source_target_pairs={{0,8},{8,0},{16,24},{24,16},{1,9},{9,1},{17,25},{25,17},{2,10},{10... | collective-permute-start | bytes 786440 | tf_op jit(solution)/shard_map/ppermute | solution.py:14
  119.9 5.6 %collective-permute-done.2 = bf16[64,16,128]{2,0,1:T(8,128)(2,1)S(1)} collective-permute-done((bf16[64,16,128]{2,0,1:T(8,128)(2,1)S(1)}, bf16[64,16,128]{2,0,1:T(8,128)(2,1)S(1)}, u32[]{:S(2)}, u32[]{:S(2)}) %collective-permute-start.2) | collective-permute-done | bytes 262176 | tf_op jit(solution)/shard_map/ppermute | solution.py:14
  125.5 0.6 fusion.62
  126.1 0.4 fusion.42
  126.5 3.1 %collective-permute-done.5 = bf16[64,16,128]{2,0,1:T(8,128)(2,1)S(1)} collective-permute-done((bf16[64,16,128]{2,0,1:T(8,128)(2,1)S(1)}, bf16[64,16,128]{2,0,1:T(8,128)(2,1)S(1)}, u32[]{:S(2)}, u32[]{:S(2)}) %collective-permute-start.5) | collective-permute-done | bytes 262176 | tf_op jit(solution)/shard_map/ppermute | solution.py:14
  129.6 0.6 fusion.20
  130.3 0.3 copy.75
  130.6 0.2 broadcast_in_dim.106
  130.7 1.8 %copy.76 = f32[256,16,128]{0,2,1:T(8,128)} copy(f32[256,16,128]{2,1,0:T(8,128)S(1)} %bitcast.79) | data formatting | bytes 4194304 | tf_op jit(solution)/shard_map/reshape | solution.py:68
  132.9 3.0 %fusion.18 = bf16[256,16,128]{0,2,1:T(8,128)(2,1)S(1)} fusion(f32[256,16,128]{0,2,1:T(8,128)} %copy.76, f32[16,128,256]{2,1,0:T(8,128)} %fusion.3, f32[256,16]{0,1:T(8,128)S(1)} %get-tuple-element.13, f32[16,128]{1,0:T(8,128)S(1)} %broadcast_divide_fusion, f32[256,16]{0,1:T(8,128)S(1)} %get-tuple-element.16, f32[256,16]{0,1:T(8,128)S(1)} %get-tuple-element.14, ...), kind=kLoop, calls=%fused_computation.20 | loop fusion | flops 4194304 | bytes 5332992 | tf_op jit(solution)/shard_map/convert_element_type | solution.py:89
  135.9 1.4 %copy.77 = bf16[256,2048]{1,0:T(8,128)(2,1)} copy(bf16[256,2048]{0,1:T(8,128)(2,1)S(1)} %bitcast.84) | data formatting | bytes 2097152 | tf_op jit(solution)/shard_map/convert_element_type | solution.py:89
  (37 shorter events, 1.2 us)
Async XLA Ops:
  0.0 5.9 %copy-start.1 = (bf16[256,2048]{1,0:T(8,128)(2,1)S(1)}, bf16[256,2048]{1,0:T(8,128)(2,1)}, u32[]{:S(2)}) copy-start(bf16[256,2048]{1,0:T(8,128)(2,1)} %param.7) | copy-start | bytes 3145732
  1.6 5.6 %copy-start.2 = (bf16[256,2048]{1,0:T(8,128)(2,1)S(1)}, bf16[256,2048]{1,0:T(8,128)(2,1)}, u32[]{:S(2)}) copy-start(bf16[256,2048]{1,0:T(8,128)(2,1)} %param.5) | copy-start | bytes 3145732
  2.9 5.5 %copy-start.7 = (s32[16]{0:T(128)S(1)}, s32[16]{0:T(128)}, u32[]{:S(2)}) copy-start(s32[16]{0:T(128)} %param.8) | copy-start | bytes 196
  2.9 94.7 %collective-permute-start = (bf16[256,16,128]{2,0,1:T(8,128)(2,1)}, bf16[256,16,128]{2,0,1:T(8,128)(2,1)}, u32[]{:S(2)}, u32[]{:S(2)}) collective-permute-start(bf16[256,16,128]{2,0,1:T(8,128)(2,1)} %copy.58), channel_id=1, source_target_pairs={{0,8},{8,0},{16,24},{24,16},{1,9},{9,1},{17,25},{25,17},{2,10},{10... | collective-permute-start | bytes 3145736 | tf_op jit(solution)/shard_map/ppermute | solution.py:14
  7.2 87.8 %collective-permute-start.3 = (bf16[256,16,128]{0,2,1:T(8,128)(2,1)}, bf16[256,16,128]{0,2,1:T(8,128)(2,1)}, u32[]{:S(2)}, u32[]{:S(2)}) collective-permute-start(bf16[256,16,128]{0,2,1:T(8,128)(2,1)} %bitcast.10), channel_id=1, source_target_pairs={{0,8},{8,0},{16,24},{24,16},{1,9},{9,1},{17,25},{25,17},{2,10},{10... | collective-permute-start | bytes 3145736 | tf_op jit(solution)/shard_map/ppermute | solution.py:14
  7.2 2.4 %copy-start = (bf16[256,2048]{1,0:T(8,128)(2,1)S(1)}, bf16[256,2048]{1,0:T(8,128)(2,1)}, u32[]{:S(2)}) copy-start(bf16[256,2048]{1,0:T(8,128)(2,1)} %param.6) | copy-start | bytes 3145732
  8.4 2.5 %copy-start.6 = (s32[16]{0:T(128)S(1)}, s32[16]{0:T(128)}, u32[]{:S(2)}) copy-start(s32[16]{0:T(128)} %param.9) | copy-start | bytes 196
  13.2 84.4 %copy-start.3 = (bf16[32,8,16,128]{3,2,1,0:T(8,128)(2,1)S(1)}, bf16[32,8,16,128]{3,2,1,0:T(8,128)(2,1)}, u32[]{:S(2)}) copy-start(bf16[32,8,16,128]{3,2,1,0:T(8,128)(2,1)} %copy.87) | copy-start | bytes 3145732
  13.2 84.4 %copy-start.4 = (bf16[32,8,16,128]{3,2,1,0:T(8,128)(2,1)S(1)}, bf16[32,8,16,128]{3,2,1,0:T(8,128)(2,1)}, u32[]{:S(2)}) copy-start(bf16[32,8,16,128]{3,2,1,0:T(8,128)(2,1)} %copy.89) | copy-start | bytes 3145732
  97.6 6.6 %copy-start.5 = (bf16[256,16,128]{2,0,1:T(8,128)(2,1)S(1)}, bf16[256,16,128]{2,0,1:T(8,128)(2,1)}, u32[]{:S(2)}) copy-start(bf16[256,16,128]{2,0,1:T(8,128)(2,1)} %copy.58) | copy-start | bytes 3145732
  102.0 15.8 %collective-permute-start.4 = (bf16[64,16,128]{2,0,1:T(8,128)(2,1)S(1)}, bf16[64,16,128]{2,0,1:T(8,128)(2,1)S(1)}, u32[]{:S(2)}, u32[]{:S(2)}) collective-permute-start(bf16[64,16,128]{2,0,1:T(8,128)(2,1)S(1)} %copy.73), channel_id=1, source_target_pairs={{0,16},{8,24},{16,0},{24,8},{1,17},{9,25},{17,1},{25,9},{2,18},{10... | collective-permute-start | bytes 786440 | tf_op jit(solution)/shard_map/ppermute | solution.py:14
  102.7 13.6 %collective-permute-start.1 = (bf16[64,16,128]{2,0,1:T(8,128)(2,1)S(1)}, bf16[64,16,128]{2,0,1:T(8,128)(2,1)S(1)}, u32[]{:S(2)}, u32[]{:S(2)}) collective-permute-start(bf16[64,16,128]{2,0,1:T(8,128)(2,1)S(1)} %copy.62), channel_id=1, source_target_pairs={{0,16},{8,24},{16,0},{24,8},{1,17},{9,25},{17,1},{25,9},{2,18},{10... | collective-permute-start | bytes 786440 | tf_op jit(solution)/shard_map/ppermute | solution.py:14
  116.3 9.2 %collective-permute-start.2 = (bf16[64,16,128]{2,0,1:T(8,128)(2,1)S(1)}, bf16[64,16,128]{2,0,1:T(8,128)(2,1)S(1)}, u32[]{:S(2)}, u32[]{:S(2)}) collective-permute-start(bf16[64,16,128]{2,0,1:T(8,128)(2,1)S(1)} %collective-permute-done.1), channel_id=1, source_target_pairs={{0,8},{8,0},{16,24},{24,16},{1,9},{9,1},{17,25},{25,17},{2,10},{10... | collective-permute-start | bytes 786440 | tf_op jit(solution)/shard_map/ppermute | solution.py:14
  117.8 11.8 %collective-permute-start.5 = (bf16[64,16,128]{2,0,1:T(8,128)(2,1)S(1)}, bf16[64,16,128]{2,0,1:T(8,128)(2,1)S(1)}, u32[]{:S(2)}, u32[]{:S(2)}) collective-permute-start(bf16[64,16,128]{2,0,1:T(8,128)(2,1)S(1)} %collective-permute-done.4), channel_id=1, source_target_pairs={{0,8},{8,0},{16,24},{24,16},{1,9},{9,1},{17,25},{25,17},{2,10},{10... | collective-permute-start | bytes 786440 | tf_op jit(solution)/shard_map/ppermute | solution.py:14
where the time goes:
time: 138 us; the launch traced here: 137 us
  blocking collectives  81 us (59%)
  local copies, waits for them, and re-layouts  16.1 us (12%)
  waiting for transfers between devices  13.6 us (10%)
  other arithmetic  10.5 us (8%)
  matrix products  8.63 us (6%)
  starting transfers between devices  7.2 us (5%)
    all_gather x1, blocking collectives, on_device(): lax.all_gather(coarse_key_rows, ('inner', 'outer'), axis=0, tiled=True)  43.7 us
    all_gather x1, blocking collectives, on_device(): lax.all_gather(coarse_value_rows, ('inner', 'outer'), axis=0, tiled=True)  37.3 us
    ppermute x6, waiting for transfers between devices, partner(): return lax.ppermute(value, axis, pairs)  13.6 us
    ppermute x6, starting transfers between devices, partner(): return lax.ppermute(value, axis, pairs)  7.2 us
    unnamed x21, local copies, waits for them, and re-layouts  6.57 us
    dot_general x3, matrix products, attend(): jnp.einsum('qhk,khe->qhe', weights.astype(jnp.bfloat16), value_part, pref...  5.4 us
    reduce_sum x2, other arithmetic, pick_dilated_rows(): return jnp.sum(kept, axis=1)  5.13 us
    dot_general x3, matrix products, attend(): jnp.einsum('qhe,khe->qhk', query_part, key_part, preferred_element_type=j...  3.23 us
  transfers between devices with their start and end apart: 6, of which 3 were waited for; matrix products, arithmetic and copies ran while one was open for 15% of the time, Pallas kernels for 0%

commit v1 on v0

v1 whole, which is shorter than its diff:
```python
import functools

import jax
import jax.numpy as jnp
from jax import lax
from jax.experimental import pallas as pl
from jax.experimental.pallas import tpu as pltpu
from jax.sharding import PartitionSpec as P

HEAD_COUNT = 16
HEAD_FEATURES = 128
MIDDLE_DILATION = 4
CHUNKS = (6, 5, 3, 2)
LOG2_E = 1.4426950408889634
MASKED = -1e30


def partner(value, axis, mask):
    pairs = [(source, source ^ mask) for source in range(lax.axis_size(axis))]
    return lax.ppermute(value, axis, pairs)


def member_first(rows, shift):
    members = rows // MIDDLE_DILATION
    row = lax.broadcasted_iota(jnp.int32, (rows, rows), 0)
    token = lax.broadcasted_iota(jnp.int32, (rows, rows), 1)
    slot = row // members
    wanted = MIDDLE_DILATION * (row % members) + (shift + slot) % MIDDLE_DILATION
    return (token == wanted).astype(jnp.float32).astype(jnp.bfloat16)


def fill_orders(order_ref):
    for shift in range(MIDDLE_DILATION):
        order_ref[shift] = member_first(order_ref.shape[1], shift)


def dot(a, b):
    return jnp.dot(a, b, preferred_element_type=jnp.float32)


def head_columns(head):
    return slice(head * HEAD_FEATURES, (head + 1) * HEAD_FEATURES)


def prepare_kernel(chunks, middle_ref, coarse_ref, k_ref, v_ref, members_ref, vm_ref, *rest):
    vr_refs, coarse_out_ref, order_ref = rest[: len(chunks)], rest[-2], rest[-1]
    rows = k_ref.shape[0]
    members = rows // MIDDLE_DILATION
    fill_orders(order_ref)
    head_row = lax.broadcasted_iota(jnp.int32, (HEAD_COUNT, rows), 0)
    token = lax.broadcasted_iota(jnp.int32, (HEAD_COUNT, rows), 1)
    coarse_k = jnp.zeros((HEAD_COUNT, HEAD_FEATURES), jnp.float32)
    coarse_v = jnp.zeros((HEAD_COUNT, HEAD_FEATURES), jnp.float32)
    head = 0
    for chunk, vr_ref in zip(chunks, vr_refs):
        for place in range(chunk):
            columns = head_columns(head)
            order = order_ref[middle_ref[head]]
            k, v = k_ref[:, columns], v_ref[:, columns]
            v_ordered = dot(order, v).astype(jnp.bfloat16)
            k_members = dot(order[:members], k).astype(jnp.bfloat16)
            members_ref[:members, columns] = k_members
            members_ref[members:, columns] = v_ordered[:members]
            vm_ref[:, columns] = v_ordered[:members]
            vr_ref[:, head_columns(place)] = v_ordered[members:]
            chosen = (head_row == head) & (token == coarse_ref[head])
            chosen = chosen.astype(jnp.float32).astype(jnp.bfloat16)
            coarse_k += dot(chosen, k)
            coarse_v += dot(chosen, v)
            head += 1
    coarse_out_ref[0, :HEAD_COUNT] = coarse_k.astype(jnp.bfloat16)
    coarse_out_ref[0, HEAD_COUNT:] = coarse_v.astype(jnp.bfloat16)


def reorder_kernel(middle_ref, k_ref, ordered_ref, members_ref, order_ref):
    members = members_ref.shape[0]
    fill_orders(order_ref)
    for head in range(HEAD_COUNT):
        columns = head_columns(head)
        ordered = dot(order_ref[middle_ref[head]], k_ref[:, columns]).astype(jnp.bfloat16)
        ordered_ref[:, columns] = ordered
        members_ref[:, columns] = ordered[:members]


def attend_kernel(
    first, middle_ref, coarse_ref, q_ref, k_ref, v_ref, kp_ref, vm_ref, vr_ref, cross_ref, diagonal_k_ref,
    diagonal_v_ref, ck_ref, cv_ref, *rest,
):
    out_ref = rest[-1]
    head = first + pl.program_id(0)
    shift, spot = middle_ref[head], coarse_ref[head]
    rows = q_ref.shape[0]
    members = rows // MIDDLE_DILATION
    q = q_ref[...]

    def scores(keys):
        return lax.dot_general(q, keys, (((1,), (1,)), ((), ())), preferred_element_type=jnp.float32)

    row = lax.broadcasted_iota(jnp.int32, (rows, 1), 0)
    row_is_member = row % MIDDLE_DILATION == shift
    own = scores(k_ref[...])
    other = scores(kp_ref[...])
    far_keys = jnp.concatenate([cross_ref[:members], diagonal_k_ref[...]], axis=0)
    far_values = jnp.concatenate([cross_ref[members:], diagonal_v_ref[...]], axis=0)
    far = jnp.where(row_is_member, scores(far_keys), MASKED)
    coarse = jnp.where(row == spot, scores(ck_ref[0]), MASKED)
    top = jnp.max(jnp.maximum(own, other), axis=1, keepdims=True)
    top = jnp.maximum(top, jnp.max(far, axis=1, keepdims=True))
    top = jnp.maximum(top, jnp.max(coarse, axis=1, keepdims=True))
    scale = HEAD_FEATURES ** (-0.5) * LOG2_E

    def weights(part):
        return jnp.exp2((part - top) * scale)

    column = lax.broadcasted_iota(jnp.int32, (1, rows), 1)
    own_twice = row_is_member & (column % MIDDLE_DILATION == shift)
    other_twice = row_is_member & (column < members)
    own, other, far, coarse = weights(own), weights(other), weights(far), weights(coarse)
    own = jnp.where(own_twice, own + own, own)
    other = jnp.where(other_twice, other + other, other)
    total = jnp.sum(own + other, axis=1, keepdims=True)
    total += jnp.sum(far, axis=1, keepdims=True) + jnp.sum(coarse, axis=1, keepdims=True)
    other = other.astype(jnp.bfloat16)
    other_values = jnp.concatenate([vm_ref[...], vr_ref[...]], axis=0)
    summed = dot(own.astype(jnp.bfloat16), v_ref[...])
    summed += dot(other, other_values)
    summed += dot(far.astype(jnp.bfloat16), far_values)
    summed += dot(coarse.astype(jnp.bfloat16), cv_ref[0])
    out_ref[...] = (summed / total).astype(jnp.bfloat16)


def cost(flops, moved, exps=0):
    return pl.CostEstimate(flops=int(flops), bytes_accessed=int(moved), transcendentals=int(exps))


def gather_all(value):
    for axis in ("outer", "inner"):
        size = lax.axis_size(axis)
        if size & (size - 1):
            value = lax.all_gather(value, axis, axis=0, tiled=True)
            continue
        order = [2**j for j in range(size.bit_length() - 1)]
        for mask in order:
            value = jnp.concatenate([value, partner(value, axis, mask)], axis=0)
    return value


def on_device(query, keys, values, middle_head_shift, coarse_head_shift):
    rows, width = query.shape
    members = rows // MIDDLE_DILATION
    bf16 = jnp.bfloat16
    smem = pl.BlockSpec(memory_space=pltpu.SMEM)
    vmem = pl.BlockSpec(memory_space=pltpu.VMEM)
    params = pltpu.CompilerParams(vmem_limit_bytes=32 * 1024 * 1024)
    order_scratch = pltpu.VMEM((MIDDLE_DILATION, rows, rows), bf16)

    other_keys = partner(keys, "inner", 1)
    prepared = pl.pallas_call(
        functools.partial(prepare_kernel, CHUNKS),
        out_shape=[
            jax.ShapeDtypeStruct((2 * members, width), bf16),
            jax.ShapeDtypeStruct((members, width), bf16),
            *[jax.ShapeDtypeStruct((rows - members, c * HEAD_FEATURES), bf16) for c in CHUNKS],
            jax.ShapeDtypeStruct((1, 2 * HEAD_COUNT, HEAD_FEATURES), bf16),
        ],
        in_specs=[smem, smem, vmem, vmem],
        out_specs=[vmem] * (3 + len(CHUNKS)),
        scratch_shapes=[order_scratch],
        compiler_params=params,
        cost_estimate=cost(2 * rows * rows * width * 1.5, 5 * rows * width * 2),
        name="prepare",
    )(middle_head_shift, coarse_head_shift, keys, values)
    own_members, own_vm, own_vr, coarse = prepared[0], prepared[1], prepared[2:-1], prepared[-1]
    coarse = gather_all(coarse)
    devices = coarse.shape[0]
    coarse = jnp.transpose(coarse, (1, 0, 2))
    cross = partner(own_members, "inner", 2)
    other_vm = partner(own_vm, "inner", 1)
    other_vr = [partner(piece, "inner", 1) for piece in own_vr]
    other_ordered, other_km = pl.pallas_call(
        reorder_kernel,
        out_shape=[
            jax.ShapeDtypeStruct((rows, width), bf16),
            jax.ShapeDtypeStruct((members, width), bf16),
        ],
        in_specs=[smem, vmem],
        out_specs=[vmem, vmem],
        scratch_shapes=[order_scratch],
        compiler_params=params,
        cost_estimate=cost(2 * rows * rows * width, 3 * rows * width * 2),
        name="reorder",
    )(middle_head_shift, other_keys)
    diagonal_k = partner(other_km, "inner", 2)
    diagonal_v = partner(other_vm, "inner", 2)

    out = None
    first = 0
    for chunk, vr in zip(CHUNKS, other_vr):

        def column_block(count, first=first):
            return pl.BlockSpec((count, HEAD_FEATURES), lambda i: (0, first + i))

        whole, part = column_block(rows), column_block(members)
        own_chunk = pl.BlockSpec((rows - members, HEAD_FEATURES), lambda i: (0, i))
        coarse_k = pl.BlockSpec((1, devices, HEAD_FEATURES), lambda i, first=first: (first + i, 0, 0))
        coarse_v = pl.BlockSpec((1, devices, HEAD_FEATURES), lambda i, first=first: (HEAD_COUNT + first + i, 0, 0))
        args = [middle_head_shift, coarse_head_shift, query, keys, values, other_ordered, other_vm, vr, cross]
        args += [diagonal_k, diagonal_v, coarse, coarse]
        specs = [smem, smem, whole, whole, whole, whole, part, own_chunk, column_block(2 * members)]
        specs += [part, part, coarse_k, coarse_v]
        aliases = {}
        if out is not None:
            aliases = {len(args): 0}
            args.append(out)
            specs.append(pl.BlockSpec(memory_space=pl.ANY))
        pairs = rows * (2 * rows + 2 * members + devices) * chunk
        out = pl.pallas_call(
            functools.partial(attend_kernel, first),
            out_shape=jax.ShapeDtypeStruct((rows, width), bf16),
            grid=(chunk,),
            in_specs=specs,
            out_specs=whole,
            input_output_aliases=aliases,
            compiler_params=params,
            cost_estimate=cost(4 * pairs * HEAD_FEATURES, 6 * rows * HEAD_FEATURES * 2 * chunk, pairs),
            name="attend",
        )(*args)
        first += chunk
    return out


def solution(mesh):
    placed = (
        P(("outer", "inner"), None),
        P(("outer", "inner"), None),
        P(("outer", "inner"), None),
        P(),
        P(),
    )
    return jax.shard_map(
        on_device,
        mesh=mesh,
        in_specs=placed,
        out_specs=P(("outer", "inner"), None),
        check_vma=False,
    )
```

time: 138 us -> 71.8 us (0.52)
  blocking collectives: 81 us -> 0 us
  Pallas kernels: 0 us -> 24.4 us
  starting transfers between devices: 7.2 us -> 19.2 us
  other arithmetic: 10.5 us -> 0.19 us
  matrix products: 8.63 us -> 0 us
  local copies, waits for them, and re-layouts: 16.1 us -> 9.99 us
  waiting for transfers between devices: 13.6 us -> 16.8 us
    all_gather x2 -> x0, blocking collectives: 81 us -> none  [the longest x1 43.7 us: on_device(): lax.all_gather(coarse_key_rows, ('inner', 'outer'), axis=0, tiled=True)]
    pallas_call x0 -> x6, Pallas kernels: none -> 24.4 us  [the longest x4 18.6 us: on_device(): pl.pallas_call(functools.partial(attend_kernel, first), out_shape=jax.Sha...]
    ppermute x6 -> x14, starting transfers between devices: 7.2 us -> 19.2 us  [partner(): return lax.ppermute(value, axis, pairs)]
    dot_general x6 -> x0, matrix products: 8.63 us -> none  [the longest x3 5.4 us: attend(): jnp.einsum('qhk,khe->qhe', weights.astype(jnp.bfloat16), value_part, pref...]
    reduce_sum x4 -> x0, other arithmetic: 6.91 us -> none  [the longest x2 5.13 us: pick_dilated_rows(): return jnp.sum(kept, axis=1)]
    convert_element_type x2 -> x0, other arithmetic: 3.18 us -> none  [the longest x1 2.99 us: on_device(): return mixed.reshape(count, HEAD_COUNT * HEAD_FEATURES).astype(jnp.bfloat16)]
    reshape x2 -> x0, local copies, waits for them, and re-layouts: 3.16 us -> none  [the longest x1 1.83 us: on_device(): middle_output_dense = jnp.broadcast_to(middle_output_sparse[:, None], (pi...]
    ppermute x6 -> x14, waiting for transfers between devices: 13.6 us -> 16.8 us  [partner(): return lax.ppermute(value, axis, pairs)]
  transfers between devices with their start and end apart: 6 -> 14, of which waited for: 3 -> 5; matrix products, arithmetic and copies ran while one was open for 15% -> 4% of each run, Pallas kernels for 0% -> 30%
where the time goes in v1:
time: 71.8 us; the launch traced here: 70.6 us
  Pallas kernels  24.4 us (34%)
  starting transfers between devices  19.2 us (27%)
  waiting for transfers between devices  16.8 us (23%)
  local copies, waits for them, and re-layouts  9.99 us (14%)
    ppermute x14, starting transfers between devices, partner(): return lax.ppermute(value, axis, pairs)  19.2 us
    pallas_call x4, Pallas kernels, on_device(): pl.pallas_call(functools.partial(attend_kernel, first), out_shape=jax.Sha...  18.6 us
    ppermute x14, waiting for transfers between devices, partner(): return lax.ppermute(value, axis, pairs)  16.8 us
    unnamed x38, local copies, waits for them, and re-layouts  7.16 us
    pallas_call x1, Pallas kernels, on_device(): pl.pallas_call(functools.partial(prepare_kernel, CHUNKS), out_shape=[jax....  2.94 us
    pallas_call x1, Pallas kernels, on_device(): pl.pallas_call(reorder_kernel, out_shape=[jax.ShapeDtypeStruct((rows, wid...  2.87 us
    concatenate x2, local copies, waits for them, and re-layouts, gather_all(): value = jnp.concatenate([value, partner(value, axis, mask)], axis=0)  2.81 us
  transfers between devices with their start and end apart: 14, of which 5 were waited for; matrix products, arithmetic and copies ran while one was open for 4% of the time, Pallas kernels for 30%

profile of v1, /device:TPU:0, one launch (start us, length us, event | category | flops | bytes accessed | tf_op | source)
XLA Modules:
  0.0 70.6 jit_solution(15045397470879876224)
XLA Ops:
  0.0 2.9 %collective-permute-start = (bf16[256,2048]{1,0:T(8,128)(2,1)}, bf16[256,2048]{1,0:T(8,128)(2,1)}, u32[]{:S(2)}, u32[]{:S(2)}) collective-permute-start(bf16[256,2048]{1,0:T(8,128)(2,1)} %k_ref.9), channel_id=1, source_target_pairs={{0,8},{8,0},{16,24},{24,16},{1,9},{9,1},{17,25},{25,17},{2,10},{10... | collective-permute-start | bytes 3145736 | tf_op jit(solution)/shard_map/ppermute | solution.py:20
  2.9 1.3 %copy-done = bf16[256,2048]{1,0:T(8,128)(2,1)S(1)} copy-done((bf16[256,2048]{1,0:T(8,128)(2,1)S(1)}, bf16[256,2048]{1,0:T(8,128)(2,1)}, u32[]{:S(2)}) %copy-start) | copy-done | bytes 1048600
  4.2 1.2 %copy-done.2 = bf16[256,2048]{1,0:T(8,128)(2,1)S(1)} copy-done((bf16[256,2048]{1,0:T(8,128)(2,1)S(1)}, bf16[256,2048]{1,0:T(8,128)(2,1)}, u32[]{:S(2)}) %copy-start.2) | copy-done | bytes 1048600
  5.4 0.7 copy-done.7
  6.1 0.7 copy-done.10
  6.7 2.9 %prepare.1 = (bf16[128,2048]{1,0:T(8,128)(2,1)}, bf16[64,2048]{1,0:T(8,128)(2,1)}, bf16[192,768]{1,0:T(8,128)(2,1)}, bf16[192,640]{1,0:T(8,128)(2,1)}, bf16[192,...) custom-call(s32[16]{0:T(128)S(1)} %copy-done.7, s32[16]{0:T(128)S(1)} %copy-done.10, ...), custom_call_target="tpu_custom_call" | custom-call | flops 402653184 | bytes 5242880 | tf_op jit(solution)/shard_map/prepare/pallas_call | solution.py:158
  9.8 1.2 %collective-permute-done.6 = bf16[1,32,128]{2,0,1:T(2,128)(2,1)S(1)} collective-permute-done((bf16[1,32,128]{2,0,1:T(2,128)(2,1)S(1)}, bf16[1,32,128]{2,0,1:T(2,128)(2,1)S(1)}, u32[]{:S(2)}, u32[]{:S(2)}) %collective-permute-start.6) | collective-permute-done | bytes 8224 | tf_op jit(solution)/shard_map/ppermute | solution.py:20
  11.0 1.6 %collective-permute-start.7 = (bf16[2,32,128]{2,0,1:T(2,128)(2,1)S(1)}, bf16[2,32,128]{2,0,1:T(2,128)(2,1)S(1)}, u32[]{:S(2)}, u32[]{:S(2)}) collective-permute-start(bf16[2,32,128]{2,0,1:T(2,128)(2,1)S(1)} %pad_maximum_fusion.2), channel_id=1, source_target_pairs={{0,2},{1,3},{2,0},{3,1},{4,6},{5,7},{6,4},{7,5},{8,10},{9,11},{10,... | collective-permute-start | bytes 49160 | tf_op jit(solution)/shard_map/ppermute | solution.py:20
  12.7 0.5 collective-permute-start.1
  13.2 1.6 %collective-permute-done.7 = bf16[2,32,128]{2,0,1:T(2,128)(2,1)S(1)} collective-permute-done((bf16[2,32,128]{2,0,1:T(2,128)(2,1)S(1)}, bf16[2,32,128]{2,0,1:T(2,128)(2,1)S(1)}, u32[]{:S(2)}, u32[]{:S(2)}) %collective-permute-start.7) | collective-permute-done | bytes 16416 | tf_op jit(solution)/shard_map/ppermute | solution.py:20
  14.9 2.7 %collective-permute-start.8 = (bf16[4,32,128]{2,0,1:T(4,128)(2,1)S(1)}, bf16[4,32,128]{2,0,1:T(4,128)(2,1)S(1)}, u32[]{:S(2)}, u32[]{:S(2)}) collective-permute-start(bf16[4,32,128]{2,0,1:T(4,128)(2,1)S(1)} %pad_maximum_fusion.1), channel_id=1, source_target_pairs={{0,4},{1,5},{2,6},{3,7},{4,0},{5,1},{6,2},{7,3},{8,12},{9,13},{10,... | collective-permute-start | bytes 98312 | tf_op jit(solution)/shard_map/ppermute | solution.py:20
  17.5 1.5 %collective-permute-start.3 = (bf16[128,2048]{1,0:T(8,128)(2,1)}, bf16[128,2048]{1,0:T(8,128)(2,1)}, u32[]{:S(2)}, u32[]{:S(2)}) collective-permute-start(bf16[128,2048]{1,0:T(8,128)(2,1)} %get-tuple-element.17), channel_id=1, source_target_pairs={{0,16},{8,24},{16,0},{24,8},{1,17},{9,25},{17,1},{25,9},{2,18},{10... | collective-permute-start | bytes 1572872 | tf_op jit(solution)/shard_map/ppermute | solution.py:20
  19.1 0.7 collective-permute-done.8
  19.9 0.4 collective-permute-start.9
  20.3 1.7 %collective-permute-start.13 = (bf16[192,768]{1,0:T(8,128)(2,1)}, bf16[192,768]{1,0:T(8,128)(2,1)}, u32[]{:S(2)}, u32[]{:S(2)}) collective-permute-start(bf16[192,768]{1,0:T(8,128)(2,1)} %get-tuple-element.22), channel_id=1, source_target_pairs={{0,8},{8,0},{16,24},{24,16},{1,9},{9,1},{17,25},{25,17},{2,10},{10... | collective-permute-start | bytes 884744 | tf_op jit(solution)/shard_map/ppermute | solution.py:20
  21.9 12.2 %collective-permute-done.9 = bf16[8,32,128]{2,0,1:T(8,128)(2,1)S(1)} collective-permute-done((bf16[8,32,128]{2,0,1:T(8,128)(2,1)S(1)}, bf16[8,32,128]{2,0,1:T(8,128)(2,1)S(1)}, u32[]{:S(2)}, u32[]{:S(2)}) %collective-permute-start.9) | collective-permute-done | bytes 65568 | tf_op jit(solution)/shard_map/ppermute | solution.py:20
  34.3 0.5 copy-done.16
  34.8 2.1 %collective-permute-start.10 = (bf16[16,32,128]{2,0,1:T(8,128)(2,1)S(1)}, bf16[16,32,128]{2,0,1:T(8,128)(2,1)S(1)}, u32[]{:S(2)}, u32[]{:S(2)}) collective-permute-start(bf16[16,32,128]{2,0,1:T(8,128)(2,1)S(1)} %concatenate.22), channel_id=1, source_target_pairs={{0,16},{8,24},{16,0},{24,8},{1,17},{9,25},{17,1},{25,9},{2,18},{10... | collective-permute-start | bytes 393224 | tf_op jit(solution)/shard_map/ppermute | solution.py:20
  36.9 2.9 %reorder.1 = (bf16[256,2048]{1,0:T(8,128)(2,1)S(1)}, bf16[64,2048]{1,0:T(8,128)(2,1)}) custom-call(s32[16]{0:T(128)S(1)} %copy-done.8, bf16[256,2048]{1,0:T(8,128)(2,1)} %collective-permute-done.k_ref), custom_call_target="tpu_custom_call" | custom-call | flops 268435456 | bytes 3145728 | tf_op jit(solution)/shard_map/reorder/pallas_call | solution.py:180
  39.8 1.0 %copy-done.5 = bf16[256,2048]{1,0:T(8,128)(2,1)} copy-done((bf16[256,2048]{1,0:T(8,128)(2,1)}, bf16[256,2048]{1,0:T(8,128)(2,1)S(1)}, u32[]{:S(2)}) %copy-start.5) | copy-done | bytes 1048600
  40.8 2.0 %collective-permute-start.4 = (bf16[64,2048]{1,0:T(8,128)(2,1)}, bf16[64,2048]{1,0:T(8,128)(2,1)}, u32[]{:S(2)}, u32[]{:S(2)}) collective-permute-start(bf16[64,2048]{1,0:T(8,128)(2,1)} %get-tuple-element.18), channel_id=1, source_target_pairs={{0,16},{8,24},{16,0},{24,8},{1,17},{9,25},{17,1},{25,9},{2,18},{10... | collective-permute-start | bytes 786440 | tf_op jit(solution)/shard_map/ppermute | solution.py:20
  42.8 1.5 %collective-permute-start.12 = (bf16[192,640]{1,0:T(8,128)(2,1)}, bf16[192,640]{1,0:T(8,128)(2,1)}, u32[]{:S(2)}, u32[]{:S(2)}) collective-permute-start(bf16[192,640]{1,0:T(8,128)(2,1)} %get-tuple-element.21), channel_id=1, source_target_pairs={{0,8},{8,0},{16,24},{24,16},{1,9},{9,1},{17,25},{25,17},{2,10},{10... | collective-permute-start | bytes 737288 | tf_op jit(solution)/shard_map/ppermute | solution.py:20
  44.3 0.6 collective-permute-start.11
  44.9 2.7 %concatenate.23 = bf16[32,32,128]{2,0,1:T(8,128)(2,1)S(1)} concatenate(bf16[1,32,128]{2,0,1:T(2,128)(2,1)} %copy-done.13, bf16[1,32,128]{2,0,1:T(2,128)(2,1)} %copy-done.14, bf16[2,32,128]{2,0,1:T(2,128)(2,1)} %copy-done.17, bf16[4,32,128]{2,0,1:T(4,128)(2,1)} %copy-done.15, bf16[8,32,128]{2,0,1:T(8,128)(2,1)} %copy-done.16, bf16[16,32,128]{2,0,1:T(8,128)(2,1)} %copy-done.18), dimensions={0} | concatenate | bytes 524288 | tf_op jit(solution)/shard_map/concatenate | solution.py:144
  47.6 1.5 %collective-permute-start.2 = (bf16[192,256]{1,0:T(8,128)(2,1)}, bf16[192,256]{1,0:T(8,128)(2,1)S(1)}, u32[]{:S(2)}, u32[]{:S(2)}) collective-permute-start(bf16[192,256]{1,0:T(8,128)(2,1)} %copy-done.12), channel_id=1, source_target_pairs={{0,8},{8,0},{16,24},{24,16},{1,9},{9,1},{17,25},{25,17},{2,10},{10... | collective-permute-start | bytes 294920 | tf_op jit(solution)/shard_map/ppermute | solution.py:20
  49.1 1.0 %collective-permute-done.4.diagonal_k_ref = bf16[64,2048]{1,0:T(8,128)(2,1)} collective-permute-done((bf16[64,2048]{1,0:T(8,128)(2,1)}, bf16[64,2048]{1,0:T(8,128)(2,1)}, u32[]{:S(2)}, u32[]{:S(2)}) %collective-permute-start.4) | collective-permute-done | bytes 262176 | tf_op jit(solution)/shard_map/ppermute | solution.py:20
  50.1 0.6 copy-done.9
  50.8 1.2 %copy-done.6 = bf16[256,2048]{1,0:T(8,128)(2,1)S(1)} copy-done((bf16[256,2048]{1,0:T(8,128)(2,1)S(1)}, bf16[256,2048]{1,0:T(8,128)(2,1)}, u32[]{:S(2)}) %copy-start.6) | copy-done | bytes 1048600
  52.0 6.3 %attend.4.rest_0_ = bf16[256,2048]{1,0:T(8,128)(2,1)} custom-call(s32[16]{0:T(128)S(1)} %copy-done.9, s32[16]{0:T(128)S(1)} %copy-done.11, bf16[256,2048]{1,0:T(8,128)(2,1)S(1)} %copy-done.4, bf16[256,2048]{1,0:T(8,128)(2,1)S(1)} %copy-done.1, bf16[256,2048]{1,0:T(8,128)(2,1)S(1)} %copy-done.3, bf16[256,2048]{1,0:T(8,128)(2,1)S(1)} %copy-done.6, ...), custom_call_target="tpu_custom_call" | custom-call | flops 528482304 | bytes 2359296 | tf_op jit(solution)/shard_map/attend/pallas_call | solution.py:217
  58.3 5.5 %attend.5.rest_0_ = bf16[256,2048]{1,0:T(8,128)(2,1)} custom-call(s32[16]{0:T(128)S(1)} %copy-done.9, s32[16]{0:T(128)S(1)} %copy-done.11, bf16[256,2048]{1,0:T(8,128)(2,1)S(1)} %copy-done.4, bf16[256,2048]{1,0:T(8,128)(2,1)S(1)} %copy-done.1, bf16[256,2048]{1,0:T(8,128)(2,1)S(1)} %copy-done.3, ...), custom_call_target="tpu_custom_call", output_to_operand_aliasing={{}: (13, {})} | custom-call | flops 440401920 | bytes 1966080 | tf_op jit(solution)/shard_map/attend/pallas_call | solution.py:217
  63.9 3.8 %attend.6.rest_0_ = bf16[256,2048]{1,0:T(8,128)(2,1)} custom-call(s32[16]{0:T(128)S(1)} %copy-done.9, s32[16]{0:T(128)S(1)} %copy-done.11, bf16[256,2048]{1,0:T(8,128)(2,1)S(1)} %copy-done.4, bf16[256,2048]{1,0:T(8,128)(2,1)S(1)} %copy-done.1, bf16[256,2048]{1,0:T(8,128)(2,1)S(1)} %copy-done.3, ...), custom_call_target="tpu_custom_call", output_to_operand_aliasing={{}: (13, {})} | custom-call | flops 264241152 | bytes 1179648 | tf_op jit(solution)/shard_map/attend/pallas_call | solution.py:217
  67.7 2.9 %attend.7 = bf16[256,2048]{1,0:T(8,128)(2,1)} custom-call(s32[16]{0:T(128)S(1)} %copy-done.9, s32[16]{0:T(128)S(1)} %copy-done.11, bf16[256,2048]{1,0:T(8,128)(2,1)S(1)} %copy-done.4, bf16[256,2048]{1,0:T(8,128)(2,1)S(1)} %copy-done.1, bf16[256,2048]{1,0:T(8,128)(2,1)S(1)} %copy-done.3, ...), custom_call_target="tpu_custom_call", output_to_operand_aliasing={{}: (13, {})} | custom-call | flops 176160768 | bytes 786432 | tf_op jit(solution)/shard_map/attend/pallas_call | solution.py:217
  (46 shorter events, 0.5 us)
Async XLA Ops:
  0.0 36.9 %collective-permute-start = (bf16[256,2048]{1,0:T(8,128)(2,1)}, bf16[256,2048]{1,0:T(8,128)(2,1)}, u32[]{:S(2)}, u32[]{:S(2)}) collective-permute-start(bf16[256,2048]{1,0:T(8,128)(2,1)} %k_ref.9), channel_id=1, source_target_pairs={{0,8},{8,0},{16,24},{24,16},{1,9},{9,1},{17,25},{25,17},{2,10},{10... | collective-permute-start | bytes 3145736 | tf_op jit(solution)/shard_map/ppermute | solution.py:20
  2.9 1.3 %copy-start = (bf16[256,2048]{1,0:T(8,128)(2,1)S(1)}, bf16[256,2048]{1,0:T(8,128)(2,1)}, u32[]{:S(2)}) copy-start(bf16[256,2048]{1,0:T(8,128)(2,1)} %k_ref.9) | copy-start | bytes 3145732
  4.2 1.2 %copy-start.2 = (bf16[256,2048]{1,0:T(8,128)(2,1)S(1)}, bf16[256,2048]{1,0:T(8,128)(2,1)}, u32[]{:S(2)}) copy-start(bf16[256,2048]{1,0:T(8,128)(2,1)} %v_ref.9) | copy-start | bytes 3145732
  5.4 0.7 copy-start.7
  6.1 0.7 copy-start.10
  6.7 43.4 %copy-start.4 = (bf16[256,2048]{1,0:T(8,128)(2,1)S(1)}, bf16[256,2048]{1,0:T(8,128)(2,1)}, u32[]{:S(2)}) copy-start(bf16[256,2048]{1,0:T(8,128)(2,1)} %q_ref.7) | copy-start | bytes 3145732
  9.7 10.2 %copy-start.12 = (bf16[192,256]{1,0:T(8,128)(2,1)}, bf16[192,256]{1,0:T(8,128)(2,1)S(1)}, u32[]{:S(2)}) copy-start(bf16[192,256]{1,0:T(8,128)(2,1)S(1)} %get-tuple-element.16) | copy-start | bytes 294916
  9.7 24.5 %copy-start.13 = (bf16[1,32,128]{2,0,1:T(2,128)(2,1)}, bf16[1,32,128]{2,0,1:T(2,128)(2,1)S(1)}, u32[]{:S(2)}) copy-start(bf16[1,32,128]{2,0,1:T(2,128)(2,1)S(1)} %copy.14) | copy-start | bytes 24580
  9.7 1.2 %collective-permute-start.6 = (bf16[1,32,128]{2,0,1:T(2,128)(2,1)S(1)}, bf16[1,32,128]{2,0,1:T(2,128)(2,1)S(1)}, u32[]{:S(2)}, u32[]{:S(2)}) collective-permute-start(bf16[1,32,128]{2,0,1:T(2,128)(2,1)S(1)} %copy.14), channel_id=1, source_target_pairs={{0,1},{1,0},{2,3},{3,2},{4,5},{5,4},{6,7},{7,6},{8,9},{9,8},{10,11... | collective-permute-start | bytes 24584 | tf_op jit(solution)/shard_map/ppermute | solution.py:20
  11.0 23.2 %copy-start.14 = (bf16[1,32,128]{2,0,1:T(2,128)(2,1)}, bf16[1,32,128]{2,0,1:T(2,128)(2,1)S(1)}, u32[]{:S(2)}) copy-start(bf16[1,32,128]{2,0,1:T(2,128)(2,1)S(1)} %collective-permute-done.6) | copy-start | bytes 24580
  11.0 26.0 %copy-start.8 = (s32[16]{0:T(128)S(1)}, s32[16]{0:T(128)}, u32[]{:S(2)}) copy-start(s32[16]{0:T(128)} %middle_ref.11) | copy-start | bytes 196
  11.0 3.8 %collective-permute-start.7 = (bf16[2,32,128]{2,0,1:T(2,128)(2,1)S(1)}, bf16[2,32,128]{2,0,1:T(2,128)(2,1)S(1)}, u32[]{:S(2)}, u32[]{:S(2)}) collective-permute-start(bf16[2,32,128]{2,0,1:T(2,128)(2,1)S(1)} %pad_maximum_fusion.2), channel_id=1, source_target_pairs={{0,2},{1,3},{2,0},{3,1},{4,6},{5,7},{6,4},{7,5},{8,10},{9,11},{10,... | collective-permute-start | bytes 49160 | tf_op jit(solution)/shard_map/ppermute | solution.py:20
  12.7 37.5 %copy-start.1 = (bf16[256,2048]{1,0:T(8,128)(2,1)S(1)}, bf16[256,2048]{1,0:T(8,128)(2,1)}, u32[]{:S(2)}) copy-start(bf16[256,2048]{1,0:T(8,128)(2,1)} %k_ref.9) | copy-start | bytes 3145732
  12.7 37.5 %copy-start.3 = (bf16[256,2048]{1,0:T(8,128)(2,1)S(1)}, bf16[256,2048]{1,0:T(8,128)(2,1)}, u32[]{:S(2)}) copy-start(bf16[256,2048]{1,0:T(8,128)(2,1)} %v_ref.9) | copy-start | bytes 3145732
  12.7 24.2 %collective-permute-start.1 = (bf16[64,2048]{1,0:T(8,128)(2,1)}, bf16[64,2048]{1,0:T(8,128)(2,1)}, u32[]{:S(2)}, u32[]{:S(2)}) collective-permute-start(bf16[64,2048]{1,0:T(8,128)(2,1)} %get-tuple-element.15), channel_id=1, source_target_pairs={{0,8},{8,0},{16,24},{24,16},{1,9},{9,1},{17,25},{25,17},{2,10},{10... | collective-permute-start | bytes 786440 | tf_op jit(solution)/shard_map/ppermute | solution.py:20
  14.8 19.4 %copy-start.17 = (bf16[2,32,128]{2,0,1:T(2,128)(2,1)}, bf16[2,32,128]{2,0,1:T(2,128)(2,1)S(1)}, u32[]{:S(2)}) copy-start(bf16[2,32,128]{2,0,1:T(2,128)(2,1)S(1)} %collective-permute-done.7) | copy-start | bytes 49156
  14.9 4.9 %collective-permute-start.8 = (bf16[4,32,128]{2,0,1:T(4,128)(2,1)S(1)}, bf16[4,32,128]{2,0,1:T(4,128)(2,1)S(1)}, u32[]{:S(2)}, u32[]{:S(2)}) collective-permute-start(bf16[4,32,128]{2,0,1:T(4,128)(2,1)S(1)} %pad_maximum_fusion.1), channel_id=1, source_target_pairs={{0,4},{1,5},{2,6},{3,7},{4,0},{5,1},{6,2},{7,3},{8,12},{9,13},{10,... | collective-permute-start | bytes 98312 | tf_op jit(solution)/shard_map/ppermute | solution.py:20
  17.5 31.5 %collective-permute-start.3 = (bf16[128,2048]{1,0:T(8,128)(2,1)}, bf16[128,2048]{1,0:T(8,128)(2,1)}, u32[]{:S(2)}, u32[]{:S(2)}) collective-permute-start(bf16[128,2048]{1,0:T(8,128)(2,1)} %get-tuple-element.17), channel_id=1, source_target_pairs={{0,16},{8,24},{16,0},{24,8},{1,17},{9,25},{17,1},{25,9},{2,18},{10... | collective-permute-start | bytes 1572872 | tf_op jit(solution)/shard_map/ppermute | solution.py:20
  19.8 14.4 %copy-start.15 = (bf16[4,32,128]{2,0,1:T(4,128)(2,1)}, bf16[4,32,128]{2,0,1:T(4,128)(2,1)S(1)}, u32[]{:S(2)}) copy-start(bf16[4,32,128]{2,0,1:T(4,128)(2,1)S(1)} %collective-permute-done.8) | copy-start | bytes 98308
  19.9 14.3 %collective-permute-start.9 = (bf16[8,32,128]{2,0,1:T(8,128)(2,1)S(1)}, bf16[8,32,128]{2,0,1:T(8,128)(2,1)S(1)}, u32[]{:S(2)}, u32[]{:S(2)}) collective-permute-start(bf16[8,32,128]{2,0,1:T(8,128)(2,1)S(1)} %pad_maximum_fusion), channel_id=1, source_target_pairs={{0,8},{8,0},{16,24},{24,16},{1,9},{9,1},{17,25},{25,17},{2,10},{10... | collective-permute-start | bytes 196616 | tf_op jit(solution)/shard_map/ppermute | solution.py:20
  20.3 24.0 %collective-permute-start.13 = (bf16[192,768]{1,0:T(8,128)(2,1)}, bf16[192,768]{1,0:T(8,128)(2,1)}, u32[]{:S(2)}, u32[]{:S(2)}) collective-permute-start(bf16[192,768]{1,0:T(8,128)(2,1)} %get-tuple-element.22), channel_id=1, source_target_pairs={{0,8},{8,0},{16,24},{24,16},{1,9},{9,1},{17,25},{25,17},{2,10},{10... | collective-permute-start | bytes 884744 | tf_op jit(solution)/shard_map/ppermute | solution.py:20
  34.8 8.0 %collective-permute-start.10 = (bf16[16,32,128]{2,0,1:T(8,128)(2,1)S(1)}, bf16[16,32,128]{2,0,1:T(8,128)(2,1)S(1)}, u32[]{:S(2)}, u32[]{:S(2)}) collective-permute-start(bf16[16,32,128]{2,0,1:T(8,128)(2,1)S(1)} %concatenate.22), channel_id=1, source_target_pairs={{0,16},{8,24},{16,0},{24,8},{1,17},{9,25},{17,1},{25,9},{2,18},{10... | collective-permute-start | bytes 393224 | tf_op jit(solution)/shard_map/ppermute | solution.py:20
  36.9 10.7 %collective-permute-start.5 = (bf16[64,2048]{1,0:T(8,128)(2,1)}, bf16[64,2048]{1,0:T(8,128)(2,1)}, u32[]{:S(2)}, u32[]{:S(2)}) collective-permute-start(bf16[64,2048]{1,0:T(8,128)(2,1)} %collective-permute-done.1.vm_ref), channel_id=1, source_target_pairs={{0,16},{8,24},{16,0},{24,8},{1,17},{9,25},{17,1},{25,9},{2,18},{10... | collective-permute-start | bytes 786440 | tf_op jit(solution)/shard_map/ppermute | solution.py:20
  39.8 1.0 %copy-start.5 = (bf16[256,2048]{1,0:T(8,128)(2,1)}, bf16[256,2048]{1,0:T(8,128)(2,1)S(1)}, u32[]{:S(2)}) copy-start(bf16[256,2048]{1,0:T(8,128)(2,1)S(1)} %get-tuple-element.14.kp_ref) | copy-start | bytes 3145732
  40.8 9.3 %collective-permute-start.4 = (bf16[64,2048]{1,0:T(8,128)(2,1)}, bf16[64,2048]{1,0:T(8,128)(2,1)}, u32[]{:S(2)}, u32[]{:S(2)}) collective-permute-start(bf16[64,2048]{1,0:T(8,128)(2,1)} %get-tuple-element.18), channel_id=1, source_target_pairs={{0,16},{8,24},{16,0},{24,8},{1,17},{9,25},{17,1},{25,9},{2,18},{10... | collective-permute-start | bytes 786440 | tf_op jit(solution)/shard_map/ppermute | solution.py:20
  42.8 1.5 %copy-start.18 = (bf16[16,32,128]{2,0,1:T(8,128)(2,1)}, bf16[16,32,128]{2,0,1:T(8,128)(2,1)S(1)}, u32[]{:S(2)}) copy-start(bf16[16,32,128]{2,0,1:T(8,128)(2,1)S(1)} %collective-permute-done.10) | copy-start | bytes 393220
  42.8 15.5 %collective-permute-start.12 = (bf16[192,640]{1,0:T(8,128)(2,1)}, bf16[192,640]{1,0:T(8,128)(2,1)}, u32[]{:S(2)}, u32[]{:S(2)}) collective-permute-start(bf16[192,640]{1,0:T(8,128)(2,1)} %get-tuple-element.21), channel_id=1, source_target_pairs={{0,8},{8,0},{16,24},{24,16},{1,9},{9,1},{17,25},{25,17},{2,10},{10... | collective-permute-start | bytes 737288 | tf_op jit(solution)/shard_map/ppermute | solution.py:20
  44.3 19.6 %collective-permute-start.11 = (bf16[192,384]{1,0:T(8,128)(2,1)}, bf16[192,384]{1,0:T(8,128)(2,1)S(1)}, u32[]{:S(2)}, u32[]{:S(2)}) collective-permute-start(bf16[192,384]{1,0:T(8,128)(2,1)} %get-tuple-element.20), channel_id=1, source_target_pairs={{0,8},{8,0},{16,24},{24,16},{1,9},{9,1},{17,25},{25,17},{2,10},{10... | collective-permute-start | bytes 442376 | tf_op jit(solution)/shard_map/ppermute | solution.py:20
  47.6 20.1 %collective-permute-start.2 = (bf16[192,256]{1,0:T(8,128)(2,1)}, bf16[192,256]{1,0:T(8,128)(2,1)S(1)}, u32[]{:S(2)}, u32[]{:S(2)}) collective-permute-start(bf16[192,256]{1,0:T(8,128)(2,1)} %copy-done.12), channel_id=1, source_target_pairs={{0,8},{8,0},{16,24},{24,16},{1,9},{9,1},{17,25},{25,17},{2,10},{10... | collective-permute-start | bytes 294920 | tf_op jit(solution)/shard_map/ppermute | solution.py:20
  50.1 0.7 copy-start.9
  50.1 0.7 copy-start.11
  50.8 1.2 %copy-start.6 = (bf16[256,2048]{1,0:T(8,128)(2,1)S(1)}, bf16[256,2048]{1,0:T(8,128)(2,1)}, u32[]{:S(2)}) copy-start(bf16[256,2048]{1,0:T(8,128)(2,1)} %copy-done.5) | copy-start | bytes 3145732
  (1 other events, 0.6 us)

commit v2 on v1

v2 whole, which is shorter than its diff:
```python
import functools

import jax
import jax.numpy as jnp
from jax import lax
from jax.experimental import pallas as pl
from jax.experimental.pallas import tpu as pltpu
from jax.sharding import PartitionSpec as P

HEAD_COUNT = 16
HEAD_FEATURES = 128
MIDDLE_DILATION = 4
CHUNKS = (12, 4)
GROUP = 4
LANES = 128
SUBLANES = 16
EXP2_SCALE = HEAD_FEATURES ** (-0.5) * 1.4426950408889634
MASKED = -1e30


def partner(value, axis, mask):
    pairs = [(source, source ^ mask) for source in range(lax.axis_size(axis))]
    return lax.ppermute(value, axis, pairs)


def one_hot(mask):
    return mask.astype(jnp.float32).astype(jnp.bfloat16)


def fill_orders(order_ref):
    rows = order_ref.shape[1]
    members = rows // MIDDLE_DILATION
    group = lax.broadcasted_iota(jnp.int32, (members, rows), 0)
    token = lax.broadcasted_iota(jnp.int32, (members, rows), 1)
    for place in range(MIDDLE_DILATION):
        block = one_hot(token == MIDDLE_DILATION * group + place)
        for shift in range(MIDDLE_DILATION):
            slot = (place - shift) % MIDDLE_DILATION
            order_ref[shift, slot * members : (slot + 1) * members] = block


def dot(a, b):
    return jnp.dot(a, b, preferred_element_type=jnp.float32)


def head_columns(head):
    return slice(head * HEAD_FEATURES, (head + 1) * HEAD_FEATURES)


def prepare_kernel(chunks, middle_ref, coarse_ref, k_ref, v_ref, members_ref, vm_ref, *rest):
    vr_refs, coarse_out_ref, order_ref = rest[: len(chunks)], rest[-2], rest[-1]
    rows = k_ref.shape[0]
    members = rows // MIDDLE_DILATION
    fill_orders(order_ref)
    token = lax.broadcasted_iota(jnp.int32, (SUBLANES, rows), 1)
    first_row = lax.broadcasted_iota(jnp.int32, (SUBLANES, rows), 0) == 0
    second_row = lax.broadcasted_iota(jnp.int32, (SUBLANES, rows), 0) == 1
    head = 0
    for chunk, vr_ref in zip(chunks, vr_refs):
        for place in range(chunk):
            columns = head_columns(head)
            order = order_ref[middle_ref[head]]
            k, v = k_ref[:, columns], v_ref[:, columns]
            v_ordered = dot(order, v).astype(jnp.bfloat16)
            k_members = dot(order[:members], k).astype(jnp.bfloat16)
            members_ref[:members, columns] = k_members
            members_ref[members:, columns] = v_ordered[:members]
            vm_ref[:, columns] = v_ordered[:members]
            vr_ref[:, head_columns(place)] = v_ordered[members:]
            chosen = token == coarse_ref[head]
            picked = dot(one_hot(chosen & first_row), k) + dot(one_hot(chosen & second_row), v)
            coarse_out_ref[:, columns] = picked[:2].astype(jnp.bfloat16)
            head += 1


def reorder_kernel(middle_ref, k_ref, ordered_ref, members_ref, order_ref):
    members = members_ref.shape[0]
    fill_orders(order_ref)
    for head in range(HEAD_COUNT):
        columns = head_columns(head)
        ordered = dot(order_ref[middle_ref[head]], k_ref[:, columns]).astype(jnp.bfloat16)
        ordered_ref[:, columns] = ordered
        members_ref[:, columns] = ordered[:members]


def dot_keys(q, keys):
    return lax.dot_general(q, keys, (((1,), (1,)), ((), ())), preferred_element_type=jnp.float32)


def side_by_side(columns):
    rows = columns[0].shape[0]
    lane = lax.broadcasted_iota(jnp.int32, (rows, LANES), 1)
    result = jnp.zeros((rows, LANES), jnp.float32)
    for place, column in enumerate(columns):
        result = jnp.where(lane == place, column, result)
    return result


def member_rows(rows, shift):
    row = lax.broadcasted_iota(jnp.int32, (rows, 1), 0)
    return (row & (MIDDLE_DILATION - 1)) == shift


def lane_tiles(part):
    return [part[:, i : i + LANES] for i in range(0, part.shape[1], LANES)]


def weights(part, top):
    return jnp.exp2((part - top) * EXP2_SCALE)


def first_kernel(first, middle_ref, q_ref, k_ref, v_ref, kp_ref, own_ref, other_ref, state_ref):
    rows = q_ref.shape[0]
    members = rows // MIDDLE_DILATION
    column = lax.broadcasted_iota(jnp.int32, (1, rows), 1)
    tops, totals = [], []
    for place in range(GROUP):
        columns = head_columns(place)
        shift = middle_ref[first + GROUP * pl.program_id(0) + place]
        q = q_ref[:, columns]
        own = dot_keys(q, k_ref[:, columns])
        other = dot_keys(q, kp_ref[:, columns])
        top = functools.reduce(jnp.maximum, lane_tiles(own) + lane_tiles(other))
        top = jnp.max(top, axis=1, keepdims=True)
        row_is_member = member_rows(rows, shift)
        own, other = weights(own, top), weights(other, top)
        own_member = row_is_member & ((column & (MIDDLE_DILATION - 1)) == shift)
        own = jnp.where(own_member, own + own, own)
        twice = other[:, :LANES]
        twice = jnp.where(row_is_member & (column[:, :LANES] < members), twice + twice, twice)
        other = jnp.concatenate([twice, other[:, LANES:]], axis=1)
        total = functools.reduce(jnp.add, lane_tiles(own) + lane_tiles(other))
        tops.append(top)
        totals.append(jnp.sum(total, axis=1, keepdims=True))
        own_ref[:, columns] = dot(own.astype(jnp.bfloat16), v_ref[:, columns])
        other_ref[place] = other.astype(jnp.bfloat16)
    state_ref[...] = side_by_side(tops + totals)


def extra_kernel(
    middle_ref, coarse_ref, q_ref, own_ref, state_ref, cross_ref, diagonal_k_ref, diagonal_v_ref, coarse_kv_ref,
    sum_ref, share_ref,
):
    rows = q_ref.shape[0]
    members = rows // MIDDLE_DILATION
    row = lax.broadcasted_iota(jnp.int32, (rows, 1), 0)
    state = state_ref[...]
    devices = coarse_kv_ref.shape[0] // 2
    shares = []
    for place in range(GROUP):
        columns = head_columns(place)
        head = GROUP * pl.program_id(0) + place
        q = q_ref[:, columns]
        far_keys = jnp.concatenate([cross_ref[:members, columns], diagonal_k_ref[:, columns]], axis=0)
        far_values = jnp.concatenate([cross_ref[members:, columns], diagonal_v_ref[:, columns]], axis=0)
        far = jnp.where(member_rows(rows, middle_ref[head]), dot_keys(q, far_keys), MASKED)
        coarse = jnp.where(row == coarse_ref[head], dot_keys(q, coarse_kv_ref[:devices, columns]), MASKED)
        before = state[:, place : place + 1]
        top = jnp.maximum(before, jnp.max(far, axis=1, keepdims=True))
        top = jnp.maximum(top, jnp.max(coarse, axis=1, keepdims=True))
        far, coarse = weights(far, top), weights(coarse, top)
        kept = weights(before, top)
        total = kept * state[:, GROUP + place : GROUP + place + 1]
        total += jnp.sum(far, axis=1, keepdims=True) + jnp.sum(coarse, axis=1, keepdims=True)
        inverse = 1.0 / total
        share = kept * inverse
        summed = dot(far.astype(jnp.bfloat16), far_values) + dot(coarse.astype(jnp.bfloat16), coarse_kv_ref[devices:, columns])
        sum_ref[:, columns] = summed * inverse + own_ref[:, columns] * share
        shares.append(share)
    share_ref[...] = side_by_side(shares)


def finish_kernel(count, lane, sum_ref, share_ref, other_ref, vm_ref, vr_ref, *rest):
    out_ref = rest[-1]
    for place in range(count):
        columns = head_columns(place)
        values = jnp.concatenate([vm_ref[:, columns], vr_ref[:, columns]], axis=0)
        share = share_ref[:, lane + place : lane + place + 1]
        result = sum_ref[:, columns] + share * dot(other_ref[place], values)
        out_ref[:, columns] = result.astype(jnp.bfloat16)


def cost():
    return pl.CostEstimate(flops=0, bytes_accessed=0, transcendentals=0)


def gather_all(value, axis):
    size = lax.axis_size(axis)
    if size & (size - 1):
        return lax.all_gather(value, axis, axis=0, tiled=True)
    for j in range(size.bit_length() - 1):
        value = jnp.concatenate([value, partner(value, axis, 2**j)], axis=0)
    return value


def on_device(query, keys, values, middle_head_shift, coarse_head_shift):
    rows, width = query.shape
    members = rows // MIDDLE_DILATION
    bf16 = jnp.bfloat16
    smem = pl.BlockSpec(memory_space=pltpu.SMEM)
    vmem = pl.BlockSpec(memory_space=pltpu.VMEM)
    params = pltpu.CompilerParams(vmem_limit_bytes=32 * 1024 * 1024)
    order_scratch = pltpu.VMEM((MIDDLE_DILATION, rows, rows), bf16)

    other_keys = partner(keys, "inner", 1)
    prepared = pl.pallas_call(
        functools.partial(prepare_kernel, CHUNKS),
        out_shape=[
            jax.ShapeDtypeStruct((2 * members, width), bf16),
            jax.ShapeDtypeStruct((members, width), bf16),
            *[jax.ShapeDtypeStruct((rows - members, c * HEAD_FEATURES), bf16) for c in CHUNKS],
            jax.ShapeDtypeStruct((2, width), bf16),
        ],
        in_specs=[smem, smem, vmem, vmem],
        out_specs=[vmem] * (3 + len(CHUNKS)),
        scratch_shapes=[order_scratch],
        compiler_params=params,
        cost_estimate=cost(),
        name="prepare",
    )(middle_head_shift, coarse_head_shift, keys, values)
    own_members, own_vm, own_vr, coarse = prepared[0], prepared[1], prepared[2:-1], prepared[-1]
    cross = partner(own_members, "inner", 2)
    near = gather_all(coarse, "outer")
    near_cross = partner(near, "inner", 2)
    sent = jnp.concatenate([own_vm, near], axis=0)
    cross, own_vr = lax.optimization_barrier((cross, own_vr))
    other_vm = partner(sent, "inner", 1)
    other_vr = [partner(piece, "inner", 1) for piece in own_vr]
    other_ordered, other_km = pl.pallas_call(
        reorder_kernel,
        out_shape=[
            jax.ShapeDtypeStruct((rows, width), bf16),
            jax.ShapeDtypeStruct((members, width), bf16),
        ],
        in_specs=[smem, vmem],
        out_specs=[vmem, vmem],
        scratch_shapes=[order_scratch],
        compiler_params=params,
        cost_estimate=cost(),
        name="reorder",
    )(middle_head_shift, other_keys)
    diagonal_k = partner(other_km, "inner", 2)
    diagonal_v = partner(lax.optimization_barrier((other_vm, other_ordered))[0], "inner", 2)
    coarse = jnp.concatenate([near, near_cross, other_vm[members:], diagonal_v[members:]], axis=0)
    devices = coarse.shape[0] // 2
    coarse = coarse.reshape(devices, 2, width).transpose(1, 0, 2).reshape(2 * devices, width)

    def columns_of(count, heads=GROUP, first=0):
        return pl.BlockSpec((count, heads * HEAD_FEATURES), lambda i: (0, first // heads + i))

    groups = HEAD_COUNT // GROUP
    whole, part = columns_of(rows), columns_of(members)
    lanes = pl.BlockSpec((rows, LANES), lambda i: (0, i))
    per_head = pl.BlockSpec((GROUP, rows, rows), lambda i: (i, 0, 0))
    own_sum, other_weights, state = pl.pallas_call(
        functools.partial(first_kernel, 0),
        out_shape=[
            jax.ShapeDtypeStruct((rows, width), jnp.float32),
            jax.ShapeDtypeStruct((HEAD_COUNT, rows, rows), bf16),
            jax.ShapeDtypeStruct((rows, groups * LANES), jnp.float32),
        ],
        grid=(groups,),
        in_specs=[smem, whole, whole, whole, whole],
        out_specs=[whole, per_head, lanes],
        compiler_params=params,
        cost_estimate=cost(),
        name="first",
    )(middle_head_shift, query, keys, values, other_ordered)

    all_sum, share = pl.pallas_call(
        extra_kernel,
        out_shape=[
            jax.ShapeDtypeStruct((rows, width), jnp.float32),
            jax.ShapeDtypeStruct((rows, groups * LANES), jnp.float32),
        ],
        grid=(groups,),
        in_specs=[smem, smem, whole, whole, lanes, columns_of(2 * members), part, part, columns_of(2 * devices)],
        out_specs=[whole, lanes],
        compiler_params=params,
        cost_estimate=cost(),
        name="extra",
    )(
        middle_head_shift, coarse_head_shift, query, own_sum, state, cross, diagonal_k, diagonal_v, coarse
    )

    out = None
    first = 0
    for chunk, vr in zip(CHUNKS, other_vr):
        heads = min(GROUP, chunk)
        lane = first % GROUP
        block = columns_of(rows, heads, first)
        args = [all_sum, share, other_weights, other_vm, vr]
        specs = [
            block,
            pl.BlockSpec((rows, LANES), lambda i, first=first: (0, first // GROUP + i)),
            pl.BlockSpec((heads, rows, rows), lambda i, first=first, heads=heads: (first // heads + i, 0, 0)),
            columns_of(members, heads, first),
            columns_of(rows - members, heads),
        ]
        aliases = {}
        if out is not None:
            aliases = {len(args): 0}
            args.append(out)
            specs.append(pl.BlockSpec(memory_space=pl.ANY))
        out = pl.pallas_call(
            functools.partial(finish_kernel, heads, lane),
            out_shape=jax.ShapeDtypeStruct((rows, width), bf16),
            grid=(chunk // heads,),
            in_specs=specs,
            out_specs=block,
            input_output_aliases=aliases,
            compiler_params=params,
            cost_estimate=cost(),
            name="finish",
        )(*args)
        first += chunk
    return out


def solution(mesh):
    placed = (
        P(("outer", "inner"), None),
        P(("outer", "inner"), None),
        P(("outer", "inner"), None),
        P(),
        P(),
    )
    return jax.shard_map(
        on_device,
        mesh=mesh,
        in_specs=placed,
        out_specs=P(("outer", "inner"), None),
        check_vma=False,
    )
```

time: 71.8 us -> 81.7 us (1.14)
  local copies, waits for them, and re-layouts: 9.99 us -> 26.2 us
  starting transfers between devices: 19.2 us -> 15.3 us
  waiting for transfers between devices: 16.8 us -> 13.7 us
  Pallas kernels: 24.4 us -> 25.5 us
    unnamed x38, local copies, waits for them, and re-layouts: 7.16 us -> 14.4 us
    concatenate x2, local copies, waits for them, and re-layouts: 2.81 us -> 7.61 us  [the longest x1 5.63 us: on_device(): jnp.concatenate([near, near_cross, other_vm[members:], diagonal_v[members...]
    ppermute x14 -> x11, starting transfers between devices: 19.2 us -> 15.3 us  [partner(): return lax.ppermute(value, axis, pairs)]
    ppermute x14 -> x11, waiting for transfers between devices: 16.8 us -> 13.7 us  [partner(): return lax.ppermute(value, axis, pairs)]
    pallas_call x4, Pallas kernels: 18.6 us -> 21.2 us  [the longest x1 9.36 us: on_device(): pl.pallas_call(extra_kernel, out_shape=[jax.ShapeDtypeStruct((rows, width...]
    reshape x0 -> x1, local copies, waits for them, and re-layouts: none -> 1.85 us  [on_device(): coarse.reshape(devices, 2, width).transpose(1, 0, 2)]
    slice x0 -> x2, local copies, waits for them, and re-layouts: none -> 1.27 us  [the longest x1 0.64 us: on_device(): diagonal_v[members:]]
    transpose x0 -> x1, local copies, waits for them, and re-layouts: none -> 1.03 us  [on_device(): coarse.reshape(devices, 2, width).transpose(1, 0, 2)]
  transfers between devices with their start and end apart: 14 -> 11, of which waited for: 5 -> 5; matrix products, arithmetic and copies ran while one was open for 4% -> 15% of each run, Pallas kernels for 30% -> 29%
where the time goes in v2:
time: 81.7 us; the launch traced here: 80.9 us
  local copies, waits for them, and re-layouts  26.2 us (32%)
  Pallas kernels  25.5 us (31%)
  starting transfers between devices  15.3 us (19%)
  waiting for transfers between devices  13.7 us (17%)
    ppermute x11, starting transfers between devices, partner(): return lax.ppermute(value, axis, pairs)  15.3 us
    unnamed x38, local copies, waits for them, and re-layouts  14.4 us
    ppermute x11, waiting for transfers between devices, partner(): return lax.ppermute(value, axis, pairs)  13.7 us
    pallas_call x1, Pallas kernels, on_device(): pl.pallas_call(extra_kernel, out_shape=[jax.ShapeDtypeStruct((rows, width...  9.36 us
    pallas_call x1, Pallas kernels, on_device(): pl.pallas_call(functools.partial(first_kernel, 0), out_shape=[jax.ShapeDt...  6.56 us
    concatenate x1, local copies, waits for them, and re-layouts, on_device(): jnp.concatenate([near, near_cross, other_vm[members:], diagonal_v[members...  5.63 us
    pallas_call x2, Pallas kernels, on_device(): pl.pallas_call(functools.partial(finish_kernel, heads, lane), out_shape=j...  5.31 us
    pallas_call x1, Pallas kernels, on_device(): pl.pallas_call(functools.partial(prepare_kernel, CHUNKS), out_shape=[jax....  2.36 us
  transfers between devices with their start and end apart: 11, of which 5 were waited for; matrix products, arithmetic and copies ran while one was open for 15% of the time, Pallas kernels for 29%

profile of v2, /device:TPU:0, one launch (start us, length us, event | category | flops | bytes accessed | tf_op | source)
XLA Modules:
  0.0 80.9 jit_solution(3515697598863281031)
XLA Ops:
  0.0 2.9 %collective-permute-start = (bf16[256,2048]{1,0:T(8,128)(2,1)}, bf16[256,2048]{1,0:T(8,128)(2,1)S(1)}, u32[]{:S(2)}, u32[]{:S(2)}) collective-permute-start(bf16[256,2048]{1,0:T(8,128)(2,1)} %k_ref.3), channel_id=1, source_target_pairs={{0,8},{8,0},{16,24},{24,16},{1,9},{9,1},{17,25},{25,17},{2,10},{10... | collective-permute-start | bytes 3145736 | tf_op jit(solution)/shard_map/ppermute | solution.py:23
  2.9 1.3 %copy-done = bf16[256,2048]{1,0:T(8,128)(2,1)S(1)} copy-done((bf16[256,2048]{1,0:T(8,128)(2,1)S(1)}, bf16[256,2048]{1,0:T(8,128)(2,1)}, u32[]{:S(2)}) %copy-start) | copy-done | bytes 1048600
  4.2 1.2 %copy-done.2 = bf16[256,2048]{1,0:T(8,128)(2,1)S(1)} copy-done((bf16[256,2048]{1,0:T(8,128)(2,1)S(1)}, bf16[256,2048]{1,0:T(8,128)(2,1)}, u32[]{:S(2)}) %copy-start.2) | copy-done | bytes 1048600
  6.7 2.4 %prepare.1 = (bf16[128,2048]{1,0:T(8,128)(2,1)S(1)}, bf16[64,2048]{1,0:T(8,128)(2,1)S(1)}, bf16[192,1536]{1,0:T(8,128)(2,1)}, bf16[192,512]{1,0:T(8,128)(2,1)S(1)}, bf16[2,2048]{1,0:T(2,128)(2,1)S(1)}) custom-call(s32[16]{0:T(128)S(1)} %copy-done.14, s32[16]{0:T(128)S(1)} %copy-done.16, bf16[256,2048]{1,0:T(8,128)(2,1)S(1)} %copy-done, ...), custom_call_target="tpu_custom_call" | custom-call | tf_op jit(solution)/shard_map/prepare/pallas_call | solution.py:206
  9.8 1.5 %collective-permute-start.1 = (bf16[128,2048]{1,0:T(8,128)(2,1)S(1)}, bf16[128,2048]{1,0:T(8,128)(2,1)S(1)}, u32[]{:S(2)}, u32[]{:S(2)}) collective-permute-start(bf16[128,2048]{1,0:T(8,128)(2,1)S(1)} %get-tuple-element.24), channel_id=1, source_target_pairs={{0,16},{8,24},{16,0},{24,8},{1,17},{9,25},{17,1},{25,9},{2,18},{10... | collective-permute-start | bytes 1572872 | tf_op jit(solution)/shard_map/ppermute | solution.py:23
  11.3 1.6 %collective-permute-start.4 = (bf16[4,2048]{1,0:T(4,128)(2,1)S(1)}, bf16[4,2048]{1,0:T(4,128)(2,1)S(1)}, u32[]{:S(2)}, u32[]{:S(2)}) collective-permute-start(bf16[4,2048]{1,0:T(4,128)(2,1)S(1)} %pad_maximum_fusion.2), channel_id=1, source_target_pairs={{0,2},{1,3},{2,0},{3,1},{4,6},{5,7},{6,4},{7,5},{8,10},{9,11},{10,... | collective-permute-start | bytes 49160 | tf_op jit(solution)/shard_map/ppermute | solution.py:23
  13.0 2.2 %collective-permute-done.4 = bf16[4,2048]{1,0:T(4,128)(2,1)S(1)} collective-permute-done((bf16[4,2048]{1,0:T(4,128)(2,1)S(1)}, bf16[4,2048]{1,0:T(4,128)(2,1)S(1)}, u32[]{:S(2)}, u32[]{:S(2)}) %collective-permute-start.4) | collective-permute-done | bytes 16416 | tf_op jit(solution)/shard_map/ppermute | solution.py:23
  15.2 2.7 %collective-permute-start.5 = (bf16[8,2048]{1,0:T(8,128)(2,1)S(1)}, bf16[8,2048]{1,0:T(8,128)(2,1)S(1)}, u32[]{:S(2)}, u32[]{:S(2)}) collective-permute-start(bf16[8,2048]{1,0:T(8,128)(2,1)S(1)} %pad_maximum_fusion.1), channel_id=1, source_target_pairs={{0,4},{1,5},{2,6},{3,7},{4,0},{5,1},{6,2},{7,3},{8,12},{9,13},{10,... | collective-permute-start | bytes 98312 | tf_op jit(solution)/shard_map/ppermute | solution.py:23
  17.8 2.2 %collective-permute-done.5 = bf16[8,2048]{1,0:T(8,128)(2,1)S(1)} collective-permute-done((bf16[8,2048]{1,0:T(8,128)(2,1)S(1)}, bf16[8,2048]{1,0:T(8,128)(2,1)S(1)}, u32[]{:S(2)}, u32[]{:S(2)}) %collective-permute-start.5) | collective-permute-done | bytes 32800 | tf_op jit(solution)/shard_map/ppermute | solution.py:23
  20.1 2.0 %concatenate.21 = bf16[80,2048]{1,0:T(8,128)(2,1)} concatenate(bf16[64,2048]{1,0:T(8,128)(2,1)S(1)} %get-tuple-element.29, bf16[2,2048]{1,0:T(2,128)(2,1)S(1)} %get-tuple-element.30, bf16[2,2048]{1,0:T(2,128)(2,1)S(1)} %collective-permute-done.3, bf16[4,2048]{1,0:T(4,128)(2,1)S(1)} %collective-permute-done.4, bf16[8,2048]{1,0:T(8,128)(2,1)S(1)} %collective-permute-done.5), dimensions={0} | concatenate | bytes 655360 | tf_op jit(solution)/shard_map/concatenate | solution.py:225
  22.6 1.6 %collective-permute-done.1.cross_ref = bf16[128,2048]{1,0:T(8,128)(2,1)S(1)} collective-permute-done((bf16[128,2048]{1,0:T(8,128)(2,1)S(1)}, bf16[128,2048]{1,0:T(8,128)(2,1)S(1)}, u32[]{:S(2)}, u32[]{:S(2)}) %collective-permute-start.1) | collective-permute-done | bytes 524320 | tf_op jit(solution)/shard_map/ppermute | solution.py:23
  24.4 2.7 %collective-permute-done.k_ref = bf16[256,2048]{1,0:T(8,128)(2,1)S(1)} collective-permute-done((bf16[256,2048]{1,0:T(8,128)(2,1)}, bf16[256,2048]{1,0:T(8,128)(2,1)S(1)}, u32[]{:S(2)}, u32[]{:S(2)}) %collective-permute-start) | collective-permute-done | bytes 1048608 | tf_op jit(solution)/shard_map/ppermute | solution.py:23
  27.1 1.9 %reorder.1 = (bf16[256,2048]{1,0:T(8,128)(2,1)S(1)}, bf16[64,2048]{1,0:T(8,128)(2,1)}) custom-call(s32[16]{0:T(128)S(1)} %copy-done.15, bf16[256,2048]{1,0:T(8,128)(2,1)S(1)} %collective-permute-done.k_ref), custom_call_target="tpu_custom_call" | custom-call | tf_op jit(solution)/shard_map/reorder/pallas_call | solution.py:229
  29.1 5.1 %collective-permute-done.6.vm_ref = bf16[80,2048]{1,0:T(8,128)(2,1)S(1)} collective-permute-done((bf16[80,2048]{1,0:T(8,128)(2,1)}, bf16[80,2048]{1,0:T(8,128)(2,1)S(1)}, u32[]{:S(2)}, u32[]{:S(2)}) %collective-permute-start.6) | collective-permute-done | bytes 327712 | tf_op jit(solution)/shard_map/ppermute | solution.py:23
  34.2 2.1 %collective-permute-start.7 = (bf16[80,2048]{1,0:T(8,128)(2,1)S(1)}, bf16[80,2048]{1,0:T(8,128)(2,1)S(1)}, u32[]{:S(2)}, u32[]{:S(2)}) collective-permute-start(bf16[80,2048]{1,0:T(8,128)(2,1)S(1)} %collective-permute-done.6.vm_ref), channel_id=1, source_target_pairs={{0,16},{8,24},{16,0},{24,8},{1,17},{9,25},{17,1},{25,9},{2,18},{10... | collective-permute-start | bytes 983048 | tf_op jit(solution)/shard_map/ppermute | solution.py:23
  36.2 1.5 %collective-permute-start.9 = (bf16[192,512]{1,0:T(8,128)(2,1)}, bf16[192,512]{1,0:T(8,128)(2,1)}, u32[]{:S(2)}, u32[]{:S(2)}) collective-permute-start(bf16[192,512]{1,0:T(8,128)(2,1)} %copy-done.18), channel_id=1, source_target_pairs={{0,8},{8,0},{16,24},{24,16},{1,9},{9,1},{17,25},{25,17},{2,10},{10... | collective-permute-start | bytes 589832 | tf_op jit(solution)/shard_map/ppermute | solution.py:23
  38.3 1.6 %collective-permute-start.8 = (bf16[16,2048]{1,0:T(8,128)(2,1)S(1)}, bf16[16,2048]{1,0:T(8,128)(2,1)}, u32[]{:S(2)}, u32[]{:S(2)}) collective-permute-start(bf16[16,2048]{1,0:T(8,128)(2,1)S(1)} %pad_maximum_fusion), channel_id=1, source_target_pairs={{0,16},{8,24},{16,0},{24,8},{1,17},{9,25},{17,1},{25,9},{2,18},{10... | collective-permute-start | bytes 196616 | tf_op jit(solution)/shard_map/ppermute | solution.py:23
  40.5 1.2 %copy-done.3 = bf16[256,2048]{1,0:T(8,128)(2,1)S(1)} copy-done((bf16[256,2048]{1,0:T(8,128)(2,1)S(1)}, bf16[256,2048]{1,0:T(8,128)(2,1)}, u32[]{:S(2)}) %copy-start.3) | copy-done | bytes 1048600
  41.7 1.2 %copy-done.4 = bf16[256,2048]{1,0:T(8,128)(2,1)S(1)} copy-done((bf16[256,2048]{1,0:T(8,128)(2,1)S(1)}, bf16[256,2048]{1,0:T(8,128)(2,1)}, u32[]{:S(2)}) %copy-start.4) | copy-done | bytes 1048600
  43.0 6.6 %first.1 = (f32[256,2048]{1,0:T(8,128)S(1)}, bf16[16,256,256]{2,1,0:T(8,128)(2,1)S(1)}, f32[256,512]{1,0:T(8,128)S(1)}) custom-call(s32[16]{0:T(128)S(1)} %copy-done.15, bf16[256,2048]{1,0:T(8,128)(2,1)S(1)} %copy-done.4, bf16[256,2048]{1,0:T(8,128)(2,1)S(1)} %copy-done.1, bf16[256,2048]{1,0:T(8,128)(2,1)S(1)} %copy-done.3, ...), custom_call_target="tpu_custom_call" | custom-call | tf_op jit(solution)/shard_map/first/pallas_call | solution.py:255
  49.5 1.3 %copy-done.6 = f32[256,2048]{1,0:T(8,128)} copy-done((f32[256,2048]{1,0:T(8,128)}, f32[256,2048]{1,0:T(8,128)S(1)}, u32[]{:S(2)}) %copy-start.6) | copy-done | bytes 2097176
  50.9 0.8 copy-done.10
  53.1 5.6 %concatenate.23 = bf16[64,2048]{1,0:T(8,128)(2,1)} concatenate(bf16[2,2048]{1,0:T(2,128)(2,1)S(1)} %get-tuple-element.30, bf16[2,2048]{1,0:T(2,128)(2,1)S(1)} %collective-permute-done.3, bf16[4,2048]{1,0:T(4,128)(2,1)S(1)} %collective-permute-done.4, bf16[8,2048]{1,0:T(8,128)(2,1)S(1)} %collective-permute-done.5, bf16[16,2048]{1,0:T(8,128)(2,1)} %collective-permute-done.8, ...), dimensions={0} | concatenate | bytes 524288 | tf_op jit(solution)/shard_map/concatenate | solution.py:244
  58.7 1.9 %reshape.6 = bf16[32,2,2048]{2,1,0:T(2,128)(2,1)} reshape(bf16[64,2048]{1,0:T(8,128)(2,1)} %concatenate.23) | data formatting | bytes 524288 | tf_op jit(solution)/shard_map/reshape | solution.py:246
  60.5 1.0 %copy.7 = bf16[2,32,2048]{2,1,0:T(8,128)(2,1)S(1)} copy(bf16[2,32,2048]{2,0,1:T(2,128)(2,1)} %bitcast.3) | data formatting | bytes 524288 | tf_op jit(solution)/shard_map/transpose | solution.py:246
  61.6 1.6 %copy-done.7 = f32[256,2048]{1,0:T(8,128)S(1)} copy-done((f32[256,2048]{1,0:T(8,128)S(1)}, f32[256,2048]{1,0:T(8,128)}, u32[]{:S(2)}) %copy-start.7) | copy-done | bytes 2097176
  63.2 1.0 %copy-done.9 = bf16[128,2048]{1,0:T(8,128)(2,1)S(1)} copy-done((bf16[128,2048]{1,0:T(8,128)(2,1)S(1)}, bf16[128,2048]{1,0:T(8,128)(2,1)}, u32[]{:S(2)}) %copy-start.9) | copy-done | bytes 524312
  64.2 1.0 %copy-done.11 = f32[256,512]{1,0:T(8,128)S(1)} copy-done((f32[256,512]{1,0:T(8,128)S(1)}, f32[256,512]{1,0:T(8,128)}, u32[]{:S(2)}) %copy-start.11) | copy-done | bytes 524312
  65.3 1.0 %copy-done.13 = bf16[80,2048]{1,0:T(8,128)(2,1)S(1)} copy-done((bf16[80,2048]{1,0:T(8,128)(2,1)S(1)}, bf16[80,2048]{1,0:T(8,128)(2,1)}, u32[]{:S(2)}) %copy-start.13) | copy-done | bytes 327704
  66.3 9.4 %extra.1 = (f32[256,2048]{1,0:T(8,128)S(1)}, f32[256,512]{1,0:T(8,128)S(1)}) custom-call(s32[16]{0:T(128)S(1)} %copy-done.15, s32[16]{0:T(128)S(1)} %copy-done.17, bf16[256,2048]{1,0:T(8,128)(2,1)S(1)} %copy-done.5, f32[256,2048]{1,0:T(8,128)S(1)} %copy-done.7, f32[256,512]{1,0:T(8,128)S(1)} %copy-done.11, bf16[128,2048]{1,0:T(8,128)(2,1)S(1)} %copy-done.9, ...), custom_call_target="tpu_custom_call" | custom-call | tf_op jit(solution)/shard_map/extra/pallas_call | solution.py:270
  75.6 3.3 %finish.2.rest_0_ = bf16[256,2048]{1,0:T(8,128)(2,1)} custom-call(f32[256,2048]{1,0:T(8,128)S(1)} %get-tuple-element.32.sum_ref, f32[256,512]{1,0:T(8,128)S(1)} %get-tuple-element.33.share_ref, bf16[16,256,256]{2,1,0:T(8,128)(2,1)S(1)} %get-tuple-element.34.other_ref, bf16[80,2048]{1,0:T(8,128)(2,1)S(1)} %collective-permute-done.6.vm_ref, ...), custom_call_target="tpu_custom_call" | custom-call | tf_op jit(solution)/shard_map/finish/pallas_call | solution.py:305
  79.0 2.0 %finish.3 = bf16[256,2048]{1,0:T(8,128)(2,1)} custom-call(f32[256,2048]{1,0:T(8,128)S(1)} %get-tuple-element.32.sum_ref, f32[256,512]{1,0:T(8,128)S(1)} %get-tuple-element.33.share_ref, bf16[16,256,256]{2,1,0:T(8,128)(2,1)S(1)} %get-tuple-element.34.other_ref, bf16[80,2048]{1,0:T(8,128)(2,1)S(1)} %collective-permute-done.6.vm_ref, ...), custom_call_target="tpu_custom_call", output_to_operand_aliasing={{}: (5, {})} | custom-call | tf_op jit(solution)/shard_map/finish/pallas_call | solution.py:305
  (43 shorter events, 5.5 us)
Async XLA Ops:
  0.0 27.1 %collective-permute-start = (bf16[256,2048]{1,0:T(8,128)(2,1)}, bf16[256,2048]{1,0:T(8,128)(2,1)S(1)}, u32[]{:S(2)}, u32[]{:S(2)}) collective-permute-start(bf16[256,2048]{1,0:T(8,128)(2,1)} %k_ref.3), channel_id=1, source_target_pairs={{0,8},{8,0},{16,24},{24,16},{1,9},{9,1},{17,25},{25,17},{2,10},{10... | collective-permute-start | bytes 3145736 | tf_op jit(solution)/shard_map/ppermute | solution.py:23
  2.9 1.3 %copy-start = (bf16[256,2048]{1,0:T(8,128)(2,1)S(1)}, bf16[256,2048]{1,0:T(8,128)(2,1)}, u32[]{:S(2)}) copy-start(bf16[256,2048]{1,0:T(8,128)(2,1)} %k_ref.3) | copy-start | bytes 3145732
  4.2 1.2 %copy-start.2 = (bf16[256,2048]{1,0:T(8,128)(2,1)S(1)}, bf16[256,2048]{1,0:T(8,128)(2,1)}, u32[]{:S(2)}) copy-start(bf16[256,2048]{1,0:T(8,128)(2,1)} %v_ref.3) | copy-start | bytes 3145732
  5.4 0.7 copy-start.14
  6.1 0.7 copy-start.16
  6.7 20.4 %copy-start.15 = (s32[16]{0:T(128)S(1)}, s32[16]{0:T(128)}, u32[]{:S(2)}) copy-start(s32[16]{0:T(128)} %middle_ref.7) | copy-start | bytes 196
  6.7 33.8 %copy-start.1 = (bf16[256,2048]{1,0:T(8,128)(2,1)S(1)}, bf16[256,2048]{1,0:T(8,128)(2,1)}, u32[]{:S(2)}) copy-start(bf16[256,2048]{1,0:T(8,128)(2,1)} %k_ref.3) | copy-start | bytes 3145732
  9.1 0.7 copy-start.18
  9.8 1.5 %collective-permute-start.3 = (bf16[2,2048]{1,0:T(2,128)(2,1)S(1)}, bf16[2,2048]{1,0:T(2,128)(2,1)S(1)}, u32[]{:S(2)}, u32[]{:S(2)}) collective-permute-start(bf16[2,2048]{1,0:T(2,128)(2,1)S(1)} %get-tuple-element.30), channel_id=1, source_target_pairs={{0,1},{1,0},{2,3},{3,2},{4,5},{5,4},{6,7},{7,6},{8,9},{9,8},{10,11... | collective-permute-start | bytes 24584 | tf_op jit(solution)/shard_map/ppermute | solution.py:23
  9.8 14.3 %collective-permute-start.1 = (bf16[128,2048]{1,0:T(8,128)(2,1)S(1)}, bf16[128,2048]{1,0:T(8,128)(2,1)S(1)}, u32[]{:S(2)}, u32[]{:S(2)}) collective-permute-start(bf16[128,2048]{1,0:T(8,128)(2,1)S(1)} %get-tuple-element.24), channel_id=1, source_target_pairs={{0,16},{8,24},{16,0},{24,8},{1,17},{9,25},{17,1},{25,9},{2,18},{10... | collective-permute-start | bytes 1572872 | tf_op jit(solution)/shard_map/ppermute | solution.py:23
  11.3 3.8 %collective-permute-start.4 = (bf16[4,2048]{1,0:T(4,128)(2,1)S(1)}, bf16[4,2048]{1,0:T(4,128)(2,1)S(1)}, u32[]{:S(2)}, u32[]{:S(2)}) collective-permute-start(bf16[4,2048]{1,0:T(4,128)(2,1)S(1)} %pad_maximum_fusion.2), channel_id=1, source_target_pairs={{0,2},{1,3},{2,0},{3,1},{4,6},{5,7},{6,4},{7,5},{8,10},{9,11},{10,... | collective-permute-start | bytes 49160 | tf_op jit(solution)/shard_map/ppermute | solution.py:23
  15.2 4.9 %collective-permute-start.5 = (bf16[8,2048]{1,0:T(8,128)(2,1)S(1)}, bf16[8,2048]{1,0:T(8,128)(2,1)S(1)}, u32[]{:S(2)}, u32[]{:S(2)}) collective-permute-start(bf16[8,2048]{1,0:T(8,128)(2,1)S(1)} %pad_maximum_fusion.1), channel_id=1, source_target_pairs={{0,4},{1,5},{2,6},{3,7},{4,0},{5,1},{6,2},{7,3},{8,12},{9,13},{10,... | collective-permute-start | bytes 98312 | tf_op jit(solution)/shard_map/ppermute | solution.py:23
  22.0 12.1 %collective-permute-start.6 = (bf16[80,2048]{1,0:T(8,128)(2,1)}, bf16[80,2048]{1,0:T(8,128)(2,1)S(1)}, u32[]{:S(2)}, u32[]{:S(2)}) collective-permute-start(bf16[80,2048]{1,0:T(8,128)(2,1)} %concatenate.21), channel_id=1, source_target_pairs={{0,8},{8,0},{16,24},{24,16},{1,9},{9,1},{17,25},{25,17},{2,10},{10... | collective-permute-start | bytes 983048 | tf_op jit(solution)/shard_map/ppermute | solution.py:23
  24.1 15.8 %copy-start.8 = (bf16[128,2048]{1,0:T(8,128)(2,1)}, bf16[128,2048]{1,0:T(8,128)(2,1)S(1)}, u32[]{:S(2)}) copy-start(bf16[128,2048]{1,0:T(8,128)(2,1)S(1)} %collective-permute-done.1.cross_ref) | copy-start | bytes 1572868
  24.1 51.5 %collective-permute-start.10 = (bf16[192,1536]{1,0:T(8,128)(2,1)}, bf16[192,1536]{1,0:T(8,128)(2,1)}, u32[]{:S(2)}, u32[]{:S(2)}) collective-permute-start(bf16[192,1536]{1,0:T(8,128)(2,1)} %get-tuple-element.36), channel_id=1, source_target_pairs={{0,8},{8,0},{16,24},{24,16},{1,9},{9,1},{17,25},{25,17},{2,10},{10... | collective-permute-start | bytes 1769480 | tf_op jit(solution)/shard_map/ppermute | solution.py:23
  34.2 17.5 %collective-permute-start.7 = (bf16[80,2048]{1,0:T(8,128)(2,1)S(1)}, bf16[80,2048]{1,0:T(8,128)(2,1)S(1)}, u32[]{:S(2)}, u32[]{:S(2)}) collective-permute-start(bf16[80,2048]{1,0:T(8,128)(2,1)S(1)} %collective-permute-done.6.vm_ref), channel_id=1, source_target_pairs={{0,16},{8,24},{16,0},{24,8},{1,17},{9,25},{17,1},{25,9},{2,18},{10... | collective-permute-start | bytes 983048 | tf_op jit(solution)/shard_map/ppermute | solution.py:23
  36.2 42.7 %collective-permute-start.9 = (bf16[192,512]{1,0:T(8,128)(2,1)}, bf16[192,512]{1,0:T(8,128)(2,1)}, u32[]{:S(2)}, u32[]{:S(2)}) collective-permute-start(bf16[192,512]{1,0:T(8,128)(2,1)} %copy-done.18), channel_id=1, source_target_pairs={{0,8},{8,0},{16,24},{24,16},{1,9},{9,1},{17,25},{25,17},{2,10},{10... | collective-permute-start | bytes 589832 | tf_op jit(solution)/shard_map/ppermute | solution.py:23
  37.7 23.8 %collective-permute-start.2 = (bf16[64,2048]{1,0:T(8,128)(2,1)}, bf16[64,2048]{1,0:T(8,128)(2,1)}, u32[]{:S(2)}, u32[]{:S(2)}) collective-permute-start(bf16[64,2048]{1,0:T(8,128)(2,1)} %get-tuple-element.28), channel_id=1, source_target_pairs={{0,16},{8,24},{16,0},{24,8},{1,17},{9,25},{17,1},{25,9},{2,18},{10... | collective-permute-start | bytes 786440 | tf_op jit(solution)/shard_map/ppermute | solution.py:23
  38.3 14.8 %collective-permute-start.8 = (bf16[16,2048]{1,0:T(8,128)(2,1)S(1)}, bf16[16,2048]{1,0:T(8,128)(2,1)}, u32[]{:S(2)}, u32[]{:S(2)}) collective-permute-start(bf16[16,2048]{1,0:T(8,128)(2,1)S(1)} %pad_maximum_fusion), channel_id=1, source_target_pairs={{0,16},{8,24},{16,0},{24,8},{1,17},{9,25},{17,1},{25,9},{2,18},{10... | collective-permute-start | bytes 196616 | tf_op jit(solution)/shard_map/ppermute | solution.py:23
  40.5 1.2 %copy-start.3 = (bf16[256,2048]{1,0:T(8,128)(2,1)S(1)}, bf16[256,2048]{1,0:T(8,128)(2,1)}, u32[]{:S(2)}) copy-start(bf16[256,2048]{1,0:T(8,128)(2,1)} %v_ref.3) | copy-start | bytes 3145732
  41.7 1.2 %copy-start.4 = (bf16[256,2048]{1,0:T(8,128)(2,1)S(1)}, bf16[256,2048]{1,0:T(8,128)(2,1)}, u32[]{:S(2)}) copy-start(bf16[256,2048]{1,0:T(8,128)(2,1)} %q_ref.3) | copy-start | bytes 3145732
  43.0 18.6 %copy-start.17 = (s32[16]{0:T(128)S(1)}, s32[16]{0:T(128)}, u32[]{:S(2)}) copy-start(s32[16]{0:T(128)} %coarse_ref.3) | copy-start | bytes 196
  49.5 1.4 %copy-start.6 = (f32[256,2048]{1,0:T(8,128)}, f32[256,2048]{1,0:T(8,128)S(1)}, u32[]{:S(2)}) copy-start(f32[256,2048]{1,0:T(8,128)S(1)} %get-tuple-element.22.own_ref) | copy-start | bytes 6291460
  50.9 0.8 copy-start.10
  51.7 9.9 %copy-start.5 = (bf16[256,2048]{1,0:T(8,128)(2,1)S(1)}, bf16[256,2048]{1,0:T(8,128)(2,1)}, u32[]{:S(2)}) copy-start(bf16[256,2048]{1,0:T(8,128)(2,1)} %q_ref.3) | copy-start | bytes 3145732
  52.3 0.7 copy-start.12
  61.6 1.6 %copy-start.7 = (f32[256,2048]{1,0:T(8,128)S(1)}, f32[256,2048]{1,0:T(8,128)}, u32[]{:S(2)}) copy-start(f32[256,2048]{1,0:T(8,128)} %copy-done.6) | copy-start | bytes 6291460
  63.2 1.0 %copy-start.9 = (bf16[128,2048]{1,0:T(8,128)(2,1)S(1)}, bf16[128,2048]{1,0:T(8,128)(2,1)}, u32[]{:S(2)}) copy-start(bf16[128,2048]{1,0:T(8,128)(2,1)} %copy-done.8) | copy-start | bytes 1572868
  64.2 1.0 %copy-start.11 = (f32[256,512]{1,0:T(8,128)S(1)}, f32[256,512]{1,0:T(8,128)}, u32[]{:S(2)}) copy-start(f32[256,512]{1,0:T(8,128)} %copy-done.10) | copy-start | bytes 1572868
  65.3 1.0 %copy-start.13 = (bf16[80,2048]{1,0:T(8,128)(2,1)S(1)}, bf16[80,2048]{1,0:T(8,128)(2,1)}, u32[]{:S(2)}) copy-start(bf16[80,2048]{1,0:T(8,128)(2,1)} %copy-done.12) | copy-start | bytes 983044

commit v3 on v2

v3 whole, which is shorter than its diff:
```python
import functools

import jax
import jax.numpy as jnp
from jax import lax
from jax.experimental import pallas as pl
from jax.experimental.pallas import tpu as pltpu
from jax.sharding import PartitionSpec as P

HEAD_COUNT = 16
HEAD_FEATURES = 128
MIDDLE_DILATION = 4
CHUNKS = (12, 4)
GROUP = 4
LANES = 128
SUBLANES = 16
EXP2_SCALE = HEAD_FEATURES ** (-0.5) * 1.4426950408889634
MASKED = -1e30


def partner(value, axis, mask):
    pairs = [(source, source ^ mask) for source in range(lax.axis_size(axis))]
    return lax.ppermute(value, axis, pairs)


def one_hot(mask):
    return mask.astype(jnp.float32).astype(jnp.bfloat16)


def fill_orders(order_ref):
    rows = order_ref.shape[1]
    members = rows // MIDDLE_DILATION
    group = lax.broadcasted_iota(jnp.int32, (members, rows), 0)
    token = lax.broadcasted_iota(jnp.int32, (members, rows), 1)
    for place in range(MIDDLE_DILATION):
        block = one_hot(token == MIDDLE_DILATION * group + place)
        for shift in range(MIDDLE_DILATION):
            slot = (place - shift) % MIDDLE_DILATION
            order_ref[shift, slot * members : (slot + 1) * members] = block


def dot(a, b):
    return jnp.dot(a, b, preferred_element_type=jnp.float32)


def head_columns(head):
    return slice(head * HEAD_FEATURES, (head + 1) * HEAD_FEATURES)


def prepare_kernel(chunks, middle_ref, coarse_ref, k_ref, v_ref, members_ref, vm_ref, *rest):
    vr_refs, coarse_out_ref, order_ref = rest[: len(chunks)], rest[-2], rest[-1]
    rows = k_ref.shape[0]
    members = rows // MIDDLE_DILATION
    fill_orders(order_ref)
    token = lax.broadcasted_iota(jnp.int32, (SUBLANES, rows), 1)
    first_row = lax.broadcasted_iota(jnp.int32, (SUBLANES, rows), 0) == 0
    second_row = lax.broadcasted_iota(jnp.int32, (SUBLANES, rows), 0) == 1
    head = 0
    for chunk, vr_ref in zip(chunks, vr_refs):
        for place in range(chunk):
            columns = head_columns(head)
            order = order_ref[middle_ref[head]]
            k, v = k_ref[:, columns], v_ref[:, columns]
            v_ordered = dot(order, v).astype(jnp.bfloat16)
            k_members = dot(order[:members], k).astype(jnp.bfloat16)
            members_ref[:members, columns] = k_members
            members_ref[members:, columns] = v_ordered[:members]
            vm_ref[:members, columns] = v_ordered[:members]
            vr_ref[:, head_columns(place)] = v_ordered[members:]
            chosen = token == coarse_ref[head]
            picked = dot(one_hot(chosen & first_row), k) + dot(one_hot(chosen & second_row), v)
            coarse_out_ref[:, columns] = picked[:2].astype(jnp.bfloat16)
            head += 1


def append_kernel(near_ref, vm_ref, out_ref, semaphore):
    rows = near_ref.shape[0]
    first = out_ref.shape[0] - rows
    copy = pltpu.make_async_copy(near_ref, out_ref.at[pl.ds(first, rows)], semaphore)
    copy.start()
    copy.wait()


def reorder_kernel(middle_ref, k_ref, near_ref, ordered_ref, members_ref, order_ref):
    members = k_ref.shape[0] // MIDDLE_DILATION
    fill_orders(order_ref)
    members_ref[members:] = near_ref[...]
    for head in range(HEAD_COUNT):
        columns = head_columns(head)
        ordered = dot(order_ref[middle_ref[head]], k_ref[:, columns]).astype(jnp.bfloat16)
        ordered_ref[:, columns] = ordered
        members_ref[:members, columns] = ordered[:members]


def dot_keys(q, keys):
    return lax.dot_general(q, keys, (((1,), (1,)), ((), ())), preferred_element_type=jnp.float32)


def dot_rows(a, b):
    return lax.dot_general(a, b, (((0,), (0,)), ((), ())), preferred_element_type=jnp.float32)


def side_by_side(columns):
    rows = columns[0].shape[0]
    lane = lax.broadcasted_iota(jnp.int32, (rows, LANES), 1)
    result = jnp.zeros((rows, LANES), jnp.float32)
    for place, column in enumerate(columns):
        result = jnp.where(lane == place, column, result)
    return result


def member_rows(rows, shift):
    row = lax.broadcasted_iota(jnp.int32, (rows, 1), 0)
    return (row & (MIDDLE_DILATION - 1)) == shift


def lane_tiles(part):
    return [part[:, i : i + LANES] for i in range(0, part.shape[1], LANES)]


def weights(part, top):
    return jnp.exp2((part - top) * EXP2_SCALE)


def first_kernel(first, middle_ref, q_ref, k_ref, v_ref, kp_ref, own_ref, other_ref, state_ref):
    rows = q_ref.shape[0]
    members = rows // MIDDLE_DILATION
    column = lax.broadcasted_iota(jnp.int32, (1, rows), 1)
    tops, totals = [], []
    for place in range(GROUP):
        columns = head_columns(place)
        shift = middle_ref[first + GROUP * pl.program_id(0) + place]
        q = q_ref[:, columns]
        own = dot_keys(q, k_ref[:, columns])
        other = dot_keys(q, kp_ref[:, columns])
        top = functools.reduce(jnp.maximum, lane_tiles(own) + lane_tiles(other))
        top = jnp.max(top, axis=1, keepdims=True)
        row_is_member = member_rows(rows, shift)
        own, other = weights(own, top), weights(other, top)
        own_member = row_is_member & ((column & (MIDDLE_DILATION - 1)) == shift)
        own = jnp.where(own_member, own + own, own)
        twice = other[:, :LANES]
        twice = jnp.where(row_is_member & (column[:, :LANES] < members), twice + twice, twice)
        other = jnp.concatenate([twice, other[:, LANES:]], axis=1)
        total = functools.reduce(jnp.add, lane_tiles(own) + lane_tiles(other))
        tops.append(top)
        totals.append(jnp.sum(total, axis=1, keepdims=True))
        own_ref[:, columns] = dot(own.astype(jnp.bfloat16), v_ref[:, columns])
        other_ref[place] = other.astype(jnp.bfloat16)
    state_ref[...] = side_by_side(tops + totals)


def extra_kernel(
    middle_ref, coarse_ref, q_ref, state_ref, cross_ref, diagonal_k_ref, diagonal_v_ref, near_ref, other_ref,
    sum_ref, share_ref,
):
    rows = q_ref.shape[0]
    members = rows // MIDDLE_DILATION
    token = lax.broadcasted_iota(jnp.int32, (1, rows), 1)
    state = state_ref[...].T
    shares = []
    for place in range(GROUP):
        columns = head_columns(place)
        head = GROUP * pl.program_id(0) + place
        q = q_ref[:, columns]
        far_keys = jnp.concatenate([cross_ref[:members, columns], diagonal_k_ref[:members, columns]], axis=0)
        far_values = jnp.concatenate([cross_ref[members:, columns], diagonal_v_ref[:members, columns]], axis=0)
        pieces = [near_ref[:, columns]] + [
            ref[members:, columns] for ref in (other_ref, diagonal_k_ref, diagonal_v_ref)
        ]
        pairs = jnp.concatenate(pieces, axis=0)
        is_key = (lax.broadcasted_iota(jnp.int32, (pairs.shape[0], 1), 0) & 1) == 0
        row_is_member = (token & (MIDDLE_DILATION - 1)) == middle_ref[head]
        far = jnp.where(row_is_member, dot_keys(far_keys, q), MASKED)
        coarse = jnp.where(is_key & (token == coarse_ref[head]), dot_keys(pairs, q), MASKED)
        before = state[place : place + 1]
        top = jnp.maximum(before, jnp.max(far, axis=0, keepdims=True))
        top = jnp.maximum(top, jnp.max(coarse, axis=0, keepdims=True))
        far, coarse = weights(far, top), weights(coarse, top)
        kept = weights(before, top)
        total = kept * state[GROUP + place : GROUP + place + 1]
        total += jnp.sum(far, axis=0, keepdims=True) + jnp.sum(coarse, axis=0, keepdims=True)
        inverse = 1.0 / total
        coarse = pltpu.roll(coarse, 1, 0)
        summed = dot_rows(far_values, far.astype(jnp.bfloat16)) + dot_rows(pairs, coarse.astype(jnp.bfloat16))
        sum_ref[:, columns] = (summed * inverse).T
        shares.append(kept * inverse)
    shares.append(jnp.zeros((SUBLANES - GROUP, rows), jnp.float32))
    share_ref[:, :SUBLANES] = jnp.concatenate(shares, axis=0).T


def finish_kernel(count, lane, sum_ref, share_ref, own_ref, other_ref, vm_ref, vr_ref, *rest):
    out_ref = rest[-1]
    for place in range(count):
        columns = head_columns(place)
        values = jnp.concatenate([vm_ref[:, columns], vr_ref[:, columns]], axis=0)
        share = share_ref[:, lane + place : lane + place + 1]
        result = own_ref[:, columns] + dot(other_ref[place], values)
        out_ref[:, columns] = (sum_ref[:, columns] + share * result).astype(jnp.bfloat16)


def cost():
    return pl.CostEstimate(flops=0, bytes_accessed=0, transcendentals=0)


def gather_all(value, axis):
    size = lax.axis_size(axis)
    if size & (size - 1):
        return lax.all_gather(value, axis, axis=0, tiled=True)
    bits = [2**j for j in range(size.bit_length() - 1)]
    for step in [bits[:1]] + [bits[j : j + 2] for j in range(1, len(bits), 2)]:
        masks = step + [sum(step)] if len(step) == 2 else step
        value = jnp.concatenate([value] + [partner(value, axis, mask) for mask in masks], axis=0)
    return value


def on_device(query, keys, values, middle_head_shift, coarse_head_shift):
    rows, width = query.shape
    members = rows // MIDDLE_DILATION
    near_rows = 2 * lax.axis_size("outer")
    bf16 = jnp.bfloat16
    smem = pl.BlockSpec(memory_space=pltpu.SMEM)
    vmem = pl.BlockSpec(memory_space=pltpu.VMEM)
    anywhere = pl.BlockSpec(memory_space=pl.ANY)
    params = pltpu.CompilerParams(vmem_limit_bytes=24 * 1024 * 1024)
    order_scratch = pltpu.VMEM((MIDDLE_DILATION, rows, rows), bf16)

    def columns_of(count, heads=GROUP, first=0):
        return pl.BlockSpec((count, heads * HEAD_FEATURES), lambda i: (0, first // heads + i))

    def call(kernel, name, **options):
        return pl.pallas_call(kernel, name=name, compiler_params=params, cost_estimate=cost(), **options)

    other_keys = partner(keys, "inner", 1)
    prepared = call(
        functools.partial(prepare_kernel, CHUNKS),
        "prepare",
        out_shape=[
            pltpu.HBM((2 * members, width), bf16),
            pltpu.HBM((members + near_rows, width), bf16),
            *[pltpu.HBM((rows - members, c * HEAD_FEATURES), bf16) for c in CHUNKS],
            jax.ShapeDtypeStruct((2, width), bf16),
        ],
        in_specs=[smem, smem, vmem, vmem],
        out_specs=[vmem] * (3 + len(CHUNKS)),
        scratch_shapes=[order_scratch],
    )(middle_head_shift, coarse_head_shift, keys, values)
    own_members, own_vm, own_vr, coarse = prepared[0], prepared[1], prepared[2:-1], prepared[-1]
    cross = partner(own_members, "inner", 2)
    near = gather_all(coarse, "outer")
    own_vm = call(
        append_kernel,
        "append",
        out_shape=pltpu.HBM(own_vm.shape, bf16),
        in_specs=[vmem, anywhere],
        out_specs=anywhere,
        input_output_aliases={1: 0},
        scratch_shapes=[pltpu.SemaphoreType.DMA],
    )(near, own_vm)
    other_vm = partner(own_vm, "inner", 1)
    cross, own_vr = lax.optimization_barrier((cross, own_vr))
    other_vr = [partner(piece, "inner", 1) for piece in own_vr]
    other_ordered, other_km = call(
        reorder_kernel,
        "reorder",
        out_shape=[pltpu.HBM((rows, width), bf16), pltpu.HBM((members + near_rows, width), bf16)],
        in_specs=[smem, vmem, vmem],
        out_specs=[vmem, vmem],
        scratch_shapes=[order_scratch],
    )(middle_head_shift, other_keys, near)
    diagonal_k = partner(other_km, "inner", 2)
    diagonal_v = partner(lax.optimization_barrier((other_vm, other_ordered))[0], "inner", 2)

    groups = HEAD_COUNT // GROUP
    whole, with_near = columns_of(rows), columns_of(members + near_rows)
    lanes = pl.BlockSpec((rows, LANES), lambda i: (0, i))
    own_sum, other_weights, state = call(
        functools.partial(first_kernel, 0),
        "first",
        out_shape=[
            pltpu.HBM((rows, width), jnp.float32),
            pltpu.HBM((HEAD_COUNT, rows, rows), bf16),
            pltpu.HBM((rows, groups * LANES), jnp.float32),
        ],
        grid=(groups,),
        in_specs=[smem, whole, whole, whole, whole],
        out_specs=[whole, pl.BlockSpec((GROUP, rows, rows), lambda i: (i, 0, 0)), lanes],
    )(middle_head_shift, query, keys, values, other_ordered)
    extra_sum, share = call(
        extra_kernel,
        "extra",
        out_shape=[pltpu.HBM((rows, width), jnp.float32), pltpu.HBM((rows, groups * LANES), jnp.float32)],
        grid=(groups,),
        in_specs=[
            smem, smem, whole, lanes, columns_of(2 * members), with_near, with_near, columns_of(near_rows), with_near
        ],
        out_specs=[whole, lanes],
    )(middle_head_shift, coarse_head_shift, query, state, cross, diagonal_k, diagonal_v, near, other_vm)

    out = None
    first = 0
    for chunk, vr in zip(CHUNKS, other_vr):
        heads = min(GROUP, chunk)
        block = columns_of(rows, heads, first)
        args = [extra_sum, share, own_sum, other_weights, other_vm, vr]
        specs = [
            block,
            pl.BlockSpec((rows, LANES), lambda i, first=first: (0, first // GROUP + i)),
            block,
            pl.BlockSpec((heads, rows, rows), lambda i, first=first, heads=heads: (first // heads + i, 0, 0)),
            columns_of(members, heads, first),
            columns_of(rows - members, heads),
        ]
        aliases = {}
        if out is not None:
            aliases = {len(args): 0}
            args.append(out)
            specs.append(anywhere)
        out = call(
            functools.partial(finish_kernel, heads, first % GROUP),
            "finish",
            out_shape=jax.ShapeDtypeStruct((rows, width), bf16),
            grid=(chunk // heads,),
            in_specs=specs,
            out_specs=block,
            input_output_aliases=aliases,
        )(*args)
        first += chunk
    return out


def solution(mesh):
    placed = (
        P(("outer", "inner"), None),
        P(("outer", "inner"), None),
        P(("outer", "inner"), None),
        P(),
        P(),
    )
    return jax.shard_map(
        on_device,
        mesh=mesh,
        in_specs=placed,
        out_specs=P(("outer", "inner"), None),
        check_vma=False,
    )
```

time: 81.7 us -> 61.3 us (0.75)
  local copies, waits for them, and re-layouts: 26.2 us -> 11.2 us
  Pallas kernels: 25.5 us -> 22.8 us
  waiting for transfers between devices: 13.7 us -> 11.2 us
    concatenate x2 -> x1, local copies, waits for them, and re-layouts: 7.61 us -> 0.08 us  [gather_all(): jnp.concatenate([value] + [partner(value, axis, mask) for mask in masks],...]
    unnamed x38 -> x30, local copies, waits for them, and re-layouts: 14.4 us -> 11.1 us
    pallas_call x6 -> x7, Pallas kernels: 25.5 us -> 22.8 us  [the longest x1 7.35 us: on_device(): call(functools.partial(first_kernel, 0), 'first', out_shape=[pltpu.HBM((r...]
    ppermute x11, waiting for transfers between devices: 13.7 us -> 11.2 us  [partner(): return lax.ppermute(value, axis, pairs)]
    reshape x1 -> x0, local copies, waits for them, and re-layouts: 1.85 us -> none  [on_device(): coarse.reshape(devices, 2, width).transpose(1, 0, 2)]
    slice x2 -> x0, local copies, waits for them, and re-layouts: 1.27 us -> none  [the longest x1 0.64 us: on_device(): diagonal_v[members:]]
    transpose x1 -> x0, local copies, waits for them, and re-layouts: 1.03 us -> none  [on_device(): coarse.reshape(devices, 2, width).transpose(1, 0, 2)]
  transfers between devices with their start and end apart: 11 -> 11, of which waited for: 5 -> 6; matrix products, arithmetic and copies ran while one was open for 15% -> 0% of each run, Pallas kernels for 29% -> 36%
where the time goes in v3:
time: 61.3 us; the launch traced here: 60.8 us
  Pallas kernels  22.8 us (37%)
  starting transfers between devices  15.5 us (25%)
  local copies, waits for them, and re-layouts  11.2 us (18%)
  waiting for transfers between devices  11.2 us (18%)
    ppermute x11, starting transfers between devices, partner(): return lax.ppermute(value, axis, pairs)  15.5 us
    ppermute x11, waiting for transfers between devices, partner(): return lax.ppermute(value, axis, pairs)  11.2 us
    unnamed x30, local copies, waits for them, and re-layouts  11.1 us
    pallas_call x1, Pallas kernels, on_device(): call(functools.partial(first_kernel, 0), 'first', out_shape=[pltpu.HBM((r...  7.35 us
    pallas_call x1, Pallas kernels, on_device(): call(extra_kernel, 'extra', out_shape=[pltpu.HBM((rows, width), jnp.float...  5.78 us
    pallas_call x2, Pallas kernels, on_device(): call(functools.partial(finish_kernel, heads, first % GROUP), 'finish', ou...  3.25 us
    pallas_call x1, Pallas kernels, on_device(): call(reorder_kernel, 'reorder', out_shape=[pltpu.HBM((rows, width), bf16)...  2.99 us
    pallas_call x1, Pallas kernels, on_device(): call(functools.partial(prepare_kernel, CHUNKS), 'prepare', out_shape=[plt...  2.81 us
  transfers between devices with their start and end apart: 11, of which 6 were waited for; matrix products, arithmetic and copies ran while one was open for 0% of the time, Pallas kernels for 36%

profile of v3, /device:TPU:0, one launch (start us, length us, event | category | flops | bytes accessed | tf_op | source)
XLA Modules:
  0.0 60.8 jit_solution(6253848212841841339)
XLA Ops:
  0.0 2.9 %collective-permute-start = (bf16[256,2048]{1,0:T(8,128)(2,1)}, bf16[256,2048]{1,0:T(8,128)(2,1)}, u32[]{:S(2)}, u32[]{:S(2)}) collective-permute-start(bf16[256,2048]{1,0:T(8,128)(2,1)} %k_ref.3), channel_id=1, source_target_pairs={{0,8},{8,0},{16,24},{24,16},{1,9},{9,1},{17,25},{25,17},{2,10},{10... | collective-permute-start | bytes 3145736 | tf_op jit(solution)/shard_map/ppermute | solution.py:23
  2.9 1.3 %copy-done.4 = bf16[256,2048]{1,0:T(8,128)(2,1)S(1)} copy-done((bf16[256,2048]{1,0:T(8,128)(2,1)S(1)}, bf16[256,2048]{1,0:T(8,128)(2,1)}, u32[]{:S(2)}) %copy-start.4) | copy-done | bytes 1048600
  4.2 1.2 %copy-done.6 = bf16[256,2048]{1,0:T(8,128)(2,1)S(1)} copy-done((bf16[256,2048]{1,0:T(8,128)(2,1)S(1)}, bf16[256,2048]{1,0:T(8,128)(2,1)}, u32[]{:S(2)}) %copy-start.6) | copy-done | bytes 1048600
  5.4 0.7 %copy-done.11 = s32[16]{0:T(128)S(1)} copy-done((s32[16]{0:T(128)S(1)}, s32[16]{0:T(128)}, u32[]{:S(2)}) %copy-start.11) | copy-done | bytes 88
  6.1 0.7 %copy-done.13 = s32[16]{0:T(128)S(1)} copy-done((s32[16]{0:T(128)S(1)}, s32[16]{0:T(128)}, u32[]{:S(2)}) %copy-start.13) | copy-done | bytes 88
  6.7 2.8 %prepare.1 = (bf16[128,2048]{1,0:T(8,128)(2,1)}, bf16[80,2048]{1,0:T(8,128)(2,1)}, bf16[192,1536]{1,0:T(8,128)(2,1)}, bf16[192,512]{1,0:T(8,128)(2,1)}, bf16[2,2048]{1,0:T(2,128)(2,1)S(1)}) custom-call(s32[16]{0:T(128)S(1)} %copy-done.11, s32[16]{0:T(128)S(1)} %copy-done.13, bf16[256,2048]{1,0:T(8,128)(2,1)S(1)} %copy-done.4, bf16[256,2048]{1,0:T(8,128)(2,1)S(1)} %copy-done.6), custom_call_target="tpu_custom_call" | custom-call | tf_op jit(solution)/shard_map/prepare/pallas_call | solution.py:235
  9.6 1.5 %collective-permute-start.5 = (bf16[128,2048]{1,0:T(8,128)(2,1)}, bf16[128,2048]{1,0:T(8,128)(2,1)}, u32[]{:S(2)}, u32[]{:S(2)}) collective-permute-start(bf16[128,2048]{1,0:T(8,128)(2,1)} %get-tuple-element.24), channel_id=1, source_target_pairs={{0,16},{8,24},{16,0},{24,8},{1,17},{9,25},{17,1},{25,9},{2,18},{10... | collective-permute-start | bytes 1572872 | tf_op jit(solution)/shard_map/ppermute | solution.py:23
  11.1 1.2 %collective-permute-done.1 = bf16[2,2048]{1,0:T(2,128)(2,1)S(1)} collective-permute-done((bf16[2,2048]{1,0:T(2,128)(2,1)S(1)}, bf16[2,2048]{1,0:T(2,128)(2,1)S(1)}, u32[]{:S(2)}, u32[]{:S(2)}) %collective-permute-start.1) | collective-permute-done | bytes 8224 | tf_op jit(solution)/shard_map/ppermute | solution.py:23
  12.3 3.7 %collective-permute-start.4 = (bf16[4,2048]{1,0:T(4,128)(2,1)S(1)}, bf16[4,2048]{1,0:T(4,128)(2,1)S(1)}, u32[]{:S(2)}, u32[]{:S(2)}) collective-permute-start(bf16[4,2048]{1,0:T(4,128)(2,1)S(1)} %pad_maximum_fusion), channel_id=1, source_target_pairs={{0,6},{1,7},{2,4},{3,5},{4,2},{5,3},{6,0},{7,1},{8,14},{9,15},{10,... | collective-permute-start | bytes 49160 | tf_op jit(solution)/shard_map/ppermute | solution.py:23
  15.9 0.8 %collective-permute-start.2 = (bf16[4,2048]{1,0:T(4,128)(2,1)S(1)}, bf16[4,2048]{1,0:T(4,128)(2,1)S(1)}, u32[]{:S(2)}, u32[]{:S(2)}) collective-permute-start(bf16[4,2048]{1,0:T(4,128)(2,1)S(1)} %pad_maximum_fusion), channel_id=1, source_target_pairs={{0,2},{1,3},{2,0},{3,1},{4,6},{5,7},{6,4},{7,5},{8,10},{9,11},{10,... | collective-permute-start | bytes 49160 | tf_op jit(solution)/shard_map/ppermute | solution.py:23
  16.7 1.1 %collective-permute-done.4 = bf16[4,2048]{1,0:T(4,128)(2,1)S(1)} collective-permute-done((bf16[4,2048]{1,0:T(4,128)(2,1)S(1)}, bf16[4,2048]{1,0:T(4,128)(2,1)S(1)}, u32[]{:S(2)}, u32[]{:S(2)}) %collective-permute-start.4) | collective-permute-done | bytes 16416 | tf_op jit(solution)/shard_map/ppermute | solution.py:23
  17.9 2.7 %collective-permute-done.3 = bf16[4,2048]{1,0:T(4,128)(2,1)S(1)} collective-permute-done((bf16[4,2048]{1,0:T(4,128)(2,1)S(1)}, bf16[4,2048]{1,0:T(4,128)(2,1)S(1)}, u32[]{:S(2)}, u32[]{:S(2)}) %collective-permute-start.3) | collective-permute-done | bytes 16416 | tf_op jit(solution)/shard_map/ppermute | solution.py:23
  20.7 0.6 %append.1 = bf16[80,2048]{1,0:T(8,128)(2,1)} custom-call(bf16[16,2048]{1,0:T(8,128)(2,1)S(1)} %concatenate.8.near_ref, bf16[80,2048]{1,0:T(8,128)(2,1)} %get-tuple-element.29.vm_ref), custom_call_target="tpu_custom_call", output_to_operand_aliasing={{}: (1, {})} | custom-call | tf_op jit(solution)/shard_map/append/pallas_call | solution.py:251
  21.3 0.6 collective-permute-start.7
  21.9 1.4 %collective-permute-done.5.cross_ref = bf16[128,2048]{1,0:T(8,128)(2,1)} collective-permute-done((bf16[128,2048]{1,0:T(8,128)(2,1)}, bf16[128,2048]{1,0:T(8,128)(2,1)}, u32[]{:S(2)}, u32[]{:S(2)}) %collective-permute-start.5) | collective-permute-done | bytes 524320 | tf_op jit(solution)/shard_map/ppermute | solution.py:23
  23.2 0.4 collective-permute-start.10
  23.6 3.6 %collective-permute-done.k_ref = bf16[256,2048]{1,0:T(8,128)(2,1)} collective-permute-done((bf16[256,2048]{1,0:T(8,128)(2,1)}, bf16[256,2048]{1,0:T(8,128)(2,1)}, u32[]{:S(2)}, u32[]{:S(2)}) %collective-permute-start) | collective-permute-done | bytes 1048608 | tf_op jit(solution)/shard_map/ppermute | solution.py:23
  27.2 0.7 %copy-done.12 = s32[16]{0:T(128)S(1)} copy-done((s32[16]{0:T(128)S(1)}, s32[16]{0:T(128)}, u32[]{:S(2)}) %copy-start.12) | copy-done | bytes 88
  27.9 3.0 %reorder.1 = (bf16[256,2048]{1,0:T(8,128)(2,1)}, bf16[80,2048]{1,0:T(8,128)(2,1)}) custom-call(s32[16]{0:T(128)S(1)} %copy-done.12, bf16[256,2048]{1,0:T(8,128)(2,1)} %collective-permute-done.k_ref, bf16[16,2048]{1,0:T(8,128)(2,1)S(1)} %concatenate.8.near_ref), custom_call_target="tpu_custom_call" | custom-call | tf_op jit(solution)/shard_map/reorder/pallas_call | solution.py:263
  30.9 2.1 %collective-permute-start.6 = (bf16[80,2048]{1,0:T(8,128)(2,1)}, bf16[80,2048]{1,0:T(8,128)(2,1)S(1)}, u32[]{:S(2)}, u32[]{:S(2)}) collective-permute-start(bf16[80,2048]{1,0:T(8,128)(2,1)} %get-tuple-element.28), channel_id=1, source_target_pairs={{0,16},{8,24},{16,0},{24,8},{1,17},{9,25},{17,1},{25,9},{2,18},{10... | collective-permute-start | bytes 983048 | tf_op jit(solution)/shard_map/ppermute | solution.py:23
  33.0 1.2 %collective-permute-done.7.other_ref.vm_ref = bf16[80,2048]{1,0:T(8,128)(2,1)S(1)} collective-permute-done((bf16[80,2048]{1,0:T(8,128)(2,1)}, bf16[80,2048]{1,0:T(8,128)(2,1)S(1)}, u32[]{:S(2)}, u32[]{:S(2)}) %collective-permute-start.7) | collective-permute-done | bytes 327712 | tf_op jit(solution)/shard_map/ppermute | solution.py:23
  34.2 2.1 %collective-permute-start.8 = (bf16[80,2048]{1,0:T(8,128)(2,1)S(1)}, bf16[80,2048]{1,0:T(8,128)(2,1)S(1)}, u32[]{:S(2)}, u32[]{:S(2)}) collective-permute-start(bf16[80,2048]{1,0:T(8,128)(2,1)S(1)} %collective-permute-done.7.other_ref.vm_ref), channel_id=1, source_target_pairs={{0,16},{8,24},{16,0},{24,8},{1,17},{9,25},{17,1},{25,9},{2,18},{10... | collective-permute-start | bytes 983048 | tf_op jit(solution)/shard_map/ppermute | solution.py:23
  36.3 1.5 %collective-permute-start.9 = (bf16[192,512]{1,0:T(8,128)(2,1)}, bf16[192,512]{1,0:T(8,128)(2,1)S(1)}, u32[]{:S(2)}, u32[]{:S(2)}) collective-permute-start(bf16[192,512]{1,0:T(8,128)(2,1)} %get-tuple-element.35), channel_id=1, source_target_pairs={{0,8},{8,0},{16,24},{24,16},{1,9},{9,1},{17,25},{25,17},{2,10},{10... | collective-permute-start | bytes 589832 | tf_op jit(solution)/shard_map/ppermute | solution.py:23
  37.8 1.2 %copy-done.9 = bf16[256,2048]{1,0:T(8,128)(2,1)S(1)} copy-done((bf16[256,2048]{1,0:T(8,128)(2,1)S(1)}, bf16[256,2048]{1,0:T(8,128)(2,1)}, u32[]{:S(2)}) %copy-start.9) | copy-done | bytes 1048600
  39.0 7.4 %first.1 = (f32[256,2048]{1,0:T(8,128)}, bf16[16,256,256]{2,1,0:T(8,128)(2,1)}, f32[256,512]{1,0:T(8,128)}) custom-call(s32[16]{0:T(128)S(1)} %copy-done.12, bf16[256,2048]{1,0:T(8,128)(2,1)S(1)} %copy-done.3, bf16[256,2048]{1,0:T(8,128)(2,1)S(1)} %copy-done.5, bf16[256,2048]{1,0:T(8,128)(2,1)S(1)} %copy-done.7, bf16[256,2048]{1,0:T(8,128)(2,1)S(1)} %copy-done.9), custom_call_target="tpu_custom_call" | custom-call | tf_op jit(solution)/shard_map/first/pallas_call | solution.py:277
  46.4 1.2 %copy-done.10 = f32[256,512]{1,0:T(8,128)S(1)} copy-done((f32[256,512]{1,0:T(8,128)S(1)}, f32[256,512]{1,0:T(8,128)}, u32[]{:S(2)}) %copy-start.10) | copy-done | bytes 524312
  47.5 5.8 %extra.1 = (f32[256,2048]{1,0:T(8,128)}, f32[256,512]{1,0:T(8,128)}) custom-call(s32[16]{0:T(128)S(1)} %copy-done.12, s32[16]{0:T(128)S(1)} %copy-done.14, bf16[256,2048]{1,0:T(8,128)(2,1)S(1)} %copy-done.3, f32[256,512]{1,0:T(8,128)S(1)} %copy-done.10, bf16[128,2048]{1,0:T(8,128)(2,1)} %collective-permute-done.5.cross_ref, ...), custom_call_target="tpu_custom_call" | custom-call | tf_op jit(solution)/shard_map/extra/pallas_call | solution.py:289
  53.4 1.6 %copy-done.1 = bf16[16,256,256]{2,1,0:T(8,128)(2,1)S(1)} copy-done((bf16[16,256,256]{2,1,0:T(8,128)(2,1)S(1)}, bf16[16,256,256]{2,1,0:T(8,128)(2,1)}, u32[]{:S(2)}) %copy-start.1) | copy-done | bytes 2097176
  54.9 1.6 %copy-done.2 = f32[256,2048]{1,0:T(8,128)S(1)} copy-done((f32[256,2048]{1,0:T(8,128)S(1)}, f32[256,2048]{1,0:T(8,128)}, u32[]{:S(2)}) %copy-start.2) | copy-done | bytes 2097176
  56.5 1.0 %copy-done.8 = f32[256,512]{1,0:T(8,128)S(1)} copy-done((f32[256,512]{1,0:T(8,128)S(1)}, f32[256,512]{1,0:T(8,128)}, u32[]{:S(2)}) %copy-start.8) | copy-done | bytes 524312
  57.6 2.2 %finish.2.rest_0_ = bf16[256,2048]{1,0:T(8,128)(2,1)} custom-call(f32[256,2048]{1,0:T(8,128)S(1)} %copy-done.2, f32[256,512]{1,0:T(8,128)S(1)} %copy-done.8, f32[256,2048]{1,0:T(8,128)S(1)} %copy-done, bf16[16,256,256]{2,1,0:T(8,128)(2,1)S(1)} %copy-done.1, bf16[80,2048]{1,0:T(8,128)(2,1)S(1)} %collective-permute-done.7.other_ref.vm_ref, ...), custom_call_target="tpu_custom_call" | custom-call | tf_op jit(solution)/shard_map/finish/pallas_call | solution.py:319
  59.8 1.0 %finish.3 = bf16[256,2048]{1,0:T(8,128)(2,1)} custom-call(f32[256,2048]{1,0:T(8,128)S(1)} %copy-done.2, f32[256,512]{1,0:T(8,128)S(1)} %copy-done.8, f32[256,2048]{1,0:T(8,128)S(1)} %copy-done, bf16[16,256,256]{2,1,0:T(8,128)(2,1)S(1)} %copy-done.1, bf16[80,2048]{1,0:T(8,128)(2,1)S(1)} %collective-permute-done.7.other_ref.vm_ref, ...), custom_call_target="tpu_custom_call", output_to_operand_aliasing={{}: (6, {})} | custom-call | tf_op jit(solution)/shard_map/finish/pallas_call | solution.py:319
  (29 shorter events, 0.2 us)
Async XLA Ops:
  0.0 37.7 %copy-start.3 = (bf16[256,2048]{1,0:T(8,128)(2,1)S(1)}, bf16[256,2048]{1,0:T(8,128)(2,1)}, u32[]{:S(2)}) copy-start(bf16[256,2048]{1,0:T(8,128)(2,1)} %q_ref.3) | copy-start | bytes 3145732
  0.0 27.2 %collective-permute-start = (bf16[256,2048]{1,0:T(8,128)(2,1)}, bf16[256,2048]{1,0:T(8,128)(2,1)}, u32[]{:S(2)}, u32[]{:S(2)}) collective-permute-start(bf16[256,2048]{1,0:T(8,128)(2,1)} %k_ref.3), channel_id=1, source_target_pairs={{0,8},{8,0},{16,24},{24,16},{1,9},{9,1},{17,25},{25,17},{2,10},{10... | collective-permute-start | bytes 3145736 | tf_op jit(solution)/shard_map/ppermute | solution.py:23
  2.9 1.3 %copy-start.4 = (bf16[256,2048]{1,0:T(8,128)(2,1)S(1)}, bf16[256,2048]{1,0:T(8,128)(2,1)}, u32[]{:S(2)}) copy-start(bf16[256,2048]{1,0:T(8,128)(2,1)} %k_ref.3) | copy-start | bytes 3145732
  4.2 1.2 %copy-start.6 = (bf16[256,2048]{1,0:T(8,128)(2,1)S(1)}, bf16[256,2048]{1,0:T(8,128)(2,1)}, u32[]{:S(2)}) copy-start(bf16[256,2048]{1,0:T(8,128)(2,1)} %v_ref.3) | copy-start | bytes 3145732
  5.4 0.7 %copy-start.11 = (s32[16]{0:T(128)S(1)}, s32[16]{0:T(128)}, u32[]{:S(2)}) copy-start(s32[16]{0:T(128)} %middle_ref.7) | copy-start | bytes 196
  6.1 0.7 %copy-start.13 = (s32[16]{0:T(128)S(1)}, s32[16]{0:T(128)}, u32[]{:S(2)}) copy-start(s32[16]{0:T(128)} %coarse_ref.3) | copy-start | bytes 196
  6.7 31.0 %copy-start.5 = (bf16[256,2048]{1,0:T(8,128)(2,1)S(1)}, bf16[256,2048]{1,0:T(8,128)(2,1)}, u32[]{:S(2)}) copy-start(bf16[256,2048]{1,0:T(8,128)(2,1)} %k_ref.3) | copy-start | bytes 3145732
  6.7 31.0 %copy-start.7 = (bf16[256,2048]{1,0:T(8,128)(2,1)S(1)}, bf16[256,2048]{1,0:T(8,128)(2,1)}, u32[]{:S(2)}) copy-start(bf16[256,2048]{1,0:T(8,128)(2,1)} %v_ref.3) | copy-start | bytes 3145732
  9.6 13.7 %collective-permute-start.5 = (bf16[128,2048]{1,0:T(8,128)(2,1)}, bf16[128,2048]{1,0:T(8,128)(2,1)}, u32[]{:S(2)}, u32[]{:S(2)}) collective-permute-start(bf16[128,2048]{1,0:T(8,128)(2,1)} %get-tuple-element.24), channel_id=1, source_target_pairs={{0,16},{8,24},{16,0},{24,8},{1,17},{9,25},{17,1},{25,9},{2,18},{10... | collective-permute-start | bytes 1572872 | tf_op jit(solution)/shard_map/ppermute | solution.py:23
  11.1 1.2 %collective-permute-start.1 = (bf16[2,2048]{1,0:T(2,128)(2,1)S(1)}, bf16[2,2048]{1,0:T(2,128)(2,1)S(1)}, u32[]{:S(2)}, u32[]{:S(2)}) collective-permute-start(bf16[2,2048]{1,0:T(2,128)(2,1)S(1)} %get-tuple-element.21), channel_id=1, source_target_pairs={{0,1},{1,0},{2,3},{3,2},{4,5},{5,4},{6,7},{7,6},{8,9},{9,8},{10,11... | collective-permute-start | bytes 24584 | tf_op jit(solution)/shard_map/ppermute | solution.py:23
  12.3 5.6 %collective-permute-start.4 = (bf16[4,2048]{1,0:T(4,128)(2,1)S(1)}, bf16[4,2048]{1,0:T(4,128)(2,1)S(1)}, u32[]{:S(2)}, u32[]{:S(2)}) collective-permute-start(bf16[4,2048]{1,0:T(4,128)(2,1)S(1)} %pad_maximum_fusion), channel_id=1, source_target_pairs={{0,6},{1,7},{2,4},{3,5},{4,2},{5,3},{6,0},{7,1},{8,14},{9,15},{10,... | collective-permute-start | bytes 49160 | tf_op jit(solution)/shard_map/ppermute | solution.py:23
  15.9 4.6 %collective-permute-start.3 = (bf16[4,2048]{1,0:T(4,128)(2,1)S(1)}, bf16[4,2048]{1,0:T(4,128)(2,1)S(1)}, u32[]{:S(2)}, u32[]{:S(2)}) collective-permute-start(bf16[4,2048]{1,0:T(4,128)(2,1)S(1)} %pad_maximum_fusion), channel_id=1, source_target_pairs={{0,4},{1,5},{2,6},{3,7},{4,0},{5,1},{6,2},{7,3},{8,12},{9,13},{10,... | collective-permute-start | bytes 49160 | tf_op jit(solution)/shard_map/ppermute | solution.py:23
  15.9 4.6 %collective-permute-start.2 = (bf16[4,2048]{1,0:T(4,128)(2,1)S(1)}, bf16[4,2048]{1,0:T(4,128)(2,1)S(1)}, u32[]{:S(2)}, u32[]{:S(2)}) collective-permute-start(bf16[4,2048]{1,0:T(4,128)(2,1)S(1)} %pad_maximum_fusion), channel_id=1, source_target_pairs={{0,2},{1,3},{2,0},{3,1},{4,6},{5,7},{6,4},{7,5},{8,10},{9,11},{10,... | collective-permute-start | bytes 49160 | tf_op jit(solution)/shard_map/ppermute | solution.py:23
  21.3 12.9 %collective-permute-start.7 = (bf16[80,2048]{1,0:T(8,128)(2,1)}, bf16[80,2048]{1,0:T(8,128)(2,1)S(1)}, u32[]{:S(2)}, u32[]{:S(2)}) collective-permute-start(bf16[80,2048]{1,0:T(8,128)(2,1)} %append.1), channel_id=1, source_target_pairs={{0,8},{8,0},{16,24},{24,16},{1,9},{9,1},{17,25},{25,17},{2,10},{10... | collective-permute-start | bytes 983048 | tf_op jit(solution)/shard_map/ppermute | solution.py:23
  23.2 30.1 %collective-permute-start.10 = (bf16[192,1536]{1,0:T(8,128)(2,1)}, bf16[192,1536]{1,0:T(8,128)(2,1)S(1)}, u32[]{:S(2)}, u32[]{:S(2)}) collective-permute-start(bf16[192,1536]{1,0:T(8,128)(2,1)} %get-tuple-element.36), channel_id=1, source_target_pairs={{0,8},{8,0},{16,24},{24,16},{1,9},{9,1},{17,25},{25,17},{2,10},{10... | collective-permute-start | bytes 1769480 | tf_op jit(solution)/shard_map/ppermute | solution.py:23
  27.2 0.7 %copy-start.12 = (s32[16]{0:T(128)S(1)}, s32[16]{0:T(128)}, u32[]{:S(2)}) copy-start(s32[16]{0:T(128)} %middle_ref.7) | copy-start | bytes 196
  30.9 15.4 %collective-permute-start.6 = (bf16[80,2048]{1,0:T(8,128)(2,1)}, bf16[80,2048]{1,0:T(8,128)(2,1)S(1)}, u32[]{:S(2)}, u32[]{:S(2)}) collective-permute-start(bf16[80,2048]{1,0:T(8,128)(2,1)} %get-tuple-element.28), channel_id=1, source_target_pairs={{0,16},{8,24},{16,0},{24,8},{1,17},{9,25},{17,1},{25,9},{2,18},{10... | collective-permute-start | bytes 983048 | tf_op jit(solution)/shard_map/ppermute | solution.py:23
  34.2 12.2 %copy-start.14 = (s32[16]{0:T(128)S(1)}, s32[16]{0:T(128)}, u32[]{:S(2)}) copy-start(s32[16]{0:T(128)} %coarse_ref.3) | copy-start | bytes 196
  34.2 12.2 %collective-permute-start.8 = (bf16[80,2048]{1,0:T(8,128)(2,1)S(1)}, bf16[80,2048]{1,0:T(8,128)(2,1)S(1)}, u32[]{:S(2)}, u32[]{:S(2)}) collective-permute-start(bf16[80,2048]{1,0:T(8,128)(2,1)S(1)} %collective-permute-done.7.other_ref.vm_ref), channel_id=1, source_target_pairs={{0,16},{8,24},{16,0},{24,8},{1,17},{9,25},{17,1},{25,9},{2,18},{10... | collective-permute-start | bytes 983048 | tf_op jit(solution)/shard_map/ppermute | solution.py:23
  36.3 23.5 %collective-permute-start.9 = (bf16[192,512]{1,0:T(8,128)(2,1)}, bf16[192,512]{1,0:T(8,128)(2,1)S(1)}, u32[]{:S(2)}, u32[]{:S(2)}) collective-permute-start(bf16[192,512]{1,0:T(8,128)(2,1)} %get-tuple-element.35), channel_id=1, source_target_pairs={{0,8},{8,0},{16,24},{24,16},{1,9},{9,1},{17,25},{25,17},{2,10},{10... | collective-permute-start | bytes 589832 | tf_op jit(solution)/shard_map/ppermute | solution.py:23
  37.8 1.2 %copy-start.9 = (bf16[256,2048]{1,0:T(8,128)(2,1)S(1)}, bf16[256,2048]{1,0:T(8,128)(2,1)}, u32[]{:S(2)}) copy-start(bf16[256,2048]{1,0:T(8,128)(2,1)} %get-tuple-element.22.kp_ref) | copy-start | bytes 3145732
  46.3 7.0 %copy-start = (f32[256,2048]{1,0:T(8,128)S(1)}, f32[256,2048]{1,0:T(8,128)}, u32[]{:S(2)}) copy-start(f32[256,2048]{1,0:T(8,128)} %get-tuple-element.33.own_ref) | copy-start | bytes 6291460
  46.4 1.2 %copy-start.10 = (f32[256,512]{1,0:T(8,128)S(1)}, f32[256,512]{1,0:T(8,128)}, u32[]{:S(2)}) copy-start(f32[256,512]{1,0:T(8,128)} %get-tuple-element.23.state_ref) | copy-start | bytes 1572868
  53.3 1.6 %copy-start.1 = (bf16[16,256,256]{2,1,0:T(8,128)(2,1)S(1)}, bf16[16,256,256]{2,1,0:T(8,128)(2,1)}, u32[]{:S(2)}) copy-start(bf16[16,256,256]{2,1,0:T(8,128)(2,1)} %get-tuple-element.34.other_ref) | copy-start | bytes 6291460
  54.9 1.6 %copy-start.2 = (f32[256,2048]{1,0:T(8,128)S(1)}, f32[256,2048]{1,0:T(8,128)}, u32[]{:S(2)}) copy-start(f32[256,2048]{1,0:T(8,128)} %get-tuple-element.31.sum_ref) | copy-start | bytes 6291460
  56.5 1.0 %copy-start.8 = (f32[256,512]{1,0:T(8,128)S(1)}, f32[256,512]{1,0:T(8,128)}, u32[]{:S(2)}) copy-start(f32[256,512]{1,0:T(8,128)} %get-tuple-element.32.share_ref) | copy-start | bytes 1572868

commit v4 on v3

--- a/solution.py
+++ b/solution.py
@@ -81,15 +81,17 @@
     copy.wait()
 
 
-def reorder_kernel(middle_ref, k_ref, near_ref, ordered_ref, members_ref, order_ref):
-    members = k_ref.shape[0] // MIDDLE_DILATION
-    fill_orders(order_ref)
+def pick_kernel(middle_ref, k_ref, near_ref, members_ref):
+    rows = k_ref.shape[0]
+    members = rows // MIDDLE_DILATION
     members_ref[members:] = near_ref[...]
+    group = lax.broadcasted_iota(jnp.int32, (members, rows), 0)
+    token = lax.broadcasted_iota(jnp.int32, (members, rows), 1)
+    offset = token - MIDDLE_DILATION * group
     for head in range(HEAD_COUNT):
         columns = head_columns(head)
-        ordered = dot(order_ref[middle_ref[head]], k_ref[:, columns]).astype(jnp.bfloat16)
-        ordered_ref[:, columns] = ordered
-        members_ref[:members, columns] = ordered[:members]
+        chosen = one_hot(offset == middle_ref[head])
+        members_ref[:members, columns] = dot(chosen, k_ref[:, columns]).astype(jnp.bfloat16)
 
 
 def dot_keys(q, keys):
@@ -122,7 +124,13 @@
     return jnp.exp2((part - top) * EXP2_SCALE)
 
 
-def first_kernel(first, middle_ref, q_ref, k_ref, v_ref, kp_ref, own_ref, other_ref, state_ref):
+def first_kernel(first, middle_ref, q_ref, k_ref, v_ref, kp_ref, *rest):
+    own_ref, other_ref, state_ref, order_ref = rest[-4:]
+
+    @pl.when(pl.program_id(0) == 0)
+    def _():
+        fill_orders(order_ref)
+
     rows = q_ref.shape[0]
     members = rows // MIDDLE_DILATION
     column = lax.broadcasted_iota(jnp.int32, (1, rows), 1)
@@ -132,7 +140,8 @@
         shift = middle_ref[first + GROUP * pl.program_id(0) + place]
         q = q_ref[:, columns]
         own = dot_keys(q, k_ref[:, columns])
-        other = dot_keys(q, kp_ref[:, columns])
+        other_keys = dot(order_ref[shift], kp_ref[:, columns]).astype(jnp.bfloat16)
+        other = dot_keys(q, other_keys)
         top = functools.reduce(jnp.maximum, lane_tiles(own) + lane_tiles(other))
         top = jnp.max(top, axis=1, keepdims=True)
         row_is_member = member_rows(rows, shift)
@@ -199,6 +208,10 @@
         out_ref[:, columns] = (sum_ref[:, columns] + share * result).astype(jnp.bfloat16)
 
 
+def in_hbm(array):
+    return pltpu.with_memory_space_constraint(array, pltpu.HBM)
+
+
 def cost():
     return pl.CostEstimate(flops=0, bytes_accessed=0, transcendentals=0)
 
@@ -260,32 +273,49 @@
     other_vm = partner(own_vm, "inner", 1)
     cross, own_vr = lax.optimization_barrier((cross, own_vr))
     other_vr = [partner(piece, "inner", 1) for piece in own_vr]
-    other_ordered, other_km = call(
-        reorder_kernel,
-        "reorder",
-        out_shape=[pltpu.HBM((rows, width), bf16), pltpu.HBM((members + near_rows, width), bf16)],
+    other_km = call(
+        pick_kernel,
+        "pick",
+        out_shape=pltpu.HBM((members + near_rows, width), bf16),
         in_specs=[smem, vmem, vmem],
-        out_specs=[vmem, vmem],
-        scratch_shapes=[order_scratch],
+        out_specs=vmem,
     )(middle_head_shift, other_keys, near)
     diagonal_k = partner(other_km, "inner", 2)
-    diagonal_v = partner(lax.optimization_barrier((other_vm, other_ordered))[0], "inner", 2)
 
     groups = HEAD_COUNT // GROUP
     whole, with_near = columns_of(rows), columns_of(members + near_rows)
     lanes = pl.BlockSpec((rows, LANES), lambda i: (0, i))
-    own_sum, other_weights, state = call(
-        functools.partial(first_kernel, 0),
-        "first",
-        out_shape=[
-            pltpu.HBM((rows, width), jnp.float32),
-            pltpu.HBM((HEAD_COUNT, rows, rows), bf16),
-            pltpu.HBM((rows, groups * LANES), jnp.float32),
-        ],
-        grid=(groups,),
-        in_specs=[smem, whole, whole, whole, whole],
-        out_specs=[whole, pl.BlockSpec((GROUP, rows, rows), lambda i: (i, 0, 0)), lanes],
-    )(middle_head_shift, query, keys, values, other_ordered)
+
+    keys_after = lax.optimization_barrier((other_keys, other_km))[0]
+
+    def first_part(first, heads, before):
+        def columns(count, width):
+            return pl.BlockSpec((count, width), lambda i: (0, first // GROUP + i))
+
+        block = columns(rows, GROUP * HEAD_FEATURES)
+        return call(
+            functools.partial(first_kernel, first),
+            "first",
+            out_shape=[
+                pltpu.HBM((rows, width), jnp.float32),
+                pltpu.HBM((HEAD_COUNT, rows, rows), bf16),
+                pltpu.HBM((rows, groups * LANES), jnp.float32),
+            ],
+            grid=(heads // GROUP,),
+            in_specs=[smem, block, block, block, block] + [anywhere] * len(before),
+            out_specs=[
+                block,
+                pl.BlockSpec((GROUP, rows, rows), lambda i: (first // GROUP + i, 0, 0)),
+                columns(rows, LANES),
+            ],
+            input_output_aliases={5 + i: i for i in range(len(before))},
+            scratch_shapes=[order_scratch],
+        )(middle_head_shift, in_hbm(query), in_hbm(keys), in_hbm(values), keys_after, *before)
+
+    early = groups // 2 * GROUP
+    begun = first_part(0, early, ())
+    diagonal_v = partner(lax.optimization_barrier((other_vm, begun[2]))[0], "inner", 2)
+    own_sum, other_weights, state = first_part(early, HEAD_COUNT - early, begun)
     extra_sum, share = call(
         extra_kernel,
         "extra",
@@ -295,14 +325,16 @@
             smem, smem, whole, lanes, columns_of(2 * members), with_near, with_near, columns_of(near_rows), with_near
         ],
         out_specs=[whole, lanes],
-    )(middle_head_shift, coarse_head_shift, query, state, cross, diagonal_k, diagonal_v, near, other_vm)
+    )(
+        middle_head_shift, coarse_head_shift, in_hbm(query), in_hbm(state), cross, diagonal_k, diagonal_v, near, other_vm
+    )
 
     out = None
     first = 0
     for chunk, vr in zip(CHUNKS, other_vr):
         heads = min(GROUP, chunk)
         block = columns_of(rows, heads, first)
-        args = [extra_sum, share, own_sum, other_weights, other_vm, vr]
+        args = [*map(in_hbm, (extra_sum, share, own_sum, other_weights)), other_vm, vr]
         specs = [
             block,
             pl.BlockSpec((rows, LANES), lambda i, first=first: (0, first // GROUP + i)),

time: 61.3 us -> 58.8 us (0.959)
  Pallas kernels: 22.8 us -> 30.4 us
  local copies, waits for them, and re-layouts: 11.2 us -> 3.88 us
  starting transfers between devices: 15.5 us -> 14 us
  waiting for transfers between devices: 11.2 us -> 9.98 us
    unnamed x30 -> x14, local copies, waits for them, and re-layouts: 11.1 us -> 3.8 us
    pallas_call x2 -> x3, Pallas kernels: 10.3 us -> 14.2 us  [the longest x2 12.6 us: first_part(): call(functools.partial(first_kernel, first), 'first', out_shape=[pltpu.HB...]
    pallas_call x2, Pallas kernels: 3.25 us -> 6.84 us  [on_device(): call(functools.partial(finish_kernel, heads, first % GROUP), 'finish', ou...]
    ppermute x11, starting transfers between devices: 15.5 us -> 14 us  [partner(): return lax.ppermute(value, axis, pairs)]
    ppermute x11, waiting for transfers between devices: 11.2 us -> 9.98 us  [partner(): return lax.ppermute(value, axis, pairs)]
  transfers between devices with their start and end apart: 11 -> 11, of which waited for: 6 -> 5; matrix products, arithmetic and copies ran while one was open for 0% -> 0% of each run, Pallas kernels for 36% -> 48%
where the time goes in v4:
time: 58.8 us; the launch traced here: 58.4 us
  Pallas kernels  30.4 us (52%)
  starting transfers between devices  14 us (24%)
  waiting for transfers between devices  9.98 us (17%)
  local copies, waits for them, and re-layouts  3.88 us (7%)
    ppermute x11, starting transfers between devices, partner(): return lax.ppermute(value, axis, pairs)  14 us
    pallas_call x2, Pallas kernels, first_part(): call(functools.partial(first_kernel, first), 'first', out_shape=[pltpu.HB...  12.6 us
    ppermute x11, waiting for transfers between devices, partner(): return lax.ppermute(value, axis, pairs)  9.98 us
    pallas_call x2, Pallas kernels, on_device(): call(functools.partial(finish_kernel, heads, first % GROUP), 'finish', ou...  6.84 us
    pallas_call x1, Pallas kernels, on_device(): call(extra_kernel, 'extra', out_shape=[pltpu.HBM((rows, width), jnp.float...  5.99 us
    unnamed x14, local copies, waits for them, and re-layouts  3.8 us
    pallas_call x1, Pallas kernels, on_device(): call(functools.partial(prepare_kernel, CHUNKS), 'prepare', out_shape=[plt...  2.8 us
    pallas_call x1, Pallas kernels, on_device(): call(pick_kernel, 'pick', out_shape=pltpu.HBM((members + near_rows, width...  1.59 us
  transfers between devices with their start and end apart: 11, of which 5 were waited for; matrix products, arithmetic and copies ran while one was open for 0% of the time, Pallas kernels for 48%

profile of v4, /device:TPU:0, one launch (start us, length us, event | category | flops | bytes accessed | tf_op | source)
XLA Modules:
  0.0 58.4 jit_solution(6856325495468507414)
XLA Ops:
  0.0 2.9 %collective-permute-start = (bf16[256,2048]{1,0:T(8,128)(2,1)}, bf16[256,2048]{1,0:T(8,128)(2,1)S(1)}, u32[]{:S(2)}, u32[]{:S(2)}) collective-permute-start(bf16[256,2048]{1,0:T(8,128)(2,1)} %k_ref.5), channel_id=1, source_target_pairs={{0,8},{8,0},{16,24},{24,16},{1,9},{9,1},{17,25},{25,17},{2,10},{10... | collective-permute-start | bytes 3145736 | tf_op jit(solution)/shard_map/ppermute | solution.py:23
  2.9 1.3 %copy-done = bf16[256,2048]{1,0:T(8,128)(2,1)S(1)} copy-done((bf16[256,2048]{1,0:T(8,128)(2,1)S(1)}, bf16[256,2048]{1,0:T(8,128)(2,1)}, u32[]{:S(2)}) %copy-start) | copy-done | bytes 1048600
  4.2 1.2 %copy-done.1 = bf16[256,2048]{1,0:T(8,128)(2,1)S(1)} copy-done((bf16[256,2048]{1,0:T(8,128)(2,1)S(1)}, bf16[256,2048]{1,0:T(8,128)(2,1)}, u32[]{:S(2)}) %copy-start.1) | copy-done | bytes 1048600
  5.4 0.7 %copy-done.2 = s32[16]{0:T(128)S(1)} copy-done((s32[16]{0:T(128)S(1)}, s32[16]{0:T(128)}, u32[]{:S(2)}) %copy-start.2) | copy-done | bytes 88
  6.1 0.7 %copy-done.4 = s32[16]{0:T(128)S(1)} copy-done((s32[16]{0:T(128)S(1)}, s32[16]{0:T(128)}, u32[]{:S(2)}) %copy-start.4) | copy-done | bytes 88
  6.7 2.8 %prepare.1 = (bf16[128,2048]{1,0:T(8,128)(2,1)}, bf16[80,2048]{1,0:T(8,128)(2,1)}, bf16[192,1536]{1,0:T(8,128)(2,1)}, bf16[192,512]{1,0:T(8,128)(2,1)}, bf16[2,2048]{1,0:T(2,128)(2,1)S(1)}) custom-call(s32[16]{0:T(128)S(1)} %copy-done.2, s32[16]{0:T(128)S(1)} %copy-done.4, bf16[256,2048]{1,0:T(8,128)(2,1)S(1)} %copy-done, bf16[256,2048]{1,0:T(8,128)(2,1)S(1)} %copy-done.1), custom_call_target="tpu_custom_call" | custom-call | tf_op jit(solution)/shard_map/prepare/pallas_call | solution.py:248
  9.5 1.5 %collective-permute-start.5 = (bf16[128,2048]{1,0:T(8,128)(2,1)}, bf16[128,2048]{1,0:T(8,128)(2,1)S(1)}, u32[]{:S(2)}, u32[]{:S(2)}) collective-permute-start(bf16[128,2048]{1,0:T(8,128)(2,1)} %get-tuple-element.29), channel_id=1, source_target_pairs={{0,16},{8,24},{16,0},{24,8},{1,17},{9,25},{17,1},{25,9},{2,18},{10... | collective-permute-start | bytes 1572872 | tf_op jit(solution)/shard_map/ppermute | solution.py:23
  11.1 0.0 collective-permute-start.1
  11.1 1.2 %collective-permute-done.1 = bf16[2,2048]{1,0:T(2,128)(2,1)S(1)} collective-permute-done((bf16[2,2048]{1,0:T(2,128)(2,1)S(1)}, bf16[2,2048]{1,0:T(2,128)(2,1)S(1)}, u32[]{:S(2)}, u32[]{:S(2)}) %collective-permute-start.1) | collective-permute-done | bytes 8224 | tf_op jit(solution)/shard_map/ppermute | solution.py:23
  12.3 3.7 %collective-permute-start.4 = (bf16[4,2048]{1,0:T(4,128)(2,1)S(1)}, bf16[4,2048]{1,0:T(4,128)(2,1)S(1)}, u32[]{:S(2)}, u32[]{:S(2)}) collective-permute-start(bf16[4,2048]{1,0:T(4,128)(2,1)S(1)} %pad_maximum_fusion), channel_id=1, source_target_pairs={{0,6},{1,7},{2,4},{3,5},{4,2},{5,3},{6,0},{7,1},{8,14},{9,15},{10,... | collective-permute-start | bytes 49160 | tf_op jit(solution)/shard_map/ppermute | solution.py:23
  15.9 0.8 %collective-permute-start.2 = (bf16[4,2048]{1,0:T(4,128)(2,1)S(1)}, bf16[4,2048]{1,0:T(4,128)(2,1)S(1)}, u32[]{:S(2)}, u32[]{:S(2)}) collective-permute-start(bf16[4,2048]{1,0:T(4,128)(2,1)S(1)} %pad_maximum_fusion), channel_id=1, source_target_pairs={{0,2},{1,3},{2,0},{3,1},{4,6},{5,7},{6,4},{7,5},{8,10},{9,11},{10,... | collective-permute-start | bytes 49160 | tf_op jit(solution)/shard_map/ppermute | solution.py:23
  16.7 1.1 %collective-permute-done.4 = bf16[4,2048]{1,0:T(4,128)(2,1)S(1)} collective-permute-done((bf16[4,2048]{1,0:T(4,128)(2,1)S(1)}, bf16[4,2048]{1,0:T(4,128)(2,1)S(1)}, u32[]{:S(2)}, u32[]{:S(2)}) %collective-permute-start.4) | collective-permute-done | bytes 16416 | tf_op jit(solution)/shard_map/ppermute | solution.py:23
  17.9 2.7 %collective-permute-done.3 = bf16[4,2048]{1,0:T(4,128)(2,1)S(1)} collective-permute-done((bf16[4,2048]{1,0:T(4,128)(2,1)S(1)}, bf16[4,2048]{1,0:T(4,128)(2,1)S(1)}, u32[]{:S(2)}, u32[]{:S(2)}) %collective-permute-start.3) | collective-permute-done | bytes 16416 | tf_op jit(solution)/shard_map/ppermute | solution.py:23
  20.6 0.1 concatenate.8.near_ref
  20.6 0.6 %append.1 = bf16[80,2048]{1,0:T(8,128)(2,1)} custom-call(bf16[16,2048]{1,0:T(8,128)(2,1)S(1)} %concatenate.8.near_ref, bf16[80,2048]{1,0:T(8,128)(2,1)} %get-tuple-element.33.vm_ref), custom_call_target="tpu_custom_call", output_to_operand_aliasing={{}: (1, {})} | custom-call | tf_op jit(solution)/shard_map/append/pallas_call | solution.py:264
  21.3 0.6 %collective-permute-start.7 = (bf16[80,2048]{1,0:T(8,128)(2,1)}, bf16[80,2048]{1,0:T(8,128)(2,1)S(1)}, u32[]{:S(2)}, u32[]{:S(2)}) collective-permute-start(bf16[80,2048]{1,0:T(8,128)(2,1)} %append.1), channel_id=1, source_target_pairs={{0,8},{8,0},{16,24},{24,16},{1,9},{9,1},{17,25},{25,17},{2,10},{10... | collective-permute-start | bytes 983048 | tf_op jit(solution)/shard_map/ppermute | solution.py:23
  21.9 1.3 %collective-permute-done.5.cross_ref = bf16[128,2048]{1,0:T(8,128)(2,1)S(1)} collective-permute-done((bf16[128,2048]{1,0:T(8,128)(2,1)}, bf16[128,2048]{1,0:T(8,128)(2,1)S(1)}, u32[]{:S(2)}, u32[]{:S(2)}) %collective-permute-start.5) | collective-permute-done | bytes 524320 | tf_op jit(solution)/shard_map/ppermute | solution.py:23
  23.1 0.3 collective-permute-start.10
  23.4 3.7 %collective-permute-done.k_ref.kp_ref = bf16[256,2048]{1,0:T(8,128)(2,1)S(1)} collective-permute-done((bf16[256,2048]{1,0:T(8,128)(2,1)}, bf16[256,2048]{1,0:T(8,128)(2,1)S(1)}, u32[]{:S(2)}, u32[]{:S(2)}) %collective-permute-start) | collective-permute-done | bytes 1048608 | tf_op jit(solution)/shard_map/ppermute | solution.py:23
  27.1 1.6 %pick.1 = bf16[80,2048]{1,0:T(8,128)(2,1)} custom-call(s32[16]{0:T(128)S(1)} %copy-done.3, bf16[256,2048]{1,0:T(8,128)(2,1)S(1)} %collective-permute-done.k_ref.kp_ref, bf16[16,2048]{1,0:T(8,128)(2,1)S(1)} %concatenate.8.near_ref), custom_call_target="tpu_custom_call" | custom-call | tf_op jit(solution)/shard_map/pick/pallas_call | solution.py:276
  28.7 2.1 %collective-permute-start.6 = (bf16[80,2048]{1,0:T(8,128)(2,1)}, bf16[80,2048]{1,0:T(8,128)(2,1)S(1)}, u32[]{:S(2)}, u32[]{:S(2)}) collective-permute-start(bf16[80,2048]{1,0:T(8,128)(2,1)} %pick.1), channel_id=1, source_target_pairs={{0,16},{8,24},{16,0},{24,8},{1,17},{9,25},{17,1},{25,9},{2,18},{10... | collective-permute-start | bytes 983048 | tf_op jit(solution)/shard_map/ppermute | solution.py:23
  30.8 6.3 %first.2 = (f32[256,2048]{1,0:T(8,128)}, bf16[16,256,256]{2,1,0:T(8,128)(2,1)}, f32[256,512]{1,0:T(8,128)}) custom-call(s32[16]{0:T(128)S(1)} %copy-done.3, bf16[256,2048]{1,0:T(8,128)(2,1)} %q_ref.5, bf16[256,2048]{1,0:T(8,128)(2,1)} %k_ref.5, bf16[256,2048]{1,0:T(8,128)(2,1)} %v_ref.5, bf16[256,2048]{1,0:T(8,128)(2,1)S(1)} %collective-permute-done.k_ref.kp_ref), custom_call_target="tpu_custom_call" | custom-call | tf_op jit(solution)/shard_map/first/pallas_call | solution.py:296
  37.1 0.0 collective-permute-done.7.other_ref.vm_ref
  37.1 0.1 collective-permute-start.8
  37.2 2.0 %collective-permute-start.9 = (bf16[192,512]{1,0:T(8,128)(2,1)S(1)}, bf16[192,512]{1,0:T(8,128)(2,1)S(1)}, u32[]{:S(2)}, u32[]{:S(2)}) collective-permute-start(bf16[192,512]{1,0:T(8,128)(2,1)S(1)} %copy-done.6), channel_id=1, source_target_pairs={{0,8},{8,0},{16,24},{24,16},{1,9},{9,1},{17,25},{25,17},{2,10},{10... | collective-permute-start | bytes 589832 | tf_op jit(solution)/shard_map/ppermute | solution.py:23
  39.2 6.3 %first.3 = (f32[256,2048]{1,0:T(8,128)}, bf16[16,256,256]{2,1,0:T(8,128)(2,1)}, f32[256,512]{1,0:T(8,128)}) custom-call(s32[16]{0:T(128)S(1)} %copy-done.3, bf16[256,2048]{1,0:T(8,128)(2,1)} %q_ref.5, bf16[256,2048]{1,0:T(8,128)(2,1)} %k_ref.5, bf16[256,2048]{1,0:T(8,128)(2,1)} %v_ref.5, ...), custom_call_target="tpu_custom_call", output_to_operand_aliasing={{0}: (5, {}), {1}: (6, {}), {2}: (7, {})} | custom-call | tf_op jit(solution)/shard_map/first/pallas_call | solution.py:296
  45.5 0.0 collective-permute-done.6.diagonal_k_ref
  45.5 6.0 %extra.1 = (f32[256,2048]{1,0:T(8,128)}, f32[256,512]{1,0:T(8,128)}) custom-call(s32[16]{0:T(128)S(1)} %copy-done.3, s32[16]{0:T(128)S(1)} %copy-done.5, bf16[256,2048]{1,0:T(8,128)(2,1)} %q_ref.5, f32[256,512]{1,0:T(8,128)} %get-tuple-element.28.state_ref, bf16[128,2048]{1,0:T(8,128)(2,1)S(1)} %collective-permute-done.5.cross_ref, ...), custom_call_target="tpu_custom_call" | custom-call | tf_op jit(solution)/shard_map/extra/pallas_call | solution.py:319
  51.5 0.0 collective-permute-done.10.vr_ref
  51.5 4.4 %finish.2.rest_0_ = bf16[256,2048]{1,0:T(8,128)(2,1)} custom-call(f32[256,2048]{1,0:T(8,128)} %get-tuple-element.35.sum_ref, f32[256,512]{1,0:T(8,128)} %get-tuple-element.36.share_ref, f32[256,2048]{1,0:T(8,128)} %get-tuple-element.37.own_ref, bf16[16,256,256]{2,1,0:T(8,128)(2,1)} %get-tuple-element.38.other_ref, ...), custom_call_target="tpu_custom_call" | custom-call | tf_op jit(solution)/shard_map/finish/pallas_call | solution.py:351
  55.9 0.0 collective-permute-done.9.vr_ref
  55.9 2.4 %finish.3 = bf16[256,2048]{1,0:T(8,128)(2,1)} custom-call(f32[256,2048]{1,0:T(8,128)} %get-tuple-element.35.sum_ref, f32[256,512]{1,0:T(8,128)} %get-tuple-element.36.share_ref, f32[256,2048]{1,0:T(8,128)} %get-tuple-element.37.own_ref, bf16[16,256,256]{2,1,0:T(8,128)(2,1)} %get-tuple-element.38.other_ref, ...), custom_call_target="tpu_custom_call", output_to_operand_aliasing={{}: (6, {})} | custom-call | tf_op jit(solution)/shard_map/finish/pallas_call | solution.py:351
  (14 shorter events, 0.0 us)
Async XLA Ops:
  0.0 27.1 %collective-permute-start = (bf16[256,2048]{1,0:T(8,128)(2,1)}, bf16[256,2048]{1,0:T(8,128)(2,1)S(1)}, u32[]{:S(2)}, u32[]{:S(2)}) collective-permute-start(bf16[256,2048]{1,0:T(8,128)(2,1)} %k_ref.5), channel_id=1, source_target_pairs={{0,8},{8,0},{16,24},{24,16},{1,9},{9,1},{17,25},{25,17},{2,10},{10... | collective-permute-start | bytes 3145736 | tf_op jit(solution)/shard_map/ppermute | solution.py:23
  2.9 1.3 %copy-start = (bf16[256,2048]{1,0:T(8,128)(2,1)S(1)}, bf16[256,2048]{1,0:T(8,128)(2,1)}, u32[]{:S(2)}) copy-start(bf16[256,2048]{1,0:T(8,128)(2,1)} %k_ref.5) | copy-start | bytes 3145732
  4.2 1.2 %copy-start.1 = (bf16[256,2048]{1,0:T(8,128)(2,1)S(1)}, bf16[256,2048]{1,0:T(8,128)(2,1)}, u32[]{:S(2)}) copy-start(bf16[256,2048]{1,0:T(8,128)(2,1)} %v_ref.5) | copy-start | bytes 3145732
  5.4 0.7 %copy-start.2 = (s32[16]{0:T(128)S(1)}, s32[16]{0:T(128)}, u32[]{:S(2)}) copy-start(s32[16]{0:T(128)} %middle_ref.9) | copy-start | bytes 196
  6.1 0.7 %copy-start.4 = (s32[16]{0:T(128)S(1)}, s32[16]{0:T(128)}, u32[]{:S(2)}) copy-start(s32[16]{0:T(128)} %coarse_ref.3) | copy-start | bytes 196
  6.7 20.4 %copy-start.3 = (s32[16]{0:T(128)S(1)}, s32[16]{0:T(128)}, u32[]{:S(2)}) copy-start(s32[16]{0:T(128)} %middle_ref.9) | copy-start | bytes 196
  9.5 13.6 %collective-permute-start.5 = (bf16[128,2048]{1,0:T(8,128)(2,1)}, bf16[128,2048]{1,0:T(8,128)(2,1)S(1)}, u32[]{:S(2)}, u32[]{:S(2)}) collective-permute-start(bf16[128,2048]{1,0:T(8,128)(2,1)} %get-tuple-element.29), channel_id=1, source_target_pairs={{0,16},{8,24},{16,0},{24,8},{1,17},{9,25},{17,1},{25,9},{2,18},{10... | collective-permute-start | bytes 1572872 | tf_op jit(solution)/shard_map/ppermute | solution.py:23
  11.1 1.2 %collective-permute-start.1 = (bf16[2,2048]{1,0:T(2,128)(2,1)S(1)}, bf16[2,2048]{1,0:T(2,128)(2,1)S(1)}, u32[]{:S(2)}, u32[]{:S(2)}) collective-permute-start(bf16[2,2048]{1,0:T(2,128)(2,1)S(1)} %get-tuple-element.23), channel_id=1, source_target_pairs={{0,1},{1,0},{2,3},{3,2},{4,5},{5,4},{6,7},{7,6},{8,9},{9,8},{10,11... | collective-permute-start | bytes 24584 | tf_op jit(solution)/shard_map/ppermute | solution.py:23
  12.3 5.6 %collective-permute-start.4 = (bf16[4,2048]{1,0:T(4,128)(2,1)S(1)}, bf16[4,2048]{1,0:T(4,128)(2,1)S(1)}, u32[]{:S(2)}, u32[]{:S(2)}) collective-permute-start(bf16[4,2048]{1,0:T(4,128)(2,1)S(1)} %pad_maximum_fusion), channel_id=1, source_target_pairs={{0,6},{1,7},{2,4},{3,5},{4,2},{5,3},{6,0},{7,1},{8,14},{9,15},{10,... | collective-permute-start | bytes 49160 | tf_op jit(solution)/shard_map/ppermute | solution.py:23
  15.9 4.6 %collective-permute-start.3 = (bf16[4,2048]{1,0:T(4,128)(2,1)S(1)}, bf16[4,2048]{1,0:T(4,128)(2,1)S(1)}, u32[]{:S(2)}, u32[]{:S(2)}) collective-permute-start(bf16[4,2048]{1,0:T(4,128)(2,1)S(1)} %pad_maximum_fusion), channel_id=1, source_target_pairs={{0,4},{1,5},{2,6},{3,7},{4,0},{5,1},{6,2},{7,3},{8,12},{9,13},{10,... | collective-permute-start | bytes 49160 | tf_op jit(solution)/shard_map/ppermute | solution.py:23
  15.9 4.6 %collective-permute-start.2 = (bf16[4,2048]{1,0:T(4,128)(2,1)S(1)}, bf16[4,2048]{1,0:T(4,128)(2,1)S(1)}, u32[]{:S(2)}, u32[]{:S(2)}) collective-permute-start(bf16[4,2048]{1,0:T(4,128)(2,1)S(1)} %pad_maximum_fusion), channel_id=1, source_target_pairs={{0,2},{1,3},{2,0},{3,1},{4,6},{5,7},{6,4},{7,5},{8,10},{9,11},{10,... | collective-permute-start | bytes 49160 | tf_op jit(solution)/shard_map/ppermute | solution.py:23
  21.3 15.8 %collective-permute-start.7 = (bf16[80,2048]{1,0:T(8,128)(2,1)}, bf16[80,2048]{1,0:T(8,128)(2,1)S(1)}, u32[]{:S(2)}, u32[]{:S(2)}) collective-permute-start(bf16[80,2048]{1,0:T(8,128)(2,1)} %append.1), channel_id=1, source_target_pairs={{0,8},{8,0},{16,24},{24,16},{1,9},{9,1},{17,25},{25,17},{2,10},{10... | collective-permute-start | bytes 983048 | tf_op jit(solution)/shard_map/ppermute | solution.py:23
  23.1 28.4 %collective-permute-start.10 = (bf16[192,1536]{1,0:T(8,128)(2,1)}, bf16[192,1536]{1,0:T(8,128)(2,1)S(1)}, u32[]{:S(2)}, u32[]{:S(2)}) collective-permute-start(bf16[192,1536]{1,0:T(8,128)(2,1)} %get-tuple-element.40), channel_id=1, source_target_pairs={{0,8},{8,0},{16,24},{24,16},{1,9},{9,1},{17,25},{25,17},{2,10},{10... | collective-permute-start | bytes 1769480 | tf_op jit(solution)/shard_map/ppermute | solution.py:23
  28.7 8.5 %copy-start.6 = (bf16[192,512]{1,0:T(8,128)(2,1)S(1)}, bf16[192,512]{1,0:T(8,128)(2,1)}, u32[]{:S(2)}) copy-start(bf16[192,512]{1,0:T(8,128)(2,1)} %get-tuple-element.39) | copy-start | bytes 589828
  28.7 16.8 %collective-permute-start.6 = (bf16[80,2048]{1,0:T(8,128)(2,1)}, bf16[80,2048]{1,0:T(8,128)(2,1)S(1)}, u32[]{:S(2)}, u32[]{:S(2)}) collective-permute-start(bf16[80,2048]{1,0:T(8,128)(2,1)} %pick.1), channel_id=1, source_target_pairs={{0,16},{8,24},{16,0},{24,8},{1,17},{9,25},{17,1},{25,9},{2,18},{10... | collective-permute-start | bytes 983048 | tf_op jit(solution)/shard_map/ppermute | solution.py:23
  37.1 8.4 %collective-permute-start.8 = (bf16[80,2048]{1,0:T(8,128)(2,1)S(1)}, bf16[80,2048]{1,0:T(8,128)(2,1)S(1)}, u32[]{:S(2)}, u32[]{:S(2)}) collective-permute-start(bf16[80,2048]{1,0:T(8,128)(2,1)S(1)} %collective-permute-done.7.other_ref.vm_ref), channel_id=1, source_target_pairs={{0,16},{8,24},{16,0},{24,8},{1,17},{9,25},{17,1},{25,9},{2,18},{10... | collective-permute-start | bytes 983048 | tf_op jit(solution)/shard_map/ppermute | solution.py:23
  37.2 18.7 %collective-permute-start.9 = (bf16[192,512]{1,0:T(8,128)(2,1)S(1)}, bf16[192,512]{1,0:T(8,128)(2,1)S(1)}, u32[]{:S(2)}, u32[]{:S(2)}) collective-permute-start(bf16[192,512]{1,0:T(8,128)(2,1)S(1)} %copy-done.6), channel_id=1, source_target_pairs={{0,8},{8,0},{16,24},{24,16},{1,9},{9,1},{17,25},{25,17},{2,10},{10... | collective-permute-start | bytes 589832 | tf_op jit(solution)/shard_map/ppermute | solution.py:23
  39.2 6.3 %copy-start.5 = (s32[16]{0:T(128)S(1)}, s32[16]{0:T(128)}, u32[]{:S(2)}) copy-start(s32[16]{0:T(128)} %coarse_ref.3) | copy-start | bytes 196

commit v5 on v4

v5 whole, which is shorter than its diff:
```python
import functools

import jax
import jax.numpy as jnp
from jax import lax
from jax.experimental import pallas as pl
from jax.experimental.pallas import tpu as pltpu
from jax.sharding import PartitionSpec as P

HEAD_COUNT = 16
HEAD_FEATURES = 128
MIDDLE_DILATION = 4
CHUNKS = (12, 4)
LANES = 128
SUBLANES = 16
EXP2_SCALE = HEAD_FEATURES ** (-0.5) * 1.4426950408889634
MASKED = -1e30


def partner(value, axis, mask):
    pairs = [(source, source ^ mask) for source in range(lax.axis_size(axis))]
    return lax.ppermute(value, axis, pairs)


def one_hot(mask):
    return mask.astype(jnp.float32).astype(jnp.bfloat16)


def fill_orders(order_ref):
    rows = order_ref.shape[1]
    members = rows // MIDDLE_DILATION
    group = lax.broadcasted_iota(jnp.int32, (members, rows), 0)
    token = lax.broadcasted_iota(jnp.int32, (members, rows), 1)
    for place in range(MIDDLE_DILATION):
        block = one_hot(token == MIDDLE_DILATION * group + place)
        for shift in range(MIDDLE_DILATION):
            slot = (place - shift) % MIDDLE_DILATION
            order_ref[shift, slot * members : (slot + 1) * members] = block


def dot(a, b):
    return jnp.dot(a, b, preferred_element_type=jnp.float32)


def head_columns(head):
    return slice(head * HEAD_FEATURES, (head + 1) * HEAD_FEATURES)


def prepare_kernel(chunks, middle_ref, coarse_ref, q_hbm, k_hbm, v_hbm, *rest):
    q_ref, k_ref, v_ref, members_ref, vm_ref, *vr_refs, coarse_out_ref, order_ref, semaphores = rest
    pairs = ((k_hbm, k_ref), (v_hbm, v_ref), (q_hbm, q_ref))
    copies = [pltpu.make_async_copy(*pair, semaphores.at[i]) for i, pair in enumerate(pairs)]
    for copy in copies:
        copy.start()
    rows = k_ref.shape[0]
    members = rows // MIDDLE_DILATION
    fill_orders(order_ref)
    token = lax.broadcasted_iota(jnp.int32, (SUBLANES, rows), 1)
    first_row = lax.broadcasted_iota(jnp.int32, (SUBLANES, rows), 0) == 0
    second_row = lax.broadcasted_iota(jnp.int32, (SUBLANES, rows), 0) == 1
    copies[0].wait()
    copies[1].wait()
    head = 0
    for chunk, vr_ref in zip(chunks, vr_refs):
        for place in range(chunk):
            columns = head_columns(head)
            order = order_ref[middle_ref[head]]
            k, v = k_ref[:, columns], v_ref[:, columns]
            v_ordered = dot(order, v).astype(jnp.bfloat16)
            members_ref[:members, columns] = dot(order[:members], k).astype(jnp.bfloat16)
            members_ref[members:, columns] = v_ordered[:members]
            vm_ref[:, columns] = v_ordered[:members]
            vr_ref[:, head_columns(place)] = v_ordered[members:]
            chosen = token == coarse_ref[head]
            picked = dot(one_hot(chosen & first_row), k) + dot(one_hot(chosen & second_row), v)
            coarse_out_ref[:, columns] = picked[:2].astype(jnp.bfloat16)
            head += 1
    copies[2].wait()


def join_kernel(vm_ref, near_ref, out_ref):
    members = vm_ref.shape[0]
    out_ref[:members] = vm_ref[...]
    out_ref[members:] = near_ref[...]


def pick_kernel(middle_ref, k_ref, near_ref, members_ref):
    rows = k_ref.shape[0]
    members = rows // MIDDLE_DILATION
    members_ref[members:] = near_ref[...]
    group = lax.broadcasted_iota(jnp.int32, (members, rows), 0)
    token = lax.broadcasted_iota(jnp.int32, (members, rows), 1)
    offset = token - MIDDLE_DILATION * group
    for head in range(HEAD_COUNT):
        columns = head_columns(head)
        chosen = one_hot(offset == middle_ref[head])
        members_ref[:members, columns] = dot(chosen, k_ref[:, columns]).astype(jnp.bfloat16)


def dot_keys(q, keys):
    return lax.dot_general(q, keys, (((1,), (1,)), ((), ())), preferred_element_type=jnp.float32)


def dot_rows(a, b):
    return lax.dot_general(a, b, (((0,), (0,)), ((), ())), preferred_element_type=jnp.float32)


def side_by_side(columns):
    rows = columns[0].shape[0]
    lane = lax.broadcasted_iota(jnp.int32, (rows, LANES), 1)
    result = jnp.zeros((rows, LANES), jnp.float32)
    for place, column in enumerate(columns):
        result = jnp.where(lane == place, column, result)
    return result


def member_rows(rows, shift):
    row = lax.broadcasted_iota(jnp.int32, (rows, 1), 0)
    return (row & (MIDDLE_DILATION - 1)) == shift


def lane_tiles(part):
    return [part[:, i : i + LANES] for i in range(0, part.shape[1], LANES)]


def weights(part, top):
    return jnp.exp2((part - top) * EXP2_SCALE)


def first_kernel(first, middle_ref, q_ref, k_ref, v_ref, kp_ref, own_ref, other_ref, state_ref, order_ref):
    fill_orders(order_ref)
    rows = q_ref.shape[0]
    members = rows // MIDDLE_DILATION
    column = lax.broadcasted_iota(jnp.int32, (1, rows), 1)
    tops, totals = [], []
    heads = other_ref.shape[0]
    for place in range(heads):
        columns = head_columns(first + place)
        shift = middle_ref[first + place]
        q = q_ref[:, columns]
        own = dot_keys(q, k_ref[:, columns])
        other_keys = dot(order_ref[shift], kp_ref[:, columns]).astype(jnp.bfloat16)
        other = dot_keys(q, other_keys)
        top = functools.reduce(jnp.maximum, lane_tiles(own) + lane_tiles(other))
        top = jnp.max(top, axis=1, keepdims=True)
        row_is_member = member_rows(rows, shift)
        own, other = weights(own, top), weights(other, top)
        own_member = row_is_member & ((column & (MIDDLE_DILATION - 1)) == shift)
        own = jnp.where(own_member, own + own, own)
        twice = other[:, :LANES]
        twice = jnp.where(row_is_member & (column[:, :LANES] < members), twice + twice, twice)
        other = jnp.concatenate([twice, other[:, LANES:]], axis=1)
        total = functools.reduce(jnp.add, lane_tiles(own) + lane_tiles(other))
        tops.append(top)
        totals.append(jnp.sum(total, axis=1, keepdims=True))
        own_ref[:, head_columns(place)] = dot(own.astype(jnp.bfloat16), v_ref[:, columns])
        other_ref[place] = other.astype(jnp.bfloat16)
    state_ref[...] = side_by_side(tops + totals)


def extra_kernel(
    middle_ref, coarse_ref, q_ref, state_a_ref, state_b_ref, cross_ref, diagonal_k_ref, diagonal_v_ref, near_ref,
    other_ref, sum_ref, share_ref,
):
    rows = q_ref.shape[0]
    members = rows // MIDDLE_DILATION
    half = HEAD_COUNT // 2
    token = lax.broadcasted_iota(jnp.int32, (1, rows), 1)
    states = [ref[...].T for ref in (state_a_ref, state_b_ref)]
    shares = []
    for head in range(HEAD_COUNT):
        columns = head_columns(head)
        state, place = states[head // half], head % half
        q = q_ref[:, columns]
        far_keys = jnp.concatenate([cross_ref[:members, columns], diagonal_k_ref[:members, columns]], axis=0)
        far_values = jnp.concatenate([cross_ref[members:, columns], diagonal_v_ref[:members, columns]], axis=0)
        pieces = [near_ref[:, columns]] + [
            ref[members:, columns] for ref in (other_ref, diagonal_k_ref, diagonal_v_ref)
        ]
        pairs = jnp.concatenate(pieces, axis=0)
        is_key = (lax.broadcasted_iota(jnp.int32, (pairs.shape[0], 1), 0) & 1) == 0
        row_is_member = (token & (MIDDLE_DILATION - 1)) == middle_ref[head]
        far = jnp.where(row_is_member, dot_keys(far_keys, q), MASKED)
        coarse = jnp.where(is_key & (token == coarse_ref[head]), dot_keys(pairs, q), MASKED)
        before = state[place : place + 1]
        top = jnp.maximum(before, jnp.max(far, axis=0, keepdims=True))
        top = jnp.maximum(top, jnp.max(coarse, axis=0, keepdims=True))
        far, coarse = weights(far, top), weights(coarse, top)
        kept = weights(before, top)
        total = kept * state[half + place : half + place + 1]
        total += jnp.sum(far, axis=0, keepdims=True) + jnp.sum(coarse, axis=0, keepdims=True)
        inverse = 1.0 / total
        coarse = pltpu.roll(coarse, 1, 0)
        summed = dot_rows(far_values, far.astype(jnp.bfloat16)) + dot_rows(pairs, coarse.astype(jnp.bfloat16))
        sum_ref[:, columns] = (summed * inverse).T
        shares.append(kept * inverse)
    share_ref[:, :HEAD_COUNT] = jnp.concatenate(shares, axis=0).T


def finish_kernel(heads, sum_ref, share_ref, own_a_ref, own_b_ref, other_a_ref, other_b_ref, vm_ref, vr_ref, *rest):
    out_ref, ready_ref, semaphores = rest[-3:]
    members = vr_ref.shape[0] // (MIDDLE_DILATION - 1)
    half = HEAD_COUNT // 2
    copies = []
    for place, head in enumerate(heads):
        columns = head_columns(head)
        own_ref, other_ref = ((own_a_ref, other_a_ref), (own_b_ref, other_b_ref))[head // half]
        values = jnp.concatenate([vm_ref[:members, columns], vr_ref[:, head_columns(place)]], axis=0)
        result = own_ref[:, head_columns(head % half)] + dot(other_ref[head % half], values)
        result = sum_ref[:, columns] + share_ref[:, head : head + 1] * result
        ready_ref[place] = result.astype(jnp.bfloat16)
        copies.append(pltpu.make_async_copy(ready_ref.at[place], out_ref.at[:, columns], semaphores.at[place]))
        copies[-1].start()
    for copy in copies:
        copy.wait()


def in_hbm(array):
    return pltpu.with_memory_space_constraint(array, pltpu.HBM)


def cost():
    return pl.CostEstimate(flops=0, bytes_accessed=0, transcendentals=0)


def gather_all(value, axis):
    size = lax.axis_size(axis)
    if size & (size - 1):
        return lax.all_gather(value, axis, axis=0, tiled=True)
    bits = [2**j for j in range(size.bit_length() - 1)]
    for step in [bits[:1]] + [bits[j : j + 2] for j in range(1, len(bits), 2)]:
        masks = step + [sum(step)] if len(step) == 2 else step
        value = jnp.concatenate([value] + [partner(value, axis, mask) for mask in masks], axis=0)
    return value


def on_device(query, keys, values, middle_head_shift, coarse_head_shift):
    rows, width = query.shape
    members = rows // MIDDLE_DILATION
    near_rows = 2 * lax.axis_size("outer")
    half = HEAD_COUNT // 2
    bf16, f32 = jnp.bfloat16, jnp.float32
    smem = pl.BlockSpec(memory_space=pltpu.SMEM)
    vmem = pl.BlockSpec(memory_space=pltpu.VMEM)
    anywhere = pl.BlockSpec(memory_space=pl.ANY)
    params = pltpu.CompilerParams(vmem_limit_bytes=16 * 1024 * 1024)
    orders = pltpu.VMEM((MIDDLE_DILATION, rows, rows), bf16)

    def call(kernel, name, *args, **options):
        return pl.pallas_call(kernel, name=name, compiler_params=params, cost_estimate=cost(), **options)(*args)

    other_keys = partner(keys, "inner", 1)
    q, k, v, own_members, own_vm, *own_vr, coarse = call(
        functools.partial(prepare_kernel, CHUNKS),
        "prepare",
        middle_head_shift, coarse_head_shift, in_hbm(query), in_hbm(keys), in_hbm(values),
        out_shape=[
            *[pltpu.VMEM((rows, width), bf16)] * 3,
            pltpu.VMEM((2 * members, width), bf16),
            pltpu.VMEM((members, width), bf16),
            *[pltpu.VMEM((rows - members, c * HEAD_FEATURES), bf16) for c in CHUNKS],
            pltpu.VMEM((2, width), bf16),
        ],
        in_specs=[smem, smem, anywhere, anywhere, anywhere],
        out_specs=[vmem] * (6 + len(CHUNKS)),
        scratch_shapes=[orders, pltpu.SemaphoreType.DMA((3,))],
    )
    cross = partner(own_members, "inner", 2)
    near = gather_all(coarse, "outer")
    own_vm = call(
        join_kernel,
        "join",
        own_vm, near,
        out_shape=pltpu.VMEM((members + near_rows, width), bf16),
        in_specs=[vmem, vmem],
        out_specs=vmem,
    )
    other_vm = partner(own_vm, "inner", 1)
    cross, own_vr = lax.optimization_barrier((cross, own_vr))
    other_vr = [partner(piece, "inner", 1) for piece in own_vr]
    other_km = call(
        pick_kernel,
        "pick",
        middle_head_shift, other_keys, near,
        out_shape=pltpu.VMEM((members + near_rows, width), bf16),
        in_specs=[smem, vmem, vmem],
        out_specs=vmem,
    )
    diagonal_k = partner(other_km, "inner", 2)
    other_keys = lax.optimization_barrier((other_keys, other_km))[0]

    def first_part(first, query):
        return call(
            functools.partial(first_kernel, first),
            "first",
            middle_head_shift, query, k, v, other_keys,
            out_shape=[
                pltpu.VMEM((rows, half * HEAD_FEATURES), f32),
                pltpu.VMEM((half, rows, rows), bf16),
                pltpu.VMEM((rows, LANES), f32),
            ],
            in_specs=[smem] + [vmem] * 4,
            out_specs=[vmem] * 3,
            scratch_shapes=[orders],
        )

    own_a, weights_a, state_a = first_part(0, q)
    diagonal_v = partner(lax.optimization_barrier((other_vm, state_a))[0], "inner", 2)
    own_b, weights_b, state_b = first_part(half, lax.optimization_barrier((q, state_a))[0])
    extra_sum, share = call(
        extra_kernel,
        "extra",
        middle_head_shift, coarse_head_shift, q, state_a, state_b, cross, diagonal_k, diagonal_v, near, other_vm,
        out_shape=[pltpu.VMEM((rows, width), f32), pltpu.VMEM((rows, LANES), f32)],
        in_specs=[smem, smem] + [vmem] * 8,
        out_specs=[vmem] * 2,
    )

    out = []
    first = 0
    for chunk, vr in zip(CHUNKS, other_vr):
        args = [extra_sum, share, own_a, own_b, weights_a, weights_b, other_vm, vr]
        out = [
            call(
                functools.partial(finish_kernel, range(first, first + chunk)),
                "finish",
                *args, *out,
                out_shape=jax.ShapeDtypeStruct((rows, width), bf16),
                in_specs=[vmem] * len(args) + [anywhere] * len(out),
                out_specs=anywhere,
                input_output_aliases={len(args): 0} if out else {},
                scratch_shapes=[pltpu.VMEM((chunk, rows, HEAD_FEATURES), bf16), pltpu.SemaphoreType.DMA((chunk,))],
            )
        ]
        first += chunk
    return out[0]


def solution(mesh):
    placed = (
        P(("outer", "inner"), None),
        P(("outer", "inner"), None),
        P(("outer", "inner"), None),
        P(),
        P(),
    )
    return jax.shard_map(
        on_device,
        mesh=mesh,
        in_specs=placed,
        out_specs=P(("outer", "inner"), None),
        check_vma=False,
    )
```

time: 58.8 us -> 51.4 us (0.87)
  Pallas kernels: 30.4 us -> 20.5 us
  starting transfers between devices: 14 us -> 16 us
  local copies, waits for them, and re-layouts: 3.88 us -> 4.59 us
    pallas_call x8, Pallas kernels: 30.4 us -> 20.5 us  [call(): pl.pallas_call(kernel, name=name, compiler_params=params, cost_estimate=c...]
    ppermute x11, starting transfers between devices: 14 us -> 16 us  [partner(): return lax.ppermute(value, axis, pairs)]
    concatenate x1, local copies, waits for them, and re-layouts: 0.08 us -> 0.79 us  [gather_all(): jnp.concatenate([value] + [partner(value, axis, mask) for mask in masks],...]
    unnamed x14 -> x18, local copies, waits for them, and re-layouts: 3.8 us -> 3.8 us
  transfers between devices with their start and end apart: 11 -> 11, of which waited for: 5 -> 8; matrix products, arithmetic and copies ran while one was open for 0% -> 2% of each run, Pallas kernels for 48% -> 38%
where the time goes in v5:
time: 51.4 us; the launch traced here: 51.2 us
  Pallas kernels  20.5 us (40%)
  starting transfers between devices  16 us (31%)
  waiting for transfers between devices  10 us (19%)
  local copies, waits for them, and re-layouts  4.59 us (9%)
    pallas_call x8, Pallas kernels, call(): pl.pallas_call(kernel, name=name, compiler_params=params, cost_estimate=c...  20.5 us
    ppermute x11, starting transfers between devices, partner(): return lax.ppermute(value, axis, pairs)  16 us
    ppermute x11, waiting for transfers between devices, partner(): return lax.ppermute(value, axis, pairs)  10 us
    unnamed x18, local copies, waits for them, and re-layouts  3.8 us
  transfers between devices with their start and end apart: 11, of which 8 were waited for; matrix products, arithmetic and copies ran while one was open for 2% of the time, Pallas kernels for 38%

profile of v5, /device:TPU:0, one launch (start us, length us, event | category | flops | bytes accessed | tf_op | source)
XLA Modules:
  0.0 51.2 jit_solution(17676681505366829037)
XLA Ops:
  0.0 2.9 %collective-permute-start = (bf16[256,2048]{1,0:T(8,128)(2,1)}, bf16[256,2048]{1,0:T(8,128)(2,1)S(1)}, u32[]{:S(2)}, u32[]{:S(2)}) collective-permute-start(bf16[256,2048]{1,0:T(8,128)(2,1)} %k_hbm.1), channel_id=1, source_target_pairs={{0,8},{8,0},{16,24},{24,16},{1,9},{9,1},{17,25},{25,17},{2,10},{10... | collective-permute-start | bytes 3145736 | tf_op jit(solution)/shard_map/ppermute | solution.py:22
  2.9 0.7 %copy-done.2 = s32[16]{0:T(128)S(1)} copy-done((s32[16]{0:T(128)S(1)}, s32[16]{0:T(128)}, u32[]{:S(2)}) %copy-start.2) | copy-done | bytes 88
  3.6 0.7 %copy-done.4 = s32[16]{0:T(128)S(1)} copy-done((s32[16]{0:T(128)S(1)}, s32[16]{0:T(128)}, u32[]{:S(2)}) %copy-start.4) | copy-done | bytes 88
  4.3 4.0 %prepare.1 = (bf16[256,2048]{1,0:T(8,128)(2,1)S(1)}, bf16[256,2048]{1,0:T(8,128)(2,1)S(1)}, bf16[256,2048]{1,0:T(8,128)(2,1)S(1)}, bf16[128,2048]{1,0:T(8,128)(2...) custom-call(s32[16]{0:T(128)S(1)} %copy-done.2, ...), custom_call_target="tpu_custom_call" | custom-call | tf_op jit(solution)/shard_map/prepare/pallas_call | solution.py:250
  8.3 0.0 copy-start
  8.3 1.0 %copy-done = bf16[256,2048]{1,0:T(8,128)(2,1)} copy-done((bf16[256,2048]{1,0:T(8,128)(2,1)}, bf16[256,2048]{1,0:T(8,128)(2,1)S(1)}, u32[]{:S(2)}) %copy-start) | copy-done | bytes 1048600
  9.3 0.8 %copy-done.6 = bf16[192,1536]{1,0:T(8,128)(2,1)} copy-done((bf16[192,1536]{1,0:T(8,128)(2,1)}, bf16[192,1536]{1,0:T(8,128)(2,1)S(1)}, u32[]{:S(2)}) %copy-start.6) | copy-done | bytes 589848
  10.1 0.7 %copy-done.7 = bf16[192,512]{1,0:T(8,128)(2,1)} copy-done((bf16[192,512]{1,0:T(8,128)(2,1)}, bf16[192,512]{1,0:T(8,128)(2,1)S(1)}, u32[]{:S(2)}) %copy-start.7) | copy-done | bytes 196632
  10.8 1.5 %collective-permute-start.5 = (bf16[128,2048]{1,0:T(8,128)(2,1)}, bf16[128,2048]{1,0:T(8,128)(2,1)}, u32[]{:S(2)}, u32[]{:S(2)}) collective-permute-start(bf16[128,2048]{1,0:T(8,128)(2,1)} %get-tuple-element.35), channel_id=1, source_target_pairs={{0,16},{8,24},{16,0},{24,8},{1,17},{9,25},{17,1},{25,9},{2,18},{10... | collective-permute-start | bytes 1572872 | tf_op jit(solution)/shard_map/ppermute | solution.py:22
  12.3 1.2 %collective-permute-done.1 = bf16[2,2048]{1,0:T(2,128)(2,1)S(1)} collective-permute-done((bf16[2,2048]{1,0:T(2,128)(2,1)S(1)}, bf16[2,2048]{1,0:T(2,128)(2,1)S(1)}, u32[]{:S(2)}, u32[]{:S(2)}) %collective-permute-start.1) | collective-permute-done | bytes 8224 | tf_op jit(solution)/shard_map/ppermute | solution.py:22
  13.5 1.6 %collective-permute-start.2 = (bf16[4,2048]{1,0:T(4,128)(2,1)S(1)}, bf16[4,2048]{1,0:T(4,128)(2,1)S(1)}, u32[]{:S(2)}, u32[]{:S(2)}) collective-permute-start(bf16[4,2048]{1,0:T(4,128)(2,1)S(1)} %pad_maximum_fusion), channel_id=1, source_target_pairs={{0,2},{1,3},{2,0},{3,1},{4,6},{5,7},{6,4},{7,5},{8,10},{9,11},{10,... | collective-permute-start | bytes 49160 | tf_op jit(solution)/shard_map/ppermute | solution.py:22
  15.1 2.6 %collective-permute-start.3 = (bf16[4,2048]{1,0:T(4,128)(2,1)S(1)}, bf16[4,2048]{1,0:T(4,128)(2,1)S(1)}, u32[]{:S(2)}, u32[]{:S(2)}) collective-permute-start(bf16[4,2048]{1,0:T(4,128)(2,1)S(1)} %pad_maximum_fusion), channel_id=1, source_target_pairs={{0,4},{1,5},{2,6},{3,7},{4,0},{5,1},{6,2},{7,3},{8,12},{9,13},{10,... | collective-permute-start | bytes 49160 | tf_op jit(solution)/shard_map/ppermute | solution.py:22
  17.7 0.2 collective-permute-start.4
  18.0 1.9 %collective-permute-done.3 = bf16[4,2048]{1,0:T(4,128)(2,1)S(1)} collective-permute-done((bf16[4,2048]{1,0:T(4,128)(2,1)S(1)}, bf16[4,2048]{1,0:T(4,128)(2,1)S(1)}, u32[]{:S(2)}, u32[]{:S(2)}) %collective-permute-start.3) | collective-permute-done | bytes 16416 | tf_op jit(solution)/shard_map/ppermute | solution.py:22
  19.9 3.5 %collective-permute-done.4 = bf16[4,2048]{1,0:T(4,128)(2,1)} collective-permute-done((bf16[4,2048]{1,0:T(4,128)(2,1)S(1)}, bf16[4,2048]{1,0:T(4,128)(2,1)}, u32[]{:S(2)}, u32[]{:S(2)}) %collective-permute-start.4) | collective-permute-done | bytes 16416 | tf_op jit(solution)/shard_map/ppermute | solution.py:22
  23.4 0.8 %concatenate.8.near_ref = bf16[16,2048]{1,0:T(8,128)(2,1)S(1)} concatenate(bf16[2,2048]{1,0:T(2,128)(2,1)S(1)} %get-tuple-element.30, bf16[2,2048]{1,0:T(2,128)(2,1)S(1)} %collective-permute-done.1, bf16[4,2048]{1,0:T(4,128)(2,1)S(1)} %collective-permute-done.2, bf16[4,2048]{1,0:T(4,128)(2,1)S(1)} %collective-permute-done.3, bf16[4,2048]{1,0:T(4,128)(2,1)} %collective-permute-done.4), dimensions={0} | concatenate | bytes 131072 | tf_op jit(solution)/shard_map/concatenate | solution.py:233
  24.2 0.6 %collective-permute-start.7 = (bf16[80,2048]{1,0:T(8,128)(2,1)S(1)}, bf16[80,2048]{1,0:T(8,128)(2,1)S(1)}, u32[]{:S(2)}, u32[]{:S(2)}) collective-permute-start(bf16[80,2048]{1,0:T(8,128)(2,1)S(1)} %join.1), channel_id=1, source_target_pairs={{0,8},{8,0},{16,24},{24,16},{1,9},{9,1},{17,25},{25,17},{2,10},{10... | collective-permute-start | bytes 983048 | tf_op jit(solution)/shard_map/ppermute | solution.py:22
  24.8 1.5 %collective-permute-start.10 = (bf16[192,1536]{1,0:T(8,128)(2,1)}, bf16[192,1536]{1,0:T(8,128)(2,1)S(1)}, u32[]{:S(2)}, u32[]{:S(2)}) collective-permute-start(bf16[192,1536]{1,0:T(8,128)(2,1)} %copy-done.6), channel_id=1, source_target_pairs={{0,8},{8,0},{16,24},{24,16},{1,9},{9,1},{17,25},{25,17},{2,10},{10... | collective-permute-start | bytes 1769480 | tf_op jit(solution)/shard_map/ppermute | solution.py:22
  26.3 0.8 %collective-permute-done.k_ref.kp_ref = bf16[256,2048]{1,0:T(8,128)(2,1)S(1)} collective-permute-done((bf16[256,2048]{1,0:T(8,128)(2,1)}, bf16[256,2048]{1,0:T(8,128)(2,1)S(1)}, u32[]{:S(2)}, u32[]{:S(2)}) %collective-permute-start) | collective-permute-done | bytes 1048608 | tf_op jit(solution)/shard_map/ppermute | solution.py:22
  27.1 0.8 %pick.1 = bf16[80,2048]{1,0:T(8,128)(2,1)S(1)} custom-call(s32[16]{0:T(128)S(1)} %copy-done.3, bf16[256,2048]{1,0:T(8,128)(2,1)S(1)} %collective-permute-done.k_ref.kp_ref, bf16[16,2048]{1,0:T(8,128)(2,1)S(1)} %concatenate.8.near_ref), custom_call_target="tpu_custom_call" | custom-call | tf_op jit(solution)/shard_map/pick/pallas_call | solution.py:250
  28.0 2.2 %collective-permute-start.6 = (bf16[80,2048]{1,0:T(8,128)(2,1)S(1)}, bf16[80,2048]{1,0:T(8,128)(2,1)S(1)}, u32[]{:S(2)}, u32[]{:S(2)}) collective-permute-start(bf16[80,2048]{1,0:T(8,128)(2,1)S(1)} %pick.1), channel_id=1, source_target_pairs={{0,16},{8,24},{16,0},{24,8},{1,17},{9,25},{17,1},{25,9},{2,18},{10... | collective-permute-start | bytes 983048 | tf_op jit(solution)/shard_map/ppermute | solution.py:22
  30.1 4.6 %first.2 = (f32[256,1024]{1,0:T(8,128)S(1)}, bf16[8,256,256]{2,1,0:T(8,128)(2,1)S(1)}, f32[256,128]{1,0:T(8,128)S(1)}) custom-call(s32[16]{0:T(128)S(1)} %copy-done.3, bf16[256,2048]{1,0:T(8,128)(2,1)S(1)} %get-tuple-element.33.q_ref, bf16[256,2048]{1,0:T(8,128)(2,1)S(1)} %get-tuple-element.28.k_ref, bf16[256,2048]{1,0:T(8,128)(2,1)S(1)} %copy-done.1, ...), custom_call_target="tpu_custom_call" | custom-call | tf_op jit(solution)/shard_map/first/pallas_call | solution.py:250
  34.8 0.1 collective-permute-done.7.other_ref.vm_ref
  34.9 1.3 %collective-permute-start.8 = (bf16[80,2048]{1,0:T(8,128)(2,1)S(1)}, bf16[80,2048]{1,0:T(8,128)(2,1)S(1)}, u32[]{:S(2)}, u32[]{:S(2)}) collective-permute-start(bf16[80,2048]{1,0:T(8,128)(2,1)S(1)} %collective-permute-done.7.other_ref.vm_ref), channel_id=1, source_target_pairs={{0,16},{8,24},{16,0},{24,8},{1,17},{9,25},{17,1},{25,9},{2,18},{10... | collective-permute-start | bytes 983048 | tf_op jit(solution)/shard_map/ppermute | solution.py:22
  36.3 1.5 %collective-permute-start.9 = (bf16[192,512]{1,0:T(8,128)(2,1)S(1)}, bf16[192,512]{1,0:T(8,128)(2,1)S(1)}, u32[]{:S(2)}, u32[]{:S(2)}) collective-permute-start(bf16[192,512]{1,0:T(8,128)(2,1)S(1)} %copy-done.8), channel_id=1, source_target_pairs={{0,8},{8,0},{16,24},{24,16},{1,9},{9,1},{17,25},{25,17},{2,10},{10... | collective-permute-start | bytes 589832 | tf_op jit(solution)/shard_map/ppermute | solution.py:22
  37.7 4.6 %first.3 = (f32[256,1024]{1,0:T(8,128)S(1)}, bf16[8,256,256]{2,1,0:T(8,128)(2,1)S(1)}, f32[256,128]{1,0:T(8,128)S(1)}) custom-call(s32[16]{0:T(128)S(1)} %copy-done.3, bf16[256,2048]{1,0:T(8,128)(2,1)S(1)} %get-tuple-element.33.q_ref, bf16[256,2048]{1,0:T(8,128)(2,1)S(1)} %get-tuple-element.28.k_ref, bf16[256,2048]{1,0:T(8,128)(2,1)S(1)} %copy-done.1, ...), custom_call_target="tpu_custom_call" | custom-call | tf_op jit(solution)/shard_map/first/pallas_call | solution.py:250
  42.4 0.7 %collective-permute-done.8.diagonal_v_ref = bf16[80,2048]{1,0:T(8,128)(2,1)S(1)} collective-permute-done((bf16[80,2048]{1,0:T(8,128)(2,1)S(1)}, bf16[80,2048]{1,0:T(8,128)(2,1)S(1)}, u32[]{:S(2)}, u32[]{:S(2)}) %collective-permute-start.8) | collective-permute-done | bytes 327712 | tf_op jit(solution)/shard_map/ppermute | solution.py:22
  43.1 3.9 %extra.1 = (f32[256,2048]{1,0:T(8,128)S(1)}, f32[256,128]{1,0:T(8,128)S(1)}) custom-call(s32[16]{0:T(128)S(1)} %copy-done.3, s32[16]{0:T(128)S(1)} %copy-done.5, bf16[256,2048]{1,0:T(8,128)(2,1)S(1)} %get-tuple-element.33.q_ref, f32[256,128]{1,0:T(8,128)S(1)} %get-tuple-element.32.state_a_ref, f32[256,128]{1,0:T(8,128)S(1)} %get-tuple-element.34.state_b_ref, ...), custom_call_target="tpu_custom_call" | custom-call | tf_op jit(solution)/shard_map/extra/pallas_call | solution.py:250
  47.1 0.5 collective-permute-done.10.vr_ref
  47.6 1.4 %finish.2.rest_0_ = bf16[256,2048]{1,0:T(8,128)(2,1)} custom-call(f32[256,2048]{1,0:T(8,128)S(1)} %get-tuple-element.41.sum_ref, f32[256,128]{1,0:T(8,128)S(1)} %get-tuple-element.42.share_ref, f32[256,1024]{1,0:T(8,128)S(1)} %get-tuple-element.43.own_a_ref, f32[256,1024]{1,0:T(8,128)S(1)} %get-tuple-element.44.own_b_ref, ...), custom_call_target="tpu_custom_call" | custom-call | tf_op jit(solution)/shard_map/finish/pallas_call | solution.py:250
  49.0 1.2 %collective-permute-done.9.vr_ref = bf16[192,512]{1,0:T(8,128)(2,1)S(1)} collective-permute-done((bf16[192,512]{1,0:T(8,128)(2,1)S(1)}, bf16[192,512]{1,0:T(8,128)(2,1)S(1)}, u32[]{:S(2)}, u32[]{:S(2)}) %collective-permute-start.9) | collective-permute-done | bytes 196640 | tf_op jit(solution)/shard_map/ppermute | solution.py:22
  50.2 1.0 %finish.3 = bf16[256,2048]{1,0:T(8,128)(2,1)} custom-call(f32[256,2048]{1,0:T(8,128)S(1)} %get-tuple-element.41.sum_ref, f32[256,128]{1,0:T(8,128)S(1)} %get-tuple-element.42.share_ref, f32[256,1024]{1,0:T(8,128)S(1)} %get-tuple-element.43.own_a_ref, f32[256,1024]{1,0:T(8,128)S(1)} %get-tuple-element.44.own_b_ref, ...), custom_call_target="tpu_custom_call", output_to_operand_aliasing={{}: (8, {})} | custom-call | tf_op jit(solution)/shard_map/finish/pallas_call | solution.py:250
  (18 shorter events, 0.1 us)
Async XLA Ops:
  0.0 27.1 %collective-permute-start = (bf16[256,2048]{1,0:T(8,128)(2,1)}, bf16[256,2048]{1,0:T(8,128)(2,1)S(1)}, u32[]{:S(2)}, u32[]{:S(2)}) collective-permute-start(bf16[256,2048]{1,0:T(8,128)(2,1)} %k_hbm.1), channel_id=1, source_target_pairs={{0,8},{8,0},{16,24},{24,16},{1,9},{9,1},{17,25},{25,17},{2,10},{10... | collective-permute-start | bytes 3145736 | tf_op jit(solution)/shard_map/ppermute | solution.py:22
  2.9 0.7 %copy-start.2 = (s32[16]{0:T(128)S(1)}, s32[16]{0:T(128)}, u32[]{:S(2)}) copy-start(s32[16]{0:T(128)} %middle_ref.9) | copy-start | bytes 196
  3.6 0.7 %copy-start.4 = (s32[16]{0:T(128)S(1)}, s32[16]{0:T(128)}, u32[]{:S(2)}) copy-start(s32[16]{0:T(128)} %coarse_ref.3) | copy-start | bytes 196
  4.3 22.9 %copy-start.3 = (s32[16]{0:T(128)S(1)}, s32[16]{0:T(128)}, u32[]{:S(2)}) copy-start(s32[16]{0:T(128)} %middle_ref.9) | copy-start | bytes 196
  8.3 1.0 %copy-start = (bf16[256,2048]{1,0:T(8,128)(2,1)}, bf16[256,2048]{1,0:T(8,128)(2,1)S(1)}, u32[]{:S(2)}) copy-start(bf16[256,2048]{1,0:T(8,128)(2,1)S(1)} %get-tuple-element.29.v_ref) | copy-start | bytes 3145732
  9.3 0.8 %copy-start.6 = (bf16[192,1536]{1,0:T(8,128)(2,1)}, bf16[192,1536]{1,0:T(8,128)(2,1)S(1)}, u32[]{:S(2)}) copy-start(bf16[192,1536]{1,0:T(8,128)(2,1)S(1)} %get-tuple-element.48) | copy-start | bytes 1769476
  10.1 0.7 %copy-start.7 = (bf16[192,512]{1,0:T(8,128)(2,1)}, bf16[192,512]{1,0:T(8,128)(2,1)S(1)}, u32[]{:S(2)}) copy-start(bf16[192,512]{1,0:T(8,128)(2,1)S(1)} %get-tuple-element.47) | copy-start | bytes 589828
  10.8 14.0 %collective-permute-start.5 = (bf16[128,2048]{1,0:T(8,128)(2,1)}, bf16[128,2048]{1,0:T(8,128)(2,1)}, u32[]{:S(2)}, u32[]{:S(2)}) collective-permute-start(bf16[128,2048]{1,0:T(8,128)(2,1)} %get-tuple-element.35), channel_id=1, source_target_pairs={{0,16},{8,24},{16,0},{24,8},{1,17},{9,25},{17,1},{25,9},{2,18},{10... | collective-permute-start | bytes 1572872 | tf_op jit(solution)/shard_map/ppermute | solution.py:22
  12.3 1.2 %collective-permute-start.1 = (bf16[2,2048]{1,0:T(2,128)(2,1)S(1)}, bf16[2,2048]{1,0:T(2,128)(2,1)S(1)}, u32[]{:S(2)}, u32[]{:S(2)}) collective-permute-start(bf16[2,2048]{1,0:T(2,128)(2,1)S(1)} %get-tuple-element.30), channel_id=1, source_target_pairs={{0,1},{1,0},{2,3},{3,2},{4,5},{5,4},{6,7},{7,6},{8,9},{9,8},{10,11... | collective-permute-start | bytes 24584 | tf_op jit(solution)/shard_map/ppermute | solution.py:22
  13.5 4.5 %collective-permute-start.2 = (bf16[4,2048]{1,0:T(4,128)(2,1)S(1)}, bf16[4,2048]{1,0:T(4,128)(2,1)S(1)}, u32[]{:S(2)}, u32[]{:S(2)}) collective-permute-start(bf16[4,2048]{1,0:T(4,128)(2,1)S(1)} %pad_maximum_fusion), channel_id=1, source_target_pairs={{0,2},{1,3},{2,0},{3,1},{4,6},{5,7},{6,4},{7,5},{8,10},{9,11},{10,... | collective-permute-start | bytes 49160 | tf_op jit(solution)/shard_map/ppermute | solution.py:22
  15.1 4.7 %collective-permute-start.3 = (bf16[4,2048]{1,0:T(4,128)(2,1)S(1)}, bf16[4,2048]{1,0:T(4,128)(2,1)S(1)}, u32[]{:S(2)}, u32[]{:S(2)}) collective-permute-start(bf16[4,2048]{1,0:T(4,128)(2,1)S(1)} %pad_maximum_fusion), channel_id=1, source_target_pairs={{0,4},{1,5},{2,6},{3,7},{4,0},{5,1},{6,2},{7,3},{8,12},{9,13},{10,... | collective-permute-start | bytes 49160 | tf_op jit(solution)/shard_map/ppermute | solution.py:22
  17.7 5.6 %collective-permute-start.4 = (bf16[4,2048]{1,0:T(4,128)(2,1)S(1)}, bf16[4,2048]{1,0:T(4,128)(2,1)}, u32[]{:S(2)}, u32[]{:S(2)}) collective-permute-start(bf16[4,2048]{1,0:T(4,128)(2,1)S(1)} %pad_maximum_fusion), channel_id=1, source_target_pairs={{0,6},{1,7},{2,4},{3,5},{4,2},{5,3},{6,0},{7,1},{8,14},{9,15},{10,... | collective-permute-start | bytes 49160 | tf_op jit(solution)/shard_map/ppermute | solution.py:22
  24.2 6.0 %copy-start.1 = (bf16[256,2048]{1,0:T(8,128)(2,1)S(1)}, bf16[256,2048]{1,0:T(8,128)(2,1)}, u32[]{:S(2)}) copy-start(bf16[256,2048]{1,0:T(8,128)(2,1)} %copy-done) | copy-start | bytes 3145732
  24.2 10.7 %collective-permute-start.7 = (bf16[80,2048]{1,0:T(8,128)(2,1)S(1)}, bf16[80,2048]{1,0:T(8,128)(2,1)S(1)}, u32[]{:S(2)}, u32[]{:S(2)}) collective-permute-start(bf16[80,2048]{1,0:T(8,128)(2,1)S(1)} %join.1), channel_id=1, source_target_pairs={{0,8},{8,0},{16,24},{24,16},{1,9},{9,1},{17,25},{25,17},{2,10},{10... | collective-permute-start | bytes 983048 | tf_op jit(solution)/shard_map/ppermute | solution.py:22
  24.8 22.8 %collective-permute-start.10 = (bf16[192,1536]{1,0:T(8,128)(2,1)}, bf16[192,1536]{1,0:T(8,128)(2,1)S(1)}, u32[]{:S(2)}, u32[]{:S(2)}) collective-permute-start(bf16[192,1536]{1,0:T(8,128)(2,1)} %copy-done.6), channel_id=1, source_target_pairs={{0,8},{8,0},{16,24},{24,16},{1,9},{9,1},{17,25},{25,17},{2,10},{10... | collective-permute-start | bytes 1769480 | tf_op jit(solution)/shard_map/ppermute | solution.py:22
  28.0 14.4 %collective-permute-start.6 = (bf16[80,2048]{1,0:T(8,128)(2,1)S(1)}, bf16[80,2048]{1,0:T(8,128)(2,1)S(1)}, u32[]{:S(2)}, u32[]{:S(2)}) collective-permute-start(bf16[80,2048]{1,0:T(8,128)(2,1)S(1)} %pick.1), channel_id=1, source_target_pairs={{0,16},{8,24},{16,0},{24,8},{1,17},{9,25},{17,1},{25,9},{2,18},{10... | collective-permute-start | bytes 983048 | tf_op jit(solution)/shard_map/ppermute | solution.py:22
  30.1 6.1 %copy-start.8 = (bf16[192,512]{1,0:T(8,128)(2,1)S(1)}, bf16[192,512]{1,0:T(8,128)(2,1)}, u32[]{:S(2)}) copy-start(bf16[192,512]{1,0:T(8,128)(2,1)} %copy-done.7) | copy-start | bytes 589828
  34.9 8.2 %copy-start.5 = (s32[16]{0:T(128)S(1)}, s32[16]{0:T(128)}, u32[]{:S(2)}) copy-start(s32[16]{0:T(128)} %coarse_ref.3) | copy-start | bytes 196
  34.9 8.2 %collective-permute-start.8 = (bf16[80,2048]{1,0:T(8,128)(2,1)S(1)}, bf16[80,2048]{1,0:T(8,128)(2,1)S(1)}, u32[]{:S(2)}, u32[]{:S(2)}) collective-permute-start(bf16[80,2048]{1,0:T(8,128)(2,1)S(1)} %collective-permute-done.7.other_ref.vm_ref), channel_id=1, source_target_pairs={{0,16},{8,24},{16,0},{24,8},{1,17},{9,25},{17,1},{25,9},{2,18},{10... | collective-permute-start | bytes 983048 | tf_op jit(solution)/shard_map/ppermute | solution.py:22
  36.3 13.9 %collective-permute-start.9 = (bf16[192,512]{1,0:T(8,128)(2,1)S(1)}, bf16[192,512]{1,0:T(8,128)(2,1)S(1)}, u32[]{:S(2)}, u32[]{:S(2)}) collective-permute-start(bf16[192,512]{1,0:T(8,128)(2,1)S(1)} %copy-done.8), channel_id=1, source_target_pairs={{0,8},{8,0},{16,24},{24,16},{1,9},{9,1},{17,25},{25,17},{2,10},{10... | collective-permute-start | bytes 589832 | tf_op jit(solution)/shard_map/ppermute | solution.py:22

commit v6 on v5

--- a/solution.py
+++ b/solution.py
@@ -82,6 +82,14 @@
     members = vm_ref.shape[0]
     out_ref[:members] = vm_ref[...]
     out_ref[members:] = near_ref[...]
+
+
+def stack_kernel(near_ref, *refs):
+    out_ref = refs[-1]
+    rows = near_ref.shape[0]
+    out_ref[:rows] = near_ref[...]
+    for place, ref in enumerate(refs[:-1]):
+        out_ref[(place + 1) * rows : (place + 2) * rows] = ref[ref.shape[0] - rows :]
 
 
 def pick_kernel(middle_ref, k_ref, near_ref, members_ref):
@@ -159,29 +167,26 @@
 
 
 def extra_kernel(
-    middle_ref, coarse_ref, q_ref, state_a_ref, state_b_ref, cross_ref, diagonal_k_ref, diagonal_v_ref, near_ref,
+    middle_ref, coarse_ref, q_ref, state_a_ref, state_b_ref, cross_ref, diagonal_k_ref, diagonal_v_ref, mine_ref,
     other_ref, sum_ref, share_ref,
 ):
     rows = q_ref.shape[0]
     members = rows // MIDDLE_DILATION
     half = HEAD_COUNT // 2
+    far_rows, coarse_rows = 2 * members, 2 * mine_ref.shape[0]
     token = lax.broadcasted_iota(jnp.int32, (1, rows), 1)
+    is_key = (lax.broadcasted_iota(jnp.int32, (coarse_rows, 1), 0) & 1) == 0
     states = [ref[...].T for ref in (state_a_ref, state_b_ref)]
     shares = []
     for head in range(HEAD_COUNT):
         columns = head_columns(head)
         state, place = states[head // half], head % half
-        q = q_ref[:, columns]
-        far_keys = jnp.concatenate([cross_ref[:members, columns], diagonal_k_ref[:members, columns]], axis=0)
-        far_values = jnp.concatenate([cross_ref[members:, columns], diagonal_v_ref[:members, columns]], axis=0)
-        pieces = [near_ref[:, columns]] + [
-            ref[members:, columns] for ref in (other_ref, diagonal_k_ref, diagonal_v_ref)
-        ]
-        pairs = jnp.concatenate(pieces, axis=0)
-        is_key = (lax.broadcasted_iota(jnp.int32, (pairs.shape[0], 1), 0) & 1) == 0
-        row_is_member = (token & (MIDDLE_DILATION - 1)) == middle_ref[head]
-        far = jnp.where(row_is_member, dot_keys(far_keys, q), MASKED)
-        coarse = jnp.where(is_key & (token == coarse_ref[head]), dot_keys(pairs, q), MASKED)
+        pairs = [mine_ref[:, columns], other_ref[:, columns]]
+        keys = jnp.concatenate([cross_ref[:members, columns], diagonal_k_ref[:members, columns], *pairs], axis=0)
+        values = jnp.concatenate([cross_ref[members:, columns], diagonal_v_ref[:members, columns], *pairs], axis=0)
+        scores = dot_keys(keys, q_ref[:, columns])
+        far = jnp.where((token & (MIDDLE_DILATION - 1)) == middle_ref[head], scores[:far_rows], MASKED)
+        coarse = jnp.where(is_key & (token == coarse_ref[head]), scores[far_rows:], MASKED)
         before = state[place : place + 1]
         top = jnp.maximum(before, jnp.max(far, axis=0, keepdims=True))
         top = jnp.maximum(top, jnp.max(coarse, axis=0, keepdims=True))
@@ -190,9 +195,9 @@
         total = kept * state[half + place : half + place + 1]
         total += jnp.sum(far, axis=0, keepdims=True) + jnp.sum(coarse, axis=0, keepdims=True)
         inverse = 1.0 / total
-        coarse = pltpu.roll(coarse, 1, 0)
-        summed = dot_rows(far_values, far.astype(jnp.bfloat16)) + dot_rows(pairs, coarse.astype(jnp.bfloat16))
-        sum_ref[:, columns] = (summed * inverse).T
+        shifted = pltpu.roll(coarse, 1, 0)
+        mixed = jnp.concatenate([(far * inverse).astype(jnp.bfloat16), (shifted * inverse).astype(jnp.bfloat16)], axis=0)
+        sum_ref[:, columns] = dot_rows(mixed, values)
         shares.append(kept * inverse)
     share_ref[:, :HEAD_COUNT] = jnp.concatenate(shares, axis=0).T
 
@@ -223,12 +228,11 @@
     return pl.CostEstimate(flops=0, bytes_accessed=0, transcendentals=0)
 
 
-def gather_all(value, axis):
+def gather_upper(value, axis):
     size = lax.axis_size(axis)
-    if size & (size - 1):
-        return lax.all_gather(value, axis, axis=0, tiled=True)
-    bits = [2**j for j in range(size.bit_length() - 1)]
-    for step in [bits[:1]] + [bits[j : j + 2] for j in range(1, len(bits), 2)]:
+    assert size & (size - 1) == 0
+    bits = [2**j for j in range(1, size.bit_length() - 1)]
+    for step in [bits[j : j + 2] for j in range(0, len(bits), 2)]:
         masks = step + [sum(step)] if len(step) == 2 else step
         value = jnp.concatenate([value] + [partner(value, axis, mask) for mask in masks], axis=0)
     return value
@@ -237,7 +241,7 @@
 def on_device(query, keys, values, middle_head_shift, coarse_head_shift):
     rows, width = query.shape
     members = rows // MIDDLE_DILATION
-    near_rows = 2 * lax.axis_size("outer")
+    near_rows = lax.axis_size("outer")
     half = HEAD_COUNT // 2
     bf16, f32 = jnp.bfloat16, jnp.float32
     smem = pl.BlockSpec(memory_space=pltpu.SMEM)
@@ -266,7 +270,7 @@
         scratch_shapes=[orders, pltpu.SemaphoreType.DMA((3,))],
     )
     cross = partner(own_members, "inner", 2)
-    near = gather_all(coarse, "outer")
+    near = gather_upper(coarse, "outer")
     own_vm = call(
         join_kernel,
         "join",
@@ -307,10 +311,20 @@
     own_a, weights_a, state_a = first_part(0, q)
     diagonal_v = partner(lax.optimization_barrier((other_vm, state_a))[0], "inner", 2)
     own_b, weights_b, state_b = first_part(half, lax.optimization_barrier((q, state_a))[0])
+    diagonal_v = lax.optimization_barrier((diagonal_v, state_b))[0]
+    mine = call(
+        stack_kernel,
+        "stack",
+        near, other_vm, diagonal_k, diagonal_v,
+        out_shape=pltpu.VMEM((lax.axis_size("inner") * near_rows, width), bf16),
+        in_specs=[vmem] * 4,
+        out_specs=vmem,
+    )
     extra_sum, share = call(
         extra_kernel,
         "extra",
-        middle_head_shift, coarse_head_shift, q, state_a, state_b, cross, diagonal_k, diagonal_v, near, other_vm,
+        middle_head_shift, coarse_head_shift, q, state_a, state_b, cross, diagonal_k, diagonal_v, mine,
+        partner(mine, "outer", 1),
         out_shape=[pltpu.VMEM((rows, width), f32), pltpu.VMEM((rows, LANES), f32)],
         in_specs=[smem, smem] + [vmem] * 8,
         out_specs=[vmem] * 2,

time: 51.4 us -> 54.7 us (1.064)
  waiting for transfers between devices: 10 us -> 19.8 us
  local copies, waits for them, and re-layouts: 4.59 us -> 1.31 us
  starting transfers between devices: 16 us -> 14 us
  Pallas kernels: 20.5 us -> 19.4 us
    ppermute x11, waiting for transfers between devices: 10 us -> 19.8 us  [partner(): return lax.ppermute(value, axis, pairs)]
    unnamed x18 -> x4, local copies, waits for them, and re-layouts: 3.8 us -> 1.31 us
    ppermute x11, starting transfers between devices: 16 us -> 14 us  [partner(): return lax.ppermute(value, axis, pairs)]
    pallas_call x8 -> x9, Pallas kernels: 20.5 us -> 19.4 us  [call(): pl.pallas_call(kernel, name=name, compiler_params=params, cost_estimate=c...]
    concatenate x1 -> x0, local copies, waits for them, and re-layouts: 0.79 us -> none  [gather_all(): jnp.concatenate([value] + [partner(value, axis, mask) for mask in masks],...]
  transfers between devices with their start and end apart: 11 -> 11, of which waited for: 8 -> 8; matrix products, arithmetic and copies ran while one was open for 2% -> 0% of each run, Pallas kernels for 38% -> 34%
where the time goes in v6:
time: 54.7 us; the launch traced here: 54.5 us
  waiting for transfers between devices  19.8 us (36%)
  Pallas kernels  19.4 us (35%)
  starting transfers between devices  14 us (26%)
  local copies, waits for them, and re-layouts  1.31 us (2%)
    ppermute x11, waiting for transfers between devices, partner(): return lax.ppermute(value, axis, pairs)  19.8 us
    pallas_call x9, Pallas kernels, call(): pl.pallas_call(kernel, name=name, compiler_params=params, cost_estimate=c...  19.4 us
    ppermute x11, starting transfers between devices, partner(): return lax.ppermute(value, axis, pairs)  14 us
    unnamed x4, local copies, waits for them, and re-layouts  1.31 us
  transfers between devices with their start and end apart: 11, of which 8 were waited for; matrix products, arithmetic and copies ran while one was open for 0% of the time, Pallas kernels for 34%

profile of v6, /device:TPU:0, one launch (start us, length us, event | category | flops | bytes accessed | tf_op | source)
XLA Modules:
  0.0 54.5 jit_solution(7158368628234657124)
XLA Ops:
  0.0 2.9 %collective-permute-start = (bf16[256,2048]{1,0:T(8,128)(2,1)}, bf16[256,2048]{1,0:T(8,128)(2,1)S(1)}, u32[]{:S(2)}, u32[]{:S(2)}) collective-permute-start(bf16[256,2048]{1,0:T(8,128)(2,1)} %k_hbm.1), channel_id=1, source_target_pairs={{0,8},{8,0},{16,24},{24,16},{1,9},{9,1},{17,25},{25,17},{2,10},{10... | collective-permute-start | bytes 3145736 | tf_op jit(solution)/shard_map/ppermute | solution.py:22
  2.9 0.0 copy-start
  2.9 0.7 %copy-done = s32[16]{0:T(128)S(1)} copy-done((s32[16]{0:T(128)S(1)}, s32[16]{0:T(128)}, u32[]{:S(2)}) %copy-start) | copy-done | bytes 88
  3.6 0.7 %copy-done.1 = s32[16]{0:T(128)S(1)} copy-done((s32[16]{0:T(128)S(1)}, s32[16]{0:T(128)}, u32[]{:S(2)}) %copy-start.1) | copy-done | bytes 88
  4.3 3.2 %prepare.1 = (bf16[256,2048]{1,0:T(8,128)(2,1)S(1)}, bf16[256,2048]{1,0:T(8,128)(2,1)S(1)}, bf16[256,2048]{1,0:T(8,128)(2,1)S(1)}, bf16[128,2048]{1,0:T(8,128)(2...) custom-call(s32[16]{0:T(128)S(1)} %copy-done, ...), custom_call_target="tpu_custom_call" | custom-call | tf_op jit(solution)/shard_map/prepare/pallas_call | solution.py:254
  7.5 1.6 %collective-permute-start.4 = (bf16[128,2048]{1,0:T(8,128)(2,1)S(1)}, bf16[128,2048]{1,0:T(8,128)(2,1)S(1)}, u32[]{:S(2)}, u32[]{:S(2)}) collective-permute-start(bf16[128,2048]{1,0:T(8,128)(2,1)S(1)} %get-tuple-element.36), channel_id=1, source_target_pairs={{0,16},{8,24},{16,0},{24,8},{1,17},{9,25},{17,1},{25,9},{2,18},{10... | collective-permute-start | bytes 1572872 | tf_op jit(solution)/shard_map/ppermute | solution.py:22
  9.1 3.6 %collective-permute-start.3 = (bf16[2,2048]{1,0:T(2,128)(2,1)S(1)}, bf16[2,2048]{1,0:T(2,128)(2,1)S(1)}, u32[]{:S(2)}, u32[]{:S(2)}) collective-permute-start(bf16[2,2048]{1,0:T(2,128)(2,1)S(1)} %get-tuple-element.31), channel_id=1, source_target_pairs={{0,6},{1,7},{2,4},{3,5},{4,2},{5,3},{6,0},{7,1},{8,14},{9,15},{10,... | collective-permute-start | bytes 24584 | tf_op jit(solution)/shard_map/ppermute | solution.py:22
  12.7 0.0 collective-permute-start.2
  12.7 0.8 %collective-permute-start.1 = (bf16[2,2048]{1,0:T(2,128)(2,1)S(1)}, bf16[2,2048]{1,0:T(2,128)(2,1)S(1)}, u32[]{:S(2)}, u32[]{:S(2)}) collective-permute-start(bf16[2,2048]{1,0:T(2,128)(2,1)S(1)} %get-tuple-element.31), channel_id=1, source_target_pairs={{0,2},{1,3},{2,0},{3,1},{4,6},{5,7},{6,4},{7,5},{8,10},{9,11},{10,... | collective-permute-start | bytes 24584 | tf_op jit(solution)/shard_map/ppermute | solution.py:22
  13.5 1.1 %collective-permute-done.3 = bf16[2,2048]{1,0:T(2,128)(2,1)S(1)} collective-permute-done((bf16[2,2048]{1,0:T(2,128)(2,1)S(1)}, bf16[2,2048]{1,0:T(2,128)(2,1)S(1)}, u32[]{:S(2)}, u32[]{:S(2)}) %collective-permute-start.3) | collective-permute-done | bytes 8224 | tf_op jit(solution)/shard_map/ppermute | solution.py:22
  14.5 2.7 %collective-permute-done.2 = bf16[2,2048]{1,0:T(2,128)(2,1)S(1)} collective-permute-done((bf16[2,2048]{1,0:T(2,128)(2,1)S(1)}, bf16[2,2048]{1,0:T(2,128)(2,1)S(1)}, u32[]{:S(2)}, u32[]{:S(2)}) %collective-permute-start.2) | collective-permute-done | bytes 8224 | tf_op jit(solution)/shard_map/ppermute | solution.py:22
  17.2 0.0 collective-permute-done.1
  17.3 0.6 %collective-permute-start.6 = (bf16[72,2048]{1,0:T(8,128)(2,1)S(1)}, bf16[72,2048]{1,0:T(8,128)(2,1)S(1)}, u32[]{:S(2)}, u32[]{:S(2)}) collective-permute-start(bf16[72,2048]{1,0:T(8,128)(2,1)S(1)} %join.1), channel_id=1, source_target_pairs={{0,8},{8,0},{16,24},{24,16},{1,9},{9,1},{17,25},{25,17},{2,10},{10... | collective-permute-start | bytes 884744 | tf_op jit(solution)/shard_map/ppermute | solution.py:22
  17.9 3.0 %collective-permute-done.4.cross_ref = bf16[128,2048]{1,0:T(8,128)(2,1)S(1)} collective-permute-done((bf16[128,2048]{1,0:T(8,128)(2,1)S(1)}, bf16[128,2048]{1,0:T(8,128)(2,1)S(1)}, u32[]{:S(2)}, u32[]{:S(2)}) %collective-permute-start.4) | collective-permute-done | bytes 524320 | tf_op jit(solution)/shard_map/ppermute | solution.py:22
  21.0 0.3 collective-permute-start.10
  21.3 5.9 %collective-permute-done.k_ref.kp_ref = bf16[256,2048]{1,0:T(8,128)(2,1)S(1)} collective-permute-done((bf16[256,2048]{1,0:T(8,128)(2,1)}, bf16[256,2048]{1,0:T(8,128)(2,1)S(1)}, u32[]{:S(2)}, u32[]{:S(2)}) %collective-permute-start) | collective-permute-done | bytes 1048608 | tf_op jit(solution)/shard_map/ppermute | solution.py:22
  27.1 0.8 %pick.1 = bf16[72,2048]{1,0:T(8,128)(2,1)S(1)} custom-call(s32[16]{0:T(128)S(1)} %copy-done, bf16[256,2048]{1,0:T(8,128)(2,1)S(1)} %collective-permute-done.k_ref.kp_ref, bf16[8,2048]{1,0:T(8,128)(2,1)S(1)} %pad_maximum_fusion.near_ref), custom_call_target="tpu_custom_call" | custom-call | tf_op jit(solution)/shard_map/pick/pallas_call | solution.py:254
  28.0 4.6 %first.2 = (f32[256,1024]{1,0:T(8,128)S(1)}, bf16[8,256,256]{2,1,0:T(8,128)(2,1)S(1)}, f32[256,128]{1,0:T(8,128)S(1)}) custom-call(s32[16]{0:T(128)S(1)} %copy-done, bf16[256,2048]{1,0:T(8,128)(2,1)S(1)} %get-tuple-element.34.q_ref, bf16[256,2048]{1,0:T(8,128)(2,1)S(1)} %get-tuple-element.29.k_ref, bf16[256,2048]{1,0:T(8,128)(2,1)S(1)} %get-tuple-element.30.v_ref, ...), custom_call_target="tpu_custom_call" | custom-call | tf_op jit(solution)/shard_map/first/pallas_call | solution.py:254
  32.6 0.8 %collective-permute-done.6.refs_0_.vm_ref = bf16[72,2048]{1,0:T(8,128)(2,1)S(1)} collective-permute-done((bf16[72,2048]{1,0:T(8,128)(2,1)S(1)}, bf16[72,2048]{1,0:T(8,128)(2,1)S(1)}, u32[]{:S(2)}, u32[]{:S(2)}) %collective-permute-start.6) | collective-permute-done | bytes 294944 | tf_op jit(solution)/shard_map/ppermute | solution.py:22
  33.5 2.1 %collective-permute-start.7 = (bf16[72,2048]{1,0:T(8,128)(2,1)S(1)}, bf16[72,2048]{1,0:T(8,128)(2,1)S(1)}, u32[]{:S(2)}, u32[]{:S(2)}) collective-permute-start(bf16[72,2048]{1,0:T(8,128)(2,1)S(1)} %collective-permute-done.6.refs_0_.vm_ref), channel_id=1, source_target_pairs={{0,16},{8,24},{16,0},{24,8},{1,17},{9,25},{17,1},{25,9},{2,18},{10... | collective-permute-start | bytes 884744 | tf_op jit(solution)/shard_map/ppermute | solution.py:22
  35.5 0.0 collective-permute-start.5
  35.6 2.0 %collective-permute-start.9 = (bf16[192,512]{1,0:T(8,128)(2,1)S(1)}, bf16[192,512]{1,0:T(8,128)(2,1)S(1)}, u32[]{:S(2)}, u32[]{:S(2)}) collective-permute-start(bf16[192,512]{1,0:T(8,128)(2,1)S(1)} %get-tuple-element.49), channel_id=1, source_target_pairs={{0,8},{8,0},{16,24},{24,16},{1,9},{9,1},{17,25},{25,17},{2,10},{10... | collective-permute-start | bytes 589832 | tf_op jit(solution)/shard_map/ppermute | solution.py:22
  37.5 4.6 %first.3 = (f32[256,1024]{1,0:T(8,128)S(1)}, bf16[8,256,256]{2,1,0:T(8,128)(2,1)S(1)}, f32[256,128]{1,0:T(8,128)S(1)}) custom-call(s32[16]{0:T(128)S(1)} %copy-done, bf16[256,2048]{1,0:T(8,128)(2,1)S(1)} %get-tuple-element.34.q_ref, bf16[256,2048]{1,0:T(8,128)(2,1)S(1)} %get-tuple-element.29.k_ref, bf16[256,2048]{1,0:T(8,128)(2,1)S(1)} %get-tuple-element.30.v_ref, ...), custom_call_target="tpu_custom_call" | custom-call | tf_op jit(solution)/shard_map/first/pallas_call | solution.py:254
  42.2 1.3 %collective-permute-done.7.refs_2_.diagonal_v_ref = bf16[72,2048]{1,0:T(8,128)(2,1)S(1)} collective-permute-done((bf16[72,2048]{1,0:T(8,128)(2,1)S(1)}, bf16[72,2048]{1,0:T(8,128)(2,1)S(1)}, u32[]{:S(2)}, u32[]{:S(2)}) %collective-permute-start.7) | collective-permute-done | bytes 294944 | tf_op jit(solution)/shard_map/ppermute | solution.py:22
  43.5 3.7 %collective-permute-done.5.refs_1_.diagonal_k_ref = bf16[72,2048]{1,0:T(8,128)(2,1)S(1)} collective-permute-done((bf16[72,2048]{1,0:T(8,128)(2,1)S(1)}, bf16[72,2048]{1,0:T(8,128)(2,1)S(1)}, u32[]{:S(2)}, u32[]{:S(2)}) %collective-permute-start.5) | collective-permute-done | bytes 294944 | tf_op jit(solution)/shard_map/ppermute | solution.py:22
  47.2 0.1 collective-permute-start.8
  47.2 1.3 %collective-permute-done.8.other_ref = bf16[32,2048]{1,0:T(8,128)(2,1)S(1)} collective-permute-done((bf16[32,2048]{1,0:T(8,128)(2,1)S(1)}, bf16[32,2048]{1,0:T(8,128)(2,1)S(1)}, u32[]{:S(2)}, u32[]{:S(2)}) %collective-permute-start.8) | collective-permute-done | bytes 131104 | tf_op jit(solution)/shard_map/ppermute | solution.py:22
  48.6 3.5 %extra.1 = (f32[256,2048]{1,0:T(8,128)S(1)}, f32[256,128]{1,0:T(8,128)S(1)}) custom-call(s32[16]{0:T(128)S(1)} %copy-done, s32[16]{0:T(128)S(1)} %copy-done.1, bf16[256,2048]{1,0:T(8,128)(2,1)S(1)} %get-tuple-element.34.q_ref, f32[256,128]{1,0:T(8,128)S(1)} %get-tuple-element.33.state_a_ref, f32[256,128]{1,0:T(8,128)S(1)} %get-tuple-element.35.state_b_ref, ...), custom_call_target="tpu_custom_call" | custom-call | tf_op jit(solution)/shard_map/extra/pallas_call | solution.py:254
  52.1 0.0 collective-permute-done.10.vr_ref
  52.1 1.4 %finish.2.rest_0_ = bf16[256,2048]{1,0:T(8,128)(2,1)} custom-call(f32[256,2048]{1,0:T(8,128)S(1)} %get-tuple-element.43.sum_ref, f32[256,128]{1,0:T(8,128)S(1)} %get-tuple-element.44.share_ref, f32[256,1024]{1,0:T(8,128)S(1)} %get-tuple-element.45.own_a_ref, f32[256,1024]{1,0:T(8,128)S(1)} %get-tuple-element.46.own_b_ref, ...), custom_call_target="tpu_custom_call" | custom-call | tf_op jit(solution)/shard_map/finish/pallas_call | solution.py:254
  53.5 0.0 collective-permute-done.9.vr_ref
  53.5 1.0 %finish.3 = bf16[256,2048]{1,0:T(8,128)(2,1)} custom-call(f32[256,2048]{1,0:T(8,128)S(1)} %get-tuple-element.43.sum_ref, f32[256,128]{1,0:T(8,128)S(1)} %get-tuple-element.44.share_ref, f32[256,1024]{1,0:T(8,128)S(1)} %get-tuple-element.45.own_a_ref, f32[256,1024]{1,0:T(8,128)S(1)} %get-tuple-element.46.own_b_ref, ...), custom_call_target="tpu_custom_call", output_to_operand_aliasing={{}: (8, {})} | custom-call | tf_op jit(solution)/shard_map/finish/pallas_call | solution.py:254
  (4 shorter events, 0.1 us)
Async XLA Ops:
  0.0 27.1 %collective-permute-start = (bf16[256,2048]{1,0:T(8,128)(2,1)}, bf16[256,2048]{1,0:T(8,128)(2,1)S(1)}, u32[]{:S(2)}, u32[]{:S(2)}) collective-permute-start(bf16[256,2048]{1,0:T(8,128)(2,1)} %k_hbm.1), channel_id=1, source_target_pairs={{0,8},{8,0},{16,24},{24,16},{1,9},{9,1},{17,25},{25,17},{2,10},{10... | collective-permute-start | bytes 3145736 | tf_op jit(solution)/shard_map/ppermute | solution.py:22
  2.9 0.7 %copy-start = (s32[16]{0:T(128)S(1)}, s32[16]{0:T(128)}, u32[]{:S(2)}) copy-start(s32[16]{0:T(128)} %middle_ref.9) | copy-start | bytes 196
  3.6 0.7 %copy-start.1 = (s32[16]{0:T(128)S(1)}, s32[16]{0:T(128)}, u32[]{:S(2)}) copy-start(s32[16]{0:T(128)} %coarse_ref.3) | copy-start | bytes 196
  7.5 13.4 %collective-permute-start.4 = (bf16[128,2048]{1,0:T(8,128)(2,1)S(1)}, bf16[128,2048]{1,0:T(8,128)(2,1)S(1)}, u32[]{:S(2)}, u32[]{:S(2)}) collective-permute-start(bf16[128,2048]{1,0:T(8,128)(2,1)S(1)} %get-tuple-element.36), channel_id=1, source_target_pairs={{0,16},{8,24},{16,0},{24,8},{1,17},{9,25},{17,1},{25,9},{2,18},{10... | collective-permute-start | bytes 1572872 | tf_op jit(solution)/shard_map/ppermute | solution.py:22
  9.1 5.4 %collective-permute-start.3 = (bf16[2,2048]{1,0:T(2,128)(2,1)S(1)}, bf16[2,2048]{1,0:T(2,128)(2,1)S(1)}, u32[]{:S(2)}, u32[]{:S(2)}) collective-permute-start(bf16[2,2048]{1,0:T(2,128)(2,1)S(1)} %get-tuple-element.31), channel_id=1, source_target_pairs={{0,6},{1,7},{2,4},{3,5},{4,2},{5,3},{6,0},{7,1},{8,14},{9,15},{10,... | collective-permute-start | bytes 24584 | tf_op jit(solution)/shard_map/ppermute | solution.py:22
  12.7 4.5 %collective-permute-start.2 = (bf16[2,2048]{1,0:T(2,128)(2,1)S(1)}, bf16[2,2048]{1,0:T(2,128)(2,1)S(1)}, u32[]{:S(2)}, u32[]{:S(2)}) collective-permute-start(bf16[2,2048]{1,0:T(2,128)(2,1)S(1)} %get-tuple-element.31), channel_id=1, source_target_pairs={{0,4},{1,5},{2,6},{3,7},{4,0},{5,1},{6,2},{7,3},{8,12},{9,13},{10,... | collective-permute-start | bytes 24584 | tf_op jit(solution)/shard_map/ppermute | solution.py:22
  12.7 4.5 %collective-permute-start.1 = (bf16[2,2048]{1,0:T(2,128)(2,1)S(1)}, bf16[2,2048]{1,0:T(2,128)(2,1)S(1)}, u32[]{:S(2)}, u32[]{:S(2)}) collective-permute-start(bf16[2,2048]{1,0:T(2,128)(2,1)S(1)} %get-tuple-element.31), channel_id=1, source_target_pairs={{0,2},{1,3},{2,0},{3,1},{4,6},{5,7},{6,4},{7,5},{8,10},{9,11},{10,... | collective-permute-start | bytes 24584 | tf_op jit(solution)/shard_map/ppermute | solution.py:22
  17.3 16.1 %collective-permute-start.6 = (bf16[72,2048]{1,0:T(8,128)(2,1)S(1)}, bf16[72,2048]{1,0:T(8,128)(2,1)S(1)}, u32[]{:S(2)}, u32[]{:S(2)}) collective-permute-start(bf16[72,2048]{1,0:T(8,128)(2,1)S(1)} %join.1), channel_id=1, source_target_pairs={{0,8},{8,0},{16,24},{24,16},{1,9},{9,1},{17,25},{25,17},{2,10},{10... | collective-permute-start | bytes 884744 | tf_op jit(solution)/shard_map/ppermute | solution.py:22
  21.0 31.1 %collective-permute-start.10 = (bf16[192,1536]{1,0:T(8,128)(2,1)S(1)}, bf16[192,1536]{1,0:T(8,128)(2,1)S(1)}, u32[]{:S(2)}, u32[]{:S(2)}) collective-permute-start(bf16[192,1536]{1,0:T(8,128)(2,1)S(1)} %get-tuple-element.50), channel_id=1, source_target_pairs={{0,8},{8,0},{16,24},{24,16},{1,9},{9,1},{17,25},{25,17},{2,10},{10... | collective-permute-start | bytes 1769480 | tf_op jit(solution)/shard_map/ppermute | solution.py:22
  33.5 10.0 %collective-permute-start.7 = (bf16[72,2048]{1,0:T(8,128)(2,1)S(1)}, bf16[72,2048]{1,0:T(8,128)(2,1)S(1)}, u32[]{:S(2)}, u32[]{:S(2)}) collective-permute-start(bf16[72,2048]{1,0:T(8,128)(2,1)S(1)} %collective-permute-done.6.refs_0_.vm_ref), channel_id=1, source_target_pairs={{0,16},{8,24},{16,0},{24,8},{1,17},{9,25},{17,1},{25,9},{2,18},{10... | collective-permute-start | bytes 884744 | tf_op jit(solution)/shard_map/ppermute | solution.py:22
  35.5 11.6 %collective-permute-start.5 = (bf16[72,2048]{1,0:T(8,128)(2,1)S(1)}, bf16[72,2048]{1,0:T(8,128)(2,1)S(1)}, u32[]{:S(2)}, u32[]{:S(2)}) collective-permute-start(bf16[72,2048]{1,0:T(8,128)(2,1)S(1)} %pick.1), channel_id=1, source_target_pairs={{0,16},{8,24},{16,0},{24,8},{1,17},{9,25},{17,1},{25,9},{2,18},{10... | collective-permute-start | bytes 884744 | tf_op jit(solution)/shard_map/ppermute | solution.py:22
  35.6 18.0 %collective-permute-start.9 = (bf16[192,512]{1,0:T(8,128)(2,1)S(1)}, bf16[192,512]{1,0:T(8,128)(2,1)S(1)}, u32[]{:S(2)}, u32[]{:S(2)}) collective-permute-start(bf16[192,512]{1,0:T(8,128)(2,1)S(1)} %get-tuple-element.49), channel_id=1, source_target_pairs={{0,8},{8,0},{16,24},{24,16},{1,9},{9,1},{17,25},{25,17},{2,10},{10... | collective-permute-start | bytes 589832 | tf_op jit(solution)/shard_map/ppermute | solution.py:22
  47.2 1.4 %collective-permute-start.8 = (bf16[32,2048]{1,0:T(8,128)(2,1)S(1)}, bf16[32,2048]{1,0:T(8,128)(2,1)S(1)}, u32[]{:S(2)}, u32[]{:S(2)}) collective-permute-start(bf16[32,2048]{1,0:T(8,128)(2,1)S(1)} %stack.1.mine_ref), channel_id=1, source_target_pairs={{0,1},{1,0},{2,3},{3,2},{4,5},{5,4},{6,7},{7,6},{8,9},{9,8},{10,11... | collective-permute-start | bytes 393224 | tf_op jit(solution)/shard_map/ppermute | solution.py:22

commit v7 on v6

--- a/solution.py
+++ b/solution.py
@@ -310,7 +310,7 @@
 
     own_a, weights_a, state_a = first_part(0, q)
     diagonal_v = partner(lax.optimization_barrier((other_vm, state_a))[0], "inner", 2)
-    own_b, weights_b, state_b = first_part(half, lax.optimization_barrier((q, state_a))[0])
+    own_b, weights_b, state_b = first_part(half, lax.optimization_barrier((q, state_a, diagonal_k))[0])
     diagonal_v = lax.optimization_barrier((diagonal_v, state_b))[0]
     mine = call(
         stack_kernel,

time: 54.7 us -> 50.6 us (0.925)
  waiting for transfers between devices: 19.8 us -> 15.4 us
    ppermute x11, waiting for transfers between devices: 19.8 us -> 15.4 us  [partner(): return lax.ppermute(value, axis, pairs)]
    unnamed x4 -> x6, local copies, waits for them, and re-layouts: 1.31 us -> 1.32 us
  transfers between devices with their start and end apart: 11 -> 11, of which waited for: 8 -> 6; matrix products, arithmetic and copies ran while one was open for 0% -> 0% of each run, Pallas kernels for 34% -> 36%
where the time goes in v7:
time: 50.6 us; the launch traced here: 50.5 us
  Pallas kernels  19.3 us (38%)
  waiting for transfers between devices  15.4 us (30%)
  starting transfers between devices  14.3 us (28%)
  local copies, waits for them, and re-layouts  1.32 us (3%)
    pallas_call x9, Pallas kernels, call(): pl.pallas_call(kernel, name=name, compiler_params=params, cost_estimate=c...  19.3 us
    ppermute x11, waiting for transfers between devices, partner(): return lax.ppermute(value, axis, pairs)  15.4 us
    ppermute x11, starting transfers between devices, partner(): return lax.ppermute(value, axis, pairs)  14.3 us
    unnamed x6, local copies, waits for them, and re-layouts  1.32 us
  transfers between devices with their start and end apart: 11, of which 6 were waited for; matrix products, arithmetic and copies ran while one was open for 0% of the time, Pallas kernels for 36%

profile of v7, /device:TPU:0, one launch (start us, length us, event | category | flops | bytes accessed | tf_op | source)
XLA Modules:
  0.0 50.5 jit_solution(17107375228567060591)
XLA Ops:
  0.0 2.9 %collective-permute-start = (bf16[256,2048]{1,0:T(8,128)(2,1)}, bf16[256,2048]{1,0:T(8,128)(2,1)S(1)}, u32[]{:S(2)}, u32[]{:S(2)}) collective-permute-start(bf16[256,2048]{1,0:T(8,128)(2,1)} %k_hbm.1), channel_id=1, source_target_pairs={{0,8},{8,0},{16,24},{24,16},{1,9},{9,1},{17,25},{25,17},{2,10},{10... | collective-permute-start | bytes 3145736 | tf_op jit(solution)/shard_map/ppermute | solution.py:22
  2.9 0.7 %copy-done = s32[16]{0:T(128)S(1)} copy-done((s32[16]{0:T(128)S(1)}, s32[16]{0:T(128)}, u32[]{:S(2)}) %copy-start) | copy-done | bytes 88
  3.6 0.7 %copy-done.1 = s32[16]{0:T(128)S(1)} copy-done((s32[16]{0:T(128)S(1)}, s32[16]{0:T(128)}, u32[]{:S(2)}) %copy-start.1) | copy-done | bytes 88
  4.3 3.2 %prepare.1 = (bf16[256,2048]{1,0:T(8,128)(2,1)S(1)}, bf16[256,2048]{1,0:T(8,128)(2,1)S(1)}, bf16[256,2048]{1,0:T(8,128)(2,1)S(1)}, bf16[128,2048]{1,0:T(8,128)(2...) custom-call(s32[16]{0:T(128)S(1)} %copy-done, ...), custom_call_target="tpu_custom_call" | custom-call | tf_op jit(solution)/shard_map/prepare/pallas_call | solution.py:254
  7.5 1.6 %collective-permute-start.5 = (bf16[128,2048]{1,0:T(8,128)(2,1)S(1)}, bf16[128,2048]{1,0:T(8,128)(2,1)S(1)}, u32[]{:S(2)}, u32[]{:S(2)}) collective-permute-start(bf16[128,2048]{1,0:T(8,128)(2,1)S(1)} %get-tuple-element.36), channel_id=1, source_target_pairs={{0,16},{8,24},{16,0},{24,8},{1,17},{9,25},{17,1},{25,9},{2,18},{10... | collective-permute-start | bytes 1572872 | tf_op jit(solution)/shard_map/ppermute | solution.py:22
  9.1 3.6 %collective-permute-start.3 = (bf16[2,2048]{1,0:T(2,128)(2,1)S(1)}, bf16[2,2048]{1,0:T(2,128)(2,1)S(1)}, u32[]{:S(2)}, u32[]{:S(2)}) collective-permute-start(bf16[2,2048]{1,0:T(2,128)(2,1)S(1)} %get-tuple-element.31), channel_id=1, source_target_pairs={{0,6},{1,7},{2,4},{3,5},{4,2},{5,3},{6,0},{7,1},{8,14},{9,15},{10,... | collective-permute-start | bytes 24584 | tf_op jit(solution)/shard_map/ppermute | solution.py:22
  12.7 0.0 collective-permute-start.2
  12.7 0.8 %collective-permute-start.1 = (bf16[2,2048]{1,0:T(2,128)(2,1)S(1)}, bf16[2,2048]{1,0:T(2,128)(2,1)S(1)}, u32[]{:S(2)}, u32[]{:S(2)}) collective-permute-start(bf16[2,2048]{1,0:T(2,128)(2,1)S(1)} %get-tuple-element.31), channel_id=1, source_target_pairs={{0,2},{1,3},{2,0},{3,1},{4,6},{5,7},{6,4},{7,5},{8,10},{9,11},{10,... | collective-permute-start | bytes 24584 | tf_op jit(solution)/shard_map/ppermute | solution.py:22
  13.5 1.1 %collective-permute-done.3 = bf16[2,2048]{1,0:T(2,128)(2,1)S(1)} collective-permute-done((bf16[2,2048]{1,0:T(2,128)(2,1)S(1)}, bf16[2,2048]{1,0:T(2,128)(2,1)S(1)}, u32[]{:S(2)}, u32[]{:S(2)}) %collective-permute-start.3) | collective-permute-done | bytes 8224 | tf_op jit(solution)/shard_map/ppermute | solution.py:22
  14.5 2.7 %collective-permute-done.2 = bf16[2,2048]{1,0:T(2,128)(2,1)S(1)} collective-permute-done((bf16[2,2048]{1,0:T(2,128)(2,1)S(1)}, bf16[2,2048]{1,0:T(2,128)(2,1)S(1)}, u32[]{:S(2)}, u32[]{:S(2)}) %collective-permute-start.2) | collective-permute-done | bytes 8224 | tf_op jit(solution)/shard_map/ppermute | solution.py:22
  17.2 0.0 collective-permute-done.1
  17.3 0.6 %collective-permute-start.6 = (bf16[72,2048]{1,0:T(8,128)(2,1)S(1)}, bf16[72,2048]{1,0:T(8,128)(2,1)S(1)}, u32[]{:S(2)}, u32[]{:S(2)}) collective-permute-start(bf16[72,2048]{1,0:T(8,128)(2,1)S(1)} %join.1), channel_id=1, source_target_pairs={{0,8},{8,0},{16,24},{24,16},{1,9},{9,1},{17,25},{25,17},{2,10},{10... | collective-permute-start | bytes 884744 | tf_op jit(solution)/shard_map/ppermute | solution.py:22
  17.9 3.0 %collective-permute-done.5.cross_ref = bf16[128,2048]{1,0:T(8,128)(2,1)S(1)} collective-permute-done((bf16[128,2048]{1,0:T(8,128)(2,1)S(1)}, bf16[128,2048]{1,0:T(8,128)(2,1)S(1)}, u32[]{:S(2)}, u32[]{:S(2)}) %collective-permute-start.5) | collective-permute-done | bytes 524320 | tf_op jit(solution)/shard_map/ppermute | solution.py:22
  21.0 0.3 collective-permute-start.10
  21.3 5.9 %collective-permute-done.k_ref.kp_ref = bf16[256,2048]{1,0:T(8,128)(2,1)S(1)} collective-permute-done((bf16[256,2048]{1,0:T(8,128)(2,1)}, bf16[256,2048]{1,0:T(8,128)(2,1)S(1)}, u32[]{:S(2)}, u32[]{:S(2)}) %collective-permute-start) | collective-permute-done | bytes 1048608 | tf_op jit(solution)/shard_map/ppermute | solution.py:22
  27.1 0.8 %pick.1 = bf16[72,2048]{1,0:T(8,128)(2,1)S(1)} custom-call(s32[16]{0:T(128)S(1)} %copy-done, bf16[256,2048]{1,0:T(8,128)(2,1)S(1)} %collective-permute-done.k_ref.kp_ref, bf16[8,2048]{1,0:T(8,128)(2,1)S(1)} %pad_maximum_fusion.near_ref), custom_call_target="tpu_custom_call" | custom-call | tf_op jit(solution)/shard_map/pick/pallas_call | solution.py:254
  28.0 2.2 %collective-permute-start.4 = (bf16[72,2048]{1,0:T(8,128)(2,1)S(1)}, bf16[72,2048]{1,0:T(8,128)(2,1)S(1)}, u32[]{:S(2)}, u32[]{:S(2)}) collective-permute-start(bf16[72,2048]{1,0:T(8,128)(2,1)S(1)} %pick.1), channel_id=1, source_target_pairs={{0,16},{8,24},{16,0},{24,8},{1,17},{9,25},{17,1},{25,9},{2,18},{10... | collective-permute-start | bytes 884744 | tf_op jit(solution)/shard_map/ppermute | solution.py:22
  30.1 4.6 %first.2 = (f32[256,1024]{1,0:T(8,128)S(1)}, bf16[8,256,256]{2,1,0:T(8,128)(2,1)S(1)}, f32[256,128]{1,0:T(8,128)S(1)}) custom-call(s32[16]{0:T(128)S(1)} %copy-done, bf16[256,2048]{1,0:T(8,128)(2,1)S(1)} %get-tuple-element.34.q_ref, bf16[256,2048]{1,0:T(8,128)(2,1)S(1)} %get-tuple-element.29.k_ref, bf16[256,2048]{1,0:T(8,128)(2,1)S(1)} %get-tuple-element.30.v_ref, ...), custom_call_target="tpu_custom_call" | custom-call | tf_op jit(solution)/shard_map/first/pallas_call | solution.py:254
  34.8 0.0 collective-permute-done.6.refs_0_.vm_ref
  34.8 0.0 copy-start.2
  34.8 0.7 %collective-permute-start.7 = (bf16[72,2048]{1,0:T(8,128)(2,1)S(1)}, bf16[72,2048]{1,0:T(8,128)(2,1)S(1)}, u32[]{:S(2)}, u32[]{:S(2)}) collective-permute-start(bf16[72,2048]{1,0:T(8,128)(2,1)S(1)} %collective-permute-done.6.refs_0_.vm_ref), channel_id=1, source_target_pairs={{0,16},{8,24},{16,0},{24,8},{1,17},{9,25},{17,1},{25,9},{2,18},{10... | collective-permute-start | bytes 884744 | tf_op jit(solution)/shard_map/ppermute | solution.py:22
  35.5 1.5 %collective-permute-start.9 = (bf16[192,512]{1,0:T(8,128)(2,1)S(1)}, bf16[192,512]{1,0:T(8,128)(2,1)S(1)}, u32[]{:S(2)}, u32[]{:S(2)}) collective-permute-start(bf16[192,512]{1,0:T(8,128)(2,1)S(1)} %get-tuple-element.49), channel_id=1, source_target_pairs={{0,8},{8,0},{16,24},{24,16},{1,9},{9,1},{17,25},{25,17},{2,10},{10... | collective-permute-start | bytes 589832 | tf_op jit(solution)/shard_map/ppermute | solution.py:22
  37.0 0.0 collective-permute-done.4.refs_1_.diagonal_k_ref
  37.0 4.6 %first.3 = (f32[256,1024]{1,0:T(8,128)S(1)}, bf16[8,256,256]{2,1,0:T(8,128)(2,1)S(1)}, f32[256,128]{1,0:T(8,128)S(1)}) custom-call(s32[16]{0:T(128)S(1)} %copy-done, bf16[256,2048]{1,0:T(8,128)(2,1)S(1)} %get-tuple-element.34.q_ref, bf16[256,2048]{1,0:T(8,128)(2,1)S(1)} %get-tuple-element.29.k_ref, bf16[256,2048]{1,0:T(8,128)(2,1)S(1)} %get-tuple-element.30.v_ref, ...), custom_call_target="tpu_custom_call" | custom-call | tf_op jit(solution)/shard_map/first/pallas_call | solution.py:254
  41.7 0.0 collective-permute-done.7.refs_2_.diagonal_v_ref
  41.7 0.1 collective-permute-start.8
  41.8 1.3 %collective-permute-done.8.other_ref = bf16[32,2048]{1,0:T(8,128)(2,1)S(1)} collective-permute-done((bf16[32,2048]{1,0:T(8,128)(2,1)S(1)}, bf16[32,2048]{1,0:T(8,128)(2,1)S(1)}, u32[]{:S(2)}, u32[]{:S(2)}) %collective-permute-start.8) | collective-permute-done | bytes 131104 | tf_op jit(solution)/shard_map/ppermute | solution.py:22
  43.2 3.5 %extra.1 = (f32[256,2048]{1,0:T(8,128)S(1)}, f32[256,128]{1,0:T(8,128)S(1)}) custom-call(s32[16]{0:T(128)S(1)} %copy-done, s32[16]{0:T(128)S(1)} %copy-done.2, bf16[256,2048]{1,0:T(8,128)(2,1)S(1)} %get-tuple-element.34.q_ref, f32[256,128]{1,0:T(8,128)S(1)} %get-tuple-element.33.state_a_ref, f32[256,128]{1,0:T(8,128)S(1)} %get-tuple-element.35.state_b_ref, ...), custom_call_target="tpu_custom_call" | custom-call | tf_op jit(solution)/shard_map/extra/pallas_call | solution.py:254
  46.7 0.0 collective-permute-done.10.vr_ref
  46.7 1.4 %finish.2.rest_0_ = bf16[256,2048]{1,0:T(8,128)(2,1)} custom-call(f32[256,2048]{1,0:T(8,128)S(1)} %get-tuple-element.43.sum_ref, f32[256,128]{1,0:T(8,128)S(1)} %get-tuple-element.44.share_ref, f32[256,1024]{1,0:T(8,128)S(1)} %get-tuple-element.45.own_a_ref, f32[256,1024]{1,0:T(8,128)S(1)} %get-tuple-element.46.own_b_ref, ...), custom_call_target="tpu_custom_call" | custom-call | tf_op jit(solution)/shard_map/finish/pallas_call | solution.py:254
  48.1 1.4 %collective-permute-done.9.vr_ref = bf16[192,512]{1,0:T(8,128)(2,1)S(1)} collective-permute-done((bf16[192,512]{1,0:T(8,128)(2,1)S(1)}, bf16[192,512]{1,0:T(8,128)(2,1)S(1)}, u32[]{:S(2)}, u32[]{:S(2)}) %collective-permute-start.9) | collective-permute-done | bytes 196640 | tf_op jit(solution)/shard_map/ppermute | solution.py:22
  49.5 1.0 %finish.3 = bf16[256,2048]{1,0:T(8,128)(2,1)} custom-call(f32[256,2048]{1,0:T(8,128)S(1)} %get-tuple-element.43.sum_ref, f32[256,128]{1,0:T(8,128)S(1)} %get-tuple-element.44.share_ref, f32[256,1024]{1,0:T(8,128)S(1)} %get-tuple-element.45.own_a_ref, f32[256,1024]{1,0:T(8,128)S(1)} %get-tuple-element.46.own_b_ref, ...), custom_call_target="tpu_custom_call", output_to_operand_aliasing={{}: (8, {})} | custom-call | tf_op jit(solution)/shard_map/finish/pallas_call | solution.py:254
  (6 shorter events, 0.1 us)
Async XLA Ops:
  0.0 27.1 %collective-permute-start = (bf16[256,2048]{1,0:T(8,128)(2,1)}, bf16[256,2048]{1,0:T(8,128)(2,1)S(1)}, u32[]{:S(2)}, u32[]{:S(2)}) collective-permute-start(bf16[256,2048]{1,0:T(8,128)(2,1)} %k_hbm.1), channel_id=1, source_target_pairs={{0,8},{8,0},{16,24},{24,16},{1,9},{9,1},{17,25},{25,17},{2,10},{10... | collective-permute-start | bytes 3145736 | tf_op jit(solution)/shard_map/ppermute | solution.py:22
  2.9 0.7 %copy-start = (s32[16]{0:T(128)S(1)}, s32[16]{0:T(128)}, u32[]{:S(2)}) copy-start(s32[16]{0:T(128)} %middle_ref.9) | copy-start | bytes 196
  3.6 0.7 %copy-start.1 = (s32[16]{0:T(128)S(1)}, s32[16]{0:T(128)}, u32[]{:S(2)}) copy-start(s32[16]{0:T(128)} %coarse_ref.3) | copy-start | bytes 196
  7.5 13.4 %collective-permute-start.5 = (bf16[128,2048]{1,0:T(8,128)(2,1)S(1)}, bf16[128,2048]{1,0:T(8,128)(2,1)S(1)}, u32[]{:S(2)}, u32[]{:S(2)}) collective-permute-start(bf16[128,2048]{1,0:T(8,128)(2,1)S(1)} %get-tuple-element.36), channel_id=1, source_target_pairs={{0,16},{8,24},{16,0},{24,8},{1,17},{9,25},{17,1},{25,9},{2,18},{10... | collective-permute-start | bytes 1572872 | tf_op jit(solution)/shard_map/ppermute | solution.py:22
  9.1 5.4 %collective-permute-start.3 = (bf16[2,2048]{1,0:T(2,128)(2,1)S(1)}, bf16[2,2048]{1,0:T(2,128)(2,1)S(1)}, u32[]{:S(2)}, u32[]{:S(2)}) collective-permute-start(bf16[2,2048]{1,0:T(2,128)(2,1)S(1)} %get-tuple-element.31), channel_id=1, source_target_pairs={{0,6},{1,7},{2,4},{3,5},{4,2},{5,3},{6,0},{7,1},{8,14},{9,15},{10,... | collective-permute-start | bytes 24584 | tf_op jit(solution)/shard_map/ppermute | solution.py:22
  12.7 4.5 %collective-permute-start.2 = (bf16[2,2048]{1,0:T(2,128)(2,1)S(1)}, bf16[2,2048]{1,0:T(2,128)(2,1)S(1)}, u32[]{:S(2)}, u32[]{:S(2)}) collective-permute-start(bf16[2,2048]{1,0:T(2,128)(2,1)S(1)} %get-tuple-element.31), channel_id=1, source_target_pairs={{0,4},{1,5},{2,6},{3,7},{4,0},{5,1},{6,2},{7,3},{8,12},{9,13},{10,... | collective-permute-start | bytes 24584 | tf_op jit(solution)/shard_map/ppermute | solution.py:22
  12.7 4.5 %collective-permute-start.1 = (bf16[2,2048]{1,0:T(2,128)(2,1)S(1)}, bf16[2,2048]{1,0:T(2,128)(2,1)S(1)}, u32[]{:S(2)}, u32[]{:S(2)}) collective-permute-start(bf16[2,2048]{1,0:T(2,128)(2,1)S(1)} %get-tuple-element.31), channel_id=1, source_target_pairs={{0,2},{1,3},{2,0},{3,1},{4,6},{5,7},{6,4},{7,5},{8,10},{9,11},{10,... | collective-permute-start | bytes 24584 | tf_op jit(solution)/shard_map/ppermute | solution.py:22
  17.3 17.5 %collective-permute-start.6 = (bf16[72,2048]{1,0:T(8,128)(2,1)S(1)}, bf16[72,2048]{1,0:T(8,128)(2,1)S(1)}, u32[]{:S(2)}, u32[]{:S(2)}) collective-permute-start(bf16[72,2048]{1,0:T(8,128)(2,1)S(1)} %join.1), channel_id=1, source_target_pairs={{0,8},{8,0},{16,24},{24,16},{1,9},{9,1},{17,25},{25,17},{2,10},{10... | collective-permute-start | bytes 884744 | tf_op jit(solution)/shard_map/ppermute | solution.py:22
  21.0 25.7 %collective-permute-start.10 = (bf16[192,1536]{1,0:T(8,128)(2,1)S(1)}, bf16[192,1536]{1,0:T(8,128)(2,1)S(1)}, u32[]{:S(2)}, u32[]{:S(2)}) collective-permute-start(bf16[192,1536]{1,0:T(8,128)(2,1)S(1)} %get-tuple-element.50), channel_id=1, source_target_pairs={{0,8},{8,0},{16,24},{24,16},{1,9},{9,1},{17,25},{25,17},{2,10},{10... | collective-permute-start | bytes 1769480 | tf_op jit(solution)/shard_map/ppermute | solution.py:22
  28.0 9.1 %collective-permute-start.4 = (bf16[72,2048]{1,0:T(8,128)(2,1)S(1)}, bf16[72,2048]{1,0:T(8,128)(2,1)S(1)}, u32[]{:S(2)}, u32[]{:S(2)}) collective-permute-start(bf16[72,2048]{1,0:T(8,128)(2,1)S(1)} %pick.1), channel_id=1, source_target_pairs={{0,16},{8,24},{16,0},{24,8},{1,17},{9,25},{17,1},{25,9},{2,18},{10... | collective-permute-start | bytes 884744 | tf_op jit(solution)/shard_map/ppermute | solution.py:22
  34.8 8.4 %copy-start.2 = (s32[16]{0:T(128)S(1)}, s32[16]{0:T(128)}, u32[]{:S(2)}) copy-start(s32[16]{0:T(128)} %coarse_ref.3) | copy-start | bytes 196
  34.8 6.9 %collective-permute-start.7 = (bf16[72,2048]{1,0:T(8,128)(2,1)S(1)}, bf16[72,2048]{1,0:T(8,128)(2,1)S(1)}, u32[]{:S(2)}, u32[]{:S(2)}) collective-permute-start(bf16[72,2048]{1,0:T(8,128)(2,1)S(1)} %collective-permute-done.6.refs_0_.vm_ref), channel_id=1, source_target_pairs={{0,16},{8,24},{16,0},{24,8},{1,17},{9,25},{17,1},{25,9},{2,18},{10... | collective-permute-start | bytes 884744 | tf_op jit(solution)/shard_map/ppermute | solution.py:22
  35.5 13.9 %collective-permute-start.9 = (bf16[192,512]{1,0:T(8,128)(2,1)S(1)}, bf16[192,512]{1,0:T(8,128)(2,1)S(1)}, u32[]{:S(2)}, u32[]{:S(2)}) collective-permute-start(bf16[192,512]{1,0:T(8,128)(2,1)S(1)} %get-tuple-element.49), channel_id=1, source_target_pairs={{0,8},{8,0},{16,24},{24,16},{1,9},{9,1},{17,25},{25,17},{2,10},{10... | collective-permute-start | bytes 589832 | tf_op jit(solution)/shard_map/ppermute | solution.py:22
  41.7 1.4 %collective-permute-start.8 = (bf16[32,2048]{1,0:T(8,128)(2,1)S(1)}, bf16[32,2048]{1,0:T(8,128)(2,1)S(1)}, u32[]{:S(2)}, u32[]{:S(2)}) collective-permute-start(bf16[32,2048]{1,0:T(8,128)(2,1)S(1)} %stack.1.mine_ref), channel_id=1, source_target_pairs={{0,1},{1,0},{2,3},{3,2},{4,5},{5,4},{6,7},{7,6},{8,9},{9,8},{10,11... | collective-permute-start | bytes 393224 | tf_op jit(solution)/shard_map/ppermute | solution.py:22

commit v8 on v7

--- a/solution.py
+++ b/solution.py
@@ -10,7 +10,7 @@
 HEAD_COUNT = 16
 HEAD_FEATURES = 128
 MIDDLE_DILATION = 4
-CHUNKS = (12, 4)
+CHUNKS = (14, 2)
 LANES = 128
 SUBLANES = 16
 EXP2_SCALE = HEAD_FEATURES ** (-0.5) * 1.4426950408889634
@@ -20,6 +20,16 @@
 def partner(value, axis, mask):
     pairs = [(source, source ^ mask) for source in range(lax.axis_size(axis))]
     return lax.ppermute(value, axis, pairs)
+
+
+def partner_elsewhere(value, inner_mask):
+    outer = lax.axis_size("outer")
+    outer_mask = 2 if outer > 2 else 0
+    pairs = []
+    for i in range(lax.axis_size("inner")):
+        for o in range(outer):
+            pairs.append((i * outer + o, (i ^ inner_mask) * outer + (o ^ outer_mask)))
+    return lax.ppermute(value, ("inner", "outer"), pairs)
 
 
 def one_hot(mask):
@@ -78,31 +88,16 @@
     copies[2].wait()
 
 
-def join_kernel(vm_ref, near_ref, out_ref):
-    members = vm_ref.shape[0]
-    out_ref[:members] = vm_ref[...]
-    out_ref[members:] = near_ref[...]
-
-
-def stack_kernel(near_ref, *refs):
-    out_ref = refs[-1]
-    rows = near_ref.shape[0]
-    out_ref[:rows] = near_ref[...]
-    for place, ref in enumerate(refs[:-1]):
-        out_ref[(place + 1) * rows : (place + 2) * rows] = ref[ref.shape[0] - rows :]
-
-
-def pick_kernel(middle_ref, k_ref, near_ref, members_ref):
+def pick_kernel(middle_ref, k_ref, members_ref):
     rows = k_ref.shape[0]
     members = rows // MIDDLE_DILATION
-    members_ref[members:] = near_ref[...]
     group = lax.broadcasted_iota(jnp.int32, (members, rows), 0)
     token = lax.broadcasted_iota(jnp.int32, (members, rows), 1)
     offset = token - MIDDLE_DILATION * group
     for head in range(HEAD_COUNT):
         columns = head_columns(head)
         chosen = one_hot(offset == middle_ref[head])
-        members_ref[:members, columns] = dot(chosen, k_ref[:, columns]).astype(jnp.bfloat16)
+        members_ref[:, columns] = dot(chosen, k_ref[:, columns]).astype(jnp.bfloat16)
 
 
 def dot_keys(q, keys):
@@ -182,8 +177,8 @@
         columns = head_columns(head)
         state, place = states[head // half], head % half
         pairs = [mine_ref[:, columns], other_ref[:, columns]]
-        keys = jnp.concatenate([cross_ref[:members, columns], diagonal_k_ref[:members, columns], *pairs], axis=0)
-        values = jnp.concatenate([cross_ref[members:, columns], diagonal_v_ref[:members, columns], *pairs], axis=0)
+        keys = jnp.concatenate([cross_ref[:members, columns], diagonal_k_ref[:, columns], *pairs], axis=0)
+        values = jnp.concatenate([cross_ref[members:, columns], diagonal_v_ref[:, columns], *pairs], axis=0)
         scores = dot_keys(keys, q_ref[:, columns])
         far = jnp.where((token & (MIDDLE_DILATION - 1)) == middle_ref[head], scores[:far_rows], MASKED)
         coarse = jnp.where(is_key & (token == coarse_ref[head]), scores[far_rows:], MASKED)
@@ -204,13 +199,12 @@
 
 def finish_kernel(heads, sum_ref, share_ref, own_a_ref, own_b_ref, other_a_ref, other_b_ref, vm_ref, vr_ref, *rest):
     out_ref, ready_ref, semaphores = rest[-3:]
-    members = vr_ref.shape[0] // (MIDDLE_DILATION - 1)
     half = HEAD_COUNT // 2
     copies = []
     for place, head in enumerate(heads):
         columns = head_columns(head)
         own_ref, other_ref = ((own_a_ref, other_a_ref), (own_b_ref, other_b_ref))[head // half]
-        values = jnp.concatenate([vm_ref[:members, columns], vr_ref[:, head_columns(place)]], axis=0)
+        values = jnp.concatenate([vm_ref[:, columns], vr_ref[:, head_columns(place)]], axis=0)
         result = own_ref[:, head_columns(head % half)] + dot(other_ref[head % half], values)
         result = sum_ref[:, columns] + share_ref[:, head : head + 1] * result
         ready_ref[place] = result.astype(jnp.bfloat16)
@@ -241,7 +235,6 @@
 def on_device(query, keys, values, middle_head_shift, coarse_head_shift):
     rows, width = query.shape
     members = rows // MIDDLE_DILATION
-    near_rows = lax.axis_size("outer")
     half = HEAD_COUNT // 2
     bf16, f32 = jnp.bfloat16, jnp.float32
     smem = pl.BlockSpec(memory_space=pltpu.SMEM)
@@ -270,28 +263,23 @@
         scratch_shapes=[orders, pltpu.SemaphoreType.DMA((3,))],
     )
     cross = partner(own_members, "inner", 2)
-    near = gather_upper(coarse, "outer")
-    own_vm = call(
-        join_kernel,
-        "join",
-        own_vm, near,
-        out_shape=pltpu.VMEM((members + near_rows, width), bf16),
-        in_specs=[vmem, vmem],
-        out_specs=vmem,
-    )
     other_vm = partner(own_vm, "inner", 1)
-    cross, own_vr = lax.optimization_barrier((cross, own_vr))
+    coarse = jnp.concatenate([coarse, partner_elsewhere(coarse, 1)], axis=0)
+    coarse = gather_upper(coarse, "outer")
+    coarse, own_vr = lax.optimization_barrier((coarse, own_vr))
     other_vr = [partner(piece, "inner", 1) for piece in own_vr]
     other_km = call(
         pick_kernel,
         "pick",
-        middle_head_shift, other_keys, near,
-        out_shape=pltpu.VMEM((members + near_rows, width), bf16),
-        in_specs=[smem, vmem, vmem],
+        middle_head_shift, lax.optimization_barrier((other_keys, cross))[0],
+        out_shape=pltpu.VMEM((members, width), bf16),
+        in_specs=[smem, vmem],
         out_specs=vmem,
     )
     diagonal_k = partner(other_km, "inner", 2)
-    other_keys = lax.optimization_barrier((other_keys, other_km))[0]
+    mine = jnp.concatenate([coarse, partner_elsewhere(coarse, 2)], axis=0)
+    other_cores = partner(mine, "outer", 1)
+    other_keys = lax.optimization_barrier((other_keys, other_km, other_cores))[0]
 
     def first_part(first, query):
         return call(
@@ -311,20 +299,11 @@
     own_a, weights_a, state_a = first_part(0, q)
     diagonal_v = partner(lax.optimization_barrier((other_vm, state_a))[0], "inner", 2)
     own_b, weights_b, state_b = first_part(half, lax.optimization_barrier((q, state_a, diagonal_k))[0])
-    diagonal_v = lax.optimization_barrier((diagonal_v, state_b))[0]
-    mine = call(
-        stack_kernel,
-        "stack",
-        near, other_vm, diagonal_k, diagonal_v,
-        out_shape=pltpu.VMEM((lax.axis_size("inner") * near_rows, width), bf16),
-        in_specs=[vmem] * 4,
-        out_specs=vmem,
-    )
     extra_sum, share = call(
         extra_kernel,
         "extra",
         middle_head_shift, coarse_head_shift, q, state_a, state_b, cross, diagonal_k, diagonal_v, mine,
-        partner(mine, "outer", 1),
+        other_cores,
         out_shape=[pltpu.VMEM((rows, width), f32), pltpu.VMEM((rows, LANES), f32)],
         in_specs=[smem, smem] + [vmem] * 8,
         out_specs=[vmem] * 2,

time: 50.6 us -> 53.1 us (1.049)
  waiting for transfers between devices: 15.4 us -> 10.7 us
  local copies, waits for them, and re-layouts: 1.32 us -> 5.85 us
  Pallas kernels: 19.3 us -> 20.7 us
  starting transfers between devices: 14.3 us -> 15.4 us
    ppermute x11, waiting for transfers between devices: 15.4 us -> 4.36 us  [partner(): return lax.ppermute(value, axis, pairs)]
    ppermute x0 -> x2, waiting for transfers between devices: none -> 6.37 us  [partner_elsewhere(): return lax.ppermute(value, ('inner', 'outer'), pairs)]
    concatenate x0 -> x2, local copies, waits for them, and re-layouts: none -> 2.71 us  [the longest x1 2.71 us: gather_upper(): jnp.concatenate([value] + [partner(value, axis, mask) for mask in masks],...]
    ppermute x0 -> x2, starting transfers between devices: none -> 2.39 us  [partner_elsewhere(): return lax.ppermute(value, ('inner', 'outer'), pairs)]
    unnamed x6 -> x15, local copies, waits for them, and re-layouts: 1.32 us -> 3.14 us
    pallas_call x9 -> x7, Pallas kernels: 19.3 us -> 20.7 us  [call(): pl.pallas_call(kernel, name=name, compiler_params=params, cost_estimate=c...]
    ppermute x11, starting transfers between devices: 14.3 us -> 13 us  [partner(): return lax.ppermute(value, axis, pairs)]
  transfers between devices with their start and end apart: 11 -> 13, of which waited for: 6 -> 6; matrix products, arithmetic and copies ran while one was open for 0% -> 7% of each run, Pallas kernels for 36% -> 37%
where the time goes in v8:
time: 53.1 us; the launch traced here: 52.8 us
  Pallas kernels  20.7 us (39%)
  starting transfers between devices  15.4 us (29%)
  waiting for transfers between devices  10.7 us (20%)
  local copies, waits for them, and re-layouts  5.85 us (11%)
    pallas_call x7, Pallas kernels, call(): pl.pallas_call(kernel, name=name, compiler_params=params, cost_estimate=c...  20.7 us
    ppermute x11, starting transfers between devices, partner(): return lax.ppermute(value, axis, pairs)  13 us
    ppermute x2, waiting for transfers between devices, partner_elsewhere(): return lax.ppermute(value, ('inner', 'outer'), pairs)  6.37 us
    ppermute x11, waiting for transfers between devices, partner(): return lax.ppermute(value, axis, pairs)  4.36 us
    unnamed x15, local copies, waits for them, and re-layouts  3.14 us
    concatenate x1, local copies, waits for them, and re-layouts, gather_upper(): jnp.concatenate([value] + [partner(value, axis, mask) for mask in masks],...  2.71 us
    ppermute x2, starting transfers between devices, partner_elsewhere(): return lax.ppermute(value, ('inner', 'outer'), pairs)  2.39 us
  transfers between devices with their start and end apart: 13, of which 6 were waited for; matrix products, arithmetic and copies ran while one was open for 7% of the time, Pallas kernels for 37%

profile of v8, /device:TPU:0, one launch (start us, length us, event | category | flops | bytes accessed | tf_op | source)
XLA Modules:
  0.0 52.8 jit_solution(17621165440503419523)
XLA Ops:
  0.0 2.9 %collective-permute-start = (bf16[256,2048]{1,0:T(8,128)(2,1)}, bf16[256,2048]{1,0:T(8,128)(2,1)S(1)}, u32[]{:S(2)}, u32[]{:S(2)}) collective-permute-start(bf16[256,2048]{1,0:T(8,128)(2,1)} %k_hbm.1), channel_id=1, source_target_pairs={{0,8},{8,0},{16,24},{24,16},{1,9},{9,1},{17,25},{25,17},{2,10},{10... | collective-permute-start | bytes 3145736 | tf_op jit(solution)/shard_map/ppermute | solution.py:22
  2.9 0.7 %copy-done.2 = s32[16]{0:T(128)S(1)} copy-done((s32[16]{0:T(128)S(1)}, s32[16]{0:T(128)}, u32[]{:S(2)}) %copy-start.2) | copy-done | bytes 88
  3.6 0.7 %copy-done.4 = s32[16]{0:T(128)S(1)} copy-done((s32[16]{0:T(128)S(1)}, s32[16]{0:T(128)}, u32[]{:S(2)}) %copy-start.4) | copy-done | bytes 88
  4.3 4.2 %prepare.1 = (bf16[256,2048]{1,0:T(8,128)(2,1)S(1)}, bf16[256,2048]{1,0:T(8,128)(2,1)S(1)}, bf16[256,2048]{1,0:T(8,128)(2,1)S(1)}, bf16[128,2048]{1,0:T(8,128)(2...) custom-call(s32[16]{0:T(128)S(1)} %copy-done.2, ...), custom_call_target="tpu_custom_call" | custom-call | tf_op jit(solution)/shard_map/prepare/pallas_call | solution.py:247
  8.4 0.0 copy-start
  8.5 1.0 %copy-done = bf16[256,2048]{1,0:T(8,128)(2,1)} copy-done((bf16[256,2048]{1,0:T(8,128)(2,1)}, bf16[256,2048]{1,0:T(8,128)(2,1)S(1)}, u32[]{:S(2)}) %copy-start) | copy-done | bytes 1048600
  9.4 1.5 %collective-permute-start.2 = (bf16[2,2048]{1,0:T(2,128)(2,1)S(1)}, bf16[2,2048]{1,0:T(2,128)(2,1)S(1)}, u32[]{:S(2)}, u32[]{:S(2)}) collective-permute-start(bf16[2,2048]{1,0:T(2,128)(2,1)S(1)} %get-tuple-element.33), channel_id=1, source_target_pairs={{0,10},{1,11},{2,8},{3,9},{4,14},{5,15},{6,12},{7,13},{8,2},{9,3},... | collective-permute-start | bytes 24584 | tf_op jit(solution)/shard_map/ppermute | solution.py:32
  11.0 3.1 %collective-permute-done.2 = bf16[2,2048]{1,0:T(2,128)(2,1)S(1)} collective-permute-done((bf16[2,2048]{1,0:T(2,128)(2,1)S(1)}, bf16[2,2048]{1,0:T(2,128)(2,1)S(1)}, u32[]{:S(2)}, u32[]{:S(2)}) %collective-permute-start.2) | collective-permute-done | bytes 8224 | tf_op jit(solution)/shard_map/ppermute | solution.py:32
  14.1 3.7 %collective-permute-start.5 = (bf16[4,2048]{1,0:T(4,128)(2,1)S(1)}, bf16[4,2048]{1,0:T(4,128)(2,1)S(1)}, u32[]{:S(2)}, u32[]{:S(2)}) collective-permute-start(bf16[4,2048]{1,0:T(4,128)(2,1)S(1)} %pad_maximum_fusion), channel_id=1, source_target_pairs={{0,6},{1,7},{2,4},{3,5},{4,2},{5,3},{6,0},{7,1},{8,14},{9,15},{10,... | collective-permute-start | bytes 49160 | tf_op jit(solution)/shard_map/ppermute | solution.py:22
  17.8 0.0 collective-permute-start.4
  17.8 0.8 %collective-permute-start.3 = (bf16[4,2048]{1,0:T(4,128)(2,1)S(1)}, bf16[4,2048]{1,0:T(4,128)(2,1)}, u32[]{:S(2)}, u32[]{:S(2)}) collective-permute-start(bf16[4,2048]{1,0:T(4,128)(2,1)S(1)} %pad_maximum_fusion), channel_id=1, source_target_pairs={{0,2},{1,3},{2,0},{3,1},{4,6},{5,7},{6,4},{7,5},{8,10},{9,11},{10,... | collective-permute-start | bytes 49160 | tf_op jit(solution)/shard_map/ppermute | solution.py:22
  18.6 0.4 collective-permute-start.9
  18.9 0.8 %collective-permute-done.5 = bf16[4,2048]{1,0:T(4,128)(2,1)S(1)} collective-permute-done((bf16[4,2048]{1,0:T(4,128)(2,1)S(1)}, bf16[4,2048]{1,0:T(4,128)(2,1)S(1)}, u32[]{:S(2)}, u32[]{:S(2)}) %collective-permute-start.5) | collective-permute-done | bytes 16416 | tf_op jit(solution)/shard_map/ppermute | solution.py:22
  19.7 1.5 %collective-permute-start.1 = (bf16[128,2048]{1,0:T(8,128)(2,1)}, bf16[128,2048]{1,0:T(8,128)(2,1)}, u32[]{:S(2)}, u32[]{:S(2)}) collective-permute-start(bf16[128,2048]{1,0:T(8,128)(2,1)} %get-tuple-element.31), channel_id=1, source_target_pairs={{0,16},{8,24},{16,0},{24,8},{1,17},{9,25},{17,1},{25,9},{2,18},{10... | collective-permute-start | bytes 1572872 | tf_op jit(solution)/shard_map/ppermute | solution.py:22
  21.3 1.3 %collective-permute-done.4 = bf16[4,2048]{1,0:T(4,128)(2,1)} collective-permute-done((bf16[4,2048]{1,0:T(4,128)(2,1)S(1)}, bf16[4,2048]{1,0:T(4,128)(2,1)}, u32[]{:S(2)}, u32[]{:S(2)}) %collective-permute-start.4) | collective-permute-done | bytes 16416 | tf_op jit(solution)/shard_map/ppermute | solution.py:22
  22.5 2.7 %concatenate.11 = bf16[16,2048]{1,0:T(8,128)(2,1)} concatenate(bf16[2,2048]{1,0:T(2,128)(2,1)S(1)} %get-tuple-element.33, bf16[2,2048]{1,0:T(2,128)(2,1)S(1)} %collective-permute-done.2, bf16[4,2048]{1,0:T(4,128)(2,1)} %collective-permute-done.3, bf16[4,2048]{1,0:T(4,128)(2,1)} %collective-permute-done.4, bf16[4,2048]{1,0:T(4,128)(2,1)S(1)} %collective-permute-done.5), dimensions={0} | concatenate | bytes 131072 | tf_op jit(solution)/shard_map/concatenate | solution.py:231
  25.2 0.8 %collective-permute-start.6 = (bf16[16,2048]{1,0:T(8,128)(2,1)}, bf16[16,2048]{1,0:T(8,128)(2,1)S(1)}, u32[]{:S(2)}, u32[]{:S(2)}) collective-permute-start(bf16[16,2048]{1,0:T(8,128)(2,1)} %concatenate.11), channel_id=1, source_target_pairs={{0,18},{1,19},{2,16},{3,17},{4,22},{5,23},{6,20},{7,21},{8,26},{9,... | collective-permute-start | bytes 196616 | tf_op jit(solution)/shard_map/ppermute | solution.py:32
  26.1 0.5 %collective-permute-start.12 = (bf16[192,1792]{1,0:T(8,128)(2,1)}, bf16[192,1792]{1,0:T(8,128)(2,1)S(1)}, u32[]{:S(2)}, u32[]{:S(2)}) collective-permute-start(bf16[192,1792]{1,0:T(8,128)(2,1)} %copy-done.6), channel_id=1, source_target_pairs={{0,8},{8,0},{16,24},{24,16},{1,9},{9,1},{17,25},{25,17},{2,10},{10... | collective-permute-start | bytes 2064392 | tf_op jit(solution)/shard_map/ppermute | solution.py:22
  26.6 0.8 %constant_dynamic-update-slice_fusion.1 = bf16[32,2048]{1,0:T(8,128)(2,1)S(1)} fusion(bf16[16,2048]{1,0:T(8,128)(2,1)} %concatenate.11), kind=kLoop, calls=%fused_computation.2 | loop fusion | bytes 131072
  27.4 3.3 %collective-permute-done.6 = bf16[16,2048]{1,0:T(8,128)(2,1)S(1)} collective-permute-done((bf16[16,2048]{1,0:T(8,128)(2,1)}, bf16[16,2048]{1,0:T(8,128)(2,1)S(1)}, u32[]{:S(2)}, u32[]{:S(2)}) %collective-permute-start.6) | collective-permute-done | bytes 65568 | tf_op jit(solution)/shard_map/ppermute | solution.py:32
  30.7 1.9 %collective-permute-done.1.cross_ref = bf16[128,2048]{1,0:T(8,128)(2,1)} collective-permute-done((bf16[128,2048]{1,0:T(8,128)(2,1)}, bf16[128,2048]{1,0:T(8,128)(2,1)}, u32[]{:S(2)}, u32[]{:S(2)}) %collective-permute-start.1) | collective-permute-done | bytes 524320 | tf_op jit(solution)/shard_map/ppermute | solution.py:22
  32.6 0.8 %pick.1 = bf16[64,2048]{1,0:T(8,128)(2,1)S(1)} custom-call(s32[16]{0:T(128)S(1)} %copy-done.3, bf16[256,2048]{1,0:T(8,128)(2,1)S(1)} %collective-permute-done.k_ref.kp_ref), custom_call_target="tpu_custom_call" | custom-call | tf_op jit(solution)/shard_map/pick/pallas_call | solution.py:247
  33.4 1.6 %collective-permute-start.8 = (bf16[64,2048]{1,0:T(8,128)(2,1)S(1)}, bf16[64,2048]{1,0:T(8,128)(2,1)S(1)}, u32[]{:S(2)}, u32[]{:S(2)}) collective-permute-start(bf16[64,2048]{1,0:T(8,128)(2,1)S(1)} %pick.1), channel_id=1, source_target_pairs={{0,16},{8,24},{16,0},{24,8},{1,17},{9,25},{17,1},{25,9},{2,18},{10... | collective-permute-start | bytes 786440 | tf_op jit(solution)/shard_map/ppermute | solution.py:22
  35.0 4.6 %first.2 = (f32[256,1024]{1,0:T(8,128)S(1)}, bf16[8,256,256]{2,1,0:T(8,128)(2,1)S(1)}, f32[256,128]{1,0:T(8,128)S(1)}) custom-call(s32[16]{0:T(128)S(1)} %copy-done.3, bf16[256,2048]{1,0:T(8,128)(2,1)S(1)} %get-tuple-element.39.q_ref, bf16[256,2048]{1,0:T(8,128)(2,1)S(1)} %get-tuple-element.29.k_ref, bf16[256,2048]{1,0:T(8,128)(2,1)S(1)} %copy-done.1, ...), custom_call_target="tpu_custom_call" | custom-call | tf_op jit(solution)/shard_map/first/pallas_call | solution.py:247
  39.7 0.0 copy-start.5
  39.7 0.6 %collective-permute-start.10 = (bf16[64,2048]{1,0:T(8,128)(2,1)S(1)}, bf16[64,2048]{1,0:T(8,128)(2,1)S(1)}, u32[]{:S(2)}, u32[]{:S(2)}) collective-permute-start(bf16[64,2048]{1,0:T(8,128)(2,1)S(1)} %collective-permute-done.9.vm_ref), channel_id=1, source_target_pairs={{0,16},{8,24},{16,0},{24,8},{1,17},{9,25},{17,1},{25,9},{2,18},{10... | collective-permute-start | bytes 786440 | tf_op jit(solution)/shard_map/ppermute | solution.py:22
  40.2 1.0 %collective-permute-start.11 = (bf16[192,256]{1,0:T(8,128)(2,1)S(1)}, bf16[192,256]{1,0:T(8,128)(2,1)S(1)}, u32[]{:S(2)}, u32[]{:S(2)}) collective-permute-start(bf16[192,256]{1,0:T(8,128)(2,1)S(1)} %get-tuple-element.49), channel_id=1, source_target_pairs={{0,8},{8,0},{16,24},{24,16},{1,9},{9,1},{17,25},{25,17},{2,10},{10... | collective-permute-start | bytes 294920 | tf_op jit(solution)/shard_map/ppermute | solution.py:22
  41.2 4.6 %first.3 = (f32[256,1024]{1,0:T(8,128)S(1)}, bf16[8,256,256]{2,1,0:T(8,128)(2,1)S(1)}, f32[256,128]{1,0:T(8,128)S(1)}) custom-call(s32[16]{0:T(128)S(1)} %copy-done.3, bf16[256,2048]{1,0:T(8,128)(2,1)S(1)} %get-tuple-element.39.q_ref, bf16[256,2048]{1,0:T(8,128)(2,1)S(1)} %get-tuple-element.29.k_ref, bf16[256,2048]{1,0:T(8,128)(2,1)S(1)} %copy-done.1, ...), custom_call_target="tpu_custom_call" | custom-call | tf_op jit(solution)/shard_map/first/pallas_call | solution.py:247
  45.9 0.4 collective-permute-done.10.diagonal_v_ref
  46.3 4.0 %extra.1 = (f32[256,2048]{1,0:T(8,128)S(1)}, f32[256,128]{1,0:T(8,128)S(1)}) custom-call(s32[16]{0:T(128)S(1)} %copy-done.3, s32[16]{0:T(128)S(1)} %copy-done.5, bf16[256,2048]{1,0:T(8,128)(2,1)S(1)} %get-tuple-element.39.q_ref, f32[256,128]{1,0:T(8,128)S(1)} %get-tuple-element.38.state_a_ref, f32[256,128]{1,0:T(8,128)S(1)} %get-tuple-element.40.state_b_ref, ...), custom_call_target="tpu_custom_call" | custom-call | tf_op jit(solution)/shard_map/extra/pallas_call | solution.py:247
  50.3 1.5 %finish.2.rest_0_ = bf16[256,2048]{1,0:T(8,128)(2,1)} custom-call(f32[256,2048]{1,0:T(8,128)S(1)} %get-tuple-element.43.sum_ref, f32[256,128]{1,0:T(8,128)S(1)} %get-tuple-element.44.share_ref, f32[256,1024]{1,0:T(8,128)S(1)} %get-tuple-element.45.own_a_ref, f32[256,1024]{1,0:T(8,128)S(1)} %get-tuple-element.46.own_b_ref, ...), custom_call_target="tpu_custom_call" | custom-call | tf_op jit(solution)/shard_map/finish/pallas_call | solution.py:247
  51.9 0.9 %finish.3 = bf16[256,2048]{1,0:T(8,128)(2,1)} custom-call(f32[256,2048]{1,0:T(8,128)S(1)} %get-tuple-element.43.sum_ref, f32[256,128]{1,0:T(8,128)S(1)} %get-tuple-element.44.share_ref, f32[256,1024]{1,0:T(8,128)S(1)} %get-tuple-element.45.own_a_ref, f32[256,1024]{1,0:T(8,128)S(1)} %get-tuple-element.46.own_b_ref, ...), custom_call_target="tpu_custom_call", output_to_operand_aliasing={{}: (8, {})} | custom-call | tf_op jit(solution)/shard_map/finish/pallas_call | solution.py:247
  (19 shorter events, 0.1 us)
Async XLA Ops:
  0.0 32.6 %collective-permute-start = (bf16[256,2048]{1,0:T(8,128)(2,1)}, bf16[256,2048]{1,0:T(8,128)(2,1)S(1)}, u32[]{:S(2)}, u32[]{:S(2)}) collective-permute-start(bf16[256,2048]{1,0:T(8,128)(2,1)} %k_hbm.1), channel_id=1, source_target_pairs={{0,8},{8,0},{16,24},{24,16},{1,9},{9,1},{17,25},{25,17},{2,10},{10... | collective-permute-start | bytes 3145736 | tf_op jit(solution)/shard_map/ppermute | solution.py:22
  2.9 0.7 %copy-start.2 = (s32[16]{0:T(128)S(1)}, s32[16]{0:T(128)}, u32[]{:S(2)}) copy-start(s32[16]{0:T(128)} %middle_ref.9) | copy-start | bytes 196
  3.6 0.7 %copy-start.4 = (s32[16]{0:T(128)S(1)}, s32[16]{0:T(128)}, u32[]{:S(2)}) copy-start(s32[16]{0:T(128)} %coarse_ref.3) | copy-start | bytes 196
  4.3 28.3 %copy-start.3 = (s32[16]{0:T(128)S(1)}, s32[16]{0:T(128)}, u32[]{:S(2)}) copy-start(s32[16]{0:T(128)} %middle_ref.9) | copy-start | bytes 196
  8.4 1.0 %copy-start = (bf16[256,2048]{1,0:T(8,128)(2,1)}, bf16[256,2048]{1,0:T(8,128)(2,1)S(1)}, u32[]{:S(2)}) copy-start(bf16[256,2048]{1,0:T(8,128)(2,1)S(1)} %get-tuple-element.30.v_ref) | copy-start | bytes 3145732
  9.4 9.1 %copy-start.6 = (bf16[192,1792]{1,0:T(8,128)(2,1)}, bf16[192,1792]{1,0:T(8,128)(2,1)S(1)}, u32[]{:S(2)}) copy-start(bf16[192,1792]{1,0:T(8,128)(2,1)S(1)} %get-tuple-element.50) | copy-start | bytes 2064388
  9.4 4.7 %collective-permute-start.2 = (bf16[2,2048]{1,0:T(2,128)(2,1)S(1)}, bf16[2,2048]{1,0:T(2,128)(2,1)S(1)}, u32[]{:S(2)}, u32[]{:S(2)}) collective-permute-start(bf16[2,2048]{1,0:T(2,128)(2,1)S(1)} %get-tuple-element.33), channel_id=1, source_target_pairs={{0,10},{1,11},{2,8},{3,9},{4,14},{5,15},{6,12},{7,13},{8,2},{9,3},... | collective-permute-start | bytes 24584 | tf_op jit(solution)/shard_map/ppermute | solution.py:32
  14.1 5.6 %collective-permute-start.5 = (bf16[4,2048]{1,0:T(4,128)(2,1)S(1)}, bf16[4,2048]{1,0:T(4,128)(2,1)S(1)}, u32[]{:S(2)}, u32[]{:S(2)}) collective-permute-start(bf16[4,2048]{1,0:T(4,128)(2,1)S(1)} %pad_maximum_fusion), channel_id=1, source_target_pairs={{0,6},{1,7},{2,4},{3,5},{4,2},{5,3},{6,0},{7,1},{8,14},{9,15},{10,... | collective-permute-start | bytes 49160 | tf_op jit(solution)/shard_map/ppermute | solution.py:22
  17.8 4.7 %collective-permute-start.4 = (bf16[4,2048]{1,0:T(4,128)(2,1)S(1)}, bf16[4,2048]{1,0:T(4,128)(2,1)}, u32[]{:S(2)}, u32[]{:S(2)}) collective-permute-start(bf16[4,2048]{1,0:T(4,128)(2,1)S(1)} %pad_maximum_fusion), channel_id=1, source_target_pairs={{0,4},{1,5},{2,6},{3,7},{4,0},{5,1},{6,2},{7,3},{8,12},{9,13},{10,... | collective-permute-start | bytes 49160 | tf_op jit(solution)/shard_map/ppermute | solution.py:22
  17.8 4.7 %collective-permute-start.3 = (bf16[4,2048]{1,0:T(4,128)(2,1)S(1)}, bf16[4,2048]{1,0:T(4,128)(2,1)}, u32[]{:S(2)}, u32[]{:S(2)}) collective-permute-start(bf16[4,2048]{1,0:T(4,128)(2,1)S(1)} %pad_maximum_fusion), channel_id=1, source_target_pairs={{0,2},{1,3},{2,0},{3,1},{4,6},{5,7},{6,4},{7,5},{8,10},{9,11},{10,... | collective-permute-start | bytes 49160 | tf_op jit(solution)/shard_map/ppermute | solution.py:22
  18.6 21.1 %collective-permute-start.9 = (bf16[64,2048]{1,0:T(8,128)(2,1)}, bf16[64,2048]{1,0:T(8,128)(2,1)S(1)}, u32[]{:S(2)}, u32[]{:S(2)}) collective-permute-start(bf16[64,2048]{1,0:T(8,128)(2,1)} %get-tuple-element.41), channel_id=1, source_target_pairs={{0,8},{8,0},{16,24},{24,16},{1,9},{9,1},{17,25},{25,17},{2,10},{10... | collective-permute-start | bytes 786440 | tf_op jit(solution)/shard_map/ppermute | solution.py:22
  19.7 12.8 %collective-permute-start.1 = (bf16[128,2048]{1,0:T(8,128)(2,1)}, bf16[128,2048]{1,0:T(8,128)(2,1)}, u32[]{:S(2)}, u32[]{:S(2)}) collective-permute-start(bf16[128,2048]{1,0:T(8,128)(2,1)} %get-tuple-element.31), channel_id=1, source_target_pairs={{0,16},{8,24},{16,0},{24,8},{1,17},{9,25},{17,1},{25,9},{2,18},{10... | collective-permute-start | bytes 1572872 | tf_op jit(solution)/shard_map/ppermute | solution.py:22
  25.2 9.8 %copy-start.1 = (bf16[256,2048]{1,0:T(8,128)(2,1)S(1)}, bf16[256,2048]{1,0:T(8,128)(2,1)}, u32[]{:S(2)}) copy-start(bf16[256,2048]{1,0:T(8,128)(2,1)} %copy-done) | copy-start | bytes 3145732
  25.2 5.5 %collective-permute-start.6 = (bf16[16,2048]{1,0:T(8,128)(2,1)}, bf16[16,2048]{1,0:T(8,128)(2,1)S(1)}, u32[]{:S(2)}, u32[]{:S(2)}) collective-permute-start(bf16[16,2048]{1,0:T(8,128)(2,1)} %concatenate.11), channel_id=1, source_target_pairs={{0,18},{1,19},{2,16},{3,17},{4,22},{5,23},{6,20},{7,21},{8,26},{9,... | collective-permute-start | bytes 196616 | tf_op jit(solution)/shard_map/ppermute | solution.py:32
  26.1 24.3 %collective-permute-start.12 = (bf16[192,1792]{1,0:T(8,128)(2,1)}, bf16[192,1792]{1,0:T(8,128)(2,1)S(1)}, u32[]{:S(2)}, u32[]{:S(2)}) collective-permute-start(bf16[192,1792]{1,0:T(8,128)(2,1)} %copy-done.6), channel_id=1, source_target_pairs={{0,8},{8,0},{16,24},{24,16},{1,9},{9,1},{17,25},{25,17},{2,10},{10... | collective-permute-start | bytes 2064392 | tf_op jit(solution)/shard_map/ppermute | solution.py:22
  30.7 4.3 %collective-permute-start.7 = (bf16[32,2048]{1,0:T(8,128)(2,1)S(1)}, bf16[32,2048]{1,0:T(8,128)(2,1)S(1)}, u32[]{:S(2)}, u32[]{:S(2)}) collective-permute-start(bf16[32,2048]{1,0:T(8,128)(2,1)S(1)} %constant_dynamic-update-slice_fusion.mine_ref), channel_id=1, source_target_pairs={{0,1},{1,0},{2,3},{3,2},{4,5},{5,4},{6,7},{7,6},{8,9},{9,8},{10,11... | collective-permute-start | bytes 393224 | tf_op jit(solution)/shard_map/ppermute | solution.py:22
  33.4 7.8 %collective-permute-start.8 = (bf16[64,2048]{1,0:T(8,128)(2,1)S(1)}, bf16[64,2048]{1,0:T(8,128)(2,1)S(1)}, u32[]{:S(2)}, u32[]{:S(2)}) collective-permute-start(bf16[64,2048]{1,0:T(8,128)(2,1)S(1)} %pick.1), channel_id=1, source_target_pairs={{0,16},{8,24},{16,0},{24,8},{1,17},{9,25},{17,1},{25,9},{2,18},{10... | collective-permute-start | bytes 786440 | tf_op jit(solution)/shard_map/ppermute | solution.py:22
  39.7 6.7 %copy-start.5 = (s32[16]{0:T(128)S(1)}, s32[16]{0:T(128)}, u32[]{:S(2)}) copy-start(s32[16]{0:T(128)} %coarse_ref.3) | copy-start | bytes 196
  39.7 6.7 %collective-permute-start.10 = (bf16[64,2048]{1,0:T(8,128)(2,1)S(1)}, bf16[64,2048]{1,0:T(8,128)(2,1)S(1)}, u32[]{:S(2)}, u32[]{:S(2)}) collective-permute-start(bf16[64,2048]{1,0:T(8,128)(2,1)S(1)} %collective-permute-done.9.vm_ref), channel_id=1, source_target_pairs={{0,16},{8,24},{16,0},{24,8},{1,17},{9,25},{17,1},{25,9},{2,18},{10... | collective-permute-start | bytes 786440 | tf_op jit(solution)/shard_map/ppermute | solution.py:22
  40.2 11.6 %collective-permute-start.11 = (bf16[192,256]{1,0:T(8,128)(2,1)S(1)}, bf16[192,256]{1,0:T(8,128)(2,1)S(1)}, u32[]{:S(2)}, u32[]{:S(2)}) collective-permute-start(bf16[192,256]{1,0:T(8,128)(2,1)S(1)} %get-tuple-element.49), channel_id=1, source_target_pairs={{0,8},{8,0},{16,24},{24,16},{1,9},{9,1},{17,25},{25,17},{2,10},{10... | collective-permute-start | bytes 294920 | tf_op jit(solution)/shard_map/ppermute | solution.py:22

commit v9 on v8

--- a/solution.py
+++ b/solution.py
@@ -10,7 +10,7 @@
 HEAD_COUNT = 16
 HEAD_FEATURES = 128
 MIDDLE_DILATION = 4
-CHUNKS = (14, 2)
+CHUNKS = (12, 4)
 LANES = 128
 SUBLANES = 16
 EXP2_SCALE = HEAD_FEATURES ** (-0.5) * 1.4426950408889634
@@ -240,7 +240,7 @@
     smem = pl.BlockSpec(memory_space=pltpu.SMEM)
     vmem = pl.BlockSpec(memory_space=pltpu.VMEM)
     anywhere = pl.BlockSpec(memory_space=pl.ANY)
-    params = pltpu.CompilerParams(vmem_limit_bytes=16 * 1024 * 1024)
+    params = pltpu.CompilerParams(vmem_limit_bytes=8 * 1024 * 1024)
     orders = pltpu.VMEM((MIDDLE_DILATION, rows, rows), bf16)
 
     def call(kernel, name, *args, **options):
@@ -263,23 +263,21 @@
         scratch_shapes=[orders, pltpu.SemaphoreType.DMA((3,))],
     )
     cross = partner(own_members, "inner", 2)
+    near = gather_upper(jnp.concatenate([coarse, partner_elsewhere(coarse, 1)], axis=0), "outer")
+    near, own_vm = lax.optimization_barrier((near, own_vm))
     other_vm = partner(own_vm, "inner", 1)
-    coarse = jnp.concatenate([coarse, partner_elsewhere(coarse, 1)], axis=0)
-    coarse = gather_upper(coarse, "outer")
-    coarse, own_vr = lax.optimization_barrier((coarse, own_vr))
+    cross, own_vr = lax.optimization_barrier((cross, own_vr))
     other_vr = [partner(piece, "inner", 1) for piece in own_vr]
     other_km = call(
         pick_kernel,
         "pick",
-        middle_head_shift, lax.optimization_barrier((other_keys, cross))[0],
+        middle_head_shift, other_keys,
         out_shape=pltpu.VMEM((members, width), bf16),
         in_specs=[smem, vmem],
         out_specs=vmem,
     )
     diagonal_k = partner(other_km, "inner", 2)
-    mine = jnp.concatenate([coarse, partner_elsewhere(coarse, 2)], axis=0)
-    other_cores = partner(mine, "outer", 1)
-    other_keys = lax.optimization_barrier((other_keys, other_km, other_cores))[0]
+    other_keys = lax.optimization_barrier((other_keys, other_km))[0]
 
     def first_part(first, query):
         return call(
@@ -299,11 +297,12 @@
     own_a, weights_a, state_a = first_part(0, q)
     diagonal_v = partner(lax.optimization_barrier((other_vm, state_a))[0], "inner", 2)
     own_b, weights_b, state_b = first_part(half, lax.optimization_barrier((q, state_a, diagonal_k))[0])
+    mine = jnp.concatenate([near, partner_elsewhere(near, 2)], axis=0)
     extra_sum, share = call(
         extra_kernel,
         "extra",
         middle_head_shift, coarse_head_shift, q, state_a, state_b, cross, diagonal_k, diagonal_v, mine,
-        other_cores,
+        partner(mine, "outer", 1),
         out_shape=[pltpu.VMEM((rows, width), f32), pltpu.VMEM((rows, LANES), f32)],
         in_specs=[smem, smem] + [vmem] * 8,
         out_specs=[vmem] * 2,

time: 53.1 us -> 50.1 us (0.944)
  local copies, waits for them, and re-layouts: 5.85 us -> 2.38 us
  waiting for transfers between devices: 10.7 us -> 11.5 us
    ppermute x11, waiting for transfers between devices: 4.36 us -> 8.38 us  [partner(): return lax.ppermute(value, axis, pairs)]
    ppermute x2, waiting for transfers between devices: 6.37 us -> 3.11 us  [partner_elsewhere(): return lax.ppermute(value, ('inner', 'outer'), pairs)]
    concatenate x1, local copies, waits for them, and re-layouts: 2.71 us -> 0.08 us  [gather_upper(): jnp.concatenate([value] + [partner(value, axis, mask) for mask in masks],...]
    ppermute x11, starting transfers between devices: 13 us -> 13.8 us  [partner(): return lax.ppermute(value, axis, pairs)]
    ppermute x2, starting transfers between devices: 2.39 us -> 1.55 us  [partner_elsewhere(): return lax.ppermute(value, ('inner', 'outer'), pairs)]
    unnamed x15 -> x17, local copies, waits for them, and re-layouts: 3.14 us -> 2.3 us
  transfers between devices with their start and end apart: 13 -> 13, of which waited for: 6 -> 7; matrix products, arithmetic and copies ran while one was open for 7% -> 0% of each run, Pallas kernels for 37% -> 39%
where the time goes in v9:
time: 50.1 us; the launch traced here: 49.9 us
  Pallas kernels  20.5 us (41%)
  starting transfers between devices  15.4 us (31%)
  waiting for transfers between devices  11.5 us (23%)
  local copies, waits for them, and re-layouts  2.38 us (5%)
    pallas_call x7, Pallas kernels, call(): pl.pallas_call(kernel, name=name, compiler_params=params, cost_estimate=c...  20.5 us
    ppermute x11, starting transfers between devices, partner(): return lax.ppermute(value, axis, pairs)  13.8 us
    ppermute x11, waiting for transfers between devices, partner(): return lax.ppermute(value, axis, pairs)  8.38 us
    ppermute x2, waiting for transfers between devices, partner_elsewhere(): return lax.ppermute(value, ('inner', 'outer'), pairs)  3.11 us
    unnamed x17, local copies, waits for them, and re-layouts  2.3 us
    ppermute x2, starting transfers between devices, partner_elsewhere(): return lax.ppermute(value, ('inner', 'outer'), pairs)  1.55 us
  transfers between devices with their start and end apart: 13, of which 7 were waited for; matrix products, arithmetic and copies ran while one was open for 0% of the time, Pallas kernels for 39%

profile of v9, /device:TPU:0, one launch (start us, length us, event | category | flops | bytes accessed | tf_op | source)
XLA Modules:
  0.0 49.9 jit_solution(7989900806555897313)
XLA Ops:
  0.0 2.9 %collective-permute-start = (bf16[256,2048]{1,0:T(8,128)(2,1)}, bf16[256,2048]{1,0:T(8,128)(2,1)S(1)}, u32[]{:S(2)}, u32[]{:S(2)}) collective-permute-start(bf16[256,2048]{1,0:T(8,128)(2,1)} %k_hbm.1), channel_id=1, source_target_pairs={{0,8},{8,0},{16,24},{24,16},{1,9},{9,1},{17,25},{25,17},{2,10},{10... | collective-permute-start | bytes 3145736 | tf_op jit(solution)/shard_map/ppermute | solution.py:22
  2.9 0.7 %copy-done.2 = s32[16]{0:T(128)S(1)} copy-done((s32[16]{0:T(128)S(1)}, s32[16]{0:T(128)}, u32[]{:S(2)}) %copy-start.2) | copy-done | bytes 88
  3.6 0.7 %copy-done.4 = s32[16]{0:T(128)S(1)} copy-done((s32[16]{0:T(128)S(1)}, s32[16]{0:T(128)}, u32[]{:S(2)}) %copy-start.4) | copy-done | bytes 88
  4.3 4.1 %prepare.1 = (bf16[256,2048]{1,0:T(8,128)(2,1)S(1)}, bf16[256,2048]{1,0:T(8,128)(2,1)S(1)}, bf16[256,2048]{1,0:T(8,128)(2,1)S(1)}, bf16[128,2048]{1,0:T(8,128)(2...) custom-call(s32[16]{0:T(128)S(1)} %copy-done.2, ...), custom_call_target="tpu_custom_call" | custom-call | tf_op jit(solution)/shard_map/prepare/pallas_call | solution.py:247
  8.3 0.0 copy-start
  8.3 1.0 %copy-done = bf16[256,2048]{1,0:T(8,128)(2,1)} copy-done((bf16[256,2048]{1,0:T(8,128)(2,1)}, bf16[256,2048]{1,0:T(8,128)(2,1)S(1)}, u32[]{:S(2)}) %copy-start) | copy-done | bytes 1048600
  9.3 1.5 %collective-permute-start.2 = (bf16[128,2048]{1,0:T(8,128)(2,1)}, bf16[128,2048]{1,0:T(8,128)(2,1)}, u32[]{:S(2)}, u32[]{:S(2)}) collective-permute-start(bf16[128,2048]{1,0:T(8,128)(2,1)} %get-tuple-element.36), channel_id=1, source_target_pairs={{0,16},{8,24},{16,0},{24,8},{1,17},{9,25},{17,1},{25,9},{2,18},{10... | collective-permute-start | bytes 1572872 | tf_op jit(solution)/shard_map/ppermute | solution.py:22
  10.8 1.5 %collective-permute-start.3 = (bf16[2,2048]{1,0:T(2,128)(2,1)S(1)}, bf16[2,2048]{1,0:T(2,128)(2,1)S(1)}, u32[]{:S(2)}, u32[]{:S(2)}) collective-permute-start(bf16[2,2048]{1,0:T(2,128)(2,1)S(1)} %get-tuple-element.40), channel_id=1, source_target_pairs={{0,10},{1,11},{2,8},{3,9},{4,14},{5,15},{6,12},{7,13},{8,2},{9,3},... | collective-permute-start | bytes 24584 | tf_op jit(solution)/shard_map/ppermute | solution.py:32
  12.4 3.1 %collective-permute-done.3 = bf16[2,2048]{1,0:T(2,128)(2,1)S(1)} collective-permute-done((bf16[2,2048]{1,0:T(2,128)(2,1)S(1)}, bf16[2,2048]{1,0:T(2,128)(2,1)S(1)}, u32[]{:S(2)}, u32[]{:S(2)}) %collective-permute-start.3) | collective-permute-done | bytes 8224 | tf_op jit(solution)/shard_map/ppermute | solution.py:32
  15.5 1.6 %collective-permute-start.4 = (bf16[4,2048]{1,0:T(4,128)(2,1)S(1)}, bf16[4,2048]{1,0:T(4,128)(2,1)S(1)}, u32[]{:S(2)}, u32[]{:S(2)}) collective-permute-start(bf16[4,2048]{1,0:T(4,128)(2,1)S(1)} %pad_maximum_fusion), channel_id=1, source_target_pairs={{0,2},{1,3},{2,0},{3,1},{4,6},{5,7},{6,4},{7,5},{8,10},{9,11},{10,... | collective-permute-start | bytes 49160 | tf_op jit(solution)/shard_map/ppermute | solution.py:22
  17.2 2.6 %collective-permute-start.5 = (bf16[4,2048]{1,0:T(4,128)(2,1)S(1)}, bf16[4,2048]{1,0:T(4,128)(2,1)S(1)}, u32[]{:S(2)}, u32[]{:S(2)}) collective-permute-start(bf16[4,2048]{1,0:T(4,128)(2,1)S(1)} %pad_maximum_fusion), channel_id=1, source_target_pairs={{0,4},{1,5},{2,6},{3,7},{4,0},{5,1},{6,2},{7,3},{8,12},{9,13},{10,... | collective-permute-start | bytes 49160 | tf_op jit(solution)/shard_map/ppermute | solution.py:22
  19.7 0.2 collective-permute-start.6
  20.0 2.1 %collective-permute-done.5 = bf16[4,2048]{1,0:T(4,128)(2,1)S(1)} collective-permute-done((bf16[4,2048]{1,0:T(4,128)(2,1)S(1)}, bf16[4,2048]{1,0:T(4,128)(2,1)S(1)}, u32[]{:S(2)}, u32[]{:S(2)}) %collective-permute-start.5) | collective-permute-done | bytes 16416 | tf_op jit(solution)/shard_map/ppermute | solution.py:22
  22.0 3.3 %collective-permute-done.6 = bf16[4,2048]{1,0:T(4,128)(2,1)S(1)} collective-permute-done((bf16[4,2048]{1,0:T(4,128)(2,1)S(1)}, bf16[4,2048]{1,0:T(4,128)(2,1)S(1)}, u32[]{:S(2)}, u32[]{:S(2)}) %collective-permute-start.6) | collective-permute-done | bytes 16416 | tf_op jit(solution)/shard_map/ppermute | solution.py:22
  25.3 0.1 concatenate.11
  25.4 0.0 copy-start.1
  25.4 0.6 %collective-permute-start.7 = (bf16[64,2048]{1,0:T(8,128)(2,1)S(1)}, bf16[64,2048]{1,0:T(8,128)(2,1)S(1)}, u32[]{:S(2)}, u32[]{:S(2)}) collective-permute-start(bf16[64,2048]{1,0:T(8,128)(2,1)S(1)} %get-tuple-element.42), channel_id=1, source_target_pairs={{0,8},{8,0},{16,24},{24,16},{1,9},{9,1},{17,25},{25,17},{2,10},{10... | collective-permute-start | bytes 786440 | tf_op jit(solution)/shard_map/ppermute | solution.py:22
  26.0 1.5 %collective-permute-start.12 = (bf16[192,1536]{1,0:T(8,128)(2,1)}, bf16[192,1536]{1,0:T(8,128)(2,1)S(1)}, u32[]{:S(2)}, u32[]{:S(2)}) collective-permute-start(bf16[192,1536]{1,0:T(8,128)(2,1)} %copy-done.6), channel_id=1, source_target_pairs={{0,8},{8,0},{16,24},{24,16},{1,9},{9,1},{17,25},{25,17},{2,10},{10... | collective-permute-start | bytes 1769480 | tf_op jit(solution)/shard_map/ppermute | solution.py:22
  27.5 0.6 %collective-permute-start.11 = (bf16[192,512]{1,0:T(8,128)(2,1)}, bf16[192,512]{1,0:T(8,128)(2,1)S(1)}, u32[]{:S(2)}, u32[]{:S(2)}) collective-permute-start(bf16[192,512]{1,0:T(8,128)(2,1)} %copy-done.7), channel_id=1, source_target_pairs={{0,8},{8,0},{16,24},{24,16},{1,9},{9,1},{17,25},{25,17},{2,10},{10... | collective-permute-start | bytes 589832 | tf_op jit(solution)/shard_map/ppermute | solution.py:22
  28.1 0.8 %pick.1 = bf16[64,2048]{1,0:T(8,128)(2,1)S(1)} custom-call(s32[16]{0:T(128)S(1)} %copy-done.3, bf16[256,2048]{1,0:T(8,128)(2,1)S(1)} %collective-permute-done.k_ref.kp_ref), custom_call_target="tpu_custom_call" | custom-call | tf_op jit(solution)/shard_map/pick/pallas_call | solution.py:247
  28.9 1.4 %collective-permute-start.1 = (bf16[64,2048]{1,0:T(8,128)(2,1)S(1)}, bf16[64,2048]{1,0:T(8,128)(2,1)S(1)}, u32[]{:S(2)}, u32[]{:S(2)}) collective-permute-start(bf16[64,2048]{1,0:T(8,128)(2,1)S(1)} %pick.1), channel_id=1, source_target_pairs={{0,16},{8,24},{16,0},{24,8},{1,17},{9,25},{17,1},{25,9},{2,18},{10... | collective-permute-start | bytes 786440 | tf_op jit(solution)/shard_map/ppermute | solution.py:22
  30.3 4.6 %first.2 = (f32[256,1024]{1,0:T(8,128)S(1)}, bf16[8,256,256]{2,1,0:T(8,128)(2,1)S(1)}, f32[256,128]{1,0:T(8,128)S(1)}) custom-call(s32[16]{0:T(128)S(1)} %copy-done.3, bf16[256,2048]{1,0:T(8,128)(2,1)S(1)} %get-tuple-element.34.q_ref, bf16[256,2048]{1,0:T(8,128)(2,1)S(1)} %get-tuple-element.30.k_ref, bf16[256,2048]{1,0:T(8,128)(2,1)S(1)} %copy-done.1, ...), custom_call_target="tpu_custom_call" | custom-call | tf_op jit(solution)/shard_map/first/pallas_call | solution.py:247
  35.0 0.8 %collective-permute-start.8 = (bf16[64,2048]{1,0:T(8,128)(2,1)S(1)}, bf16[64,2048]{1,0:T(8,128)(2,1)S(1)}, u32[]{:S(2)}, u32[]{:S(2)}) collective-permute-start(bf16[64,2048]{1,0:T(8,128)(2,1)S(1)} %collective-permute-done.7.vm_ref), channel_id=1, source_target_pairs={{0,16},{8,24},{16,0},{24,8},{1,17},{9,25},{17,1},{25,9},{2,18},{10... | collective-permute-start | bytes 786440 | tf_op jit(solution)/shard_map/ppermute | solution.py:22
  35.8 0.1 collective-permute-start.10
  35.8 0.1 collective-permute-done.1.diagonal_k_ref
  35.9 4.6 %first.3 = (f32[256,1024]{1,0:T(8,128)S(1)}, bf16[8,256,256]{2,1,0:T(8,128)(2,1)S(1)}, f32[256,128]{1,0:T(8,128)S(1)}) custom-call(s32[16]{0:T(128)S(1)} %copy-done.3, bf16[256,2048]{1,0:T(8,128)(2,1)S(1)} %get-tuple-element.34.q_ref, bf16[256,2048]{1,0:T(8,128)(2,1)S(1)} %get-tuple-element.30.k_ref, bf16[256,2048]{1,0:T(8,128)(2,1)S(1)} %copy-done.1, ...), custom_call_target="tpu_custom_call" | custom-call | tf_op jit(solution)/shard_map/first/pallas_call | solution.py:247
  40.6 0.8 %collective-permute-done.8.diagonal_v_ref = bf16[64,2048]{1,0:T(8,128)(2,1)S(1)} collective-permute-done((bf16[64,2048]{1,0:T(8,128)(2,1)S(1)}, bf16[64,2048]{1,0:T(8,128)(2,1)S(1)}, u32[]{:S(2)}, u32[]{:S(2)}) %collective-permute-start.8) | collective-permute-done | bytes 262176 | tf_op jit(solution)/shard_map/ppermute | solution.py:22
  41.4 4.0 %extra.1 = (f32[256,2048]{1,0:T(8,128)S(1)}, f32[256,128]{1,0:T(8,128)S(1)}) custom-call(s32[16]{0:T(128)S(1)} %copy-done.3, s32[16]{0:T(128)S(1)} %copy-done.5, bf16[256,2048]{1,0:T(8,128)(2,1)S(1)} %get-tuple-element.34.q_ref, f32[256,128]{1,0:T(8,128)S(1)} %get-tuple-element.33.state_a_ref, f32[256,128]{1,0:T(8,128)S(1)} %get-tuple-element.35.state_b_ref, ...), custom_call_target="tpu_custom_call" | custom-call | tf_op jit(solution)/shard_map/extra/pallas_call | solution.py:247
  45.4 1.4 %collective-permute-done.12.vr_ref = bf16[192,1536]{1,0:T(8,128)(2,1)S(1)} collective-permute-done((bf16[192,1536]{1,0:T(8,128)(2,1)}, bf16[192,1536]{1,0:T(8,128)(2,1)S(1)}, u32[]{:S(2)}, u32[]{:S(2)}) %collective-permute-start.12) | collective-permute-done | bytes 589856 | tf_op jit(solution)/shard_map/ppermute | solution.py:22
  46.8 1.4 %finish.2.rest_0_ = bf16[256,2048]{1,0:T(8,128)(2,1)} custom-call(f32[256,2048]{1,0:T(8,128)S(1)} %get-tuple-element.45.sum_ref, f32[256,128]{1,0:T(8,128)S(1)} %get-tuple-element.46.share_ref, f32[256,1024]{1,0:T(8,128)S(1)} %get-tuple-element.47.own_a_ref, f32[256,1024]{1,0:T(8,128)S(1)} %get-tuple-element.48.own_b_ref, ...), custom_call_target="tpu_custom_call" | custom-call | tf_op jit(solution)/shard_map/finish/pallas_call | solution.py:247
  48.2 0.7 %collective-permute-done.11.vr_ref = bf16[192,512]{1,0:T(8,128)(2,1)S(1)} collective-permute-done((bf16[192,512]{1,0:T(8,128)(2,1)}, bf16[192,512]{1,0:T(8,128)(2,1)S(1)}, u32[]{:S(2)}, u32[]{:S(2)}) %collective-permute-start.11) | collective-permute-done | bytes 196640 | tf_op jit(solution)/shard_map/ppermute | solution.py:22
  49.0 1.0 %finish.3 = bf16[256,2048]{1,0:T(8,128)(2,1)} custom-call(f32[256,2048]{1,0:T(8,128)S(1)} %get-tuple-element.45.sum_ref, f32[256,128]{1,0:T(8,128)S(1)} %get-tuple-element.46.share_ref, f32[256,1024]{1,0:T(8,128)S(1)} %get-tuple-element.47.own_a_ref, f32[256,1024]{1,0:T(8,128)S(1)} %get-tuple-element.48.own_b_ref, ...), custom_call_target="tpu_custom_call", output_to_operand_aliasing={{}: (8, {})} | custom-call | tf_op jit(solution)/shard_map/finish/pallas_call | solution.py:247
  (21 shorter events, 0.1 us)
Async XLA Ops:
  0.0 28.1 %collective-permute-start = (bf16[256,2048]{1,0:T(8,128)(2,1)}, bf16[256,2048]{1,0:T(8,128)(2,1)S(1)}, u32[]{:S(2)}, u32[]{:S(2)}) collective-permute-start(bf16[256,2048]{1,0:T(8,128)(2,1)} %k_hbm.1), channel_id=1, source_target_pairs={{0,8},{8,0},{16,24},{24,16},{1,9},{9,1},{17,25},{25,17},{2,10},{10... | collective-permute-start | bytes 3145736 | tf_op jit(solution)/shard_map/ppermute | solution.py:22
  2.9 0.7 %copy-start.2 = (s32[16]{0:T(128)S(1)}, s32[16]{0:T(128)}, u32[]{:S(2)}) copy-start(s32[16]{0:T(128)} %middle_ref.9) | copy-start | bytes 196
  3.6 0.7 %copy-start.4 = (s32[16]{0:T(128)S(1)}, s32[16]{0:T(128)}, u32[]{:S(2)}) copy-start(s32[16]{0:T(128)} %coarse_ref.3) | copy-start | bytes 196
  4.3 23.8 %copy-start.3 = (s32[16]{0:T(128)S(1)}, s32[16]{0:T(128)}, u32[]{:S(2)}) copy-start(s32[16]{0:T(128)} %middle_ref.9) | copy-start | bytes 196
  8.3 1.0 %copy-start = (bf16[256,2048]{1,0:T(8,128)(2,1)}, bf16[256,2048]{1,0:T(8,128)(2,1)S(1)}, u32[]{:S(2)}) copy-start(bf16[256,2048]{1,0:T(8,128)(2,1)S(1)} %get-tuple-element.31.v_ref) | copy-start | bytes 3145732
  9.3 6.2 %copy-start.6 = (bf16[192,1536]{1,0:T(8,128)(2,1)}, bf16[192,1536]{1,0:T(8,128)(2,1)S(1)}, u32[]{:S(2)}) copy-start(bf16[192,1536]{1,0:T(8,128)(2,1)S(1)} %get-tuple-element.52) | copy-start | bytes 1769476
  9.3 6.2 %copy-start.7 = (bf16[192,512]{1,0:T(8,128)(2,1)}, bf16[192,512]{1,0:T(8,128)(2,1)S(1)}, u32[]{:S(2)}) copy-start(bf16[192,512]{1,0:T(8,128)(2,1)S(1)} %get-tuple-element.51) | copy-start | bytes 589828
  9.3 16.7 %collective-permute-start.2 = (bf16[128,2048]{1,0:T(8,128)(2,1)}, bf16[128,2048]{1,0:T(8,128)(2,1)}, u32[]{:S(2)}, u32[]{:S(2)}) collective-permute-start(bf16[128,2048]{1,0:T(8,128)(2,1)} %get-tuple-element.36), channel_id=1, source_target_pairs={{0,16},{8,24},{16,0},{24,8},{1,17},{9,25},{17,1},{25,9},{2,18},{10... | collective-permute-start | bytes 1572872 | tf_op jit(solution)/shard_map/ppermute | solution.py:22
  10.8 4.7 %collective-permute-start.3 = (bf16[2,2048]{1,0:T(2,128)(2,1)S(1)}, bf16[2,2048]{1,0:T(2,128)(2,1)S(1)}, u32[]{:S(2)}, u32[]{:S(2)}) collective-permute-start(bf16[2,2048]{1,0:T(2,128)(2,1)S(1)} %get-tuple-element.40), channel_id=1, source_target_pairs={{0,10},{1,11},{2,8},{3,9},{4,14},{5,15},{6,12},{7,13},{8,2},{9,3},... | collective-permute-start | bytes 24584 | tf_op jit(solution)/shard_map/ppermute | solution.py:32
  15.5 4.5 %collective-permute-start.4 = (bf16[4,2048]{1,0:T(4,128)(2,1)S(1)}, bf16[4,2048]{1,0:T(4,128)(2,1)S(1)}, u32[]{:S(2)}, u32[]{:S(2)}) collective-permute-start(bf16[4,2048]{1,0:T(4,128)(2,1)S(1)} %pad_maximum_fusion), channel_id=1, source_target_pairs={{0,2},{1,3},{2,0},{3,1},{4,6},{5,7},{6,4},{7,5},{8,10},{9,11},{10,... | collective-permute-start | bytes 49160 | tf_op jit(solution)/shard_map/ppermute | solution.py:22
  17.2 4.9 %collective-permute-start.5 = (bf16[4,2048]{1,0:T(4,128)(2,1)S(1)}, bf16[4,2048]{1,0:T(4,128)(2,1)S(1)}, u32[]{:S(2)}, u32[]{:S(2)}) collective-permute-start(bf16[4,2048]{1,0:T(4,128)(2,1)S(1)} %pad_maximum_fusion), channel_id=1, source_target_pairs={{0,4},{1,5},{2,6},{3,7},{4,0},{5,1},{6,2},{7,3},{8,12},{9,13},{10,... | collective-permute-start | bytes 49160 | tf_op jit(solution)/shard_map/ppermute | solution.py:22
  19.7 5.5 %collective-permute-start.6 = (bf16[4,2048]{1,0:T(4,128)(2,1)S(1)}, bf16[4,2048]{1,0:T(4,128)(2,1)S(1)}, u32[]{:S(2)}, u32[]{:S(2)}) collective-permute-start(bf16[4,2048]{1,0:T(4,128)(2,1)S(1)} %pad_maximum_fusion), channel_id=1, source_target_pairs={{0,6},{1,7},{2,4},{3,5},{4,2},{5,3},{6,0},{7,1},{8,14},{9,15},{10,... | collective-permute-start | bytes 49160 | tf_op jit(solution)/shard_map/ppermute | solution.py:22
  25.4 5.0 %copy-start.1 = (bf16[256,2048]{1,0:T(8,128)(2,1)S(1)}, bf16[256,2048]{1,0:T(8,128)(2,1)}, u32[]{:S(2)}) copy-start(bf16[256,2048]{1,0:T(8,128)(2,1)} %copy-done) | copy-start | bytes 3145732
  25.4 9.6 %collective-permute-start.7 = (bf16[64,2048]{1,0:T(8,128)(2,1)S(1)}, bf16[64,2048]{1,0:T(8,128)(2,1)S(1)}, u32[]{:S(2)}, u32[]{:S(2)}) collective-permute-start(bf16[64,2048]{1,0:T(8,128)(2,1)S(1)} %get-tuple-element.42), channel_id=1, source_target_pairs={{0,8},{8,0},{16,24},{24,16},{1,9},{9,1},{17,25},{25,17},{2,10},{10... | collective-permute-start | bytes 786440 | tf_op jit(solution)/shard_map/ppermute | solution.py:22
  26.0 20.9 %collective-permute-start.12 = (bf16[192,1536]{1,0:T(8,128)(2,1)}, bf16[192,1536]{1,0:T(8,128)(2,1)S(1)}, u32[]{:S(2)}, u32[]{:S(2)}) collective-permute-start(bf16[192,1536]{1,0:T(8,128)(2,1)} %copy-done.6), channel_id=1, source_target_pairs={{0,8},{8,0},{16,24},{24,16},{1,9},{9,1},{17,25},{25,17},{2,10},{10... | collective-permute-start | bytes 1769480 | tf_op jit(solution)/shard_map/ppermute | solution.py:22
  27.5 8.3 %collective-permute-start.9 = (bf16[16,2048]{1,0:T(8,128)(2,1)S(1)}, bf16[16,2048]{1,0:T(8,128)(2,1)S(1)}, u32[]{:S(2)}, u32[]{:S(2)}) collective-permute-start(bf16[16,2048]{1,0:T(8,128)(2,1)S(1)} %concatenate.11), channel_id=1, source_target_pairs={{0,18},{1,19},{2,16},{3,17},{4,22},{5,23},{6,20},{7,21},{8,26},{9,... | collective-permute-start | bytes 196616 | tf_op jit(solution)/shard_map/ppermute | solution.py:32
  27.5 21.5 %collective-permute-start.11 = (bf16[192,512]{1,0:T(8,128)(2,1)}, bf16[192,512]{1,0:T(8,128)(2,1)S(1)}, u32[]{:S(2)}, u32[]{:S(2)}) collective-permute-start(bf16[192,512]{1,0:T(8,128)(2,1)} %copy-done.7), channel_id=1, source_target_pairs={{0,8},{8,0},{16,24},{24,16},{1,9},{9,1},{17,25},{25,17},{2,10},{10... | collective-permute-start | bytes 589832 | tf_op jit(solution)/shard_map/ppermute | solution.py:22
  28.9 7.0 %collective-permute-start.1 = (bf16[64,2048]{1,0:T(8,128)(2,1)S(1)}, bf16[64,2048]{1,0:T(8,128)(2,1)S(1)}, u32[]{:S(2)}, u32[]{:S(2)}) collective-permute-start(bf16[64,2048]{1,0:T(8,128)(2,1)S(1)} %pick.1), channel_id=1, source_target_pairs={{0,16},{8,24},{16,0},{24,8},{1,17},{9,25},{17,1},{25,9},{2,18},{10... | collective-permute-start | bytes 786440 | tf_op jit(solution)/shard_map/ppermute | solution.py:22
  35.0 6.4 %collective-permute-start.8 = (bf16[64,2048]{1,0:T(8,128)(2,1)S(1)}, bf16[64,2048]{1,0:T(8,128)(2,1)S(1)}, u32[]{:S(2)}, u32[]{:S(2)}) collective-permute-start(bf16[64,2048]{1,0:T(8,128)(2,1)S(1)} %collective-permute-done.7.vm_ref), channel_id=1, source_target_pairs={{0,16},{8,24},{16,0},{24,8},{1,17},{9,25},{17,1},{25,9},{2,18},{10... | collective-permute-start | bytes 786440 | tf_op jit(solution)/shard_map/ppermute | solution.py:22
  35.7 5.7 %copy-start.5 = (s32[16]{0:T(128)S(1)}, s32[16]{0:T(128)}, u32[]{:S(2)}) copy-start(s32[16]{0:T(128)} %coarse_ref.3) | copy-start | bytes 196
  35.8 4.8 %collective-permute-start.10 = (bf16[32,2048]{1,0:T(8,128)(2,1)S(1)}, bf16[32,2048]{1,0:T(8,128)(2,1)S(1)}, u32[]{:S(2)}, u32[]{:S(2)}) collective-permute-start(bf16[32,2048]{1,0:T(8,128)(2,1)S(1)} %constant_dynamic-update-slice_fusion.mine_ref), channel_id=1, source_target_pairs={{0,1},{1,0},{2,3},{3,2},{4,5},{5,4},{6,7},{7,6},{8,9},{9,8},{10,11... | collective-permute-start | bytes 393224 | tf_op jit(solution)/shard_map/ppermute | solution.py:22

commit v10 on v9

--- a/solution.py
+++ b/solution.py
@@ -222,13 +222,34 @@
     return pl.CostEstimate(flops=0, bytes_accessed=0, transcendentals=0)
 
 
+def stack_kernel(*refs):
+    out_ref, row = refs[-1], 0
+    for ref in refs[:-1]:
+        out_ref[row : row + ref.shape[0]] = ref[...]
+        row += ref.shape[0]
+
+
+def stack(*pieces):
+    vmem = pl.BlockSpec(memory_space=pltpu.VMEM)
+    rows = sum(piece.shape[0] for piece in pieces)
+    return pl.pallas_call(
+        stack_kernel,
+        name="stack",
+        out_shape=pltpu.VMEM((rows, pieces[0].shape[1]), pieces[0].dtype),
+        in_specs=[vmem] * len(pieces),
+        out_specs=vmem,
+        compiler_params=pltpu.CompilerParams(vmem_limit_bytes=8 * 1024 * 1024),
+        cost_estimate=cost(),
+    )(*pieces)
+
+
 def gather_upper(value, axis):
     size = lax.axis_size(axis)
     assert size & (size - 1) == 0
     bits = [2**j for j in range(1, size.bit_length() - 1)]
     for step in [bits[j : j + 2] for j in range(0, len(bits), 2)]:
         masks = step + [sum(step)] if len(step) == 2 else step
-        value = jnp.concatenate([value] + [partner(value, axis, mask) for mask in masks], axis=0)
+        value = stack(value, *[partner(value, axis, mask) for mask in masks])
     return value
 
 
@@ -263,7 +284,7 @@
         scratch_shapes=[orders, pltpu.SemaphoreType.DMA((3,))],
     )
     cross = partner(own_members, "inner", 2)
-    near = gather_upper(jnp.concatenate([coarse, partner_elsewhere(coarse, 1)], axis=0), "outer")
+    near = gather_upper(stack(coarse, partner_elsewhere(coarse, 1)), "outer")
     near, own_vm = lax.optimization_barrier((near, own_vm))
     other_vm = partner(own_vm, "inner", 1)
     cross, own_vr = lax.optimization_barrier((cross, own_vr))
@@ -297,7 +318,7 @@
     own_a, weights_a, state_a = first_part(0, q)
     diagonal_v = partner(lax.optimization_barrier((other_vm, state_a))[0], "inner", 2)
     own_b, weights_b, state_b = first_part(half, lax.optimization_barrier((q, state_a, diagonal_k))[0])
-    mine = jnp.concatenate([near, partner_elsewhere(near, 2)], axis=0)
+    mine = stack(near, partner_elsewhere(near, 2))
     extra_sum, share = call(
         extra_kernel,
         "extra",

time: 50.1 us -> 62.7 us (1.25)
  waiting for transfers between devices: 11.5 us -> 21.8 us
  starting transfers between devices: 15.4 us -> 19.9 us
  Pallas kernels: 20.5 us -> 19.4 us
  local copies, waits for them, and re-layouts: 2.38 us -> 1.31 us
    ppermute x11, waiting for transfers between devices: 8.38 us -> 17.6 us  [partner(): return lax.ppermute(value, axis, pairs)]
    ppermute x2, starting transfers between devices: 1.55 us -> 4.24 us  [partner_elsewhere(): return lax.ppermute(value, ('inner', 'outer'), pairs)]
    ppermute x11, starting transfers between devices: 13.8 us -> 15.7 us  [partner(): return lax.ppermute(value, axis, pairs)]
    pallas_call x7, Pallas kernels: 20.5 us -> 19.3 us  [call(): pl.pallas_call(kernel, name=name, compiler_params=params, cost_estimate=c...]
    ppermute x2, waiting for transfers between devices: 3.11 us -> 4.19 us  [partner_elsewhere(): return lax.ppermute(value, ('inner', 'outer'), pairs)]
    unnamed x17 -> x6, local copies, waits for them, and re-layouts: 2.3 us -> 1.31 us
  transfers between devices with their start and end apart: 13 -> 13, of which waited for: 7 -> 6; matrix products, arithmetic and copies ran while one was open for 0% -> 0% of each run, Pallas kernels for 39% -> 29%
where the time goes in v10:
time: 62.7 us; the launch traced here: 62.5 us
  waiting for transfers between devices  21.8 us (35%)
  starting transfers between devices  19.9 us (32%)
  Pallas kernels  19.4 us (31%)
  local copies, waits for them, and re-layouts  1.31 us (2%)
    pallas_call x7, Pallas kernels, call(): pl.pallas_call(kernel, name=name, compiler_params=params, cost_estimate=c...  19.3 us
    ppermute x11, waiting for transfers between devices, partner(): return lax.ppermute(value, axis, pairs)  17.6 us
    ppermute x11, starting transfers between devices, partner(): return lax.ppermute(value, axis, pairs)  15.7 us
    ppermute x2, starting transfers between devices, partner_elsewhere(): return lax.ppermute(value, ('inner', 'outer'), pairs)  4.24 us
    ppermute x2, waiting for transfers between devices, partner_elsewhere(): return lax.ppermute(value, ('inner', 'outer'), pairs)  4.19 us
    unnamed x6, local copies, waits for them, and re-layouts  1.31 us
  transfers between devices with their start and end apart: 13, of which 6 were waited for; matrix products, arithmetic and copies ran while one was open for 0% of the time, Pallas kernels for 29%

profile of v10, /device:TPU:0, one launch (start us, length us, event | category | flops | bytes accessed | tf_op | source)
XLA Modules:
  0.0 62.5 jit_solution(1098755337296281570)
XLA Ops:
  0.0 2.9 %collective-permute-start = (bf16[256,2048]{1,0:T(8,128)(2,1)}, bf16[256,2048]{1,0:T(8,128)(2,1)S(1)}, u32[]{:S(2)}, u32[]{:S(2)}) collective-permute-start(bf16[256,2048]{1,0:T(8,128)(2,1)} %k_hbm.1), channel_id=1, source_target_pairs={{0,8},{8,0},{16,24},{24,16},{1,9},{9,1},{17,25},{25,17},{2,10},{10... | collective-permute-start | bytes 3145736 | tf_op jit(solution)/shard_map/ppermute | solution.py:22
  2.9 0.7 %copy-done = s32[16]{0:T(128)S(1)} copy-done((s32[16]{0:T(128)S(1)}, s32[16]{0:T(128)}, u32[]{:S(2)}) %copy-start) | copy-done | bytes 88
  3.6 0.7 %copy-done.2 = s32[16]{0:T(128)S(1)} copy-done((s32[16]{0:T(128)S(1)}, s32[16]{0:T(128)}, u32[]{:S(2)}) %copy-start.2) | copy-done | bytes 88
  4.3 3.2 %prepare.1 = (bf16[256,2048]{1,0:T(8,128)(2,1)S(1)}, bf16[256,2048]{1,0:T(8,128)(2,1)S(1)}, bf16[256,2048]{1,0:T(8,128)(2,1)S(1)}, bf16[128,2048]{1,0:T(8,128)(2...) custom-call(s32[16]{0:T(128)S(1)} %copy-done, ...), custom_call_target="tpu_custom_call" | custom-call | tf_op jit(solution)/shard_map/prepare/pallas_call | solution.py:268
  7.5 1.6 %collective-permute-start.2 = (bf16[128,2048]{1,0:T(8,128)(2,1)S(1)}, bf16[128,2048]{1,0:T(8,128)(2,1)S(1)}, u32[]{:S(2)}, u32[]{:S(2)}) collective-permute-start(bf16[128,2048]{1,0:T(8,128)(2,1)S(1)} %get-tuple-element.36), channel_id=1, source_target_pairs={{0,16},{8,24},{16,0},{24,8},{1,17},{9,25},{17,1},{25,9},{2,18},{10... | collective-permute-start | bytes 1572872 | tf_op jit(solution)/shard_map/ppermute | solution.py:22
  9.1 11.9 %collective-permute-done.2.cross_ref = bf16[128,2048]{1,0:T(8,128)(2,1)S(1)} collective-permute-done((bf16[128,2048]{1,0:T(8,128)(2,1)S(1)}, bf16[128,2048]{1,0:T(8,128)(2,1)S(1)}, u32[]{:S(2)}, u32[]{:S(2)}) %collective-permute-start.2) | collective-permute-done | bytes 524320 | tf_op jit(solution)/shard_map/ppermute | solution.py:22
  21.0 0.3 collective-permute-start.12
  21.3 2.7 %collective-permute-start.3 = (bf16[2,2048]{1,0:T(2,128)(2,1)S(1)}, bf16[2,2048]{1,0:T(2,128)(2,1)S(1)}, u32[]{:S(2)}, u32[]{:S(2)}) collective-permute-start(bf16[2,2048]{1,0:T(2,128)(2,1)S(1)} %get-tuple-element.40.refs_0_), channel_id=1, source_target_pairs={{0,10},{1,11},{2,8},{3,9},{4,14},{5,15},{6,12},{7,13},{8,2},{9,3},... | collective-permute-start | bytes 24584 | tf_op jit(solution)/shard_map/ppermute | solution.py:32
  24.0 1.9 %collective-permute-done.3.refs_1_ = bf16[2,2048]{1,0:T(2,128)(2,1)S(1)} collective-permute-done((bf16[2,2048]{1,0:T(2,128)(2,1)S(1)}, bf16[2,2048]{1,0:T(2,128)(2,1)S(1)}, u32[]{:S(2)}, u32[]{:S(2)}) %collective-permute-start.3) | collective-permute-done | bytes 8224 | tf_op jit(solution)/shard_map/ppermute | solution.py:32
  25.9 1.8 %collective-permute-start.4 = (bf16[4,2048]{1,0:T(4,128)(2,1)S(1)}, bf16[4,2048]{1,0:T(4,128)(2,1)S(1)}, u32[]{:S(2)}, u32[]{:S(2)}) collective-permute-start(bf16[4,2048]{1,0:T(4,128)(2,1)S(1)} %stack.3.refs_0_), channel_id=1, source_target_pairs={{0,2},{1,3},{2,0},{3,1},{4,6},{5,7},{6,4},{7,5},{8,10},{9,11},{10,... | collective-permute-start | bytes 49160 | tf_op jit(solution)/shard_map/ppermute | solution.py:22
  27.7 2.6 %collective-permute-start.5 = (bf16[4,2048]{1,0:T(4,128)(2,1)S(1)}, bf16[4,2048]{1,0:T(4,128)(2,1)S(1)}, u32[]{:S(2)}, u32[]{:S(2)}) collective-permute-start(bf16[4,2048]{1,0:T(4,128)(2,1)S(1)} %stack.3.refs_0_), channel_id=1, source_target_pairs={{0,4},{1,5},{2,6},{3,7},{4,0},{5,1},{6,2},{7,3},{8,12},{9,13},{10,... | collective-permute-start | bytes 49160 | tf_op jit(solution)/shard_map/ppermute | solution.py:22
  30.3 0.0 collective-permute-start.6
  30.3 0.0 collective-permute-done.4.refs_1_
  30.3 2.0 %collective-permute-done.5.refs_2_ = bf16[4,2048]{1,0:T(4,128)(2,1)S(1)} collective-permute-done((bf16[4,2048]{1,0:T(4,128)(2,1)S(1)}, bf16[4,2048]{1,0:T(4,128)(2,1)S(1)}, u32[]{:S(2)}, u32[]{:S(2)}) %collective-permute-start.5) | collective-permute-done | bytes 16416 | tf_op jit(solution)/shard_map/ppermute | solution.py:22
  32.4 3.5 %collective-permute-done.6.refs_3_ = bf16[4,2048]{1,0:T(4,128)(2,1)S(1)} collective-permute-done((bf16[4,2048]{1,0:T(4,128)(2,1)S(1)}, bf16[4,2048]{1,0:T(4,128)(2,1)S(1)}, u32[]{:S(2)}, u32[]{:S(2)}) %collective-permute-start.6) | collective-permute-done | bytes 16416 | tf_op jit(solution)/shard_map/ppermute | solution.py:22
  35.9 1.5 %collective-permute-start.7 = (bf16[64,2048]{1,0:T(8,128)(2,1)S(1)}, bf16[64,2048]{1,0:T(8,128)(2,1)S(1)}, u32[]{:S(2)}, u32[]{:S(2)}) collective-permute-start(bf16[64,2048]{1,0:T(8,128)(2,1)S(1)} %get-tuple-element.42), channel_id=1, source_target_pairs={{0,8},{8,0},{16,24},{24,16},{1,9},{9,1},{17,25},{25,17},{2,10},{10... | collective-permute-start | bytes 786440 | tf_op jit(solution)/shard_map/ppermute | solution.py:22
  37.4 0.8 %pick.1 = bf16[64,2048]{1,0:T(8,128)(2,1)S(1)} custom-call(s32[16]{0:T(128)S(1)} %copy-done.1, bf16[256,2048]{1,0:T(8,128)(2,1)S(1)} %collective-permute-done.k_ref.kp_ref), custom_call_target="tpu_custom_call" | custom-call | tf_op jit(solution)/shard_map/pick/pallas_call | solution.py:268
  38.3 1.6 %collective-permute-start.1 = (bf16[64,2048]{1,0:T(8,128)(2,1)S(1)}, bf16[64,2048]{1,0:T(8,128)(2,1)S(1)}, u32[]{:S(2)}, u32[]{:S(2)}) collective-permute-start(bf16[64,2048]{1,0:T(8,128)(2,1)S(1)} %pick.1), channel_id=1, source_target_pairs={{0,16},{8,24},{16,0},{24,8},{1,17},{9,25},{17,1},{25,9},{2,18},{10... | collective-permute-start | bytes 786440 | tf_op jit(solution)/shard_map/ppermute | solution.py:22
  39.9 4.6 %first.2 = (f32[256,1024]{1,0:T(8,128)S(1)}, bf16[8,256,256]{2,1,0:T(8,128)(2,1)S(1)}, f32[256,128]{1,0:T(8,128)S(1)}) custom-call(s32[16]{0:T(128)S(1)} %copy-done.1, bf16[256,2048]{1,0:T(8,128)(2,1)S(1)} %get-tuple-element.34.q_ref, bf16[256,2048]{1,0:T(8,128)(2,1)S(1)} %get-tuple-element.30.k_ref, bf16[256,2048]{1,0:T(8,128)(2,1)S(1)} %get-tuple-element.31.v_ref, ...), custom_call_target="tpu_custom_call" | custom-call | tf_op jit(solution)/shard_map/first/pallas_call | solution.py:268
  44.5 0.2 collective-permute-done.7.vm_ref
  44.7 1.8 %collective-permute-start.8 = (bf16[64,2048]{1,0:T(8,128)(2,1)S(1)}, bf16[64,2048]{1,0:T(8,128)(2,1)S(1)}, u32[]{:S(2)}, u32[]{:S(2)}) collective-permute-start(bf16[64,2048]{1,0:T(8,128)(2,1)S(1)} %collective-permute-done.7.vm_ref), channel_id=1, source_target_pairs={{0,16},{8,24},{16,0},{24,8},{1,17},{9,25},{17,1},{25,9},{2,18},{10... | collective-permute-start | bytes 786440 | tf_op jit(solution)/shard_map/ppermute | solution.py:22
  46.5 1.5 %collective-permute-start.9 = (bf16[16,2048]{1,0:T(8,128)(2,1)S(1)}, bf16[16,2048]{1,0:T(8,128)(2,1)S(1)}, u32[]{:S(2)}, u32[]{:S(2)}) collective-permute-start(bf16[16,2048]{1,0:T(8,128)(2,1)S(1)} %stack.4.refs_0_), channel_id=1, source_target_pairs={{0,18},{1,19},{2,16},{3,17},{4,22},{5,23},{6,20},{7,21},{8,26},{9,... | collective-permute-start | bytes 196616 | tf_op jit(solution)/shard_map/ppermute | solution.py:32
  48.0 1.5 %collective-permute-start.11 = (bf16[192,512]{1,0:T(8,128)(2,1)S(1)}, bf16[192,512]{1,0:T(8,128)(2,1)S(1)}, u32[]{:S(2)}, u32[]{:S(2)}) collective-permute-start(bf16[192,512]{1,0:T(8,128)(2,1)S(1)} %get-tuple-element.51), channel_id=1, source_target_pairs={{0,8},{8,0},{16,24},{24,16},{1,9},{9,1},{17,25},{25,17},{2,10},{10... | collective-permute-start | bytes 589832 | tf_op jit(solution)/shard_map/ppermute | solution.py:22
  49.5 2.3 %collective-permute-done.9.refs_1_ = bf16[16,2048]{1,0:T(8,128)(2,1)S(1)} collective-permute-done((bf16[16,2048]{1,0:T(8,128)(2,1)S(1)}, bf16[16,2048]{1,0:T(8,128)(2,1)S(1)}, u32[]{:S(2)}, u32[]{:S(2)}) %collective-permute-start.9) | collective-permute-done | bytes 65568 | tf_op jit(solution)/shard_map/ppermute | solution.py:32
  51.8 0.1 collective-permute-start.10
  51.9 4.6 %first.3 = (f32[256,1024]{1,0:T(8,128)S(1)}, bf16[8,256,256]{2,1,0:T(8,128)(2,1)S(1)}, f32[256,128]{1,0:T(8,128)S(1)}) custom-call(s32[16]{0:T(128)S(1)} %copy-done.1, bf16[256,2048]{1,0:T(8,128)(2,1)S(1)} %get-tuple-element.34.q_ref, bf16[256,2048]{1,0:T(8,128)(2,1)S(1)} %get-tuple-element.30.k_ref, bf16[256,2048]{1,0:T(8,128)(2,1)S(1)} %get-tuple-element.31.v_ref, ...), custom_call_target="tpu_custom_call" | custom-call | tf_op jit(solution)/shard_map/first/pallas_call | solution.py:268
  56.5 0.0 collective-permute-done.8.diagonal_v_ref
  56.6 3.5 %extra.1 = (f32[256,2048]{1,0:T(8,128)S(1)}, f32[256,128]{1,0:T(8,128)S(1)}) custom-call(s32[16]{0:T(128)S(1)} %copy-done.1, s32[16]{0:T(128)S(1)} %copy-done.2, bf16[256,2048]{1,0:T(8,128)(2,1)S(1)} %get-tuple-element.34.q_ref, f32[256,128]{1,0:T(8,128)S(1)} %get-tuple-element.33.state_a_ref, f32[256,128]{1,0:T(8,128)S(1)} %get-tuple-element.35.state_b_ref, ...), custom_call_target="tpu_custom_call" | custom-call | tf_op jit(solution)/shard_map/extra/pallas_call | solution.py:268
  60.1 0.0 collective-permute-done.12.vr_ref
  60.1 1.4 %finish.2.rest_0_ = bf16[256,2048]{1,0:T(8,128)(2,1)} custom-call(f32[256,2048]{1,0:T(8,128)S(1)} %get-tuple-element.45.sum_ref, f32[256,128]{1,0:T(8,128)S(1)} %get-tuple-element.46.share_ref, f32[256,1024]{1,0:T(8,128)S(1)} %get-tuple-element.47.own_a_ref, f32[256,1024]{1,0:T(8,128)S(1)} %get-tuple-element.48.own_b_ref, ...), custom_call_target="tpu_custom_call" | custom-call | tf_op jit(solution)/shard_map/finish/pallas_call | solution.py:268
  61.5 0.0 collective-permute-done.11.vr_ref
  61.5 1.0 %finish.3 = bf16[256,2048]{1,0:T(8,128)(2,1)} custom-call(f32[256,2048]{1,0:T(8,128)S(1)} %get-tuple-element.45.sum_ref, f32[256,128]{1,0:T(8,128)S(1)} %get-tuple-element.46.share_ref, f32[256,1024]{1,0:T(8,128)S(1)} %get-tuple-element.47.own_a_ref, f32[256,1024]{1,0:T(8,128)S(1)} %get-tuple-element.48.own_b_ref, ...), custom_call_target="tpu_custom_call", output_to_operand_aliasing={{}: (8, {})} | custom-call | tf_op jit(solution)/shard_map/finish/pallas_call | solution.py:268
  (10 shorter events, 0.0 us)
Async XLA Ops:
  0.0 37.4 %collective-permute-start = (bf16[256,2048]{1,0:T(8,128)(2,1)}, bf16[256,2048]{1,0:T(8,128)(2,1)S(1)}, u32[]{:S(2)}, u32[]{:S(2)}) collective-permute-start(bf16[256,2048]{1,0:T(8,128)(2,1)} %k_hbm.1), channel_id=1, source_target_pairs={{0,8},{8,0},{16,24},{24,16},{1,9},{9,1},{17,25},{25,17},{2,10},{10... | collective-permute-start | bytes 3145736 | tf_op jit(solution)/shard_map/ppermute | solution.py:22
  2.9 0.7 %copy-start = (s32[16]{0:T(128)S(1)}, s32[16]{0:T(128)}, u32[]{:S(2)}) copy-start(s32[16]{0:T(128)} %middle_ref.9) | copy-start | bytes 196
  3.6 0.7 %copy-start.2 = (s32[16]{0:T(128)S(1)}, s32[16]{0:T(128)}, u32[]{:S(2)}) copy-start(s32[16]{0:T(128)} %coarse_ref.3) | copy-start | bytes 196
  4.3 33.2 %copy-start.1 = (s32[16]{0:T(128)S(1)}, s32[16]{0:T(128)}, u32[]{:S(2)}) copy-start(s32[16]{0:T(128)} %middle_ref.9) | copy-start | bytes 196
  7.5 13.4 %collective-permute-start.2 = (bf16[128,2048]{1,0:T(8,128)(2,1)S(1)}, bf16[128,2048]{1,0:T(8,128)(2,1)S(1)}, u32[]{:S(2)}, u32[]{:S(2)}) collective-permute-start(bf16[128,2048]{1,0:T(8,128)(2,1)S(1)} %get-tuple-element.36), channel_id=1, source_target_pairs={{0,16},{8,24},{16,0},{24,8},{1,17},{9,25},{17,1},{25,9},{2,18},{10... | collective-permute-start | bytes 1572872 | tf_op jit(solution)/shard_map/ppermute | solution.py:22
  21.0 39.1 %collective-permute-start.12 = (bf16[192,1536]{1,0:T(8,128)(2,1)S(1)}, bf16[192,1536]{1,0:T(8,128)(2,1)S(1)}, u32[]{:S(2)}, u32[]{:S(2)}) collective-permute-start(bf16[192,1536]{1,0:T(8,128)(2,1)S(1)} %get-tuple-element.52), channel_id=1, source_target_pairs={{0,8},{8,0},{16,24},{24,16},{1,9},{9,1},{17,25},{25,17},{2,10},{10... | collective-permute-start | bytes 1769480 | tf_op jit(solution)/shard_map/ppermute | solution.py:22
  21.3 4.7 %collective-permute-start.3 = (bf16[2,2048]{1,0:T(2,128)(2,1)S(1)}, bf16[2,2048]{1,0:T(2,128)(2,1)S(1)}, u32[]{:S(2)}, u32[]{:S(2)}) collective-permute-start(bf16[2,2048]{1,0:T(2,128)(2,1)S(1)} %get-tuple-element.40.refs_0_), channel_id=1, source_target_pairs={{0,10},{1,11},{2,8},{3,9},{4,14},{5,15},{6,12},{7,13},{8,2},{9,3},... | collective-permute-start | bytes 24584 | tf_op jit(solution)/shard_map/ppermute | solution.py:32
  25.9 4.4 %collective-permute-start.4 = (bf16[4,2048]{1,0:T(4,128)(2,1)S(1)}, bf16[4,2048]{1,0:T(4,128)(2,1)S(1)}, u32[]{:S(2)}, u32[]{:S(2)}) collective-permute-start(bf16[4,2048]{1,0:T(4,128)(2,1)S(1)} %stack.3.refs_0_), channel_id=1, source_target_pairs={{0,2},{1,3},{2,0},{3,1},{4,6},{5,7},{6,4},{7,5},{8,10},{9,11},{10,... | collective-permute-start | bytes 49160 | tf_op jit(solution)/shard_map/ppermute | solution.py:22
  27.7 4.6 %collective-permute-start.5 = (bf16[4,2048]{1,0:T(4,128)(2,1)S(1)}, bf16[4,2048]{1,0:T(4,128)(2,1)S(1)}, u32[]{:S(2)}, u32[]{:S(2)}) collective-permute-start(bf16[4,2048]{1,0:T(4,128)(2,1)S(1)} %stack.3.refs_0_), channel_id=1, source_target_pairs={{0,4},{1,5},{2,6},{3,7},{4,0},{5,1},{6,2},{7,3},{8,12},{9,13},{10,... | collective-permute-start | bytes 49160 | tf_op jit(solution)/shard_map/ppermute | solution.py:22
  30.3 5.5 %collective-permute-start.6 = (bf16[4,2048]{1,0:T(4,128)(2,1)S(1)}, bf16[4,2048]{1,0:T(4,128)(2,1)S(1)}, u32[]{:S(2)}, u32[]{:S(2)}) collective-permute-start(bf16[4,2048]{1,0:T(4,128)(2,1)S(1)} %stack.3.refs_0_), channel_id=1, source_target_pairs={{0,6},{1,7},{2,4},{3,5},{4,2},{5,3},{6,0},{7,1},{8,14},{9,15},{10,... | collective-permute-start | bytes 49160 | tf_op jit(solution)/shard_map/ppermute | solution.py:22
  35.9 8.9 %collective-permute-start.7 = (bf16[64,2048]{1,0:T(8,128)(2,1)S(1)}, bf16[64,2048]{1,0:T(8,128)(2,1)S(1)}, u32[]{:S(2)}, u32[]{:S(2)}) collective-permute-start(bf16[64,2048]{1,0:T(8,128)(2,1)S(1)} %get-tuple-element.42), channel_id=1, source_target_pairs={{0,8},{8,0},{16,24},{24,16},{1,9},{9,1},{17,25},{25,17},{2,10},{10... | collective-permute-start | bytes 786440 | tf_op jit(solution)/shard_map/ppermute | solution.py:22
  38.3 13.6 %collective-permute-start.1 = (bf16[64,2048]{1,0:T(8,128)(2,1)S(1)}, bf16[64,2048]{1,0:T(8,128)(2,1)S(1)}, u32[]{:S(2)}, u32[]{:S(2)}) collective-permute-start(bf16[64,2048]{1,0:T(8,128)(2,1)S(1)} %pick.1), channel_id=1, source_target_pairs={{0,16},{8,24},{16,0},{24,8},{1,17},{9,25},{17,1},{25,9},{2,18},{10... | collective-permute-start | bytes 786440 | tf_op jit(solution)/shard_map/ppermute | solution.py:22
  44.7 11.8 %collective-permute-start.8 = (bf16[64,2048]{1,0:T(8,128)(2,1)S(1)}, bf16[64,2048]{1,0:T(8,128)(2,1)S(1)}, u32[]{:S(2)}, u32[]{:S(2)}) collective-permute-start(bf16[64,2048]{1,0:T(8,128)(2,1)S(1)} %collective-permute-done.7.vm_ref), channel_id=1, source_target_pairs={{0,16},{8,24},{16,0},{24,8},{1,17},{9,25},{17,1},{25,9},{2,18},{10... | collective-permute-start | bytes 786440 | tf_op jit(solution)/shard_map/ppermute | solution.py:22
  46.5 5.3 %collective-permute-start.9 = (bf16[16,2048]{1,0:T(8,128)(2,1)S(1)}, bf16[16,2048]{1,0:T(8,128)(2,1)S(1)}, u32[]{:S(2)}, u32[]{:S(2)}) collective-permute-start(bf16[16,2048]{1,0:T(8,128)(2,1)S(1)} %stack.4.refs_0_), channel_id=1, source_target_pairs={{0,18},{1,19},{2,16},{3,17},{4,22},{5,23},{6,20},{7,21},{8,26},{9,... | collective-permute-start | bytes 196616 | tf_op jit(solution)/shard_map/ppermute | solution.py:32
  48.0 13.5 %collective-permute-start.11 = (bf16[192,512]{1,0:T(8,128)(2,1)S(1)}, bf16[192,512]{1,0:T(8,128)(2,1)S(1)}, u32[]{:S(2)}, u32[]{:S(2)}) collective-permute-start(bf16[192,512]{1,0:T(8,128)(2,1)S(1)} %get-tuple-element.51), channel_id=1, source_target_pairs={{0,8},{8,0},{16,24},{24,16},{1,9},{9,1},{17,25},{25,17},{2,10},{10... | collective-permute-start | bytes 589832 | tf_op jit(solution)/shard_map/ppermute | solution.py:22
  51.8 4.7 %collective-permute-start.10 = (bf16[32,2048]{1,0:T(8,128)(2,1)S(1)}, bf16[32,2048]{1,0:T(8,128)(2,1)S(1)}, u32[]{:S(2)}, u32[]{:S(2)}) collective-permute-start(bf16[32,2048]{1,0:T(8,128)(2,1)S(1)} %stack.5.mine_ref), channel_id=1, source_target_pairs={{0,1},{1,0},{2,3},{3,2},{4,5},{5,4},{6,7},{7,6},{8,9},{9,8},{10,11... | collective-permute-start | bytes 393224 | tf_op jit(solution)/shard_map/ppermute | solution.py:22

commit v11 on v10

--- a/solution.py
+++ b/solution.py
@@ -318,7 +318,7 @@
     own_a, weights_a, state_a = first_part(0, q)
     diagonal_v = partner(lax.optimization_barrier((other_vm, state_a))[0], "inner", 2)
     own_b, weights_b, state_b = first_part(half, lax.optimization_barrier((q, state_a, diagonal_k))[0])
-    mine = stack(near, partner_elsewhere(near, 2))
+    mine = jnp.concatenate([near, partner_elsewhere(near, 2)], axis=0)
     extra_sum, share = call(
         extra_kernel,
         "extra",

time: 62.7 us -> 50.1 us (0.80)
  waiting for transfers between devices: 21.8 us -> 13.7 us
  starting transfers between devices: 19.9 us -> 15.5 us
    ppermute x11, waiting for transfers between devices: 17.6 us -> 10.6 us  [partner(): return lax.ppermute(value, axis, pairs)]
    ppermute x2, starting transfers between devices: 4.24 us -> 1.55 us  [partner_elsewhere(): return lax.ppermute(value, ('inner', 'outer'), pairs)]
    ppermute x11, starting transfers between devices: 15.7 us -> 13.9 us  [partner(): return lax.ppermute(value, axis, pairs)]
    ppermute x2, waiting for transfers between devices: 4.19 us -> 3.11 us  [partner_elsewhere(): return lax.ppermute(value, ('inner', 'outer'), pairs)]
    unnamed x6 -> x9, local copies, waits for them, and re-layouts: 1.31 us -> 1.32 us
  transfers between devices with their start and end apart: 13 -> 13, of which waited for: 6 -> 8; matrix products, arithmetic and copies ran while one was open for 0% -> 0% of each run, Pallas kernels for 29% -> 37%
where the time goes in v11:
time: 50.1 us; the launch traced here: 49.9 us
  Pallas kernels  19.3 us (39%)
  starting transfers between devices  15.5 us (31%)
  waiting for transfers between devices  13.7 us (27%)
  local copies, waits for them, and re-layouts  1.33 us (3%)
    pallas_call x7, Pallas kernels, call(): pl.pallas_call(kernel, name=name, compiler_params=params, cost_estimate=c...  19.3 us
    ppermute x11, starting transfers between devices, partner(): return lax.ppermute(value, axis, pairs)  13.9 us
    ppermute x11, waiting for transfers between devices, partner(): return lax.ppermute(value, axis, pairs)  10.6 us
    ppermute x2, waiting for transfers between devices, partner_elsewhere(): return lax.ppermute(value, ('inner', 'outer'), pairs)  3.11 us
    ppermute x2, starting transfers between devices, partner_elsewhere(): return lax.ppermute(value, ('inner', 'outer'), pairs)  1.55 us
    unnamed x9, local copies, waits for them, and re-layouts  1.32 us
  transfers between devices with their start and end apart: 13, of which 8 were waited for; matrix products, arithmetic and copies ran while one was open for 0% of the time, Pallas kernels for 37%

profile of v11, /device:TPU:0, one launch (start us, length us, event | category | flops | bytes accessed | tf_op | source)
XLA Modules:
  0.0 49.9 jit_solution(15043118416447059909)
XLA Ops:
  0.0 2.9 %collective-permute-start = (bf16[256,2048]{1,0:T(8,128)(2,1)}, bf16[256,2048]{1,0:T(8,128)(2,1)S(1)}, u32[]{:S(2)}, u32[]{:S(2)}) collective-permute-start(bf16[256,2048]{1,0:T(8,128)(2,1)} %k_hbm.1), channel_id=1, source_target_pairs={{0,8},{8,0},{16,24},{24,16},{1,9},{9,1},{17,25},{25,17},{2,10},{10... | collective-permute-start | bytes 3145736 | tf_op jit(solution)/shard_map/ppermute | solution.py:22
  2.9 0.7 %copy-done = s32[16]{0:T(128)S(1)} copy-done((s32[16]{0:T(128)S(1)}, s32[16]{0:T(128)}, u32[]{:S(2)}) %copy-start) | copy-done | bytes 88
  3.6 0.7 %copy-done.2 = s32[16]{0:T(128)S(1)} copy-done((s32[16]{0:T(128)S(1)}, s32[16]{0:T(128)}, u32[]{:S(2)}) %copy-start.2) | copy-done | bytes 88
  4.3 3.2 %prepare.1 = (bf16[256,2048]{1,0:T(8,128)(2,1)S(1)}, bf16[256,2048]{1,0:T(8,128)(2,1)S(1)}, bf16[256,2048]{1,0:T(8,128)(2,1)S(1)}, bf16[128,2048]{1,0:T(8,128)(2...) custom-call(s32[16]{0:T(128)S(1)} %copy-done, ...), custom_call_target="tpu_custom_call" | custom-call | tf_op jit(solution)/shard_map/prepare/pallas_call | solution.py:268
  7.5 1.6 %collective-permute-start.2 = (bf16[128,2048]{1,0:T(8,128)(2,1)S(1)}, bf16[128,2048]{1,0:T(8,128)(2,1)S(1)}, u32[]{:S(2)}, u32[]{:S(2)}) collective-permute-start(bf16[128,2048]{1,0:T(8,128)(2,1)S(1)} %get-tuple-element.36), channel_id=1, source_target_pairs={{0,16},{8,24},{16,0},{24,8},{1,17},{9,25},{17,1},{25,9},{2,18},{10... | collective-permute-start | bytes 1572872 | tf_op jit(solution)/shard_map/ppermute | solution.py:22
  9.1 1.5 %collective-permute-start.3 = (bf16[2,2048]{1,0:T(2,128)(2,1)S(1)}, bf16[2,2048]{1,0:T(2,128)(2,1)S(1)}, u32[]{:S(2)}, u32[]{:S(2)}) collective-permute-start(bf16[2,2048]{1,0:T(2,128)(2,1)S(1)} %get-tuple-element.40.refs_0_), channel_id=1, source_target_pairs={{0,10},{1,11},{2,8},{3,9},{4,14},{5,15},{6,12},{7,13},{8,2},{9,3},... | collective-permute-start | bytes 24584 | tf_op jit(solution)/shard_map/ppermute | solution.py:32
  10.6 3.1 %collective-permute-done.3.refs_1_ = bf16[2,2048]{1,0:T(2,128)(2,1)S(1)} collective-permute-done((bf16[2,2048]{1,0:T(2,128)(2,1)S(1)}, bf16[2,2048]{1,0:T(2,128)(2,1)S(1)}, u32[]{:S(2)}, u32[]{:S(2)}) %collective-permute-start.3) | collective-permute-done | bytes 8224 | tf_op jit(solution)/shard_map/ppermute | solution.py:32
  13.8 1.6 %collective-permute-start.4 = (bf16[4,2048]{1,0:T(4,128)(2,1)S(1)}, bf16[4,2048]{1,0:T(4,128)(2,1)S(1)}, u32[]{:S(2)}, u32[]{:S(2)}) collective-permute-start(bf16[4,2048]{1,0:T(4,128)(2,1)S(1)} %stack.2.refs_0_), channel_id=1, source_target_pairs={{0,2},{1,3},{2,0},{3,1},{4,6},{5,7},{6,4},{7,5},{8,10},{9,11},{10,... | collective-permute-start | bytes 49160 | tf_op jit(solution)/shard_map/ppermute | solution.py:22
  15.3 2.6 %collective-permute-start.5 = (bf16[4,2048]{1,0:T(4,128)(2,1)S(1)}, bf16[4,2048]{1,0:T(4,128)(2,1)S(1)}, u32[]{:S(2)}, u32[]{:S(2)}) collective-permute-start(bf16[4,2048]{1,0:T(4,128)(2,1)S(1)} %stack.2.refs_0_), channel_id=1, source_target_pairs={{0,4},{1,5},{2,6},{3,7},{4,0},{5,1},{6,2},{7,3},{8,12},{9,13},{10,... | collective-permute-start | bytes 49160 | tf_op jit(solution)/shard_map/ppermute | solution.py:22
  17.9 0.2 collective-permute-start.6
  18.1 0.0 collective-permute-done.4.refs_1_
  18.2 2.1 %collective-permute-done.5.refs_2_ = bf16[4,2048]{1,0:T(4,128)(2,1)S(1)} collective-permute-done((bf16[4,2048]{1,0:T(4,128)(2,1)S(1)}, bf16[4,2048]{1,0:T(4,128)(2,1)S(1)}, u32[]{:S(2)}, u32[]{:S(2)}) %collective-permute-start.5) | collective-permute-done | bytes 16416 | tf_op jit(solution)/shard_map/ppermute | solution.py:22
  20.2 3.3 %collective-permute-done.6.refs_3_ = bf16[4,2048]{1,0:T(4,128)(2,1)S(1)} collective-permute-done((bf16[4,2048]{1,0:T(4,128)(2,1)S(1)}, bf16[4,2048]{1,0:T(4,128)(2,1)S(1)}, u32[]{:S(2)}, u32[]{:S(2)}) %collective-permute-start.6) | collective-permute-done | bytes 16416 | tf_op jit(solution)/shard_map/ppermute | solution.py:22
  23.5 0.6 %collective-permute-start.7 = (bf16[64,2048]{1,0:T(8,128)(2,1)S(1)}, bf16[64,2048]{1,0:T(8,128)(2,1)S(1)}, u32[]{:S(2)}, u32[]{:S(2)}) collective-permute-start(bf16[64,2048]{1,0:T(8,128)(2,1)S(1)} %get-tuple-element.42), channel_id=1, source_target_pairs={{0,8},{8,0},{16,24},{24,16},{1,9},{9,1},{17,25},{25,17},{2,10},{10... | collective-permute-start | bytes 786440 | tf_op jit(solution)/shard_map/ppermute | solution.py:22
  24.1 0.0 collective-permute-done.2.cross_ref
  24.1 1.5 %collective-permute-start.12 = (bf16[192,1536]{1,0:T(8,128)(2,1)S(1)}, bf16[192,1536]{1,0:T(8,128)(2,1)S(1)}, u32[]{:S(2)}, u32[]{:S(2)}) collective-permute-start(bf16[192,1536]{1,0:T(8,128)(2,1)S(1)} %get-tuple-element.52), channel_id=1, source_target_pairs={{0,8},{8,0},{16,24},{24,16},{1,9},{9,1},{17,25},{25,17},{2,10},{10... | collective-permute-start | bytes 1769480 | tf_op jit(solution)/shard_map/ppermute | solution.py:22
  25.6 0.6 %collective-permute-start.11 = (bf16[192,512]{1,0:T(8,128)(2,1)S(1)}, bf16[192,512]{1,0:T(8,128)(2,1)S(1)}, u32[]{:S(2)}, u32[]{:S(2)}) collective-permute-start(bf16[192,512]{1,0:T(8,128)(2,1)S(1)} %get-tuple-element.51), channel_id=1, source_target_pairs={{0,8},{8,0},{16,24},{24,16},{1,9},{9,1},{17,25},{25,17},{2,10},{10... | collective-permute-start | bytes 589832 | tf_op jit(solution)/shard_map/ppermute | solution.py:22
  26.2 1.1 %collective-permute-done.k_ref.kp_ref = bf16[256,2048]{1,0:T(8,128)(2,1)S(1)} collective-permute-done((bf16[256,2048]{1,0:T(8,128)(2,1)}, bf16[256,2048]{1,0:T(8,128)(2,1)S(1)}, u32[]{:S(2)}, u32[]{:S(2)}) %collective-permute-start) | collective-permute-done | bytes 1048608 | tf_op jit(solution)/shard_map/ppermute | solution.py:22
  27.3 0.8 %pick.1 = bf16[64,2048]{1,0:T(8,128)(2,1)S(1)} custom-call(s32[16]{0:T(128)S(1)} %copy-done.1, bf16[256,2048]{1,0:T(8,128)(2,1)S(1)} %collective-permute-done.k_ref.kp_ref), custom_call_target="tpu_custom_call" | custom-call | tf_op jit(solution)/shard_map/pick/pallas_call | solution.py:268
  28.2 2.2 %collective-permute-start.1 = (bf16[64,2048]{1,0:T(8,128)(2,1)S(1)}, bf16[64,2048]{1,0:T(8,128)(2,1)S(1)}, u32[]{:S(2)}, u32[]{:S(2)}) collective-permute-start(bf16[64,2048]{1,0:T(8,128)(2,1)S(1)} %pick.1), channel_id=1, source_target_pairs={{0,16},{8,24},{16,0},{24,8},{1,17},{9,25},{17,1},{25,9},{2,18},{10... | collective-permute-start | bytes 786440 | tf_op jit(solution)/shard_map/ppermute | solution.py:22
  30.3 4.6 %first.2 = (f32[256,1024]{1,0:T(8,128)S(1)}, bf16[8,256,256]{2,1,0:T(8,128)(2,1)S(1)}, f32[256,128]{1,0:T(8,128)S(1)}) custom-call(s32[16]{0:T(128)S(1)} %copy-done.1, bf16[256,2048]{1,0:T(8,128)(2,1)S(1)} %get-tuple-element.34.q_ref, bf16[256,2048]{1,0:T(8,128)(2,1)S(1)} %get-tuple-element.30.k_ref, bf16[256,2048]{1,0:T(8,128)(2,1)S(1)} %get-tuple-element.31.v_ref, ...), custom_call_target="tpu_custom_call" | custom-call | tf_op jit(solution)/shard_map/first/pallas_call | solution.py:268
  35.0 0.1 collective-permute-start.8
  35.1 0.0 copy-start.3
  35.1 0.1 collective-permute-start.10
  35.2 0.8 %collective-permute-done.1.diagonal_k_ref = bf16[64,2048]{1,0:T(8,128)(2,1)S(1)} collective-permute-done((bf16[64,2048]{1,0:T(8,128)(2,1)S(1)}, bf16[64,2048]{1,0:T(8,128)(2,1)S(1)}, u32[]{:S(2)}, u32[]{:S(2)}) %collective-permute-start.1) | collective-permute-done | bytes 262176 | tf_op jit(solution)/shard_map/ppermute | solution.py:22
  35.9 4.6 %first.3 = (f32[256,1024]{1,0:T(8,128)S(1)}, bf16[8,256,256]{2,1,0:T(8,128)(2,1)S(1)}, f32[256,128]{1,0:T(8,128)S(1)}) custom-call(s32[16]{0:T(128)S(1)} %copy-done.1, bf16[256,2048]{1,0:T(8,128)(2,1)S(1)} %get-tuple-element.34.q_ref, bf16[256,2048]{1,0:T(8,128)(2,1)S(1)} %get-tuple-element.30.k_ref, bf16[256,2048]{1,0:T(8,128)(2,1)S(1)} %get-tuple-element.31.v_ref, ...), custom_call_target="tpu_custom_call" | custom-call | tf_op jit(solution)/shard_map/first/pallas_call | solution.py:268
  40.6 0.8 %collective-permute-done.8.diagonal_v_ref = bf16[64,2048]{1,0:T(8,128)(2,1)S(1)} collective-permute-done((bf16[64,2048]{1,0:T(8,128)(2,1)S(1)}, bf16[64,2048]{1,0:T(8,128)(2,1)S(1)}, u32[]{:S(2)}, u32[]{:S(2)}) %collective-permute-start.8) | collective-permute-done | bytes 262176 | tf_op jit(solution)/shard_map/ppermute | solution.py:22
  41.4 3.5 %extra.1 = (f32[256,2048]{1,0:T(8,128)S(1)}, f32[256,128]{1,0:T(8,128)S(1)}) custom-call(s32[16]{0:T(128)S(1)} %copy-done.1, s32[16]{0:T(128)S(1)} %copy-done.3, bf16[256,2048]{1,0:T(8,128)(2,1)S(1)} %get-tuple-element.34.q_ref, f32[256,128]{1,0:T(8,128)S(1)} %get-tuple-element.33.state_a_ref, f32[256,128]{1,0:T(8,128)S(1)} %get-tuple-element.35.state_b_ref, ...), custom_call_target="tpu_custom_call" | custom-call | tf_op jit(solution)/shard_map/extra/pallas_call | solution.py:268
  44.9 0.6 %collective-permute-done.12.vr_ref = bf16[192,1536]{1,0:T(8,128)(2,1)S(1)} collective-permute-done((bf16[192,1536]{1,0:T(8,128)(2,1)S(1)}, bf16[192,1536]{1,0:T(8,128)(2,1)S(1)}, u32[]{:S(2)}, u32[]{:S(2)}) %collective-permute-start.12) | collective-permute-done | bytes 589856 | tf_op jit(solution)/shard_map/ppermute | solution.py:22
  45.6 1.4 %finish.2.rest_0_ = bf16[256,2048]{1,0:T(8,128)(2,1)} custom-call(f32[256,2048]{1,0:T(8,128)S(1)} %get-tuple-element.45.sum_ref, f32[256,128]{1,0:T(8,128)S(1)} %get-tuple-element.46.share_ref, f32[256,1024]{1,0:T(8,128)S(1)} %get-tuple-element.47.own_a_ref, f32[256,1024]{1,0:T(8,128)S(1)} %get-tuple-element.48.own_b_ref, ...), custom_call_target="tpu_custom_call" | custom-call | tf_op jit(solution)/shard_map/finish/pallas_call | solution.py:268
  47.0 2.0 %collective-permute-done.11.vr_ref = bf16[192,512]{1,0:T(8,128)(2,1)S(1)} collective-permute-done((bf16[192,512]{1,0:T(8,128)(2,1)S(1)}, bf16[192,512]{1,0:T(8,128)(2,1)S(1)}, u32[]{:S(2)}, u32[]{:S(2)}) %collective-permute-start.11) | collective-permute-done | bytes 196640 | tf_op jit(solution)/shard_map/ppermute | solution.py:22
  49.0 1.0 %finish.3 = bf16[256,2048]{1,0:T(8,128)(2,1)} custom-call(f32[256,2048]{1,0:T(8,128)S(1)} %get-tuple-element.45.sum_ref, f32[256,128]{1,0:T(8,128)S(1)} %get-tuple-element.46.share_ref, f32[256,1024]{1,0:T(8,128)S(1)} %get-tuple-element.47.own_a_ref, f32[256,1024]{1,0:T(8,128)S(1)} %get-tuple-element.48.own_b_ref, ...), custom_call_target="tpu_custom_call", output_to_operand_aliasing={{}: (8, {})} | custom-call | tf_op jit(solution)/shard_map/finish/pallas_call | solution.py:268
  (13 shorter events, 0.1 us)
Async XLA Ops:
  0.0 27.3 %collective-permute-start = (bf16[256,2048]{1,0:T(8,128)(2,1)}, bf16[256,2048]{1,0:T(8,128)(2,1)S(1)}, u32[]{:S(2)}, u32[]{:S(2)}) collective-permute-start(bf16[256,2048]{1,0:T(8,128)(2,1)} %k_hbm.1), channel_id=1, source_target_pairs={{0,8},{8,0},{16,24},{24,16},{1,9},{9,1},{17,25},{25,17},{2,10},{10... | collective-permute-start | bytes 3145736 | tf_op jit(solution)/shard_map/ppermute | solution.py:22
  2.9 0.7 %copy-start = (s32[16]{0:T(128)S(1)}, s32[16]{0:T(128)}, u32[]{:S(2)}) copy-start(s32[16]{0:T(128)} %middle_ref.9) | copy-start | bytes 196
  3.6 0.7 %copy-start.2 = (s32[16]{0:T(128)S(1)}, s32[16]{0:T(128)}, u32[]{:S(2)}) copy-start(s32[16]{0:T(128)} %coarse_ref.3) | copy-start | bytes 196
  4.3 23.1 %copy-start.1 = (s32[16]{0:T(128)S(1)}, s32[16]{0:T(128)}, u32[]{:S(2)}) copy-start(s32[16]{0:T(128)} %middle_ref.9) | copy-start | bytes 196
  7.5 16.6 %collective-permute-start.2 = (bf16[128,2048]{1,0:T(8,128)(2,1)S(1)}, bf16[128,2048]{1,0:T(8,128)(2,1)S(1)}, u32[]{:S(2)}, u32[]{:S(2)}) collective-permute-start(bf16[128,2048]{1,0:T(8,128)(2,1)S(1)} %get-tuple-element.36), channel_id=1, source_target_pairs={{0,16},{8,24},{16,0},{24,8},{1,17},{9,25},{17,1},{25,9},{2,18},{10... | collective-permute-start | bytes 1572872 | tf_op jit(solution)/shard_map/ppermute | solution.py:22
  9.1 4.7 %collective-permute-start.3 = (bf16[2,2048]{1,0:T(2,128)(2,1)S(1)}, bf16[2,2048]{1,0:T(2,128)(2,1)S(1)}, u32[]{:S(2)}, u32[]{:S(2)}) collective-permute-start(bf16[2,2048]{1,0:T(2,128)(2,1)S(1)} %get-tuple-element.40.refs_0_), channel_id=1, source_target_pairs={{0,10},{1,11},{2,8},{3,9},{4,14},{5,15},{6,12},{7,13},{8,2},{9,3},... | collective-permute-start | bytes 24584 | tf_op jit(solution)/shard_map/ppermute | solution.py:32
  13.8 4.4 %collective-permute-start.4 = (bf16[4,2048]{1,0:T(4,128)(2,1)S(1)}, bf16[4,2048]{1,0:T(4,128)(2,1)S(1)}, u32[]{:S(2)}, u32[]{:S(2)}) collective-permute-start(bf16[4,2048]{1,0:T(4,128)(2,1)S(1)} %stack.2.refs_0_), channel_id=1, source_target_pairs={{0,2},{1,3},{2,0},{3,1},{4,6},{5,7},{6,4},{7,5},{8,10},{9,11},{10,... | collective-permute-start | bytes 49160 | tf_op jit(solution)/shard_map/ppermute | solution.py:22
  15.3 4.9 %collective-permute-start.5 = (bf16[4,2048]{1,0:T(4,128)(2,1)S(1)}, bf16[4,2048]{1,0:T(4,128)(2,1)S(1)}, u32[]{:S(2)}, u32[]{:S(2)}) collective-permute-start(bf16[4,2048]{1,0:T(4,128)(2,1)S(1)} %stack.2.refs_0_), channel_id=1, source_target_pairs={{0,4},{1,5},{2,6},{3,7},{4,0},{5,1},{6,2},{7,3},{8,12},{9,13},{10,... | collective-permute-start | bytes 49160 | tf_op jit(solution)/shard_map/ppermute | solution.py:22
  17.9 5.5 %collective-permute-start.6 = (bf16[4,2048]{1,0:T(4,128)(2,1)S(1)}, bf16[4,2048]{1,0:T(4,128)(2,1)S(1)}, u32[]{:S(2)}, u32[]{:S(2)}) collective-permute-start(bf16[4,2048]{1,0:T(4,128)(2,1)S(1)} %stack.2.refs_0_), channel_id=1, source_target_pairs={{0,6},{1,7},{2,4},{3,5},{4,2},{5,3},{6,0},{7,1},{8,14},{9,15},{10,... | collective-permute-start | bytes 49160 | tf_op jit(solution)/shard_map/ppermute | solution.py:22
  23.5 11.5 %collective-permute-start.7 = (bf16[64,2048]{1,0:T(8,128)(2,1)S(1)}, bf16[64,2048]{1,0:T(8,128)(2,1)S(1)}, u32[]{:S(2)}, u32[]{:S(2)}) collective-permute-start(bf16[64,2048]{1,0:T(8,128)(2,1)S(1)} %get-tuple-element.42), channel_id=1, source_target_pairs={{0,8},{8,0},{16,24},{24,16},{1,9},{9,1},{17,25},{25,17},{2,10},{10... | collective-permute-start | bytes 786440 | tf_op jit(solution)/shard_map/ppermute | solution.py:22
  24.1 21.5 %collective-permute-start.12 = (bf16[192,1536]{1,0:T(8,128)(2,1)S(1)}, bf16[192,1536]{1,0:T(8,128)(2,1)S(1)}, u32[]{:S(2)}, u32[]{:S(2)}) collective-permute-start(bf16[192,1536]{1,0:T(8,128)(2,1)S(1)} %get-tuple-element.52), channel_id=1, source_target_pairs={{0,8},{8,0},{16,24},{24,16},{1,9},{9,1},{17,25},{25,17},{2,10},{10... | collective-permute-start | bytes 1769480 | tf_op jit(solution)/shard_map/ppermute | solution.py:22
  25.6 9.5 %collective-permute-start.9 = (bf16[16,2048]{1,0:T(8,128)(2,1)S(1)}, bf16[16,2048]{1,0:T(8,128)(2,1)S(1)}, u32[]{:S(2)}, u32[]{:S(2)}) collective-permute-start(bf16[16,2048]{1,0:T(8,128)(2,1)S(1)} %stack.3), channel_id=1, source_target_pairs={{0,18},{1,19},{2,16},{3,17},{4,22},{5,23},{6,20},{7,21},{8,26},{9,... | collective-permute-start | bytes 196616 | tf_op jit(solution)/shard_map/ppermute | solution.py:32
  25.6 23.4 %collective-permute-start.11 = (bf16[192,512]{1,0:T(8,128)(2,1)S(1)}, bf16[192,512]{1,0:T(8,128)(2,1)S(1)}, u32[]{:S(2)}, u32[]{:S(2)}) collective-permute-start(bf16[192,512]{1,0:T(8,128)(2,1)S(1)} %get-tuple-element.51), channel_id=1, source_target_pairs={{0,8},{8,0},{16,24},{24,16},{1,9},{9,1},{17,25},{25,17},{2,10},{10... | collective-permute-start | bytes 589832 | tf_op jit(solution)/shard_map/ppermute | solution.py:22
  28.2 7.8 %collective-permute-start.1 = (bf16[64,2048]{1,0:T(8,128)(2,1)S(1)}, bf16[64,2048]{1,0:T(8,128)(2,1)S(1)}, u32[]{:S(2)}, u32[]{:S(2)}) collective-permute-start(bf16[64,2048]{1,0:T(8,128)(2,1)S(1)} %pick.1), channel_id=1, source_target_pairs={{0,16},{8,24},{16,0},{24,8},{1,17},{9,25},{17,1},{25,9},{2,18},{10... | collective-permute-start | bytes 786440 | tf_op jit(solution)/shard_map/ppermute | solution.py:22
  35.0 6.4 %collective-permute-start.8 = (bf16[64,2048]{1,0:T(8,128)(2,1)S(1)}, bf16[64,2048]{1,0:T(8,128)(2,1)S(1)}, u32[]{:S(2)}, u32[]{:S(2)}) collective-permute-start(bf16[64,2048]{1,0:T(8,128)(2,1)S(1)} %collective-permute-done.7.vm_ref), channel_id=1, source_target_pairs={{0,16},{8,24},{16,0},{24,8},{1,17},{9,25},{17,1},{25,9},{2,18},{10... | collective-permute-start | bytes 786440 | tf_op jit(solution)/shard_map/ppermute | solution.py:22
  35.1 6.3 %copy-start.3 = (s32[16]{0:T(128)S(1)}, s32[16]{0:T(128)}, u32[]{:S(2)}) copy-start(s32[16]{0:T(128)} %coarse_ref.3) | copy-start | bytes 196
  35.1 5.5 %collective-permute-start.10 = (bf16[32,2048]{1,0:T(8,128)(2,1)S(1)}, bf16[32,2048]{1,0:T(8,128)(2,1)S(1)}, u32[]{:S(2)}, u32[]{:S(2)}) collective-permute-start(bf16[32,2048]{1,0:T(8,128)(2,1)S(1)} %constant_dynamic-update-slice_fusion.mine_ref), channel_id=1, source_target_pairs={{0,1},{1,0},{2,3},{3,2},{4,5},{5,4},{6,7},{7,6},{8,9},{9,8},{10,11... | collective-permute-start | bytes 393224 | tf_op jit(solution)/shard_map/ppermute | solution.py:22

commit v12 on v11

--- a/solution.py
+++ b/solution.py
@@ -197,18 +197,29 @@
     share_ref[:, :HEAD_COUNT] = jnp.concatenate(shares, axis=0).T
 
 
-def finish_kernel(heads, sum_ref, share_ref, own_a_ref, own_b_ref, other_a_ref, other_b_ref, vm_ref, vr_ref, *rest):
+def base_kernel(heads, sum_ref, share_ref, own_a_ref, own_b_ref, base_ref, spread_ref):
+    half = HEAD_COUNT // 2
+    rows = sum_ref.shape[0]
+    for place, head in enumerate(heads):
+        own_ref = (own_a_ref, own_b_ref)[head // half]
+        share = jnp.broadcast_to(share_ref[:, head : head + 1], (rows, HEAD_FEATURES))
+        columns = head_columns(place)
+        base_ref[:, columns] = sum_ref[:, head_columns(head)] + share * own_ref[:, head_columns(head % half)]
+        spread_ref[:, columns] = share
+
+
+def finish_kernel(heads, base_ref, spread_ref, other_a_ref, other_b_ref, vm_ref, vr_ref, *rest):
     out_ref, ready_ref, semaphores = rest[-3:]
     half = HEAD_COUNT // 2
     copies = []
     for place, head in enumerate(heads):
-        columns = head_columns(head)
-        own_ref, other_ref = ((own_a_ref, other_a_ref), (own_b_ref, other_b_ref))[head // half]
-        values = jnp.concatenate([vm_ref[:, columns], vr_ref[:, head_columns(place)]], axis=0)
-        result = own_ref[:, head_columns(head % half)] + dot(other_ref[head % half], values)
-        result = sum_ref[:, columns] + share_ref[:, head : head + 1] * result
+        columns = head_columns(place)
+        other_ref = (other_a_ref, other_b_ref)[head // half]
+        values = jnp.concatenate([vm_ref[:, head_columns(head)], vr_ref[:, columns]], axis=0)
+        result = base_ref[:, columns] + spread_ref[:, columns] * dot(other_ref[head % half], values)
         ready_ref[place] = result.astype(jnp.bfloat16)
-        copies.append(pltpu.make_async_copy(ready_ref.at[place], out_ref.at[:, columns], semaphores.at[place]))
+        target = out_ref.at[:, head_columns(head)]
+        copies.append(pltpu.make_async_copy(ready_ref.at[place], target, semaphores.at[place]))
         copies[-1].start()
     for copy in copies:
         copy.wait()
@@ -223,10 +234,8 @@
 
 
 def stack_kernel(*refs):
-    out_ref, row = refs[-1], 0
-    for ref in refs[:-1]:
-        out_ref[row : row + ref.shape[0]] = ref[...]
-        row += ref.shape[0]
+    out_ref = refs[-1]
+    out_ref[...] = jnp.concatenate([ref[...].astype(jnp.float32) for ref in refs[:-1]], axis=0).astype(out_ref.dtype)
 
 
 def stack(*pieces):
@@ -332,10 +341,19 @@
     out = []
     first = 0
     for chunk, vr in zip(CHUNKS, other_vr):
-        args = [extra_sum, share, own_a, own_b, weights_a, weights_b, other_vm, vr]
+        heads = range(first, first + chunk)
+        base, spread = call(
+            functools.partial(base_kernel, heads),
+            "base",
+            extra_sum, share, own_a, own_b,
+            out_shape=[pltpu.VMEM((rows, chunk * HEAD_FEATURES), f32)] * 2,
+            in_specs=[vmem] * 4,
+            out_specs=[vmem] * 2,
+        )
+        args = [base, spread, weights_a, weights_b, other_vm, vr]
         out = [
             call(
-                functools.partial(finish_kernel, range(first, first + chunk)),
+                functools.partial(finish_kernel, heads),
                 "finish",
                 *args, *out,
                 out_shape=jax.ShapeDtypeStruct((rows, width), bf16),

time: 50.1 us -> 50.1 us (level)
  Pallas kernels: 19.3 us -> 20 us
  waiting for transfers between devices: 13.7 us -> 13 us
    ppermute x11, waiting for transfers between devices: 10.6 us -> 9.84 us  [partner(): return lax.ppermute(value, axis, pairs)]
    pallas_call x7 -> x9, Pallas kernels: 19.3 us -> 20 us  [call(): pl.pallas_call(kernel, name=name, compiler_params=params, cost_estimate=c...]
  transfers between devices with their start and end apart: 13 -> 13, of which waited for: 8 -> 7; matrix products, arithmetic and copies ran while one was open for 0% -> 0% of each run, Pallas kernels for 37% -> 38%
where the time goes in v12:
time: 50.1 us; the launch traced here: 49.9 us
  Pallas kernels  20 us (40%)
  starting transfers between devices  15.5 us (31%)
  waiting for transfers between devices  13 us (26%)
  local copies, waits for them, and re-layouts  1.33 us (3%)
    pallas_call x9, Pallas kernels, call(): pl.pallas_call(kernel, name=name, compiler_params=params, cost_estimate=c...  20 us
    ppermute x11, starting transfers between devices, partner(): return lax.ppermute(value, axis, pairs)  14 us
    ppermute x11, waiting for transfers between devices, partner(): return lax.ppermute(value, axis, pairs)  9.84 us
    ppermute x2, waiting for transfers between devices, partner_elsewhere(): return lax.ppermute(value, ('inner', 'outer'), pairs)  3.11 us
    ppermute x2, starting transfers between devices, partner_elsewhere(): return lax.ppermute(value, ('inner', 'outer'), pairs)  1.55 us
    unnamed x9, local copies, waits for them, and re-layouts  1.32 us
  transfers between devices with their start and end apart: 13, of which 7 were waited for; matrix products, arithmetic and copies ran while one was open for 0% of the time, Pallas kernels for 38%

profile of v12, /device:TPU:0, one launch (start us, length us, event | category | flops | bytes accessed | tf_op | source)
XLA Modules:
  0.0 49.9 jit_solution(14929672295367652690)
XLA Ops:
  0.0 2.9 %collective-permute-start = (bf16[256,2048]{1,0:T(8,128)(2,1)}, bf16[256,2048]{1,0:T(8,128)(2,1)S(1)}, u32[]{:S(2)}, u32[]{:S(2)}) collective-permute-start(bf16[256,2048]{1,0:T(8,128)(2,1)} %k_hbm.1), channel_id=1, source_target_pairs={{0,8},{8,0},{16,24},{24,16},{1,9},{9,1},{17,25},{25,17},{2,10},{10... | collective-permute-start | bytes 3145736 | tf_op jit(solution)/shard_map/ppermute | solution.py:22
  2.9 0.7 %copy-done = s32[16]{0:T(128)S(1)} copy-done((s32[16]{0:T(128)S(1)}, s32[16]{0:T(128)}, u32[]{:S(2)}) %copy-start) | copy-done | bytes 88
  3.6 0.7 %copy-done.2 = s32[16]{0:T(128)S(1)} copy-done((s32[16]{0:T(128)S(1)}, s32[16]{0:T(128)}, u32[]{:S(2)}) %copy-start.2) | copy-done | bytes 88
  4.3 3.2 %prepare.1 = (bf16[256,2048]{1,0:T(8,128)(2,1)S(1)}, bf16[256,2048]{1,0:T(8,128)(2,1)S(1)}, bf16[256,2048]{1,0:T(8,128)(2,1)S(1)}, bf16[128,2048]{1,0:T(8,128)(2...) custom-call(s32[16]{0:T(128)S(1)} %copy-done, ...), custom_call_target="tpu_custom_call" | custom-call | tf_op jit(solution)/shard_map/prepare/pallas_call | solution.py:277
  7.5 1.6 %collective-permute-start.2 = (bf16[128,2048]{1,0:T(8,128)(2,1)S(1)}, bf16[128,2048]{1,0:T(8,128)(2,1)S(1)}, u32[]{:S(2)}, u32[]{:S(2)}) collective-permute-start(bf16[128,2048]{1,0:T(8,128)(2,1)S(1)} %get-tuple-element.40), channel_id=1, source_target_pairs={{0,16},{8,24},{16,0},{24,8},{1,17},{9,25},{17,1},{25,9},{2,18},{10... | collective-permute-start | bytes 1572872 | tf_op jit(solution)/shard_map/ppermute | solution.py:22
  9.1 1.5 %collective-permute-start.3 = (bf16[2,2048]{1,0:T(2,128)(2,1)S(1)}, bf16[2,2048]{1,0:T(2,128)(2,1)S(1)}, u32[]{:S(2)}, u32[]{:S(2)}) collective-permute-start(bf16[2,2048]{1,0:T(2,128)(2,1)S(1)} %get-tuple-element.44.refs_0_), channel_id=1, source_target_pairs={{0,10},{1,11},{2,8},{3,9},{4,14},{5,15},{6,12},{7,13},{8,2},{9,3},... | collective-permute-start | bytes 24584 | tf_op jit(solution)/shard_map/ppermute | solution.py:32
  10.6 3.1 %collective-permute-done.3.refs_1_ = bf16[2,2048]{1,0:T(2,128)(2,1)S(1)} collective-permute-done((bf16[2,2048]{1,0:T(2,128)(2,1)S(1)}, bf16[2,2048]{1,0:T(2,128)(2,1)S(1)}, u32[]{:S(2)}, u32[]{:S(2)}) %collective-permute-start.3) | collective-permute-done | bytes 8224 | tf_op jit(solution)/shard_map/ppermute | solution.py:32
  13.8 1.6 %collective-permute-start.4 = (bf16[4,2048]{1,0:T(4,128)(2,1)S(1)}, bf16[4,2048]{1,0:T(4,128)(2,1)S(1)}, u32[]{:S(2)}, u32[]{:S(2)}) collective-permute-start(bf16[4,2048]{1,0:T(4,128)(2,1)S(1)} %stack.2.refs_0_), channel_id=1, source_target_pairs={{0,2},{1,3},{2,0},{3,1},{4,6},{5,7},{6,4},{7,5},{8,10},{9,11},{10,... | collective-permute-start | bytes 49160 | tf_op jit(solution)/shard_map/ppermute | solution.py:22
  15.4 2.6 %collective-permute-start.5 = (bf16[4,2048]{1,0:T(4,128)(2,1)S(1)}, bf16[4,2048]{1,0:T(4,128)(2,1)S(1)}, u32[]{:S(2)}, u32[]{:S(2)}) collective-permute-start(bf16[4,2048]{1,0:T(4,128)(2,1)S(1)} %stack.2.refs_0_), channel_id=1, source_target_pairs={{0,4},{1,5},{2,6},{3,7},{4,0},{5,1},{6,2},{7,3},{8,12},{9,13},{10,... | collective-permute-start | bytes 49160 | tf_op jit(solution)/shard_map/ppermute | solution.py:22
  18.0 0.2 collective-permute-start.6
  18.2 0.0 collective-permute-done.4.refs_1_
  18.2 2.1 %collective-permute-done.5.refs_2_ = bf16[4,2048]{1,0:T(4,128)(2,1)S(1)} collective-permute-done((bf16[4,2048]{1,0:T(4,128)(2,1)S(1)}, bf16[4,2048]{1,0:T(4,128)(2,1)S(1)}, u32[]{:S(2)}, u32[]{:S(2)}) %collective-permute-start.5) | collective-permute-done | bytes 16416 | tf_op jit(solution)/shard_map/ppermute | solution.py:22
  20.3 3.3 %collective-permute-done.6.refs_3_ = bf16[4,2048]{1,0:T(4,128)(2,1)S(1)} collective-permute-done((bf16[4,2048]{1,0:T(4,128)(2,1)S(1)}, bf16[4,2048]{1,0:T(4,128)(2,1)S(1)}, u32[]{:S(2)}, u32[]{:S(2)}) %collective-permute-start.6) | collective-permute-done | bytes 16416 | tf_op jit(solution)/shard_map/ppermute | solution.py:22
  23.6 0.6 %collective-permute-start.7 = (bf16[64,2048]{1,0:T(8,128)(2,1)S(1)}, bf16[64,2048]{1,0:T(8,128)(2,1)S(1)}, u32[]{:S(2)}, u32[]{:S(2)}) collective-permute-start(bf16[64,2048]{1,0:T(8,128)(2,1)S(1)} %get-tuple-element.46), channel_id=1, source_target_pairs={{0,8},{8,0},{16,24},{24,16},{1,9},{9,1},{17,25},{25,17},{2,10},{10... | collective-permute-start | bytes 786440 | tf_op jit(solution)/shard_map/ppermute | solution.py:22
  24.2 1.5 %collective-permute-start.12 = (bf16[192,1536]{1,0:T(8,128)(2,1)S(1)}, bf16[192,1536]{1,0:T(8,128)(2,1)S(1)}, u32[]{:S(2)}, u32[]{:S(2)}) collective-permute-start(bf16[192,1536]{1,0:T(8,128)(2,1)S(1)} %get-tuple-element.60), channel_id=1, source_target_pairs={{0,8},{8,0},{16,24},{24,16},{1,9},{9,1},{17,25},{25,17},{2,10},{10... | collective-permute-start | bytes 1769480 | tf_op jit(solution)/shard_map/ppermute | solution.py:22
  25.7 0.6 %collective-permute-start.11 = (bf16[192,512]{1,0:T(8,128)(2,1)S(1)}, bf16[192,512]{1,0:T(8,128)(2,1)S(1)}, u32[]{:S(2)}, u32[]{:S(2)}) collective-permute-start(bf16[192,512]{1,0:T(8,128)(2,1)S(1)} %get-tuple-element.57), channel_id=1, source_target_pairs={{0,8},{8,0},{16,24},{24,16},{1,9},{9,1},{17,25},{25,17},{2,10},{10... | collective-permute-start | bytes 589832 | tf_op jit(solution)/shard_map/ppermute | solution.py:22
  26.3 1.0 %collective-permute-done.k_ref.kp_ref = bf16[256,2048]{1,0:T(8,128)(2,1)S(1)} collective-permute-done((bf16[256,2048]{1,0:T(8,128)(2,1)}, bf16[256,2048]{1,0:T(8,128)(2,1)S(1)}, u32[]{:S(2)}, u32[]{:S(2)}) %collective-permute-start) | collective-permute-done | bytes 1048608 | tf_op jit(solution)/shard_map/ppermute | solution.py:22
  27.3 0.8 %pick.1 = bf16[64,2048]{1,0:T(8,128)(2,1)S(1)} custom-call(s32[16]{0:T(128)S(1)} %copy-done.1, bf16[256,2048]{1,0:T(8,128)(2,1)S(1)} %collective-permute-done.k_ref.kp_ref), custom_call_target="tpu_custom_call" | custom-call | tf_op jit(solution)/shard_map/pick/pallas_call | solution.py:277
  28.2 2.2 %collective-permute-start.1 = (bf16[64,2048]{1,0:T(8,128)(2,1)S(1)}, bf16[64,2048]{1,0:T(8,128)(2,1)S(1)}, u32[]{:S(2)}, u32[]{:S(2)}) collective-permute-start(bf16[64,2048]{1,0:T(8,128)(2,1)S(1)} %pick.1), channel_id=1, source_target_pairs={{0,16},{8,24},{16,0},{24,8},{1,17},{9,25},{17,1},{25,9},{2,18},{10... | collective-permute-start | bytes 786440 | tf_op jit(solution)/shard_map/ppermute | solution.py:22
  30.3 4.6 %first.2 = (f32[256,1024]{1,0:T(8,128)S(1)}, bf16[8,256,256]{2,1,0:T(8,128)(2,1)S(1)}, f32[256,128]{1,0:T(8,128)S(1)}) custom-call(s32[16]{0:T(128)S(1)} %copy-done.1, bf16[256,2048]{1,0:T(8,128)(2,1)S(1)} %get-tuple-element.38.q_ref, bf16[256,2048]{1,0:T(8,128)(2,1)S(1)} %get-tuple-element.34.k_ref, bf16[256,2048]{1,0:T(8,128)(2,1)S(1)} %get-tuple-element.35.v_ref, ...), custom_call_target="tpu_custom_call" | custom-call | tf_op jit(solution)/shard_map/first/pallas_call | solution.py:277
  35.0 0.1 collective-permute-start.8
  35.1 0.0 copy-start.3
  35.1 0.1 collective-permute-start.10
  35.2 0.8 %collective-permute-done.1.diagonal_k_ref = bf16[64,2048]{1,0:T(8,128)(2,1)S(1)} collective-permute-done((bf16[64,2048]{1,0:T(8,128)(2,1)S(1)}, bf16[64,2048]{1,0:T(8,128)(2,1)S(1)}, u32[]{:S(2)}, u32[]{:S(2)}) %collective-permute-start.1) | collective-permute-done | bytes 262176 | tf_op jit(solution)/shard_map/ppermute | solution.py:22
  35.9 4.6 %first.3 = (f32[256,1024]{1,0:T(8,128)S(1)}, bf16[8,256,256]{2,1,0:T(8,128)(2,1)S(1)}, f32[256,128]{1,0:T(8,128)S(1)}) custom-call(s32[16]{0:T(128)S(1)} %copy-done.1, bf16[256,2048]{1,0:T(8,128)(2,1)S(1)} %get-tuple-element.38.q_ref, bf16[256,2048]{1,0:T(8,128)(2,1)S(1)} %get-tuple-element.34.k_ref, bf16[256,2048]{1,0:T(8,128)(2,1)S(1)} %get-tuple-element.35.v_ref, ...), custom_call_target="tpu_custom_call" | custom-call | tf_op jit(solution)/shard_map/first/pallas_call | solution.py:277
  40.6 0.8 %collective-permute-done.8.diagonal_v_ref = bf16[64,2048]{1,0:T(8,128)(2,1)S(1)} collective-permute-done((bf16[64,2048]{1,0:T(8,128)(2,1)S(1)}, bf16[64,2048]{1,0:T(8,128)(2,1)S(1)}, u32[]{:S(2)}, u32[]{:S(2)}) %collective-permute-start.8) | collective-permute-done | bytes 262176 | tf_op jit(solution)/shard_map/ppermute | solution.py:22
  41.4 3.5 %extra.1 = (f32[256,2048]{1,0:T(8,128)S(1)}, f32[256,128]{1,0:T(8,128)S(1)}) custom-call(s32[16]{0:T(128)S(1)} %copy-done.1, s32[16]{0:T(128)S(1)} %copy-done.3, bf16[256,2048]{1,0:T(8,128)(2,1)S(1)} %get-tuple-element.38.q_ref, f32[256,128]{1,0:T(8,128)S(1)} %get-tuple-element.37.state_a_ref, f32[256,128]{1,0:T(8,128)S(1)} %get-tuple-element.39.state_b_ref, ...), custom_call_target="tpu_custom_call" | custom-call | tf_op jit(solution)/shard_map/extra/pallas_call | solution.py:277
  44.9 0.5 %base.3 = (f32[256,1536]{1,0:T(8,128)S(1)}, f32[256,1536]{1,0:T(8,128)S(1)}) custom-call(f32[256,2048]{1,0:T(8,128)S(1)} %get-tuple-element.49.sum_ref, f32[256,128]{1,0:T(8,128)S(1)} %get-tuple-element.50.share_ref, f32[256,1024]{1,0:T(8,128)S(1)} %get-tuple-element.51.own_a_ref, f32[256,1024]{1,0:T(8,128)S(1)} %get-tuple-element.52.own_b_ref), custom_call_target="tpu_custom_call" | custom-call | tf_op jit(solution)/shard_map/base/pallas_call | solution.py:277
  45.5 0.2 base.2
  45.7 1.4 %finish.2.rest_0_ = bf16[256,2048]{1,0:T(8,128)(2,1)} custom-call(f32[256,1536]{1,0:T(8,128)S(1)} %get-tuple-element.58.base_ref, f32[256,1536]{1,0:T(8,128)S(1)} %get-tuple-element.59.spread_ref, bf16[8,256,256]{2,1,0:T(8,128)(2,1)S(1)} %get-tuple-element.55.other_a_ref, bf16[8,256,256]{2,1,0:T(8,128)(2,1)S(1)} %get-tuple-element.56.other_b_ref, ...), custom_call_target="tpu_custom_call" | custom-call | tf_op jit(solution)/shard_map/finish/pallas_call | solution.py:277
  47.1 1.9 %collective-permute-done.11.vr_ref = bf16[192,512]{1,0:T(8,128)(2,1)S(1)} collective-permute-done((bf16[192,512]{1,0:T(8,128)(2,1)S(1)}, bf16[192,512]{1,0:T(8,128)(2,1)S(1)}, u32[]{:S(2)}, u32[]{:S(2)}) %collective-permute-start.11) | collective-permute-done | bytes 196640 | tf_op jit(solution)/shard_map/ppermute | solution.py:22
  49.0 1.0 %finish.3 = bf16[256,2048]{1,0:T(8,128)(2,1)} custom-call(f32[256,512]{1,0:T(8,128)S(1)} %get-tuple-element.53.base_ref, f32[256,512]{1,0:T(8,128)S(1)} %get-tuple-element.54.spread_ref, bf16[8,256,256]{2,1,0:T(8,128)(2,1)S(1)} %get-tuple-element.55.other_a_ref, ...), custom_call_target="tpu_custom_call", output_to_operand_aliasing={{}: (6, {})} | custom-call | tf_op jit(solution)/shard_map/finish/pallas_call | solution.py:277
  (15 shorter events, 0.1 us)
Async XLA Ops:
  0.0 27.3 %collective-permute-start = (bf16[256,2048]{1,0:T(8,128)(2,1)}, bf16[256,2048]{1,0:T(8,128)(2,1)S(1)}, u32[]{:S(2)}, u32[]{:S(2)}) collective-permute-start(bf16[256,2048]{1,0:T(8,128)(2,1)} %k_hbm.1), channel_id=1, source_target_pairs={{0,8},{8,0},{16,24},{24,16},{1,9},{9,1},{17,25},{25,17},{2,10},{10... | collective-permute-start | bytes 3145736 | tf_op jit(solution)/shard_map/ppermute | solution.py:22
  2.9 0.7 %copy-start = (s32[16]{0:T(128)S(1)}, s32[16]{0:T(128)}, u32[]{:S(2)}) copy-start(s32[16]{0:T(128)} %middle_ref.9) | copy-start | bytes 196
  3.6 0.7 %copy-start.2 = (s32[16]{0:T(128)S(1)}, s32[16]{0:T(128)}, u32[]{:S(2)}) copy-start(s32[16]{0:T(128)} %coarse_ref.3) | copy-start | bytes 196
  4.3 23.1 %copy-start.1 = (s32[16]{0:T(128)S(1)}, s32[16]{0:T(128)}, u32[]{:S(2)}) copy-start(s32[16]{0:T(128)} %middle_ref.9) | copy-start | bytes 196
  7.5 16.7 %collective-permute-start.2 = (bf16[128,2048]{1,0:T(8,128)(2,1)S(1)}, bf16[128,2048]{1,0:T(8,128)(2,1)S(1)}, u32[]{:S(2)}, u32[]{:S(2)}) collective-permute-start(bf16[128,2048]{1,0:T(8,128)(2,1)S(1)} %get-tuple-element.40), channel_id=1, source_target_pairs={{0,16},{8,24},{16,0},{24,8},{1,17},{9,25},{17,1},{25,9},{2,18},{10... | collective-permute-start | bytes 1572872 | tf_op jit(solution)/shard_map/ppermute | solution.py:22
  9.1 4.7 %collective-permute-start.3 = (bf16[2,2048]{1,0:T(2,128)(2,1)S(1)}, bf16[2,2048]{1,0:T(2,128)(2,1)S(1)}, u32[]{:S(2)}, u32[]{:S(2)}) collective-permute-start(bf16[2,2048]{1,0:T(2,128)(2,1)S(1)} %get-tuple-element.44.refs_0_), channel_id=1, source_target_pairs={{0,10},{1,11},{2,8},{3,9},{4,14},{5,15},{6,12},{7,13},{8,2},{9,3},... | collective-permute-start | bytes 24584 | tf_op jit(solution)/shard_map/ppermute | solution.py:32
  13.8 4.5 %collective-permute-start.4 = (bf16[4,2048]{1,0:T(4,128)(2,1)S(1)}, bf16[4,2048]{1,0:T(4,128)(2,1)S(1)}, u32[]{:S(2)}, u32[]{:S(2)}) collective-permute-start(bf16[4,2048]{1,0:T(4,128)(2,1)S(1)} %stack.2.refs_0_), channel_id=1, source_target_pairs={{0,2},{1,3},{2,0},{3,1},{4,6},{5,7},{6,4},{7,5},{8,10},{9,11},{10,... | collective-permute-start | bytes 49160 | tf_op jit(solution)/shard_map/ppermute | solution.py:22
  15.4 4.9 %collective-permute-start.5 = (bf16[4,2048]{1,0:T(4,128)(2,1)S(1)}, bf16[4,2048]{1,0:T(4,128)(2,1)S(1)}, u32[]{:S(2)}, u32[]{:S(2)}) collective-permute-start(bf16[4,2048]{1,0:T(4,128)(2,1)S(1)} %stack.2.refs_0_), channel_id=1, source_target_pairs={{0,4},{1,5},{2,6},{3,7},{4,0},{5,1},{6,2},{7,3},{8,12},{9,13},{10,... | collective-permute-start | bytes 49160 | tf_op jit(solution)/shard_map/ppermute | solution.py:22
  18.0 5.5 %collective-permute-start.6 = (bf16[4,2048]{1,0:T(4,128)(2,1)S(1)}, bf16[4,2048]{1,0:T(4,128)(2,1)S(1)}, u32[]{:S(2)}, u32[]{:S(2)}) collective-permute-start(bf16[4,2048]{1,0:T(4,128)(2,1)S(1)} %stack.2.refs_0_), channel_id=1, source_target_pairs={{0,6},{1,7},{2,4},{3,5},{4,2},{5,3},{6,0},{7,1},{8,14},{9,15},{10,... | collective-permute-start | bytes 49160 | tf_op jit(solution)/shard_map/ppermute | solution.py:22
  23.6 11.4 %collective-permute-start.7 = (bf16[64,2048]{1,0:T(8,128)(2,1)S(1)}, bf16[64,2048]{1,0:T(8,128)(2,1)S(1)}, u32[]{:S(2)}, u32[]{:S(2)}) collective-permute-start(bf16[64,2048]{1,0:T(8,128)(2,1)S(1)} %get-tuple-element.46), channel_id=1, source_target_pairs={{0,8},{8,0},{16,24},{24,16},{1,9},{9,1},{17,25},{25,17},{2,10},{10... | collective-permute-start | bytes 786440 | tf_op jit(solution)/shard_map/ppermute | solution.py:22
  24.2 21.5 %collective-permute-start.12 = (bf16[192,1536]{1,0:T(8,128)(2,1)S(1)}, bf16[192,1536]{1,0:T(8,128)(2,1)S(1)}, u32[]{:S(2)}, u32[]{:S(2)}) collective-permute-start(bf16[192,1536]{1,0:T(8,128)(2,1)S(1)} %get-tuple-element.60), channel_id=1, source_target_pairs={{0,8},{8,0},{16,24},{24,16},{1,9},{9,1},{17,25},{25,17},{2,10},{10... | collective-permute-start | bytes 1769480 | tf_op jit(solution)/shard_map/ppermute | solution.py:22
  25.7 9.4 %collective-permute-start.9 = (bf16[16,2048]{1,0:T(8,128)(2,1)S(1)}, bf16[16,2048]{1,0:T(8,128)(2,1)S(1)}, u32[]{:S(2)}, u32[]{:S(2)}) collective-permute-start(bf16[16,2048]{1,0:T(8,128)(2,1)S(1)} %stack.3), channel_id=1, source_target_pairs={{0,18},{1,19},{2,16},{3,17},{4,22},{5,23},{6,20},{7,21},{8,26},{9,... | collective-permute-start | bytes 196616 | tf_op jit(solution)/shard_map/ppermute | solution.py:32
  25.7 23.3 %collective-permute-start.11 = (bf16[192,512]{1,0:T(8,128)(2,1)S(1)}, bf16[192,512]{1,0:T(8,128)(2,1)S(1)}, u32[]{:S(2)}, u32[]{:S(2)}) collective-permute-start(bf16[192,512]{1,0:T(8,128)(2,1)S(1)} %get-tuple-element.57), channel_id=1, source_target_pairs={{0,8},{8,0},{16,24},{24,16},{1,9},{9,1},{17,25},{25,17},{2,10},{10... | collective-permute-start | bytes 589832 | tf_op jit(solution)/shard_map/ppermute | solution.py:22
  28.2 7.8 %collective-permute-start.1 = (bf16[64,2048]{1,0:T(8,128)(2,1)S(1)}, bf16[64,2048]{1,0:T(8,128)(2,1)S(1)}, u32[]{:S(2)}, u32[]{:S(2)}) collective-permute-start(bf16[64,2048]{1,0:T(8,128)(2,1)S(1)} %pick.1), channel_id=1, source_target_pairs={{0,16},{8,24},{16,0},{24,8},{1,17},{9,25},{17,1},{25,9},{2,18},{10... | collective-permute-start | bytes 786440 | tf_op jit(solution)/shard_map/ppermute | solution.py:22
  35.0 6.4 %collective-permute-start.8 = (bf16[64,2048]{1,0:T(8,128)(2,1)S(1)}, bf16[64,2048]{1,0:T(8,128)(2,1)S(1)}, u32[]{:S(2)}, u32[]{:S(2)}) collective-permute-start(bf16[64,2048]{1,0:T(8,128)(2,1)S(1)} %collective-permute-done.7.vm_ref), channel_id=1, source_target_pairs={{0,16},{8,24},{16,0},{24,8},{1,17},{9,25},{17,1},{25,9},{2,18},{10... | collective-permute-start | bytes 786440 | tf_op jit(solution)/shard_map/ppermute | solution.py:22
  35.1 6.3 %copy-start.3 = (s32[16]{0:T(128)S(1)}, s32[16]{0:T(128)}, u32[]{:S(2)}) copy-start(s32[16]{0:T(128)} %coarse_ref.3) | copy-start | bytes 196
  35.1 5.5 %collective-permute-start.10 = (bf16[32,2048]{1,0:T(8,128)(2,1)S(1)}, bf16[32,2048]{1,0:T(8,128)(2,1)S(1)}, u32[]{:S(2)}, u32[]{:S(2)}) collective-permute-start(bf16[32,2048]{1,0:T(8,128)(2,1)S(1)} %constant_dynamic-update-slice_fusion.mine_ref), channel_id=1, source_target_pairs={{0,1},{1,0},{2,3},{3,2},{4,5},{5,4},{6,7},{7,6},{8,9},{9,8},{10,11... | collective-permute-start | bytes 393224 | tf_op jit(solution)/shard_map/ppermute | solution.py:22

commit v13 on v12

--- a/solution.py
+++ b/solution.py
@@ -10,7 +10,7 @@
 HEAD_COUNT = 16
 HEAD_FEATURES = 128
 MIDDLE_DILATION = 4
-CHUNKS = (12, 4)
+CHUNKS = (11, 4, 1)
 LANES = 128
 SUBLANES = 16
 EXP2_SCALE = HEAD_FEATURES ** (-0.5) * 1.4426950408889634
@@ -130,39 +130,48 @@
     return jnp.exp2((part - top) * EXP2_SCALE)
 
 
-def first_kernel(first, middle_ref, q_ref, k_ref, v_ref, kp_ref, own_ref, other_ref, state_ref, order_ref):
+def own_kernel(middle_ref, q_ref, k_ref, v_ref, sum_ref, state_ref):
+    rows = q_ref.shape[0]
+    column = lax.broadcasted_iota(jnp.int32, (1, rows), 1)
+    tops, totals = [], []
+    for head in range(HEAD_COUNT):
+        columns = head_columns(head)
+        shift = middle_ref[head]
+        own = dot_keys(q_ref[:, columns], k_ref[:, columns])
+        top = jnp.max(functools.reduce(jnp.maximum, lane_tiles(own)), axis=1, keepdims=True)
+        own = weights(own, top)
+        twice = member_rows(rows, shift) & ((column & (MIDDLE_DILATION - 1)) == shift)
+        own = jnp.where(twice, own + own, own)
+        tops.append(top)
+        totals.append(jnp.sum(functools.reduce(jnp.add, lane_tiles(own)), axis=1, keepdims=True))
+        sum_ref[:, columns] = dot(own.astype(jnp.bfloat16), v_ref[:, columns])
+    state_ref[...] = side_by_side(tops + totals)
+
+
+def other_kernel(first, middle_ref, q_ref, kp_ref, other_ref, state_ref, order_ref):
     fill_orders(order_ref)
     rows = q_ref.shape[0]
     members = rows // MIDDLE_DILATION
-    column = lax.broadcasted_iota(jnp.int32, (1, rows), 1)
+    column = lax.broadcasted_iota(jnp.int32, (1, LANES), 1)
     tops, totals = [], []
-    heads = other_ref.shape[0]
-    for place in range(heads):
+    for place in range(other_ref.shape[0]):
         columns = head_columns(first + place)
         shift = middle_ref[first + place]
-        q = q_ref[:, columns]
-        own = dot_keys(q, k_ref[:, columns])
         other_keys = dot(order_ref[shift], kp_ref[:, columns]).astype(jnp.bfloat16)
-        other = dot_keys(q, other_keys)
-        top = functools.reduce(jnp.maximum, lane_tiles(own) + lane_tiles(other))
-        top = jnp.max(top, axis=1, keepdims=True)
-        row_is_member = member_rows(rows, shift)
-        own, other = weights(own, top), weights(other, top)
-        own_member = row_is_member & ((column & (MIDDLE_DILATION - 1)) == shift)
-        own = jnp.where(own_member, own + own, own)
+        other = dot_keys(q_ref[:, columns], other_keys)
+        top = jnp.max(functools.reduce(jnp.maximum, lane_tiles(other)), axis=1, keepdims=True)
+        other = weights(other, top)
         twice = other[:, :LANES]
-        twice = jnp.where(row_is_member & (column[:, :LANES] < members), twice + twice, twice)
+        twice = jnp.where(member_rows(rows, shift) & (column < members), twice + twice, twice)
         other = jnp.concatenate([twice, other[:, LANES:]], axis=1)
-        total = functools.reduce(jnp.add, lane_tiles(own) + lane_tiles(other))
         tops.append(top)
-        totals.append(jnp.sum(total, axis=1, keepdims=True))
-        own_ref[:, head_columns(place)] = dot(own.astype(jnp.bfloat16), v_ref[:, columns])
+        totals.append(jnp.sum(functools.reduce(jnp.add, lane_tiles(other)), axis=1, keepdims=True))
         other_ref[place] = other.astype(jnp.bfloat16)
     state_ref[...] = side_by_side(tops + totals)
 
 
 def extra_kernel(
-    middle_ref, coarse_ref, q_ref, state_a_ref, state_b_ref, cross_ref, diagonal_k_ref, diagonal_v_ref, mine_ref,
+    middle_ref, coarse_ref, q_ref, own_state_ref, state_a_ref, state_b_ref, cross_ref, diagonal_k_ref, diagonal_v_ref, mine_ref,
     other_ref, sum_ref, share_ref,
 ):
     rows = q_ref.shape[0]
@@ -171,8 +180,9 @@
     far_rows, coarse_rows = 2 * members, 2 * mine_ref.shape[0]
     token = lax.broadcasted_iota(jnp.int32, (1, rows), 1)
     is_key = (lax.broadcasted_iota(jnp.int32, (coarse_rows, 1), 0) & 1) == 0
+    own_state = own_state_ref[...].T
     states = [ref[...].T for ref in (state_a_ref, state_b_ref)]
-    shares = []
+    own_shares, other_shares = [], []
     for head in range(HEAD_COUNT):
         columns = head_columns(head)
         state, place = states[head // half], head % half
@@ -182,30 +192,31 @@
         scores = dot_keys(keys, q_ref[:, columns])
         far = jnp.where((token & (MIDDLE_DILATION - 1)) == middle_ref[head], scores[:far_rows], MASKED)
         coarse = jnp.where(is_key & (token == coarse_ref[head]), scores[far_rows:], MASKED)
-        before = state[place : place + 1]
-        top = jnp.maximum(before, jnp.max(far, axis=0, keepdims=True))
+        own_top, other_top = own_state[head : head + 1], state[place : place + 1]
+        top = jnp.maximum(jnp.maximum(own_top, other_top), jnp.max(far, axis=0, keepdims=True))
         top = jnp.maximum(top, jnp.max(coarse, axis=0, keepdims=True))
         far, coarse = weights(far, top), weights(coarse, top)
-        kept = weights(before, top)
-        total = kept * state[half + place : half + place + 1]
+        own_kept, other_kept = weights(own_top, top), weights(other_top, top)
+        total = own_kept * own_state[HEAD_COUNT + head : HEAD_COUNT + head + 1]
+        total += other_kept * state[half + place : half + place + 1]
         total += jnp.sum(far, axis=0, keepdims=True) + jnp.sum(coarse, axis=0, keepdims=True)
         inverse = 1.0 / total
         shifted = pltpu.roll(coarse, 1, 0)
         mixed = jnp.concatenate([(far * inverse).astype(jnp.bfloat16), (shifted * inverse).astype(jnp.bfloat16)], axis=0)
         sum_ref[:, columns] = dot_rows(mixed, values)
-        shares.append(kept * inverse)
-    share_ref[:, :HEAD_COUNT] = jnp.concatenate(shares, axis=0).T
-
-
-def base_kernel(heads, sum_ref, share_ref, own_a_ref, own_b_ref, base_ref, spread_ref):
-    half = HEAD_COUNT // 2
-    rows = sum_ref.shape[0]
+        own_shares.append(own_kept * inverse)
+        other_shares.append(other_kept * inverse)
+    share_ref[:, : 2 * HEAD_COUNT] = jnp.concatenate(own_shares + other_shares, axis=0).T
+
+
+def base_kernel(heads, sum_ref, share_ref, own_ref, base_ref, spread_ref):
+    shape = (sum_ref.shape[0], HEAD_FEATURES)
     for place, head in enumerate(heads):
-        own_ref = (own_a_ref, own_b_ref)[head // half]
-        share = jnp.broadcast_to(share_ref[:, head : head + 1], (rows, HEAD_FEATURES))
-        columns = head_columns(place)
-        base_ref[:, columns] = sum_ref[:, head_columns(head)] + share * own_ref[:, head_columns(head % half)]
-        spread_ref[:, columns] = share
+        columns, place_columns = head_columns(head), head_columns(place)
+        share = share_ref[:, head : head + 1]
+        base_ref[:, place_columns] = sum_ref[:, columns] + share * own_ref[:, columns]
+        other = HEAD_COUNT + head
+        spread_ref[:, place_columns] = jnp.broadcast_to(share_ref[:, other : other + 1], shape)
 
 
 def finish_kernel(heads, base_ref, spread_ref, other_a_ref, other_b_ref, vm_ref, vr_ref, *rest):
@@ -294,7 +305,15 @@
     )
     cross = partner(own_members, "inner", 2)
     near = gather_upper(stack(coarse, partner_elsewhere(coarse, 1)), "outer")
-    near, own_vm = lax.optimization_barrier((near, own_vm))
+    own_sum, own_state = call(
+        own_kernel,
+        "own",
+        middle_head_shift, q, k, v,
+        out_shape=[pltpu.VMEM((rows, width), f32), pltpu.VMEM((rows, LANES), f32)],
+        in_specs=[smem] + [vmem] * 3,
+        out_specs=[vmem] * 2,
+    )
+    near, own_vm, own_state = lax.optimization_barrier((near, own_vm, own_state))
     other_vm = partner(own_vm, "inner", 1)
     cross, own_vr = lax.optimization_barrier((cross, own_vr))
     other_vr = [partner(piece, "inner", 1) for piece in own_vr]
@@ -309,32 +328,28 @@
     diagonal_k = partner(other_km, "inner", 2)
     other_keys = lax.optimization_barrier((other_keys, other_km))[0]
 
-    def first_part(first, query):
+    def other_part(first, query):
         return call(
-            functools.partial(first_kernel, first),
-            "first",
-            middle_head_shift, query, k, v, other_keys,
-            out_shape=[
-                pltpu.VMEM((rows, half * HEAD_FEATURES), f32),
-                pltpu.VMEM((half, rows, rows), bf16),
-                pltpu.VMEM((rows, LANES), f32),
-            ],
-            in_specs=[smem] + [vmem] * 4,
-            out_specs=[vmem] * 3,
+            functools.partial(other_kernel, first),
+            "other",
+            middle_head_shift, query, other_keys,
+            out_shape=[pltpu.VMEM((half, rows, rows), bf16), pltpu.VMEM((rows, LANES), f32)],
+            in_specs=[smem] + [vmem] * 2,
+            out_specs=[vmem] * 2,
             scratch_shapes=[orders],
         )
 
-    own_a, weights_a, state_a = first_part(0, q)
+    weights_a, state_a = other_part(0, q)
     diagonal_v = partner(lax.optimization_barrier((other_vm, state_a))[0], "inner", 2)
-    own_b, weights_b, state_b = first_part(half, lax.optimization_barrier((q, state_a, diagonal_k))[0])
+    weights_b, state_b = other_part(half, lax.optimization_barrier((q, state_a, diagonal_k))[0])
     mine = jnp.concatenate([near, partner_elsewhere(near, 2)], axis=0)
     extra_sum, share = call(
         extra_kernel,
         "extra",
-        middle_head_shift, coarse_head_shift, q, state_a, state_b, cross, diagonal_k, diagonal_v, mine,
+        middle_head_shift, coarse_head_shift, q, own_state, state_a, state_b, cross, diagonal_k, diagonal_v, mine,
         partner(mine, "outer", 1),
         out_shape=[pltpu.VMEM((rows, width), f32), pltpu.VMEM((rows, LANES), f32)],
-        in_specs=[smem, smem] + [vmem] * 8,
+        in_specs=[smem, smem] + [vmem] * 9,
         out_specs=[vmem] * 2,
     )
 
@@ -345,9 +360,9 @@
         base, spread = call(
             functools.partial(base_kernel, heads),
             "base",
-            extra_sum, share, own_a, own_b,
+            extra_sum, share, own_sum,
             out_shape=[pltpu.VMEM((rows, chunk * HEAD_FEATURES), f32)] * 2,
-            in_specs=[vmem] * 4,
+            in_specs=[vmem] * 3,
             out_specs=[vmem] * 2,
         )
         args = [base, spread, weights_a, weights_b, other_vm, vr]

time: 50.1 us -> 50.4 us (level)
  starting transfers between devices: 15.5 us -> 19.4 us
  Pallas kernels: 20 us -> 17.9 us
  waiting for transfers between devices: 13 us -> 11.4 us
    ppermute x11 -> x12, starting transfers between devices: 14 us -> 17.9 us  [partner(): return lax.ppermute(value, axis, pairs)]
    pallas_call x9 -> x12, Pallas kernels: 20 us -> 17.9 us  [call(): pl.pallas_call(kernel, name=name, compiler_params=params, cost_estimate=c...]
    ppermute x11 -> x12, waiting for transfers between devices: 9.84 us -> 8.33 us  [partner(): return lax.ppermute(value, axis, pairs)]
  transfers between devices with their start and end apart: 13 -> 14, of which waited for: 7 -> 7; matrix products, arithmetic and copies ran while one was open for 0% -> 0% of each run, Pallas kernels for 38% -> 34%
where the time goes in v13:
time: 50.4 us; the launch traced here: 50.2 us
  starting transfers between devices  19.4 us (38%)
  Pallas kernels  17.9 us (36%)
  waiting for transfers between devices  11.4 us (23%)
  local copies, waits for them, and re-layouts  1.33 us (3%)
    pallas_call x12, Pallas kernels, call(): pl.pallas_call(kernel, name=name, compiler_params=params, cost_estimate=c...  17.9 us
    ppermute x12, starting transfers between devices, partner(): return lax.ppermute(value, axis, pairs)  17.9 us
    ppermute x12, waiting for transfers between devices, partner(): return lax.ppermute(value, axis, pairs)  8.33 us
    ppermute x2, waiting for transfers between devices, partner_elsewhere(): return lax.ppermute(value, ('inner', 'outer'), pairs)  3.11 us
    ppermute x2, starting transfers between devices, partner_elsewhere(): return lax.ppermute(value, ('inner', 'outer'), pairs)  1.55 us
    unnamed x9, local copies, waits for them, and re-layouts  1.32 us
  transfers between devices with their start and end apart: 14, of which 7 were waited for; matrix products, arithmetic and copies ran while one was open for 0% of the time, Pallas kernels for 34%

profile of v13, /device:TPU:0, one launch (start us, length us, event | category | flops | bytes accessed | tf_op | source)
XLA Modules:
  0.0 50.2 jit_solution(15155992571956985476)
XLA Ops:
  0.0 2.9 %collective-permute-start.4 = (bf16[256,2048]{1,0:T(8,128)(2,1)}, bf16[256,2048]{1,0:T(8,128)(2,1)S(1)}, u32[]{:S(2)}, u32[]{:S(2)}) collective-permute-start(bf16[256,2048]{1,0:T(8,128)(2,1)} %k_hbm.1), channel_id=1, source_target_pairs={{0,8},{8,0},{16,24},{24,16},{1,9},{9,1},{17,25},{25,17},{2,10},{10... | collective-permute-start | bytes 3145736 | tf_op jit(solution)/shard_map/ppermute | solution.py:22
  2.9 0.7 %copy-done = s32[16]{0:T(128)S(1)} copy-done((s32[16]{0:T(128)S(1)}, s32[16]{0:T(128)}, u32[]{:S(2)}) %copy-start) | copy-done | bytes 88
  3.6 0.7 %copy-done.2 = s32[16]{0:T(128)S(1)} copy-done((s32[16]{0:T(128)S(1)}, s32[16]{0:T(128)}, u32[]{:S(2)}) %copy-start.2) | copy-done | bytes 88
  4.3 3.2 %prepare.1 = (bf16[256,2048]{1,0:T(8,128)(2,1)S(1)}, bf16[256,2048]{1,0:T(8,128)(2,1)S(1)}, bf16[256,2048]{1,0:T(8,128)(2,1)S(1)}, bf16[128,2048]{1,0:T(8,128)(2...) custom-call(s32[16]{0:T(128)S(1)} %copy-done, ...), custom_call_target="tpu_custom_call" | custom-call | tf_op jit(solution)/shard_map/prepare/pallas_call | solution.py:288
  7.5 1.6 %collective-permute-start.6 = (bf16[128,2048]{1,0:T(8,128)(2,1)S(1)}, bf16[128,2048]{1,0:T(8,128)(2,1)S(1)}, u32[]{:S(2)}, u32[]{:S(2)}) collective-permute-start(bf16[128,2048]{1,0:T(8,128)(2,1)S(1)} %get-tuple-element.49), channel_id=1, source_target_pairs={{0,16},{8,24},{16,0},{24,8},{1,17},{9,25},{17,1},{25,9},{2,18},{10... | collective-permute-start | bytes 1572872 | tf_op jit(solution)/shard_map/ppermute | solution.py:22
  9.1 1.5 %collective-permute-start = (bf16[2,2048]{1,0:T(2,128)(2,1)S(1)}, bf16[2,2048]{1,0:T(2,128)(2,1)S(1)}, u32[]{:S(2)}, u32[]{:S(2)}) collective-permute-start(bf16[2,2048]{1,0:T(2,128)(2,1)S(1)} %get-tuple-element.39.refs_0_), channel_id=1, source_target_pairs={{0,10},{1,11},{2,8},{3,9},{4,14},{5,15},{6,12},{7,13},{8,2},{9,3},... | collective-permute-start | bytes 24584 | tf_op jit(solution)/shard_map/ppermute | solution.py:32
  10.6 3.1 %collective-permute-done.refs_1_ = bf16[2,2048]{1,0:T(2,128)(2,1)S(1)} collective-permute-done((bf16[2,2048]{1,0:T(2,128)(2,1)S(1)}, bf16[2,2048]{1,0:T(2,128)(2,1)S(1)}, u32[]{:S(2)}, u32[]{:S(2)}) %collective-permute-start) | collective-permute-done | bytes 8224 | tf_op jit(solution)/shard_map/ppermute | solution.py:32
  13.8 1.6 %collective-permute-start.1 = (bf16[4,2048]{1,0:T(4,128)(2,1)S(1)}, bf16[4,2048]{1,0:T(4,128)(2,1)S(1)}, u32[]{:S(2)}, u32[]{:S(2)}) collective-permute-start(bf16[4,2048]{1,0:T(4,128)(2,1)S(1)} %stack.2.refs_0_), channel_id=1, source_target_pairs={{0,2},{1,3},{2,0},{3,1},{4,6},{5,7},{6,4},{7,5},{8,10},{9,11},{10,... | collective-permute-start | bytes 49160 | tf_op jit(solution)/shard_map/ppermute | solution.py:22
  15.4 2.6 %collective-permute-start.2 = (bf16[4,2048]{1,0:T(4,128)(2,1)S(1)}, bf16[4,2048]{1,0:T(4,128)(2,1)S(1)}, u32[]{:S(2)}, u32[]{:S(2)}) collective-permute-start(bf16[4,2048]{1,0:T(4,128)(2,1)S(1)} %stack.2.refs_0_), channel_id=1, source_target_pairs={{0,4},{1,5},{2,6},{3,7},{4,0},{5,1},{6,2},{7,3},{8,12},{9,13},{10,... | collective-permute-start | bytes 49160 | tf_op jit(solution)/shard_map/ppermute | solution.py:22
  18.0 0.2 collective-permute-start.3
  18.2 2.6 %own.1 = (f32[256,2048]{1,0:T(8,128)S(1)}, f32[256,128]{1,0:T(8,128)S(1)}) custom-call(s32[16]{0:T(128)S(1)} %copy-done.1, bf16[256,2048]{1,0:T(8,128)(2,1)S(1)} %get-tuple-element.47.q_ref, bf16[256,2048]{1,0:T(8,128)(2,1)S(1)} %get-tuple-element.41.k_ref, bf16[256,2048]{1,0:T(8,128)(2,1)S(1)} %get-tuple-element.42.v_ref), custom_call_target="tpu_custom_call" | custom-call | tf_op jit(solution)/shard_map/own/pallas_call | solution.py:288
  20.8 2.8 %collective-permute-done.3.refs_3_ = bf16[4,2048]{1,0:T(4,128)(2,1)S(1)} collective-permute-done((bf16[4,2048]{1,0:T(4,128)(2,1)S(1)}, bf16[4,2048]{1,0:T(4,128)(2,1)S(1)}, u32[]{:S(2)}, u32[]{:S(2)}) %collective-permute-start.3) | collective-permute-done | bytes 16416 | tf_op jit(solution)/shard_map/ppermute | solution.py:22
  23.7 0.5 collective-permute-start.7
  24.1 1.6 %collective-permute-start.13 = (bf16[192,1408]{1,0:T(8,128)(2,1)S(1)}, bf16[192,1408]{1,0:T(8,128)(2,1)S(1)}, u32[]{:S(2)}, u32[]{:S(2)}) collective-permute-start(bf16[192,1408]{1,0:T(8,128)(2,1)S(1)} %get-tuple-element.70), channel_id=1, source_target_pairs={{0,8},{8,0},{16,24},{24,16},{1,9},{9,1},{17,25},{25,17},{2,10},{10... | collective-permute-start | bytes 1622024 | tf_op jit(solution)/shard_map/ppermute | solution.py:22
  25.8 0.4 collective-permute-start.12
  26.2 1.1 %collective-permute-done.4.k_ref.kp_ref = bf16[256,2048]{1,0:T(8,128)(2,1)S(1)} collective-permute-done((bf16[256,2048]{1,0:T(8,128)(2,1)}, bf16[256,2048]{1,0:T(8,128)(2,1)S(1)}, u32[]{:S(2)}, u32[]{:S(2)}) %collective-permute-start.4) | collective-permute-done | bytes 1048608 | tf_op jit(solution)/shard_map/ppermute | solution.py:22
  27.3 0.8 %pick.1 = bf16[64,2048]{1,0:T(8,128)(2,1)S(1)} custom-call(s32[16]{0:T(128)S(1)} %copy-done.1, bf16[256,2048]{1,0:T(8,128)(2,1)S(1)} %collective-permute-done.4.k_ref.kp_ref), custom_call_target="tpu_custom_call" | custom-call | tf_op jit(solution)/shard_map/pick/pallas_call | solution.py:288
  28.2 2.2 %collective-permute-start.5 = (bf16[64,2048]{1,0:T(8,128)(2,1)S(1)}, bf16[64,2048]{1,0:T(8,128)(2,1)S(1)}, u32[]{:S(2)}, u32[]{:S(2)}) collective-permute-start(bf16[64,2048]{1,0:T(8,128)(2,1)S(1)} %pick.1), channel_id=1, source_target_pairs={{0,16},{8,24},{16,0},{24,8},{1,17},{9,25},{17,1},{25,9},{2,18},{10... | collective-permute-start | bytes 786440 | tf_op jit(solution)/shard_map/ppermute | solution.py:22
  30.3 1.6 %other.2 = (bf16[8,256,256]{2,1,0:T(8,128)(2,1)S(1)}, f32[256,128]{1,0:T(8,128)S(1)}) custom-call(s32[16]{0:T(128)S(1)} %copy-done.1, bf16[256,2048]{1,0:T(8,128)(2,1)S(1)} %get-tuple-element.47.q_ref, bf16[256,2048]{1,0:T(8,128)(2,1)S(1)} %collective-permute-done.4.k_ref.kp_ref), custom_call_target="tpu_custom_call" | custom-call | tf_op jit(solution)/shard_map/other/pallas_call | solution.py:288
  32.0 1.0 %collective-permute-done.7.vm_ref = bf16[64,2048]{1,0:T(8,128)(2,1)S(1)} collective-permute-done((bf16[64,2048]{1,0:T(8,128)(2,1)S(1)}, bf16[64,2048]{1,0:T(8,128)(2,1)S(1)}, u32[]{:S(2)}, u32[]{:S(2)}) %collective-permute-start.7) | collective-permute-done | bytes 262176 | tf_op jit(solution)/shard_map/ppermute | solution.py:22
  32.9 2.1 %collective-permute-start.8 = (bf16[64,2048]{1,0:T(8,128)(2,1)S(1)}, bf16[64,2048]{1,0:T(8,128)(2,1)S(1)}, u32[]{:S(2)}, u32[]{:S(2)}) collective-permute-start(bf16[64,2048]{1,0:T(8,128)(2,1)S(1)} %collective-permute-done.7.vm_ref), channel_id=1, source_target_pairs={{0,16},{8,24},{16,0},{24,8},{1,17},{9,25},{17,1},{25,9},{2,18},{10... | collective-permute-start | bytes 786440 | tf_op jit(solution)/shard_map/ppermute | solution.py:22
  35.1 0.7 %collective-permute-done.5.diagonal_k_ref = bf16[64,2048]{1,0:T(8,128)(2,1)S(1)} collective-permute-done((bf16[64,2048]{1,0:T(8,128)(2,1)S(1)}, bf16[64,2048]{1,0:T(8,128)(2,1)S(1)}, u32[]{:S(2)}, u32[]{:S(2)}) %collective-permute-start.5) | collective-permute-done | bytes 262176 | tf_op jit(solution)/shard_map/ppermute | solution.py:22
  35.8 2.1 %collective-permute-start.11 = (bf16[192,128]{1,0:T(8,128)(2,1)S(1)}, bf16[192,128]{1,0:T(8,128)(2,1)S(1)}, u32[]{:S(2)}, u32[]{:S(2)}) collective-permute-start(bf16[192,128]{1,0:T(8,128)(2,1)S(1)} %get-tuple-element.64), channel_id=1, source_target_pairs={{0,8},{8,0},{16,24},{24,16},{1,9},{9,1},{17,25},{25,17},{2,10},{10... | collective-permute-start | bytes 147464 | tf_op jit(solution)/shard_map/ppermute | solution.py:22
  37.9 1.6 %other.3 = (bf16[8,256,256]{2,1,0:T(8,128)(2,1)S(1)}, f32[256,128]{1,0:T(8,128)S(1)}) custom-call(s32[16]{0:T(128)S(1)} %copy-done.1, bf16[256,2048]{1,0:T(8,128)(2,1)S(1)} %get-tuple-element.47.q_ref, bf16[256,2048]{1,0:T(8,128)(2,1)S(1)} %collective-permute-done.4.k_ref.kp_ref), custom_call_target="tpu_custom_call" | custom-call | tf_op jit(solution)/shard_map/other/pallas_call | solution.py:288
  39.5 1.0 %collective-permute-done.8.diagonal_v_ref = bf16[64,2048]{1,0:T(8,128)(2,1)S(1)} collective-permute-done((bf16[64,2048]{1,0:T(8,128)(2,1)S(1)}, bf16[64,2048]{1,0:T(8,128)(2,1)S(1)}, u32[]{:S(2)}, u32[]{:S(2)}) %collective-permute-start.8) | collective-permute-done | bytes 262176 | tf_op jit(solution)/shard_map/ppermute | solution.py:22
  40.5 3.5 %extra.1 = (f32[256,2048]{1,0:T(8,128)S(1)}, f32[256,128]{1,0:T(8,128)S(1)}) custom-call(s32[16]{0:T(128)S(1)} %copy-done.1, s32[16]{0:T(128)S(1)} %copy-done.3, bf16[256,2048]{1,0:T(8,128)(2,1)S(1)} %get-tuple-element.47.q_ref, f32[256,128]{1,0:T(8,128)S(1)} %get-tuple-element.44.own_state_ref, f32[256,128]{1,0:T(8,128)S(1)} %get-tuple-element.46.state_a_ref, ...), custom_call_target="tpu_custom_call" | custom-call | tf_op jit(solution)/shard_map/extra/pallas_call | solution.py:288
  44.1 0.9 %base.5 = (f32[256,1408]{1,0:T(8,128)S(1)}, f32[256,1408]{1,0:T(8,128)S(1)}) custom-call(f32[256,2048]{1,0:T(8,128)S(1)} %get-tuple-element.57.sum_ref, f32[256,128]{1,0:T(8,128)S(1)} %get-tuple-element.58.share_ref, f32[256,2048]{1,0:T(8,128)S(1)} %get-tuple-element.59.own_ref), custom_call_target="tpu_custom_call" | custom-call | tf_op jit(solution)/shard_map/base/pallas_call | solution.py:288
  44.9 0.3 base.4
  45.4 1.3 %finish.3.rest_0_ = bf16[256,2048]{1,0:T(8,128)(2,1)} custom-call(f32[256,1408]{1,0:T(8,128)S(1)} %get-tuple-element.68.base_ref, f32[256,1408]{1,0:T(8,128)S(1)} %get-tuple-element.69.spread_ref, bf16[8,256,256]{2,1,0:T(8,128)(2,1)S(1)} %get-tuple-element.62.other_a_ref, bf16[8,256,256]{2,1,0:T(8,128)(2,1)S(1)} %get-tuple-element.63.other_b_ref, ...), custom_call_target="tpu_custom_call" | custom-call | tf_op jit(solution)/shard_map/finish/pallas_call | solution.py:288
  46.7 1.7 %collective-permute-done.12.vr_ref = bf16[192,512]{1,0:T(8,128)(2,1)S(1)} collective-permute-done((bf16[192,512]{1,0:T(8,128)(2,1)S(1)}, bf16[192,512]{1,0:T(8,128)(2,1)S(1)}, u32[]{:S(2)}, u32[]{:S(2)}) %collective-permute-start.12) | collective-permute-done | bytes 196640 | tf_op jit(solution)/shard_map/ppermute | solution.py:22
  48.4 1.0 %finish.4.rest_0_ = bf16[256,2048]{1,0:T(8,128)(2,1)} custom-call(f32[256,512]{1,0:T(8,128)S(1)} %get-tuple-element.65.base_ref, f32[256,512]{1,0:T(8,128)S(1)} %get-tuple-element.66.spread_ref, bf16[8,256,256]{2,1,0:T(8,128)(2,1)S(1)} %get-tuple-element.62.other_a_ref, ...), custom_call_target="tpu_custom_call", output_to_operand_aliasing={{}: (6, {})} | custom-call | tf_op jit(solution)/shard_map/finish/pallas_call | solution.py:288
  49.4 0.8 %finish.5 = bf16[256,2048]{1,0:T(8,128)(2,1)} custom-call(f32[256,128]{1,0:T(8,128)S(1)} %get-tuple-element.60.base_ref, f32[256,128]{1,0:T(8,128)S(1)} %get-tuple-element.61.spread_ref, bf16[8,256,256]{2,1,0:T(8,128)(2,1)S(1)} %get-tuple-element.62.other_a_ref, ...), custom_call_target="tpu_custom_call", output_to_operand_aliasing={{}: (6, {})} | custom-call | tf_op jit(solution)/shard_map/finish/pallas_call | solution.py:288
  (20 shorter events, 0.3 us)
Async XLA Ops:
  0.0 27.3 %collective-permute-start.4 = (bf16[256,2048]{1,0:T(8,128)(2,1)}, bf16[256,2048]{1,0:T(8,128)(2,1)S(1)}, u32[]{:S(2)}, u32[]{:S(2)}) collective-permute-start(bf16[256,2048]{1,0:T(8,128)(2,1)} %k_hbm.1), channel_id=1, source_target_pairs={{0,8},{8,0},{16,24},{24,16},{1,9},{9,1},{17,25},{25,17},{2,10},{10... | collective-permute-start | bytes 3145736 | tf_op jit(solution)/shard_map/ppermute | solution.py:22
  2.9 0.7 %copy-start = (s32[16]{0:T(128)S(1)}, s32[16]{0:T(128)}, u32[]{:S(2)}) copy-start(s32[16]{0:T(128)} %middle_ref.11) | copy-start | bytes 196
  3.6 0.7 %copy-start.2 = (s32[16]{0:T(128)S(1)}, s32[16]{0:T(128)}, u32[]{:S(2)}) copy-start(s32[16]{0:T(128)} %coarse_ref.3) | copy-start | bytes 196
  4.3 14.0 %copy-start.1 = (s32[16]{0:T(128)S(1)}, s32[16]{0:T(128)}, u32[]{:S(2)}) copy-start(s32[16]{0:T(128)} %middle_ref.11) | copy-start | bytes 196
  7.5 16.7 %collective-permute-start.6 = (bf16[128,2048]{1,0:T(8,128)(2,1)S(1)}, bf16[128,2048]{1,0:T(8,128)(2,1)S(1)}, u32[]{:S(2)}, u32[]{:S(2)}) collective-permute-start(bf16[128,2048]{1,0:T(8,128)(2,1)S(1)} %get-tuple-element.49), channel_id=1, source_target_pairs={{0,16},{8,24},{16,0},{24,8},{1,17},{9,25},{17,1},{25,9},{2,18},{10... | collective-permute-start | bytes 1572872 | tf_op jit(solution)/shard_map/ppermute | solution.py:22
  9.1 4.7 %collective-permute-start = (bf16[2,2048]{1,0:T(2,128)(2,1)S(1)}, bf16[2,2048]{1,0:T(2,128)(2,1)S(1)}, u32[]{:S(2)}, u32[]{:S(2)}) collective-permute-start(bf16[2,2048]{1,0:T(2,128)(2,1)S(1)} %get-tuple-element.39.refs_0_), channel_id=1, source_target_pairs={{0,10},{1,11},{2,8},{3,9},{4,14},{5,15},{6,12},{7,13},{8,2},{9,3},... | collective-permute-start | bytes 24584 | tf_op jit(solution)/shard_map/ppermute | solution.py:32
  13.8 7.1 %collective-permute-start.1 = (bf16[4,2048]{1,0:T(4,128)(2,1)S(1)}, bf16[4,2048]{1,0:T(4,128)(2,1)S(1)}, u32[]{:S(2)}, u32[]{:S(2)}) collective-permute-start(bf16[4,2048]{1,0:T(4,128)(2,1)S(1)} %stack.2.refs_0_), channel_id=1, source_target_pairs={{0,2},{1,3},{2,0},{3,1},{4,6},{5,7},{6,4},{7,5},{8,10},{9,11},{10,... | collective-permute-start | bytes 49160 | tf_op jit(solution)/shard_map/ppermute | solution.py:22
  15.4 5.4 %collective-permute-start.2 = (bf16[4,2048]{1,0:T(4,128)(2,1)S(1)}, bf16[4,2048]{1,0:T(4,128)(2,1)S(1)}, u32[]{:S(2)}, u32[]{:S(2)}) collective-permute-start(bf16[4,2048]{1,0:T(4,128)(2,1)S(1)} %stack.2.refs_0_), channel_id=1, source_target_pairs={{0,4},{1,5},{2,6},{3,7},{4,0},{5,1},{6,2},{7,3},{8,12},{9,13},{10,... | collective-permute-start | bytes 49160 | tf_op jit(solution)/shard_map/ppermute | solution.py:22
  18.0 5.6 %collective-permute-start.3 = (bf16[4,2048]{1,0:T(4,128)(2,1)S(1)}, bf16[4,2048]{1,0:T(4,128)(2,1)S(1)}, u32[]{:S(2)}, u32[]{:S(2)}) collective-permute-start(bf16[4,2048]{1,0:T(4,128)(2,1)S(1)} %stack.2.refs_0_), channel_id=1, source_target_pairs={{0,6},{1,7},{2,4},{3,5},{4,2},{5,3},{6,0},{7,1},{8,14},{9,15},{10,... | collective-permute-start | bytes 49160 | tf_op jit(solution)/shard_map/ppermute | solution.py:22
  23.7 9.3 %collective-permute-start.7 = (bf16[64,2048]{1,0:T(8,128)(2,1)S(1)}, bf16[64,2048]{1,0:T(8,128)(2,1)S(1)}, u32[]{:S(2)}, u32[]{:S(2)}) collective-permute-start(bf16[64,2048]{1,0:T(8,128)(2,1)S(1)} %get-tuple-element.54), channel_id=1, source_target_pairs={{0,8},{8,0},{16,24},{24,16},{1,9},{9,1},{17,25},{25,17},{2,10},{10... | collective-permute-start | bytes 786440 | tf_op jit(solution)/shard_map/ppermute | solution.py:22
  24.1 10.9 %collective-permute-start.9 = (bf16[16,2048]{1,0:T(8,128)(2,1)S(1)}, bf16[16,2048]{1,0:T(8,128)(2,1)S(1)}, u32[]{:S(2)}, u32[]{:S(2)}) collective-permute-start(bf16[16,2048]{1,0:T(8,128)(2,1)S(1)} %stack.3), channel_id=1, source_target_pairs={{0,18},{1,19},{2,16},{3,17},{4,22},{5,23},{6,20},{7,21},{8,26},{9,... | collective-permute-start | bytes 196616 | tf_op jit(solution)/shard_map/ppermute | solution.py:32
  24.1 21.3 %collective-permute-start.13 = (bf16[192,1408]{1,0:T(8,128)(2,1)S(1)}, bf16[192,1408]{1,0:T(8,128)(2,1)S(1)}, u32[]{:S(2)}, u32[]{:S(2)}) collective-permute-start(bf16[192,1408]{1,0:T(8,128)(2,1)S(1)} %get-tuple-element.70), channel_id=1, source_target_pairs={{0,8},{8,0},{16,24},{24,16},{1,9},{9,1},{17,25},{25,17},{2,10},{10... | collective-permute-start | bytes 1622024 | tf_op jit(solution)/shard_map/ppermute | solution.py:22
  25.8 22.7 %collective-permute-start.12 = (bf16[192,512]{1,0:T(8,128)(2,1)S(1)}, bf16[192,512]{1,0:T(8,128)(2,1)S(1)}, u32[]{:S(2)}, u32[]{:S(2)}) collective-permute-start(bf16[192,512]{1,0:T(8,128)(2,1)S(1)} %get-tuple-element.67), channel_id=1, source_target_pairs={{0,8},{8,0},{16,24},{24,16},{1,9},{9,1},{17,25},{25,17},{2,10},{10... | collective-permute-start | bytes 589832 | tf_op jit(solution)/shard_map/ppermute | solution.py:22
  28.2 12.4 %copy-start.3 = (s32[16]{0:T(128)S(1)}, s32[16]{0:T(128)}, u32[]{:S(2)}) copy-start(s32[16]{0:T(128)} %coarse_ref.3) | copy-start | bytes 196
  28.2 7.6 %collective-permute-start.5 = (bf16[64,2048]{1,0:T(8,128)(2,1)S(1)}, bf16[64,2048]{1,0:T(8,128)(2,1)S(1)}, u32[]{:S(2)}, u32[]{:S(2)}) collective-permute-start(bf16[64,2048]{1,0:T(8,128)(2,1)S(1)} %pick.1), channel_id=1, source_target_pairs={{0,16},{8,24},{16,0},{24,8},{1,17},{9,25},{17,1},{25,9},{2,18},{10... | collective-permute-start | bytes 786440 | tf_op jit(solution)/shard_map/ppermute | solution.py:22
  32.9 7.6 %collective-permute-start.8 = (bf16[64,2048]{1,0:T(8,128)(2,1)S(1)}, bf16[64,2048]{1,0:T(8,128)(2,1)S(1)}, u32[]{:S(2)}, u32[]{:S(2)}) collective-permute-start(bf16[64,2048]{1,0:T(8,128)(2,1)S(1)} %collective-permute-done.7.vm_ref), channel_id=1, source_target_pairs={{0,16},{8,24},{16,0},{24,8},{1,17},{9,25},{17,1},{25,9},{2,18},{10... | collective-permute-start | bytes 786440 | tf_op jit(solution)/shard_map/ppermute | solution.py:22
  35.0 4.5 %collective-permute-start.10 = (bf16[32,2048]{1,0:T(8,128)(2,1)S(1)}, bf16[32,2048]{1,0:T(8,128)(2,1)S(1)}, u32[]{:S(2)}, u32[]{:S(2)}) collective-permute-start(bf16[32,2048]{1,0:T(8,128)(2,1)S(1)} %constant_dynamic-update-slice_fusion.mine_ref), channel_id=1, source_target_pairs={{0,1},{1,0},{2,3},{3,2},{4,5},{5,4},{6,7},{7,6},{8,9},{9,8},{10,11... | collective-permute-start | bytes 393224 | tf_op jit(solution)/shard_map/ppermute | solution.py:22
  35.8 13.6 %collective-permute-start.11 = (bf16[192,128]{1,0:T(8,128)(2,1)S(1)}, bf16[192,128]{1,0:T(8,128)(2,1)S(1)}, u32[]{:S(2)}, u32[]{:S(2)}) collective-permute-start(bf16[192,128]{1,0:T(8,128)(2,1)S(1)} %get-tuple-element.64), channel_id=1, source_target_pairs={{0,8},{8,0},{16,24},{24,16},{1,9},{9,1},{17,25},{25,17},{2,10},{10... | collective-permute-start | bytes 147464 | tf_op jit(solution)/shard_map/ppermute | solution.py:22

commit v14 on v12

--- a/solution.py
+++ b/solution.py
@@ -10,7 +10,7 @@
 HEAD_COUNT = 16
 HEAD_FEATURES = 128
 MIDDLE_DILATION = 4
-CHUNKS = (12, 4)
+CHUNKS = (11, 3, 2)
 LANES = 128
 SUBLANES = 16
 EXP2_SCALE = HEAD_FEATURES ** (-0.5) * 1.4426950408889634
@@ -130,34 +130,46 @@
     return jnp.exp2((part - top) * EXP2_SCALE)
 
 
-def first_kernel(first, middle_ref, q_ref, k_ref, v_ref, kp_ref, own_ref, other_ref, state_ref, order_ref):
+def own_kernel(q_ref, k_ref, scores_ref, top_ref):
+    tops = []
+    for head in range(HEAD_COUNT):
+        columns = head_columns(head)
+        own = dot_keys(q_ref[:, columns], k_ref[:, columns])
+        tops.append(jnp.max(functools.reduce(jnp.maximum, lane_tiles(own)), axis=1, keepdims=True))
+        scores_ref[head] = own
+    top_ref[...] = side_by_side(tops)
+
+
+def first_kernel(
+    first, middle_ref, q_ref, scores_ref, top_ref, v_ref, kp_ref, own_ref, other_ref, state_ref, order_ref
+):
     fill_orders(order_ref)
     rows = q_ref.shape[0]
     members = rows // MIDDLE_DILATION
     column = lax.broadcasted_iota(jnp.int32, (1, rows), 1)
     tops, totals = [], []
-    heads = other_ref.shape[0]
-    for place in range(heads):
-        columns = head_columns(first + place)
-        shift = middle_ref[first + place]
-        q = q_ref[:, columns]
-        own = dot_keys(q, k_ref[:, columns])
+    for place in range(other_ref.shape[0]):
+        head = first + place
+        columns = head_columns(head)
+        shift = middle_ref[head]
+        row_is_member = member_rows(rows, shift)
         other_keys = dot(order_ref[shift], kp_ref[:, columns]).astype(jnp.bfloat16)
-        other = dot_keys(q, other_keys)
-        top = functools.reduce(jnp.maximum, lane_tiles(own) + lane_tiles(other))
-        top = jnp.max(top, axis=1, keepdims=True)
-        row_is_member = member_rows(rows, shift)
-        own, other = weights(own, top), weights(other, top)
-        own_member = row_is_member & ((column & (MIDDLE_DILATION - 1)) == shift)
-        own = jnp.where(own_member, own + own, own)
+        other = dot_keys(q_ref[:, columns], other_keys)
+        top = jnp.max(functools.reduce(jnp.maximum, lane_tiles(other)), axis=1, keepdims=True)
+        top = jnp.maximum(top, top_ref[:, head : head + 1])
+        other = weights(other, top)
         twice = other[:, :LANES]
         twice = jnp.where(row_is_member & (column[:, :LANES] < members), twice + twice, twice)
         other = jnp.concatenate([twice, other[:, LANES:]], axis=1)
-        total = functools.reduce(jnp.add, lane_tiles(own) + lane_tiles(other))
+        total = functools.reduce(jnp.add, lane_tiles(other))
+        other_ref[place] = other.astype(jnp.bfloat16)
+        own = weights(scores_ref[head], top)
+        own_member = row_is_member & ((column & (MIDDLE_DILATION - 1)) == shift)
+        own = jnp.where(own_member, own + own, own)
+        total = functools.reduce(jnp.add, lane_tiles(own), total)
         tops.append(top)
         totals.append(jnp.sum(total, axis=1, keepdims=True))
         own_ref[:, head_columns(place)] = dot(own.astype(jnp.bfloat16), v_ref[:, columns])
-        other_ref[place] = other.astype(jnp.bfloat16)
     state_ref[...] = side_by_side(tops + totals)
 
 
@@ -294,7 +306,15 @@
     )
     cross = partner(own_members, "inner", 2)
     near = gather_upper(stack(coarse, partner_elsewhere(coarse, 1)), "outer")
-    near, own_vm = lax.optimization_barrier((near, own_vm))
+    own_scores, own_top = call(
+        own_kernel,
+        "own",
+        q, k,
+        out_shape=[pltpu.VMEM((HEAD_COUNT, rows, rows), f32), pltpu.VMEM((rows, LANES), f32)],
+        in_specs=[vmem] * 2,
+        out_specs=[vmem] * 2,
+    )
+    near, own_vm, own_top = lax.optimization_barrier((near, own_vm, own_top))
     other_vm = partner(own_vm, "inner", 1)
     cross, own_vr = lax.optimization_barrier((cross, own_vr))
     other_vr = [partner(piece, "inner", 1) for piece in own_vr]
@@ -313,13 +333,13 @@
         return call(
             functools.partial(first_kernel, first),
             "first",
-            middle_head_shift, query, k, v, other_keys,
+            middle_head_shift, query, own_scores, own_top, v, other_keys,
             out_shape=[
                 pltpu.VMEM((rows, half * HEAD_FEATURES), f32),
                 pltpu.VMEM((half, rows, rows), bf16),
                 pltpu.VMEM((rows, LANES), f32),
             ],
-            in_specs=[smem] + [vmem] * 4,
+            in_specs=[smem] + [vmem] * 5,
             out_specs=[vmem] * 3,
             scratch_shapes=[orders],
         )

time: 50.1 us -> 50.2 us (level)
  waiting for transfers between devices: 13 us -> 10.6 us
  starting transfers between devices: 15.5 us -> 17.1 us
  Pallas kernels: 20 us -> 20.9 us
    ppermute x11 -> x12, waiting for transfers between devices: 9.84 us -> 7.47 us  [partner(): return lax.ppermute(value, axis, pairs)]
    ppermute x11 -> x12, starting transfers between devices: 14 us -> 15.5 us  [partner(): return lax.ppermute(value, axis, pairs)]
    pallas_call x9 -> x12, Pallas kernels: 20 us -> 20.8 us  [call(): pl.pallas_call(kernel, name=name, compiler_params=params, cost_estimate=c...]
  transfers between devices with their start and end apart: 13 -> 14, of which waited for: 7 -> 5; matrix products, arithmetic and copies ran while one was open for 0% -> 0% of each run, Pallas kernels for 38% -> 40%
where the time goes in v14:
time: 50.2 us; the launch traced here: 50 us
  Pallas kernels  20.9 us (42%)
  starting transfers between devices  17.1 us (34%)
  waiting for transfers between devices  10.6 us (21%)
  local copies, waits for them, and re-layouts  1.33 us (3%)
    pallas_call x12, Pallas kernels, call(): pl.pallas_call(kernel, name=name, compiler_params=params, cost_estimate=c...  20.8 us
    ppermute x12, starting transfers between devices, partner(): return lax.ppermute(value, axis, pairs)  15.5 us
    ppermute x12, waiting for transfers between devices, partner(): return lax.ppermute(value, axis, pairs)  7.47 us
    ppermute x2, waiting for transfers between devices, partner_elsewhere(): return lax.ppermute(value, ('inner', 'outer'), pairs)  3.11 us
    ppermute x2, starting transfers between devices, partner_elsewhere(): return lax.ppermute(value, ('inner', 'outer'), pairs)  1.55 us
    unnamed x9, local copies, waits for them, and re-layouts  1.32 us
  transfers between devices with their start and end apart: 14, of which 5 were waited for; matrix products, arithmetic and copies ran while one was open for 0% of the time, Pallas kernels for 40%

profile of v14, /device:TPU:0, one launch (start us, length us, event | category | flops | bytes accessed | tf_op | source)
XLA Modules:
  0.0 50.0 jit_solution(11548297143725084009)
XLA Ops:
  0.0 2.9 %collective-permute-start.4 = (bf16[256,2048]{1,0:T(8,128)(2,1)}, bf16[256,2048]{1,0:T(8,128)(2,1)S(1)}, u32[]{:S(2)}, u32[]{:S(2)}) collective-permute-start(bf16[256,2048]{1,0:T(8,128)(2,1)} %k_hbm.1), channel_id=1, source_target_pairs={{0,8},{8,0},{16,24},{24,16},{1,9},{9,1},{17,25},{25,17},{2,10},{10... | collective-permute-start | bytes 3145736 | tf_op jit(solution)/shard_map/ppermute | solution.py:22
  2.9 0.7 %copy-done = s32[16]{0:T(128)S(1)} copy-done((s32[16]{0:T(128)S(1)}, s32[16]{0:T(128)}, u32[]{:S(2)}) %copy-start) | copy-done | bytes 88
  3.6 0.7 %copy-done.2 = s32[16]{0:T(128)S(1)} copy-done((s32[16]{0:T(128)S(1)}, s32[16]{0:T(128)}, u32[]{:S(2)}) %copy-start.2) | copy-done | bytes 88
  4.3 3.2 %prepare.1 = (bf16[256,2048]{1,0:T(8,128)(2,1)S(1)}, bf16[256,2048]{1,0:T(8,128)(2,1)S(1)}, bf16[256,2048]{1,0:T(8,128)(2,1)S(1)}, bf16[128,2048]{1,0:T(8,128)(2...) custom-call(s32[16]{0:T(128)S(1)} %copy-done, ...), custom_call_target="tpu_custom_call" | custom-call | tf_op jit(solution)/shard_map/prepare/pallas_call | solution.py:289
  7.5 1.6 %collective-permute-start.6 = (bf16[128,2048]{1,0:T(8,128)(2,1)S(1)}, bf16[128,2048]{1,0:T(8,128)(2,1)S(1)}, u32[]{:S(2)}, u32[]{:S(2)}) collective-permute-start(bf16[128,2048]{1,0:T(8,128)(2,1)S(1)} %get-tuple-element.52), channel_id=1, source_target_pairs={{0,16},{8,24},{16,0},{24,8},{1,17},{9,25},{17,1},{25,9},{2,18},{10... | collective-permute-start | bytes 1572872 | tf_op jit(solution)/shard_map/ppermute | solution.py:22
  9.1 1.5 %collective-permute-start = (bf16[2,2048]{1,0:T(2,128)(2,1)S(1)}, bf16[2,2048]{1,0:T(2,128)(2,1)S(1)}, u32[]{:S(2)}, u32[]{:S(2)}) collective-permute-start(bf16[2,2048]{1,0:T(2,128)(2,1)S(1)} %get-tuple-element.43.refs_0_), channel_id=1, source_target_pairs={{0,10},{1,11},{2,8},{3,9},{4,14},{5,15},{6,12},{7,13},{8,2},{9,3},... | collective-permute-start | bytes 24584 | tf_op jit(solution)/shard_map/ppermute | solution.py:32
  10.6 3.1 %collective-permute-done.refs_1_ = bf16[2,2048]{1,0:T(2,128)(2,1)S(1)} collective-permute-done((bf16[2,2048]{1,0:T(2,128)(2,1)S(1)}, bf16[2,2048]{1,0:T(2,128)(2,1)S(1)}, u32[]{:S(2)}, u32[]{:S(2)}) %collective-permute-start) | collective-permute-done | bytes 8224 | tf_op jit(solution)/shard_map/ppermute | solution.py:32
  13.8 1.6 %collective-permute-start.1 = (bf16[4,2048]{1,0:T(4,128)(2,1)S(1)}, bf16[4,2048]{1,0:T(4,128)(2,1)S(1)}, u32[]{:S(2)}, u32[]{:S(2)}) collective-permute-start(bf16[4,2048]{1,0:T(4,128)(2,1)S(1)} %stack.2.refs_0_), channel_id=1, source_target_pairs={{0,2},{1,3},{2,0},{3,1},{4,6},{5,7},{6,4},{7,5},{8,10},{9,11},{10,... | collective-permute-start | bytes 49160 | tf_op jit(solution)/shard_map/ppermute | solution.py:22
  15.4 2.6 %collective-permute-start.2 = (bf16[4,2048]{1,0:T(4,128)(2,1)S(1)}, bf16[4,2048]{1,0:T(4,128)(2,1)S(1)}, u32[]{:S(2)}, u32[]{:S(2)}) collective-permute-start(bf16[4,2048]{1,0:T(4,128)(2,1)S(1)} %stack.2.refs_0_), channel_id=1, source_target_pairs={{0,4},{1,5},{2,6},{3,7},{4,0},{5,1},{6,2},{7,3},{8,12},{9,13},{10,... | collective-permute-start | bytes 49160 | tf_op jit(solution)/shard_map/ppermute | solution.py:22
  18.0 0.2 collective-permute-start.3
  18.2 0.8 %own.1 = (f32[16,256,256]{2,1,0:T(8,128)S(1)}, f32[256,128]{1,0:T(8,128)S(1)}) custom-call(bf16[256,2048]{1,0:T(8,128)(2,1)S(1)} %get-tuple-element.50.q_ref, bf16[256,2048]{1,0:T(8,128)(2,1)S(1)} %get-tuple-element.41.k_ref), custom_call_target="tpu_custom_call" | custom-call | tf_op jit(solution)/shard_map/own/pallas_call | solution.py:289
  19.1 1.2 %collective-permute-done.2.refs_2_ = bf16[4,2048]{1,0:T(4,128)(2,1)S(1)} collective-permute-done((bf16[4,2048]{1,0:T(4,128)(2,1)S(1)}, bf16[4,2048]{1,0:T(4,128)(2,1)S(1)}, u32[]{:S(2)}, u32[]{:S(2)}) %collective-permute-start.2) | collective-permute-done | bytes 16416 | tf_op jit(solution)/shard_map/ppermute | solution.py:22
  20.3 3.4 %collective-permute-done.3.refs_3_ = bf16[4,2048]{1,0:T(4,128)(2,1)S(1)} collective-permute-done((bf16[4,2048]{1,0:T(4,128)(2,1)S(1)}, bf16[4,2048]{1,0:T(4,128)(2,1)S(1)}, u32[]{:S(2)}, u32[]{:S(2)}) %collective-permute-start.3) | collective-permute-done | bytes 16416 | tf_op jit(solution)/shard_map/ppermute | solution.py:22
  23.7 0.5 collective-permute-start.7
  24.2 1.6 %collective-permute-start.13 = (bf16[192,1408]{1,0:T(8,128)(2,1)S(1)}, bf16[192,1408]{1,0:T(8,128)(2,1)S(1)}, u32[]{:S(2)}, u32[]{:S(2)}) collective-permute-start(bf16[192,1408]{1,0:T(8,128)(2,1)S(1)} %get-tuple-element.74), channel_id=1, source_target_pairs={{0,8},{8,0},{16,24},{24,16},{1,9},{9,1},{17,25},{25,17},{2,10},{10... | collective-permute-start | bytes 1622024 | tf_op jit(solution)/shard_map/ppermute | solution.py:22
  25.8 1.6 %collective-permute-done.4.k_ref.kp_ref = bf16[256,2048]{1,0:T(8,128)(2,1)S(1)} collective-permute-done((bf16[256,2048]{1,0:T(8,128)(2,1)}, bf16[256,2048]{1,0:T(8,128)(2,1)S(1)}, u32[]{:S(2)}, u32[]{:S(2)}) %collective-permute-start.4) | collective-permute-done | bytes 1048608 | tf_op jit(solution)/shard_map/ppermute | solution.py:22
  27.3 0.8 %pick.1 = bf16[64,2048]{1,0:T(8,128)(2,1)S(1)} custom-call(s32[16]{0:T(128)S(1)} %copy-done.1, bf16[256,2048]{1,0:T(8,128)(2,1)S(1)} %collective-permute-done.4.k_ref.kp_ref), custom_call_target="tpu_custom_call" | custom-call | tf_op jit(solution)/shard_map/pick/pallas_call | solution.py:289
  28.2 2.2 %collective-permute-start.5 = (bf16[64,2048]{1,0:T(8,128)(2,1)S(1)}, bf16[64,2048]{1,0:T(8,128)(2,1)S(1)}, u32[]{:S(2)}, u32[]{:S(2)}) collective-permute-start(bf16[64,2048]{1,0:T(8,128)(2,1)S(1)} %pick.1), channel_id=1, source_target_pairs={{0,16},{8,24},{16,0},{24,8},{1,17},{9,25},{17,1},{25,9},{2,18},{10... | collective-permute-start | bytes 786440 | tf_op jit(solution)/shard_map/ppermute | solution.py:22
  30.3 1.5 %collective-permute-start.12 = (bf16[192,384]{1,0:T(8,128)(2,1)S(1)}, bf16[192,384]{1,0:T(8,128)(2,1)S(1)}, u32[]{:S(2)}, u32[]{:S(2)}) collective-permute-start(bf16[192,384]{1,0:T(8,128)(2,1)S(1)} %get-tuple-element.71), channel_id=1, source_target_pairs={{0,8},{8,0},{16,24},{24,16},{1,9},{9,1},{17,25},{25,17},{2,10},{10... | collective-permute-start | bytes 442376 | tf_op jit(solution)/shard_map/ppermute | solution.py:22
  31.8 4.2 %first.2 = (f32[256,1024]{1,0:T(8,128)S(1)}, bf16[8,256,256]{2,1,0:T(8,128)(2,1)S(1)}, f32[256,128]{1,0:T(8,128)S(1)}) custom-call(s32[16]{0:T(128)S(1)} %copy-done.1, bf16[256,2048]{1,0:T(8,128)(2,1)S(1)} %get-tuple-element.50.q_ref, f32[16,256,256]{2,1,0:T(8,128)S(1)} %get-tuple-element.42.scores_ref, f32[256,128]{1,0:T(8,128)S(1)} %get-tuple-element.46.top_ref, ...), custom_call_target="tpu_custom_call" | custom-call | tf_op jit(solution)/shard_map/first/pallas_call | solution.py:289
  36.1 0.6 %collective-permute-start.8 = (bf16[64,2048]{1,0:T(8,128)(2,1)S(1)}, bf16[64,2048]{1,0:T(8,128)(2,1)S(1)}, u32[]{:S(2)}, u32[]{:S(2)}) collective-permute-start(bf16[64,2048]{1,0:T(8,128)(2,1)S(1)} %collective-permute-done.7.vm_ref), channel_id=1, source_target_pairs={{0,16},{8,24},{16,0},{24,8},{1,17},{9,25},{17,1},{25,9},{2,18},{10... | collective-permute-start | bytes 786440 | tf_op jit(solution)/shard_map/ppermute | solution.py:22
  36.7 0.1 collective-permute-start.10
  36.7 0.2 collective-permute-start.11
  36.9 4.2 %first.3 = (f32[256,1024]{1,0:T(8,128)S(1)}, bf16[8,256,256]{2,1,0:T(8,128)(2,1)S(1)}, f32[256,128]{1,0:T(8,128)S(1)}) custom-call(s32[16]{0:T(128)S(1)} %copy-done.1, bf16[256,2048]{1,0:T(8,128)(2,1)S(1)} %get-tuple-element.50.q_ref, f32[16,256,256]{2,1,0:T(8,128)S(1)} %get-tuple-element.42.scores_ref, f32[256,128]{1,0:T(8,128)S(1)} %get-tuple-element.46.top_ref, ...), custom_call_target="tpu_custom_call" | custom-call | tf_op jit(solution)/shard_map/first/pallas_call | solution.py:289
  41.2 1.3 %collective-permute-done.8.diagonal_v_ref = bf16[64,2048]{1,0:T(8,128)(2,1)S(1)} collective-permute-done((bf16[64,2048]{1,0:T(8,128)(2,1)S(1)}, bf16[64,2048]{1,0:T(8,128)(2,1)S(1)}, u32[]{:S(2)}, u32[]{:S(2)}) %collective-permute-start.8) | collective-permute-done | bytes 262176 | tf_op jit(solution)/shard_map/ppermute | solution.py:22
  42.5 3.5 %extra.1 = (f32[256,2048]{1,0:T(8,128)S(1)}, f32[256,128]{1,0:T(8,128)S(1)}) custom-call(s32[16]{0:T(128)S(1)} %copy-done.1, s32[16]{0:T(128)S(1)} %copy-done.3, bf16[256,2048]{1,0:T(8,128)(2,1)S(1)} %get-tuple-element.50.q_ref, f32[256,128]{1,0:T(8,128)S(1)} %get-tuple-element.49.state_a_ref, f32[256,128]{1,0:T(8,128)S(1)} %get-tuple-element.51.state_b_ref, ...), custom_call_target="tpu_custom_call" | custom-call | tf_op jit(solution)/shard_map/extra/pallas_call | solution.py:289
  46.0 0.1 base.3
  46.1 0.2 base.4
  46.3 0.5 base.5
  46.8 1.3 %finish.3.rest_0_ = bf16[256,2048]{1,0:T(8,128)(2,1)} custom-call(f32[256,1408]{1,0:T(8,128)S(1)} %get-tuple-element.72.base_ref, f32[256,1408]{1,0:T(8,128)S(1)} %get-tuple-element.73.spread_ref, bf16[8,256,256]{2,1,0:T(8,128)(2,1)S(1)} %get-tuple-element.66.other_a_ref, bf16[8,256,256]{2,1,0:T(8,128)(2,1)S(1)} %get-tuple-element.67.other_b_ref, ...), custom_call_target="tpu_custom_call" | custom-call | tf_op jit(solution)/shard_map/finish/pallas_call | solution.py:289
  48.2 0.9 %finish.4.rest_0_ = bf16[256,2048]{1,0:T(8,128)(2,1)} custom-call(f32[256,384]{1,0:T(8,128)S(1)} %get-tuple-element.69.base_ref, f32[256,384]{1,0:T(8,128)S(1)} %get-tuple-element.70.spread_ref, bf16[8,256,256]{2,1,0:T(8,128)(2,1)S(1)} %get-tuple-element.66.other_a_ref, ...), custom_call_target="tpu_custom_call", output_to_operand_aliasing={{}: (6, {})} | custom-call | tf_op jit(solution)/shard_map/finish/pallas_call | solution.py:289
  49.1 0.9 %finish.5 = bf16[256,2048]{1,0:T(8,128)(2,1)} custom-call(f32[256,256]{1,0:T(8,128)S(1)} %get-tuple-element.64.base_ref, f32[256,256]{1,0:T(8,128)S(1)} %get-tuple-element.65.spread_ref, bf16[8,256,256]{2,1,0:T(8,128)(2,1)S(1)} %get-tuple-element.66.other_a_ref, ...), custom_call_target="tpu_custom_call", output_to_operand_aliasing={{}: (6, {})} | custom-call | tf_op jit(solution)/shard_map/finish/pallas_call | solution.py:289
  (20 shorter events, 0.1 us)
Async XLA Ops:
  0.0 27.3 %collective-permute-start.4 = (bf16[256,2048]{1,0:T(8,128)(2,1)}, bf16[256,2048]{1,0:T(8,128)(2,1)S(1)}, u32[]{:S(2)}, u32[]{:S(2)}) collective-permute-start(bf16[256,2048]{1,0:T(8,128)(2,1)} %k_hbm.1), channel_id=1, source_target_pairs={{0,8},{8,0},{16,24},{24,16},{1,9},{9,1},{17,25},{25,17},{2,10},{10... | collective-permute-start | bytes 3145736 | tf_op jit(solution)/shard_map/ppermute | solution.py:22
  2.9 0.7 %copy-start = (s32[16]{0:T(128)S(1)}, s32[16]{0:T(128)}, u32[]{:S(2)}) copy-start(s32[16]{0:T(128)} %middle_ref.9) | copy-start | bytes 196
  3.6 0.7 %copy-start.2 = (s32[16]{0:T(128)S(1)}, s32[16]{0:T(128)}, u32[]{:S(2)}) copy-start(s32[16]{0:T(128)} %coarse_ref.3) | copy-start | bytes 196
  4.3 23.1 %copy-start.1 = (s32[16]{0:T(128)S(1)}, s32[16]{0:T(128)}, u32[]{:S(2)}) copy-start(s32[16]{0:T(128)} %middle_ref.9) | copy-start | bytes 196
  7.5 16.7 %collective-permute-start.6 = (bf16[128,2048]{1,0:T(8,128)(2,1)S(1)}, bf16[128,2048]{1,0:T(8,128)(2,1)S(1)}, u32[]{:S(2)}, u32[]{:S(2)}) collective-permute-start(bf16[128,2048]{1,0:T(8,128)(2,1)S(1)} %get-tuple-element.52), channel_id=1, source_target_pairs={{0,16},{8,24},{16,0},{24,8},{1,17},{9,25},{17,1},{25,9},{2,18},{10... | collective-permute-start | bytes 1572872 | tf_op jit(solution)/shard_map/ppermute | solution.py:22
  9.1 4.7 %collective-permute-start = (bf16[2,2048]{1,0:T(2,128)(2,1)S(1)}, bf16[2,2048]{1,0:T(2,128)(2,1)S(1)}, u32[]{:S(2)}, u32[]{:S(2)}) collective-permute-start(bf16[2,2048]{1,0:T(2,128)(2,1)S(1)} %get-tuple-element.43.refs_0_), channel_id=1, source_target_pairs={{0,10},{1,11},{2,8},{3,9},{4,14},{5,15},{6,12},{7,13},{8,2},{9,3},... | collective-permute-start | bytes 24584 | tf_op jit(solution)/shard_map/ppermute | solution.py:32
  13.8 5.3 %collective-permute-start.1 = (bf16[4,2048]{1,0:T(4,128)(2,1)S(1)}, bf16[4,2048]{1,0:T(4,128)(2,1)S(1)}, u32[]{:S(2)}, u32[]{:S(2)}) collective-permute-start(bf16[4,2048]{1,0:T(4,128)(2,1)S(1)} %stack.2.refs_0_), channel_id=1, source_target_pairs={{0,2},{1,3},{2,0},{3,1},{4,6},{5,7},{6,4},{7,5},{8,10},{9,11},{10,... | collective-permute-start | bytes 49160 | tf_op jit(solution)/shard_map/ppermute | solution.py:22
  15.4 4.9 %collective-permute-start.2 = (bf16[4,2048]{1,0:T(4,128)(2,1)S(1)}, bf16[4,2048]{1,0:T(4,128)(2,1)S(1)}, u32[]{:S(2)}, u32[]{:S(2)}) collective-permute-start(bf16[4,2048]{1,0:T(4,128)(2,1)S(1)} %stack.2.refs_0_), channel_id=1, source_target_pairs={{0,4},{1,5},{2,6},{3,7},{4,0},{5,1},{6,2},{7,3},{8,12},{9,13},{10,... | collective-permute-start | bytes 49160 | tf_op jit(solution)/shard_map/ppermute | solution.py:22
  18.0 5.6 %collective-permute-start.3 = (bf16[4,2048]{1,0:T(4,128)(2,1)S(1)}, bf16[4,2048]{1,0:T(4,128)(2,1)S(1)}, u32[]{:S(2)}, u32[]{:S(2)}) collective-permute-start(bf16[4,2048]{1,0:T(4,128)(2,1)S(1)} %stack.2.refs_0_), channel_id=1, source_target_pairs={{0,6},{1,7},{2,4},{3,5},{4,2},{5,3},{6,0},{7,1},{8,14},{9,15},{10,... | collective-permute-start | bytes 49160 | tf_op jit(solution)/shard_map/ppermute | solution.py:22
  23.7 12.4 %collective-permute-start.7 = (bf16[64,2048]{1,0:T(8,128)(2,1)S(1)}, bf16[64,2048]{1,0:T(8,128)(2,1)S(1)}, u32[]{:S(2)}, u32[]{:S(2)}) collective-permute-start(bf16[64,2048]{1,0:T(8,128)(2,1)S(1)} %get-tuple-element.57), channel_id=1, source_target_pairs={{0,8},{8,0},{16,24},{24,16},{1,9},{9,1},{17,25},{25,17},{2,10},{10... | collective-permute-start | bytes 786440 | tf_op jit(solution)/shard_map/ppermute | solution.py:22
  24.2 12.5 %collective-permute-start.9 = (bf16[16,2048]{1,0:T(8,128)(2,1)S(1)}, bf16[16,2048]{1,0:T(8,128)(2,1)S(1)}, u32[]{:S(2)}, u32[]{:S(2)}) collective-permute-start(bf16[16,2048]{1,0:T(8,128)(2,1)S(1)} %stack.3), channel_id=1, source_target_pairs={{0,18},{1,19},{2,16},{3,17},{4,22},{5,23},{6,20},{7,21},{8,26},{9,... | collective-permute-start | bytes 196616 | tf_op jit(solution)/shard_map/ppermute | solution.py:32
  24.2 22.6 %collective-permute-start.13 = (bf16[192,1408]{1,0:T(8,128)(2,1)S(1)}, bf16[192,1408]{1,0:T(8,128)(2,1)S(1)}, u32[]{:S(2)}, u32[]{:S(2)}) collective-permute-start(bf16[192,1408]{1,0:T(8,128)(2,1)S(1)} %get-tuple-element.74), channel_id=1, source_target_pairs={{0,8},{8,0},{16,24},{24,16},{1,9},{9,1},{17,25},{25,17},{2,10},{10... | collective-permute-start | bytes 1622024 | tf_op jit(solution)/shard_map/ppermute | solution.py:22
  28.2 8.6 %collective-permute-start.5 = (bf16[64,2048]{1,0:T(8,128)(2,1)S(1)}, bf16[64,2048]{1,0:T(8,128)(2,1)S(1)}, u32[]{:S(2)}, u32[]{:S(2)}) collective-permute-start(bf16[64,2048]{1,0:T(8,128)(2,1)S(1)} %pick.1), channel_id=1, source_target_pairs={{0,16},{8,24},{16,0},{24,8},{1,17},{9,25},{17,1},{25,9},{2,18},{10... | collective-permute-start | bytes 786440 | tf_op jit(solution)/shard_map/ppermute | solution.py:22
  30.3 17.8 %collective-permute-start.12 = (bf16[192,384]{1,0:T(8,128)(2,1)S(1)}, bf16[192,384]{1,0:T(8,128)(2,1)S(1)}, u32[]{:S(2)}, u32[]{:S(2)}) collective-permute-start(bf16[192,384]{1,0:T(8,128)(2,1)S(1)} %get-tuple-element.71), channel_id=1, source_target_pairs={{0,8},{8,0},{16,24},{24,16},{1,9},{9,1},{17,25},{25,17},{2,10},{10... | collective-permute-start | bytes 442376 | tf_op jit(solution)/shard_map/ppermute | solution.py:22
  36.1 6.4 %collective-permute-start.8 = (bf16[64,2048]{1,0:T(8,128)(2,1)S(1)}, bf16[64,2048]{1,0:T(8,128)(2,1)S(1)}, u32[]{:S(2)}, u32[]{:S(2)}) collective-permute-start(bf16[64,2048]{1,0:T(8,128)(2,1)S(1)} %collective-permute-done.7.vm_ref), channel_id=1, source_target_pairs={{0,16},{8,24},{16,0},{24,8},{1,17},{9,25},{17,1},{25,9},{2,18},{10... | collective-permute-start | bytes 786440 | tf_op jit(solution)/shard_map/ppermute | solution.py:22
  36.6 5.9 %copy-start.3 = (s32[16]{0:T(128)S(1)}, s32[16]{0:T(128)}, u32[]{:S(2)}) copy-start(s32[16]{0:T(128)} %coarse_ref.3) | copy-start | bytes 196
  36.7 4.5 %collective-permute-start.10 = (bf16[32,2048]{1,0:T(8,128)(2,1)S(1)}, bf16[32,2048]{1,0:T(8,128)(2,1)S(1)}, u32[]{:S(2)}, u32[]{:S(2)}) collective-permute-start(bf16[32,2048]{1,0:T(8,128)(2,1)S(1)} %constant_dynamic-update-slice_fusion.mine_ref), channel_id=1, source_target_pairs={{0,1},{1,0},{2,3},{3,2},{4,5},{5,4},{6,7},{7,6},{8,9},{9,8},{10,11... | collective-permute-start | bytes 393224 | tf_op jit(solution)/shard_map/ppermute | solution.py:22
  36.7 12.4 %collective-permute-start.11 = (bf16[192,256]{1,0:T(8,128)(2,1)S(1)}, bf16[192,256]{1,0:T(8,128)(2,1)S(1)}, u32[]{:S(2)}, u32[]{:S(2)}) collective-permute-start(bf16[192,256]{1,0:T(8,128)(2,1)S(1)} %get-tuple-element.68), channel_id=1, source_target_pairs={{0,8},{8,0},{16,24},{24,16},{1,9},{9,1},{17,25},{25,17},{2,10},{10... | collective-permute-start | bytes 294920 | tf_op jit(solution)/shard_map/ppermute | solution.py:22

commit v15 on v13

--- a/solution.py
+++ b/solution.py
@@ -10,7 +10,7 @@
 HEAD_COUNT = 16
 HEAD_FEATURES = 128
 MIDDLE_DILATION = 4
-CHUNKS = (11, 4, 1)
+CHUNKS = (12, 3, 1)
 LANES = 128
 SUBLANES = 16
 EXP2_SCALE = HEAD_FEATURES ** (-0.5) * 1.4426950408889634
@@ -130,36 +130,30 @@
     return jnp.exp2((part - top) * EXP2_SCALE)
 
 
-def own_kernel(middle_ref, q_ref, k_ref, v_ref, sum_ref, state_ref):
-    rows = q_ref.shape[0]
-    column = lax.broadcasted_iota(jnp.int32, (1, rows), 1)
-    tops, totals = [], []
+def score_kernel(q_ref, k_ref, scores_ref, top_ref):
+    tops = []
     for head in range(HEAD_COUNT):
         columns = head_columns(head)
-        shift = middle_ref[head]
         own = dot_keys(q_ref[:, columns], k_ref[:, columns])
-        top = jnp.max(functools.reduce(jnp.maximum, lane_tiles(own)), axis=1, keepdims=True)
-        own = weights(own, top)
-        twice = member_rows(rows, shift) & ((column & (MIDDLE_DILATION - 1)) == shift)
-        own = jnp.where(twice, own + own, own)
-        tops.append(top)
-        totals.append(jnp.sum(functools.reduce(jnp.add, lane_tiles(own)), axis=1, keepdims=True))
-        sum_ref[:, columns] = dot(own.astype(jnp.bfloat16), v_ref[:, columns])
-    state_ref[...] = side_by_side(tops + totals)
-
-
-def other_kernel(first, middle_ref, q_ref, kp_ref, other_ref, state_ref, order_ref):
+        tops.append(jnp.max(functools.reduce(jnp.maximum, lane_tiles(own)), axis=1, keepdims=True))
+        scores_ref[head] = own
+    top_ref[...] = side_by_side(tops)
+
+
+def other_kernel(first, middle_ref, q_ref, own_top_ref, kp_ref, other_ref, state_ref, order_ref):
     fill_orders(order_ref)
     rows = q_ref.shape[0]
     members = rows // MIDDLE_DILATION
     column = lax.broadcasted_iota(jnp.int32, (1, LANES), 1)
     tops, totals = [], []
     for place in range(other_ref.shape[0]):
-        columns = head_columns(first + place)
-        shift = middle_ref[first + place]
+        head = first + place
+        columns = head_columns(head)
+        shift = middle_ref[head]
         other_keys = dot(order_ref[shift], kp_ref[:, columns]).astype(jnp.bfloat16)
         other = dot_keys(q_ref[:, columns], other_keys)
         top = jnp.max(functools.reduce(jnp.maximum, lane_tiles(other)), axis=1, keepdims=True)
+        top = jnp.maximum(top, own_top_ref[:, head : head + 1])
         other = weights(other, top)
         twice = other[:, :LANES]
         twice = jnp.where(member_rows(rows, shift) & (column < members), twice + twice, twice)
@@ -170,8 +164,25 @@
     state_ref[...] = side_by_side(tops + totals)
 
 
+def own_kernel(middle_ref, scores_ref, state_a_ref, state_b_ref, v_ref, sum_ref, total_ref):
+    rows = v_ref.shape[0]
+    half = HEAD_COUNT // 2
+    column = lax.broadcasted_iota(jnp.int32, (1, rows), 1)
+    totals = []
+    for head in range(HEAD_COUNT):
+        columns = head_columns(head)
+        shift = middle_ref[head]
+        place = head % half
+        own = weights(scores_ref[head], (state_a_ref, state_b_ref)[head // half][:, place : place + 1])
+        twice = member_rows(rows, shift) & ((column & (MIDDLE_DILATION - 1)) == shift)
+        own = jnp.where(twice, own + own, own)
+        totals.append(jnp.sum(functools.reduce(jnp.add, lane_tiles(own)), axis=1, keepdims=True))
+        sum_ref[:, columns] = dot(own.astype(jnp.bfloat16), v_ref[:, columns])
+    total_ref[...] = side_by_side(totals)
+
+
 def extra_kernel(
-    middle_ref, coarse_ref, q_ref, own_state_ref, state_a_ref, state_b_ref, cross_ref, diagonal_k_ref, diagonal_v_ref, mine_ref,
+    middle_ref, coarse_ref, q_ref, own_total_ref, state_a_ref, state_b_ref, cross_ref, diagonal_k_ref, diagonal_v_ref, mine_ref,
     other_ref, sum_ref, share_ref,
 ):
     rows = q_ref.shape[0]
@@ -180,9 +191,9 @@
     far_rows, coarse_rows = 2 * members, 2 * mine_ref.shape[0]
     token = lax.broadcasted_iota(jnp.int32, (1, rows), 1)
     is_key = (lax.broadcasted_iota(jnp.int32, (coarse_rows, 1), 0) & 1) == 0
-    own_state = own_state_ref[...].T
+    own_totals = own_total_ref[...].T
     states = [ref[...].T for ref in (state_a_ref, state_b_ref)]
-    own_shares, other_shares = [], []
+    shares = []
     for head in range(HEAD_COUNT):
         columns = head_columns(head)
         state, place = states[head // half], head % half
@@ -192,31 +203,28 @@
         scores = dot_keys(keys, q_ref[:, columns])
         far = jnp.where((token & (MIDDLE_DILATION - 1)) == middle_ref[head], scores[:far_rows], MASKED)
         coarse = jnp.where(is_key & (token == coarse_ref[head]), scores[far_rows:], MASKED)
-        own_top, other_top = own_state[head : head + 1], state[place : place + 1]
-        top = jnp.maximum(jnp.maximum(own_top, other_top), jnp.max(far, axis=0, keepdims=True))
+        before = state[place : place + 1]
+        top = jnp.maximum(before, jnp.max(far, axis=0, keepdims=True))
         top = jnp.maximum(top, jnp.max(coarse, axis=0, keepdims=True))
         far, coarse = weights(far, top), weights(coarse, top)
-        own_kept, other_kept = weights(own_top, top), weights(other_top, top)
-        total = own_kept * own_state[HEAD_COUNT + head : HEAD_COUNT + head + 1]
-        total += other_kept * state[half + place : half + place + 1]
+        kept = weights(before, top)
+        total = kept * (state[half + place : half + place + 1] + own_totals[head : head + 1])
         total += jnp.sum(far, axis=0, keepdims=True) + jnp.sum(coarse, axis=0, keepdims=True)
         inverse = 1.0 / total
         shifted = pltpu.roll(coarse, 1, 0)
         mixed = jnp.concatenate([(far * inverse).astype(jnp.bfloat16), (shifted * inverse).astype(jnp.bfloat16)], axis=0)
         sum_ref[:, columns] = dot_rows(mixed, values)
-        own_shares.append(own_kept * inverse)
-        other_shares.append(other_kept * inverse)
-    share_ref[:, : 2 * HEAD_COUNT] = jnp.concatenate(own_shares + other_shares, axis=0).T
+        shares.append(kept * inverse)
+    share_ref[:, :HEAD_COUNT] = jnp.concatenate(shares, axis=0).T
 
 
 def base_kernel(heads, sum_ref, share_ref, own_ref, base_ref, spread_ref):
     shape = (sum_ref.shape[0], HEAD_FEATURES)
     for place, head in enumerate(heads):
         columns, place_columns = head_columns(head), head_columns(place)
-        share = share_ref[:, head : head + 1]
+        share = jnp.broadcast_to(share_ref[:, head : head + 1], shape)
         base_ref[:, place_columns] = sum_ref[:, columns] + share * own_ref[:, columns]
-        other = HEAD_COUNT + head
-        spread_ref[:, place_columns] = jnp.broadcast_to(share_ref[:, other : other + 1], shape)
+        spread_ref[:, place_columns] = share
 
 
 def finish_kernel(heads, base_ref, spread_ref, other_a_ref, other_b_ref, vm_ref, vr_ref, *rest):
@@ -305,15 +313,15 @@
     )
     cross = partner(own_members, "inner", 2)
     near = gather_upper(stack(coarse, partner_elsewhere(coarse, 1)), "outer")
-    own_sum, own_state = call(
-        own_kernel,
-        "own",
-        middle_head_shift, q, k, v,
-        out_shape=[pltpu.VMEM((rows, width), f32), pltpu.VMEM((rows, LANES), f32)],
-        in_specs=[smem] + [vmem] * 3,
+    own_scores, own_top = call(
+        score_kernel,
+        "score",
+        q, k,
+        out_shape=[pltpu.VMEM((HEAD_COUNT, rows, rows), f32), pltpu.VMEM((rows, LANES), f32)],
+        in_specs=[vmem] * 2,
         out_specs=[vmem] * 2,
     )
-    near, own_vm, own_state = lax.optimization_barrier((near, own_vm, own_state))
+    near, own_vm, own_top = lax.optimization_barrier((near, own_vm, own_top))
     other_vm = partner(own_vm, "inner", 1)
     cross, own_vr = lax.optimization_barrier((cross, own_vr))
     other_vr = [partner(piece, "inner", 1) for piece in own_vr]
@@ -332,9 +340,9 @@
         return call(
             functools.partial(other_kernel, first),
             "other",
-            middle_head_shift, query, other_keys,
+            middle_head_shift, query, own_top, other_keys,
             out_shape=[pltpu.VMEM((half, rows, rows), bf16), pltpu.VMEM((rows, LANES), f32)],
-            in_specs=[smem] + [vmem] * 2,
+            in_specs=[smem] + [vmem] * 3,
             out_specs=[vmem] * 2,
             scratch_shapes=[orders],
         )
@@ -342,11 +350,19 @@
     weights_a, state_a = other_part(0, q)
     diagonal_v = partner(lax.optimization_barrier((other_vm, state_a))[0], "inner", 2)
     weights_b, state_b = other_part(half, lax.optimization_barrier((q, state_a, diagonal_k))[0])
+    own_sum, own_total = call(
+        own_kernel,
+        "own",
+        middle_head_shift, own_scores, state_a, state_b, v,
+        out_shape=[pltpu.VMEM((rows, width), f32), pltpu.VMEM((rows, LANES), f32)],
+        in_specs=[smem] + [vmem] * 4,
+        out_specs=[vmem] * 2,
+    )
     mine = jnp.concatenate([near, partner_elsewhere(near, 2)], axis=0)
     extra_sum, share = call(
         extra_kernel,
         "extra",
-        middle_head_shift, coarse_head_shift, q, own_state, state_a, state_b, cross, diagonal_k, diagonal_v, mine,
+        middle_head_shift, coarse_head_shift, q, own_total, state_a, state_b, cross, diagonal_k, diagonal_v, mine,
         partner(mine, "outer", 1),
         out_shape=[pltpu.VMEM((rows, width), f32), pltpu.VMEM((rows, LANES), f32)],
         in_specs=[smem, smem] + [vmem] * 9,

time: 50.4 us -> 53.3 us (1.058)
  Pallas kernels: 17.9 us -> 25.2 us
  waiting for transfers between devices: 11.4 us -> 9.07 us
  starting transfers between devices: 19.4 us -> 17.2 us
    pallas_call x12 -> x13, Pallas kernels: 17.9 us -> 25.1 us  [call(): pl.pallas_call(kernel, name=name, compiler_params=params, cost_estimate=c...]
    ppermute x12, waiting for transfers between devices: 8.33 us -> 5.96 us  [partner(): return lax.ppermute(value, axis, pairs)]
    ppermute x12, starting transfers between devices: 17.9 us -> 15.6 us  [partner(): return lax.ppermute(value, axis, pairs)]
    unnamed x9 -> x7, local copies, waits for them, and re-layouts: 1.32 us -> 1.32 us
  transfers between devices with their start and end apart: 14 -> 14, of which waited for: 7 -> 5; matrix products, arithmetic and copies ran while one was open for 0% -> 0% of each run, Pallas kernels for 34% -> 46%
where the time goes in v15:
time: 53.3 us; the launch traced here: 53.1 us
  Pallas kernels  25.2 us (47%)
  starting transfers between devices  17.2 us (32%)
  waiting for transfers between devices  9.07 us (17%)
  local copies, waits for them, and re-layouts  1.33 us (2%)
    pallas_call x13, Pallas kernels, call(): pl.pallas_call(kernel, name=name, compiler_params=params, cost_estimate=c...  25.1 us
    ppermute x12, starting transfers between devices, partner(): return lax.ppermute(value, axis, pairs)  15.6 us
    ppermute x12, waiting for transfers between devices, partner(): return lax.ppermute(value, axis, pairs)  5.96 us
    ppermute x2, waiting for transfers between devices, partner_elsewhere(): return lax.ppermute(value, ('inner', 'outer'), pairs)  3.11 us
    ppermute x2, starting transfers between devices, partner_elsewhere(): return lax.ppermute(value, ('inner', 'outer'), pairs)  1.55 us
    unnamed x7, local copies, waits for them, and re-layouts  1.32 us
  transfers between devices with their start and end apart: 14, of which 5 were waited for; matrix products, arithmetic and copies ran while one was open for 0% of the time, Pallas kernels for 46%

profile of v15, /device:TPU:0, one launch (start us, length us, event | category | flops | bytes accessed | tf_op | source)
XLA Modules:
  0.0 53.1 jit_solution(3133328116007276820)
XLA Ops:
  0.0 2.9 %collective-permute-start.4 = (bf16[256,2048]{1,0:T(8,128)(2,1)}, bf16[256,2048]{1,0:T(8,128)(2,1)S(1)}, u32[]{:S(2)}, u32[]{:S(2)}) collective-permute-start(bf16[256,2048]{1,0:T(8,128)(2,1)} %k_hbm.1), channel_id=1, source_target_pairs={{0,8},{8,0},{16,24},{24,16},{1,9},{9,1},{17,25},{25,17},{2,10},{10... | collective-permute-start | bytes 3145736 | tf_op jit(solution)/shard_map/ppermute | solution.py:22
  2.9 0.7 %copy-done = s32[16]{0:T(128)S(1)} copy-done((s32[16]{0:T(128)S(1)}, s32[16]{0:T(128)}, u32[]{:S(2)}) %copy-start) | copy-done | bytes 88
  3.6 0.7 %copy-done.2 = s32[16]{0:T(128)S(1)} copy-done((s32[16]{0:T(128)S(1)}, s32[16]{0:T(128)}, u32[]{:S(2)}) %copy-start.2) | copy-done | bytes 88
  4.3 3.2 %prepare.1 = (bf16[256,2048]{1,0:T(8,128)(2,1)S(1)}, bf16[256,2048]{1,0:T(8,128)(2,1)S(1)}, bf16[256,2048]{1,0:T(8,128)(2,1)S(1)}, bf16[128,2048]{1,0:T(8,128)(2...) custom-call(s32[16]{0:T(128)S(1)} %copy-done, ...), custom_call_target="tpu_custom_call" | custom-call | tf_op jit(solution)/shard_map/prepare/pallas_call | solution.py:296
  7.5 1.6 %collective-permute-start.6 = (bf16[128,2048]{1,0:T(8,128)(2,1)S(1)}, bf16[128,2048]{1,0:T(8,128)(2,1)S(1)}, u32[]{:S(2)}, u32[]{:S(2)}) collective-permute-start(bf16[128,2048]{1,0:T(8,128)(2,1)S(1)} %get-tuple-element.53), channel_id=1, source_target_pairs={{0,16},{8,24},{16,0},{24,8},{1,17},{9,25},{17,1},{25,9},{2,18},{10... | collective-permute-start | bytes 1572872 | tf_op jit(solution)/shard_map/ppermute | solution.py:22
  9.1 1.6 %collective-permute-start = (bf16[2,2048]{1,0:T(2,128)(2,1)S(1)}, bf16[2,2048]{1,0:T(2,128)(2,1)S(1)}, u32[]{:S(2)}, u32[]{:S(2)}) collective-permute-start(bf16[2,2048]{1,0:T(2,128)(2,1)S(1)} %get-tuple-element.43.refs_0_), channel_id=1, source_target_pairs={{0,10},{1,11},{2,8},{3,9},{4,14},{5,15},{6,12},{7,13},{8,2},{9,3},... | collective-permute-start | bytes 24584 | tf_op jit(solution)/shard_map/ppermute | solution.py:32
  10.6 3.1 %collective-permute-done.refs_1_ = bf16[2,2048]{1,0:T(2,128)(2,1)S(1)} collective-permute-done((bf16[2,2048]{1,0:T(2,128)(2,1)S(1)}, bf16[2,2048]{1,0:T(2,128)(2,1)S(1)}, u32[]{:S(2)}, u32[]{:S(2)}) %collective-permute-start) | collective-permute-done | bytes 8224 | tf_op jit(solution)/shard_map/ppermute | solution.py:32
  13.8 1.6 %collective-permute-start.1 = (bf16[4,2048]{1,0:T(4,128)(2,1)S(1)}, bf16[4,2048]{1,0:T(4,128)(2,1)S(1)}, u32[]{:S(2)}, u32[]{:S(2)}) collective-permute-start(bf16[4,2048]{1,0:T(4,128)(2,1)S(1)} %stack.2.refs_0_), channel_id=1, source_target_pairs={{0,2},{1,3},{2,0},{3,1},{4,6},{5,7},{6,4},{7,5},{8,10},{9,11},{10,... | collective-permute-start | bytes 49160 | tf_op jit(solution)/shard_map/ppermute | solution.py:22
  15.4 2.6 %collective-permute-start.2 = (bf16[4,2048]{1,0:T(4,128)(2,1)S(1)}, bf16[4,2048]{1,0:T(4,128)(2,1)S(1)}, u32[]{:S(2)}, u32[]{:S(2)}) collective-permute-start(bf16[4,2048]{1,0:T(4,128)(2,1)S(1)} %stack.2.refs_0_), channel_id=1, source_target_pairs={{0,4},{1,5},{2,6},{3,7},{4,0},{5,1},{6,2},{7,3},{8,12},{9,13},{10,... | collective-permute-start | bytes 49160 | tf_op jit(solution)/shard_map/ppermute | solution.py:22
  18.0 0.2 collective-permute-start.3
  18.2 0.8 %score.1 = (f32[16,256,256]{2,1,0:T(8,128)S(1)}, f32[256,128]{1,0:T(8,128)S(1)}) custom-call(bf16[256,2048]{1,0:T(8,128)(2,1)S(1)} %get-tuple-element.49.q_ref, bf16[256,2048]{1,0:T(8,128)(2,1)S(1)} %get-tuple-element.41.k_ref), custom_call_target="tpu_custom_call" | custom-call | tf_op jit(solution)/shard_map/score/pallas_call | solution.py:296
  19.0 1.3 %collective-permute-done.2.refs_2_ = bf16[4,2048]{1,0:T(4,128)(2,1)S(1)} collective-permute-done((bf16[4,2048]{1,0:T(4,128)(2,1)S(1)}, bf16[4,2048]{1,0:T(4,128)(2,1)S(1)}, u32[]{:S(2)}, u32[]{:S(2)}) %collective-permute-start.2) | collective-permute-done | bytes 16416 | tf_op jit(solution)/shard_map/ppermute | solution.py:22
  20.3 3.2 %collective-permute-done.3.refs_3_ = bf16[4,2048]{1,0:T(4,128)(2,1)S(1)} collective-permute-done((bf16[4,2048]{1,0:T(4,128)(2,1)S(1)}, bf16[4,2048]{1,0:T(4,128)(2,1)S(1)}, u32[]{:S(2)}, u32[]{:S(2)}) %collective-permute-start.3) | collective-permute-done | bytes 16416 | tf_op jit(solution)/shard_map/ppermute | solution.py:22
  23.5 0.6 %collective-permute-start.7 = (bf16[64,2048]{1,0:T(8,128)(2,1)S(1)}, bf16[64,2048]{1,0:T(8,128)(2,1)S(1)}, u32[]{:S(2)}, u32[]{:S(2)}) collective-permute-start(bf16[64,2048]{1,0:T(8,128)(2,1)S(1)} %get-tuple-element.58), channel_id=1, source_target_pairs={{0,8},{8,0},{16,24},{24,16},{1,9},{9,1},{17,25},{25,17},{2,10},{10... | collective-permute-start | bytes 786440 | tf_op jit(solution)/shard_map/ppermute | solution.py:22
  24.2 1.5 %collective-permute-start.13 = (bf16[192,1536]{1,0:T(8,128)(2,1)S(1)}, bf16[192,1536]{1,0:T(8,128)(2,1)S(1)}, u32[]{:S(2)}, u32[]{:S(2)}) collective-permute-start(bf16[192,1536]{1,0:T(8,128)(2,1)S(1)} %get-tuple-element.74), channel_id=1, source_target_pairs={{0,8},{8,0},{16,24},{24,16},{1,9},{9,1},{17,25},{25,17},{2,10},{10... | collective-permute-start | bytes 1769480 | tf_op jit(solution)/shard_map/ppermute | solution.py:22
  25.7 0.6 %collective-permute-start.12 = (bf16[192,384]{1,0:T(8,128)(2,1)S(1)}, bf16[192,384]{1,0:T(8,128)(2,1)S(1)}, u32[]{:S(2)}, u32[]{:S(2)}) collective-permute-start(bf16[192,384]{1,0:T(8,128)(2,1)S(1)} %get-tuple-element.71), channel_id=1, source_target_pairs={{0,8},{8,0},{16,24},{24,16},{1,9},{9,1},{17,25},{25,17},{2,10},{10... | collective-permute-start | bytes 442376 | tf_op jit(solution)/shard_map/ppermute | solution.py:22
  26.3 1.1 %collective-permute-done.4.k_ref.kp_ref = bf16[256,2048]{1,0:T(8,128)(2,1)S(1)} collective-permute-done((bf16[256,2048]{1,0:T(8,128)(2,1)}, bf16[256,2048]{1,0:T(8,128)(2,1)S(1)}, u32[]{:S(2)}, u32[]{:S(2)}) %collective-permute-start.4) | collective-permute-done | bytes 1048608 | tf_op jit(solution)/shard_map/ppermute | solution.py:22
  27.3 0.8 %pick.1 = bf16[64,2048]{1,0:T(8,128)(2,1)S(1)} custom-call(s32[16]{0:T(128)S(1)} %copy-done.1, bf16[256,2048]{1,0:T(8,128)(2,1)S(1)} %collective-permute-done.4.k_ref.kp_ref), custom_call_target="tpu_custom_call" | custom-call | tf_op jit(solution)/shard_map/pick/pallas_call | solution.py:296
  28.2 2.2 %collective-permute-start.5 = (bf16[64,2048]{1,0:T(8,128)(2,1)S(1)}, bf16[64,2048]{1,0:T(8,128)(2,1)S(1)}, u32[]{:S(2)}, u32[]{:S(2)}) collective-permute-start(bf16[64,2048]{1,0:T(8,128)(2,1)S(1)} %pick.1), channel_id=1, source_target_pairs={{0,16},{8,24},{16,0},{24,8},{1,17},{9,25},{17,1},{25,9},{2,18},{10... | collective-permute-start | bytes 786440 | tf_op jit(solution)/shard_map/ppermute | solution.py:22
  30.3 4.8 %other.2 = (bf16[8,256,256]{2,1,0:T(8,128)(2,1)S(1)}, f32[256,128]{1,0:T(8,128)S(1)}) custom-call(s32[16]{0:T(128)S(1)} %copy-done.1, bf16[256,2048]{1,0:T(8,128)(2,1)S(1)} %get-tuple-element.49.q_ref, f32[256,128]{1,0:T(8,128)S(1)} %get-tuple-element.46.own_top_ref, bf16[256,2048]{1,0:T(8,128)(2,1)S(1)} %collective-permute-done.4.k_ref.kp_ref), custom_call_target="tpu_custom_call" | custom-call | tf_op jit(solution)/shard_map/other/pallas_call | solution.py:296
  35.2 0.1 collective-permute-start.8
  35.4 0.4 collective-permute-done.5.diagonal_k_ref
  35.7 1.7 %collective-permute-start.11 = (bf16[192,128]{1,0:T(8,128)(2,1)S(1)}, bf16[192,128]{1,0:T(8,128)(2,1)S(1)}, u32[]{:S(2)}, u32[]{:S(2)}) collective-permute-start(bf16[192,128]{1,0:T(8,128)(2,1)S(1)} %get-tuple-element.68), channel_id=1, source_target_pairs={{0,8},{8,0},{16,24},{24,16},{1,9},{9,1},{17,25},{25,17},{2,10},{10... | collective-permute-start | bytes 147464 | tf_op jit(solution)/shard_map/ppermute | solution.py:22
  37.4 4.8 %other.3 = (bf16[8,256,256]{2,1,0:T(8,128)(2,1)S(1)}, f32[256,128]{1,0:T(8,128)S(1)}) custom-call(s32[16]{0:T(128)S(1)} %copy-done.1, bf16[256,2048]{1,0:T(8,128)(2,1)S(1)} %get-tuple-element.49.q_ref, f32[256,128]{1,0:T(8,128)S(1)} %get-tuple-element.46.own_top_ref, bf16[256,2048]{1,0:T(8,128)(2,1)S(1)} %collective-permute-done.4.k_ref.kp_ref), custom_call_target="tpu_custom_call" | custom-call | tf_op jit(solution)/shard_map/other/pallas_call | solution.py:296
  42.3 3.0 %own.1 = (f32[256,2048]{1,0:T(8,128)S(1)}, f32[256,128]{1,0:T(8,128)S(1)}) custom-call(s32[16]{0:T(128)S(1)} %copy-done.1, f32[16,256,256]{2,1,0:T(8,128)S(1)} %get-tuple-element.42.scores_ref, f32[256,128]{1,0:T(8,128)S(1)} %get-tuple-element.48.state_a_ref, f32[256,128]{1,0:T(8,128)S(1)} %get-tuple-element.50.state_b_ref, ...), custom_call_target="tpu_custom_call" | custom-call | tf_op jit(solution)/shard_map/own/pallas_call | solution.py:296
  45.2 3.7 %extra.1 = (f32[256,2048]{1,0:T(8,128)S(1)}, f32[256,128]{1,0:T(8,128)S(1)}) custom-call(s32[16]{0:T(128)S(1)} %copy-done.1, s32[16]{0:T(128)S(1)} %copy-done.2, bf16[256,2048]{1,0:T(8,128)(2,1)S(1)} %get-tuple-element.49.q_ref, f32[256,128]{1,0:T(8,128)S(1)} %get-tuple-element.52.own_total_ref, f32[256,128]{1,0:T(8,128)S(1)} %get-tuple-element.48.state_a_ref, ...), custom_call_target="tpu_custom_call" | custom-call | tf_op jit(solution)/shard_map/extra/pallas_call | solution.py:296
  48.9 0.1 base.3
  49.0 0.2 base.4
  49.2 0.5 %base.5 = (f32[256,1536]{1,0:T(8,128)S(1)}, f32[256,1536]{1,0:T(8,128)S(1)}) custom-call(f32[256,2048]{1,0:T(8,128)S(1)} %get-tuple-element.61.sum_ref, f32[256,128]{1,0:T(8,128)S(1)} %get-tuple-element.62.share_ref, f32[256,2048]{1,0:T(8,128)S(1)} %get-tuple-element.63.own_ref), custom_call_target="tpu_custom_call" | custom-call | tf_op jit(solution)/shard_map/base/pallas_call | solution.py:296
  49.8 1.4 %finish.3.rest_0_ = bf16[256,2048]{1,0:T(8,128)(2,1)} custom-call(f32[256,1536]{1,0:T(8,128)S(1)} %get-tuple-element.72.base_ref, f32[256,1536]{1,0:T(8,128)S(1)} %get-tuple-element.73.spread_ref, bf16[8,256,256]{2,1,0:T(8,128)(2,1)S(1)} %get-tuple-element.66.other_a_ref, bf16[8,256,256]{2,1,0:T(8,128)(2,1)S(1)} %get-tuple-element.67.other_b_ref, ...), custom_call_target="tpu_custom_call" | custom-call | tf_op jit(solution)/shard_map/finish/pallas_call | solution.py:296
  51.2 0.9 %finish.4.rest_0_ = bf16[256,2048]{1,0:T(8,128)(2,1)} custom-call(f32[256,384]{1,0:T(8,128)S(1)} %get-tuple-element.69.base_ref, f32[256,384]{1,0:T(8,128)S(1)} %get-tuple-element.70.spread_ref, bf16[8,256,256]{2,1,0:T(8,128)(2,1)S(1)} %get-tuple-element.66.other_a_ref, ...), custom_call_target="tpu_custom_call", output_to_operand_aliasing={{}: (6, {})} | custom-call | tf_op jit(solution)/shard_map/finish/pallas_call | solution.py:296
  52.1 0.8 %finish.5 = bf16[256,2048]{1,0:T(8,128)(2,1)} custom-call(f32[256,128]{1,0:T(8,128)S(1)} %get-tuple-element.64.base_ref, f32[256,128]{1,0:T(8,128)S(1)} %get-tuple-element.65.spread_ref, bf16[8,256,256]{2,1,0:T(8,128)(2,1)S(1)} %get-tuple-element.66.other_a_ref, ...), custom_call_target="tpu_custom_call", output_to_operand_aliasing={{}: (6, {})} | custom-call | tf_op jit(solution)/shard_map/finish/pallas_call | solution.py:296
  (19 shorter events, 0.2 us)
Async XLA Ops:
  0.0 27.3 %collective-permute-start.4 = (bf16[256,2048]{1,0:T(8,128)(2,1)}, bf16[256,2048]{1,0:T(8,128)(2,1)S(1)}, u32[]{:S(2)}, u32[]{:S(2)}) collective-permute-start(bf16[256,2048]{1,0:T(8,128)(2,1)} %k_hbm.1), channel_id=1, source_target_pairs={{0,8},{8,0},{16,24},{24,16},{1,9},{9,1},{17,25},{25,17},{2,10},{10... | collective-permute-start | bytes 3145736 | tf_op jit(solution)/shard_map/ppermute | solution.py:22
  2.9 0.7 %copy-start = (s32[16]{0:T(128)S(1)}, s32[16]{0:T(128)}, u32[]{:S(2)}) copy-start(s32[16]{0:T(128)} %middle_ref.11) | copy-start | bytes 196
  3.6 0.7 %copy-start.2 = (s32[16]{0:T(128)S(1)}, s32[16]{0:T(128)}, u32[]{:S(2)}) copy-start(s32[16]{0:T(128)} %coarse_ref.3) | copy-start | bytes 196
  4.3 23.1 %copy-start.1 = (s32[16]{0:T(128)S(1)}, s32[16]{0:T(128)}, u32[]{:S(2)}) copy-start(s32[16]{0:T(128)} %middle_ref.11) | copy-start | bytes 196
  7.5 16.7 %collective-permute-start.6 = (bf16[128,2048]{1,0:T(8,128)(2,1)S(1)}, bf16[128,2048]{1,0:T(8,128)(2,1)S(1)}, u32[]{:S(2)}, u32[]{:S(2)}) collective-permute-start(bf16[128,2048]{1,0:T(8,128)(2,1)S(1)} %get-tuple-element.53), channel_id=1, source_target_pairs={{0,16},{8,24},{16,0},{24,8},{1,17},{9,25},{17,1},{25,9},{2,18},{10... | collective-permute-start | bytes 1572872 | tf_op jit(solution)/shard_map/ppermute | solution.py:22
  9.1 4.7 %collective-permute-start = (bf16[2,2048]{1,0:T(2,128)(2,1)S(1)}, bf16[2,2048]{1,0:T(2,128)(2,1)S(1)}, u32[]{:S(2)}, u32[]{:S(2)}) collective-permute-start(bf16[2,2048]{1,0:T(2,128)(2,1)S(1)} %get-tuple-element.43.refs_0_), channel_id=1, source_target_pairs={{0,10},{1,11},{2,8},{3,9},{4,14},{5,15},{6,12},{7,13},{8,2},{9,3},... | collective-permute-start | bytes 24584 | tf_op jit(solution)/shard_map/ppermute | solution.py:32
  13.8 5.2 %collective-permute-start.1 = (bf16[4,2048]{1,0:T(4,128)(2,1)S(1)}, bf16[4,2048]{1,0:T(4,128)(2,1)S(1)}, u32[]{:S(2)}, u32[]{:S(2)}) collective-permute-start(bf16[4,2048]{1,0:T(4,128)(2,1)S(1)} %stack.2.refs_0_), channel_id=1, source_target_pairs={{0,2},{1,3},{2,0},{3,1},{4,6},{5,7},{6,4},{7,5},{8,10},{9,11},{10,... | collective-permute-start | bytes 49160 | tf_op jit(solution)/shard_map/ppermute | solution.py:22
  15.4 4.9 %collective-permute-start.2 = (bf16[4,2048]{1,0:T(4,128)(2,1)S(1)}, bf16[4,2048]{1,0:T(4,128)(2,1)S(1)}, u32[]{:S(2)}, u32[]{:S(2)}) collective-permute-start(bf16[4,2048]{1,0:T(4,128)(2,1)S(1)} %stack.2.refs_0_), channel_id=1, source_target_pairs={{0,4},{1,5},{2,6},{3,7},{4,0},{5,1},{6,2},{7,3},{8,12},{9,13},{10,... | collective-permute-start | bytes 49160 | tf_op jit(solution)/shard_map/ppermute | solution.py:22
  18.0 5.5 %collective-permute-start.3 = (bf16[4,2048]{1,0:T(4,128)(2,1)S(1)}, bf16[4,2048]{1,0:T(4,128)(2,1)S(1)}, u32[]{:S(2)}, u32[]{:S(2)}) collective-permute-start(bf16[4,2048]{1,0:T(4,128)(2,1)S(1)} %stack.2.refs_0_), channel_id=1, source_target_pairs={{0,6},{1,7},{2,4},{3,5},{4,2},{5,3},{6,0},{7,1},{8,14},{9,15},{10,... | collective-permute-start | bytes 49160 | tf_op jit(solution)/shard_map/ppermute | solution.py:22
  23.5 11.6 %collective-permute-start.7 = (bf16[64,2048]{1,0:T(8,128)(2,1)S(1)}, bf16[64,2048]{1,0:T(8,128)(2,1)S(1)}, u32[]{:S(2)}, u32[]{:S(2)}) collective-permute-start(bf16[64,2048]{1,0:T(8,128)(2,1)S(1)} %get-tuple-element.58), channel_id=1, source_target_pairs={{0,8},{8,0},{16,24},{24,16},{1,9},{9,1},{17,25},{25,17},{2,10},{10... | collective-permute-start | bytes 786440 | tf_op jit(solution)/shard_map/ppermute | solution.py:22
  24.2 25.6 %collective-permute-start.13 = (bf16[192,1536]{1,0:T(8,128)(2,1)S(1)}, bf16[192,1536]{1,0:T(8,128)(2,1)S(1)}, u32[]{:S(2)}, u32[]{:S(2)}) collective-permute-start(bf16[192,1536]{1,0:T(8,128)(2,1)S(1)} %get-tuple-element.74), channel_id=1, source_target_pairs={{0,8},{8,0},{16,24},{24,16},{1,9},{9,1},{17,25},{25,17},{2,10},{10... | collective-permute-start | bytes 1769480 | tf_op jit(solution)/shard_map/ppermute | solution.py:22
  25.6 9.6 %collective-permute-start.9 = (bf16[16,2048]{1,0:T(8,128)(2,1)S(1)}, bf16[16,2048]{1,0:T(8,128)(2,1)S(1)}, u32[]{:S(2)}, u32[]{:S(2)}) collective-permute-start(bf16[16,2048]{1,0:T(8,128)(2,1)S(1)} %stack.3), channel_id=1, source_target_pairs={{0,18},{1,19},{2,16},{3,17},{4,22},{5,23},{6,20},{7,21},{8,26},{9,... | collective-permute-start | bytes 196616 | tf_op jit(solution)/shard_map/ppermute | solution.py:32
  25.7 25.5 %collective-permute-start.12 = (bf16[192,384]{1,0:T(8,128)(2,1)S(1)}, bf16[192,384]{1,0:T(8,128)(2,1)S(1)}, u32[]{:S(2)}, u32[]{:S(2)}) collective-permute-start(bf16[192,384]{1,0:T(8,128)(2,1)S(1)} %get-tuple-element.71), channel_id=1, source_target_pairs={{0,8},{8,0},{16,24},{24,16},{1,9},{9,1},{17,25},{25,17},{2,10},{10... | collective-permute-start | bytes 442376 | tf_op jit(solution)/shard_map/ppermute | solution.py:22
  28.2 7.6 %collective-permute-start.5 = (bf16[64,2048]{1,0:T(8,128)(2,1)S(1)}, bf16[64,2048]{1,0:T(8,128)(2,1)S(1)}, u32[]{:S(2)}, u32[]{:S(2)}) collective-permute-start(bf16[64,2048]{1,0:T(8,128)(2,1)S(1)} %pick.1), channel_id=1, source_target_pairs={{0,16},{8,24},{16,0},{24,8},{1,17},{9,25},{17,1},{25,9},{2,18},{10... | collective-permute-start | bytes 786440 | tf_op jit(solution)/shard_map/ppermute | solution.py:22
  35.2 10.1 %collective-permute-start.8 = (bf16[64,2048]{1,0:T(8,128)(2,1)S(1)}, bf16[64,2048]{1,0:T(8,128)(2,1)S(1)}, u32[]{:S(2)}, u32[]{:S(2)}) collective-permute-start(bf16[64,2048]{1,0:T(8,128)(2,1)S(1)} %collective-permute-done.7.vm_ref), channel_id=1, source_target_pairs={{0,16},{8,24},{16,0},{24,8},{1,17},{9,25},{17,1},{25,9},{2,18},{10... | collective-permute-start | bytes 786440 | tf_op jit(solution)/shard_map/ppermute | solution.py:22
  35.3 9.9 %collective-permute-start.10 = (bf16[32,2048]{1,0:T(8,128)(2,1)S(1)}, bf16[32,2048]{1,0:T(8,128)(2,1)S(1)}, u32[]{:S(2)}, u32[]{:S(2)}) collective-permute-start(bf16[32,2048]{1,0:T(8,128)(2,1)S(1)} %constant_dynamic-update-slice_fusion.mine_ref), channel_id=1, source_target_pairs={{0,1},{1,0},{2,3},{3,2},{4,5},{5,4},{6,7},{7,6},{8,9},{9,8},{10,11... | collective-permute-start | bytes 393224 | tf_op jit(solution)/shard_map/ppermute | solution.py:22
  35.7 16.4 %collective-permute-start.11 = (bf16[192,128]{1,0:T(8,128)(2,1)S(1)}, bf16[192,128]{1,0:T(8,128)(2,1)S(1)}, u32[]{:S(2)}, u32[]{:S(2)}) collective-permute-start(bf16[192,128]{1,0:T(8,128)(2,1)S(1)} %get-tuple-element.68), channel_id=1, source_target_pairs={{0,8},{8,0},{16,24},{24,16},{1,9},{9,1},{17,25},{25,17},{2,10},{10... | collective-permute-start | bytes 147464 | tf_op jit(solution)/shard_map/ppermute | solution.py:22

commit v16 on v15

--- a/solution.py
+++ b/solution.py
@@ -131,16 +131,15 @@
 
 
 def score_kernel(q_ref, k_ref, scores_ref, top_ref):
-    tops = []
     for head in range(HEAD_COUNT):
         columns = head_columns(head)
         own = dot_keys(q_ref[:, columns], k_ref[:, columns])
-        tops.append(jnp.max(functools.reduce(jnp.maximum, lane_tiles(own)), axis=1, keepdims=True))
+        top = jnp.max(functools.reduce(jnp.maximum, lane_tiles(own)), axis=1, keepdims=True)
+        top_ref[head] = jnp.broadcast_to(top, top_ref.shape[1:])
         scores_ref[head] = own
-    top_ref[...] = side_by_side(tops)
-
-
-def other_kernel(first, middle_ref, q_ref, own_top_ref, kp_ref, other_ref, state_ref, order_ref):
+
+
+def other_kernel(first, middle_ref, q_ref, own_top_ref, kp_ref, other_ref, top_ref, state_ref, order_ref):
     fill_orders(order_ref)
     rows = q_ref.shape[0]
     members = rows // MIDDLE_DILATION
@@ -153,31 +152,31 @@
         other_keys = dot(order_ref[shift], kp_ref[:, columns]).astype(jnp.bfloat16)
         other = dot_keys(q_ref[:, columns], other_keys)
         top = jnp.max(functools.reduce(jnp.maximum, lane_tiles(other)), axis=1, keepdims=True)
-        top = jnp.maximum(top, own_top_ref[:, head : head + 1])
-        other = weights(other, top)
-        twice = other[:, :LANES]
-        twice = jnp.where(member_rows(rows, shift) & (column < members), twice + twice, twice)
-        other = jnp.concatenate([twice, other[:, LANES:]], axis=1)
+        top = jnp.maximum(top, own_top_ref[head])
+        top_ref[place] = top
+        tiles = [weights(tile, top) for tile in lane_tiles(other)]
+        twice = member_rows(rows, shift) & (column < members)
+        tiles[0] = jnp.where(twice, tiles[0] + tiles[0], tiles[0])
         tops.append(top)
-        totals.append(jnp.sum(functools.reduce(jnp.add, lane_tiles(other)), axis=1, keepdims=True))
-        other_ref[place] = other.astype(jnp.bfloat16)
+        totals.append(jnp.sum(functools.reduce(jnp.add, tiles), axis=1, keepdims=True))
+        other_ref[place] = jnp.concatenate(tiles, axis=1).astype(jnp.bfloat16)
     state_ref[...] = side_by_side(tops + totals)
 
 
-def own_kernel(middle_ref, scores_ref, state_a_ref, state_b_ref, v_ref, sum_ref, total_ref):
+def own_kernel(middle_ref, scores_ref, top_a_ref, top_b_ref, v_ref, sum_ref, total_ref):
     rows = v_ref.shape[0]
     half = HEAD_COUNT // 2
-    column = lax.broadcasted_iota(jnp.int32, (1, rows), 1)
+    lane = lax.broadcasted_iota(jnp.int32, (1, LANES), 1)
     totals = []
     for head in range(HEAD_COUNT):
         columns = head_columns(head)
         shift = middle_ref[head]
-        place = head % half
-        own = weights(scores_ref[head], (state_a_ref, state_b_ref)[head // half][:, place : place + 1])
-        twice = member_rows(rows, shift) & ((column & (MIDDLE_DILATION - 1)) == shift)
-        own = jnp.where(twice, own + own, own)
-        totals.append(jnp.sum(functools.reduce(jnp.add, lane_tiles(own)), axis=1, keepdims=True))
-        sum_ref[:, columns] = dot(own.astype(jnp.bfloat16), v_ref[:, columns])
+        top = (top_a_ref, top_b_ref)[head // half][head % half]
+        twice = member_rows(rows, shift) & ((lane & (MIDDLE_DILATION - 1)) == shift)
+        tiles = [weights(tile, top) for tile in lane_tiles(scores_ref[head])]
+        tiles = [jnp.where(twice, tile + tile, tile) for tile in tiles]
+        totals.append(jnp.sum(functools.reduce(jnp.add, tiles), axis=1, keepdims=True))
+        sum_ref[:, columns] = dot(jnp.concatenate(tiles, axis=1).astype(jnp.bfloat16), v_ref[:, columns])
     total_ref[...] = side_by_side(totals)
 
 
@@ -317,7 +316,7 @@
         score_kernel,
         "score",
         q, k,
-        out_shape=[pltpu.VMEM((HEAD_COUNT, rows, rows), f32), pltpu.VMEM((rows, LANES), f32)],
+        out_shape=[pltpu.VMEM((HEAD_COUNT, rows, rows), f32), pltpu.VMEM((HEAD_COUNT, rows, LANES), f32)],
         in_specs=[vmem] * 2,
         out_specs=[vmem] * 2,
     )
@@ -341,19 +340,23 @@
             functools.partial(other_kernel, first),
             "other",
             middle_head_shift, query, own_top, other_keys,
-            out_shape=[pltpu.VMEM((half, rows, rows), bf16), pltpu.VMEM((rows, LANES), f32)],
+            out_shape=[
+                pltpu.VMEM((half, rows, rows), bf16),
+                pltpu.VMEM((half, rows, LANES), f32),
+                pltpu.VMEM((rows, LANES), f32),
+            ],
             in_specs=[smem] + [vmem] * 3,
-            out_specs=[vmem] * 2,
+            out_specs=[vmem] * 3,
             scratch_shapes=[orders],
         )
 
-    weights_a, state_a = other_part(0, q)
+    weights_a, top_a, state_a = other_part(0, q)
     diagonal_v = partner(lax.optimization_barrier((other_vm, state_a))[0], "inner", 2)
-    weights_b, state_b = other_part(half, lax.optimization_barrier((q, state_a, diagonal_k))[0])
+    weights_b, top_b, state_b = other_part(half, lax.optimization_barrier((q, state_a, diagonal_k))[0])
     own_sum, own_total = call(
         own_kernel,
         "own",
-        middle_head_shift, own_scores, state_a, state_b, v,
+        middle_head_shift, own_scores, top_a, top_b, v,
         out_shape=[pltpu.VMEM((rows, width), f32), pltpu.VMEM((rows, LANES), f32)],
         in_specs=[smem] + [vmem] * 4,
         out_specs=[vmem] * 2,

time: 53.3 us -> 50.3 us (0.944)
  Pallas kernels: 25.2 us -> 17.6 us
  waiting for transfers between devices: 9.07 us -> 12.3 us
  starting transfers between devices: 17.2 us -> 18.9 us
    pallas_call x13, Pallas kernels: 25.1 us -> 17.5 us  [call(): pl.pallas_call(kernel, name=name, compiler_params=params, cost_estimate=c...]
    ppermute x12, waiting for transfers between devices: 5.96 us -> 9.15 us  [partner(): return lax.ppermute(value, axis, pairs)]
    ppermute x12, starting transfers between devices: 15.6 us -> 17.3 us  [partner(): return lax.ppermute(value, axis, pairs)]
    unnamed x7 -> x9, local copies, waits for them, and re-layouts: 1.32 us -> 1.32 us
  transfers between devices with their start and end apart: 14 -> 14, of which waited for: 5 -> 7; matrix products, arithmetic and copies ran while one was open for 0% -> 0% of each run, Pallas kernels for 46% -> 33%
where the time goes in v16:
time: 50.3 us; the launch traced here: 50.2 us
  starting transfers between devices  18.9 us (38%)
  Pallas kernels  17.6 us (35%)
  waiting for transfers between devices  12.3 us (24%)
  local copies, waits for them, and re-layouts  1.33 us (3%)
    pallas_call x13, Pallas kernels, call(): pl.pallas_call(kernel, name=name, compiler_params=params, cost_estimate=c...  17.5 us
    ppermute x12, starting transfers between devices, partner(): return lax.ppermute(value, axis, pairs)  17.3 us
    ppermute x12, waiting for transfers between devices, partner(): return lax.ppermute(value, axis, pairs)  9.15 us
    ppermute x2, waiting for transfers between devices, partner_elsewhere(): return lax.ppermute(value, ('inner', 'outer'), pairs)  3.11 us
    ppermute x2, starting transfers between devices, partner_elsewhere(): return lax.ppermute(value, ('inner', 'outer'), pairs)  1.55 us
    unnamed x9, local copies, waits for them, and re-layouts  1.32 us
  transfers between devices with their start and end apart: 14, of which 7 were waited for; matrix products, arithmetic and copies ran while one was open for 0% of the time, Pallas kernels for 33%

profile of v16, /device:TPU:0, one launch (start us, length us, event | category | flops | bytes accessed | tf_op | source)
XLA Modules:
  0.0 50.2 jit_solution(16299085620551654887)
XLA Ops:
  0.0 2.9 %collective-permute-start.4 = (bf16[256,2048]{1,0:T(8,128)(2,1)}, bf16[256,2048]{1,0:T(8,128)(2,1)S(1)}, u32[]{:S(2)}, u32[]{:S(2)}) collective-permute-start(bf16[256,2048]{1,0:T(8,128)(2,1)} %k_hbm.1), channel_id=1, source_target_pairs={{0,8},{8,0},{16,24},{24,16},{1,9},{9,1},{17,25},{25,17},{2,10},{10... | collective-permute-start | bytes 3145736 | tf_op jit(solution)/shard_map/ppermute | solution.py:22
  2.9 0.7 %copy-done = s32[16]{0:T(128)S(1)} copy-done((s32[16]{0:T(128)S(1)}, s32[16]{0:T(128)}, u32[]{:S(2)}) %copy-start) | copy-done | bytes 88
  3.6 0.7 %copy-done.2 = s32[16]{0:T(128)S(1)} copy-done((s32[16]{0:T(128)S(1)}, s32[16]{0:T(128)}, u32[]{:S(2)}) %copy-start.2) | copy-done | bytes 88
  4.3 3.2 %prepare.1 = (bf16[256,2048]{1,0:T(8,128)(2,1)S(1)}, bf16[256,2048]{1,0:T(8,128)(2,1)S(1)}, bf16[256,2048]{1,0:T(8,128)(2,1)S(1)}, bf16[128,2048]{1,0:T(8,128)(2...) custom-call(s32[16]{0:T(128)S(1)} %copy-done, ...), custom_call_target="tpu_custom_call" | custom-call | tf_op jit(solution)/shard_map/prepare/pallas_call | solution.py:295
  7.5 1.6 %collective-permute-start.6 = (bf16[128,2048]{1,0:T(8,128)(2,1)S(1)}, bf16[128,2048]{1,0:T(8,128)(2,1)S(1)}, u32[]{:S(2)}, u32[]{:S(2)}) collective-permute-start(bf16[128,2048]{1,0:T(8,128)(2,1)S(1)} %get-tuple-element.57), channel_id=1, source_target_pairs={{0,16},{8,24},{16,0},{24,8},{1,17},{9,25},{17,1},{25,9},{2,18},{10... | collective-permute-start | bytes 1572872 | tf_op jit(solution)/shard_map/ppermute | solution.py:22
  9.1 1.5 %collective-permute-start = (bf16[2,2048]{1,0:T(2,128)(2,1)S(1)}, bf16[2,2048]{1,0:T(2,128)(2,1)S(1)}, u32[]{:S(2)}, u32[]{:S(2)}) collective-permute-start(bf16[2,2048]{1,0:T(2,128)(2,1)S(1)} %get-tuple-element.45.refs_0_), channel_id=1, source_target_pairs={{0,10},{1,11},{2,8},{3,9},{4,14},{5,15},{6,12},{7,13},{8,2},{9,3},... | collective-permute-start | bytes 24584 | tf_op jit(solution)/shard_map/ppermute | solution.py:32
  10.6 3.1 %collective-permute-done.refs_1_ = bf16[2,2048]{1,0:T(2,128)(2,1)S(1)} collective-permute-done((bf16[2,2048]{1,0:T(2,128)(2,1)S(1)}, bf16[2,2048]{1,0:T(2,128)(2,1)S(1)}, u32[]{:S(2)}, u32[]{:S(2)}) %collective-permute-start) | collective-permute-done | bytes 8224 | tf_op jit(solution)/shard_map/ppermute | solution.py:32
  13.8 1.6 %collective-permute-start.1 = (bf16[4,2048]{1,0:T(4,128)(2,1)S(1)}, bf16[4,2048]{1,0:T(4,128)(2,1)S(1)}, u32[]{:S(2)}, u32[]{:S(2)}) collective-permute-start(bf16[4,2048]{1,0:T(4,128)(2,1)S(1)} %stack.2.refs_0_), channel_id=1, source_target_pairs={{0,2},{1,3},{2,0},{3,1},{4,6},{5,7},{6,4},{7,5},{8,10},{9,11},{10,... | collective-permute-start | bytes 49160 | tf_op jit(solution)/shard_map/ppermute | solution.py:22
  15.4 2.6 %collective-permute-start.2 = (bf16[4,2048]{1,0:T(4,128)(2,1)S(1)}, bf16[4,2048]{1,0:T(4,128)(2,1)S(1)}, u32[]{:S(2)}, u32[]{:S(2)}) collective-permute-start(bf16[4,2048]{1,0:T(4,128)(2,1)S(1)} %stack.2.refs_0_), channel_id=1, source_target_pairs={{0,4},{1,5},{2,6},{3,7},{4,0},{5,1},{6,2},{7,3},{8,12},{9,13},{10,... | collective-permute-start | bytes 49160 | tf_op jit(solution)/shard_map/ppermute | solution.py:22
  18.0 0.2 collective-permute-start.3
  18.2 0.8 %score.1 = (f32[16,256,256]{2,1,0:T(8,128)S(1)}, f32[16,256,128]{2,1,0:T(8,128)S(1)}) custom-call(bf16[256,2048]{1,0:T(8,128)(2,1)S(1)} %get-tuple-element.52.q_ref, bf16[256,2048]{1,0:T(8,128)(2,1)S(1)} %get-tuple-element.43.k_ref), custom_call_target="tpu_custom_call" | custom-call | tf_op jit(solution)/shard_map/score/pallas_call | solution.py:295
  19.0 1.2 %collective-permute-done.2.refs_2_ = bf16[4,2048]{1,0:T(4,128)(2,1)S(1)} collective-permute-done((bf16[4,2048]{1,0:T(4,128)(2,1)S(1)}, bf16[4,2048]{1,0:T(4,128)(2,1)S(1)}, u32[]{:S(2)}, u32[]{:S(2)}) %collective-permute-start.2) | collective-permute-done | bytes 16416 | tf_op jit(solution)/shard_map/ppermute | solution.py:22
  20.3 3.3 %collective-permute-done.3.refs_3_ = bf16[4,2048]{1,0:T(4,128)(2,1)S(1)} collective-permute-done((bf16[4,2048]{1,0:T(4,128)(2,1)S(1)}, bf16[4,2048]{1,0:T(4,128)(2,1)S(1)}, u32[]{:S(2)}, u32[]{:S(2)}) %collective-permute-start.3) | collective-permute-done | bytes 16416 | tf_op jit(solution)/shard_map/ppermute | solution.py:22
  23.6 0.6 %collective-permute-start.7 = (bf16[64,2048]{1,0:T(8,128)(2,1)S(1)}, bf16[64,2048]{1,0:T(8,128)(2,1)S(1)}, u32[]{:S(2)}, u32[]{:S(2)}) collective-permute-start(bf16[64,2048]{1,0:T(8,128)(2,1)S(1)} %get-tuple-element.62), channel_id=1, source_target_pairs={{0,8},{8,0},{16,24},{24,16},{1,9},{9,1},{17,25},{25,17},{2,10},{10... | collective-permute-start | bytes 786440 | tf_op jit(solution)/shard_map/ppermute | solution.py:22
  24.2 1.5 %collective-permute-start.13 = (bf16[192,1536]{1,0:T(8,128)(2,1)S(1)}, bf16[192,1536]{1,0:T(8,128)(2,1)S(1)}, u32[]{:S(2)}, u32[]{:S(2)}) collective-permute-start(bf16[192,1536]{1,0:T(8,128)(2,1)S(1)} %get-tuple-element.78), channel_id=1, source_target_pairs={{0,8},{8,0},{16,24},{24,16},{1,9},{9,1},{17,25},{25,17},{2,10},{10... | collective-permute-start | bytes 1769480 | tf_op jit(solution)/shard_map/ppermute | solution.py:22
  25.7 0.6 %collective-permute-start.12 = (bf16[192,384]{1,0:T(8,128)(2,1)S(1)}, bf16[192,384]{1,0:T(8,128)(2,1)S(1)}, u32[]{:S(2)}, u32[]{:S(2)}) collective-permute-start(bf16[192,384]{1,0:T(8,128)(2,1)S(1)} %get-tuple-element.75), channel_id=1, source_target_pairs={{0,8},{8,0},{16,24},{24,16},{1,9},{9,1},{17,25},{25,17},{2,10},{10... | collective-permute-start | bytes 442376 | tf_op jit(solution)/shard_map/ppermute | solution.py:22
  26.3 1.1 %collective-permute-done.4.k_ref.kp_ref = bf16[256,2048]{1,0:T(8,128)(2,1)S(1)} collective-permute-done((bf16[256,2048]{1,0:T(8,128)(2,1)}, bf16[256,2048]{1,0:T(8,128)(2,1)S(1)}, u32[]{:S(2)}, u32[]{:S(2)}) %collective-permute-start.4) | collective-permute-done | bytes 1048608 | tf_op jit(solution)/shard_map/ppermute | solution.py:22
  27.3 0.8 %pick.1 = bf16[64,2048]{1,0:T(8,128)(2,1)S(1)} custom-call(s32[16]{0:T(128)S(1)} %copy-done.1, bf16[256,2048]{1,0:T(8,128)(2,1)S(1)} %collective-permute-done.4.k_ref.kp_ref), custom_call_target="tpu_custom_call" | custom-call | tf_op jit(solution)/shard_map/pick/pallas_call | solution.py:295
  28.2 2.2 %collective-permute-start.5 = (bf16[64,2048]{1,0:T(8,128)(2,1)S(1)}, bf16[64,2048]{1,0:T(8,128)(2,1)S(1)}, u32[]{:S(2)}, u32[]{:S(2)}) collective-permute-start(bf16[64,2048]{1,0:T(8,128)(2,1)S(1)} %pick.1), channel_id=1, source_target_pairs={{0,16},{8,24},{16,0},{24,8},{1,17},{9,25},{17,1},{25,9},{2,18},{10... | collective-permute-start | bytes 786440 | tf_op jit(solution)/shard_map/ppermute | solution.py:22
  30.3 1.7 %other.2 = (bf16[8,256,256]{2,1,0:T(8,128)(2,1)S(1)}, f32[8,256,128]{2,1,0:T(8,128)S(1)}, f32[256,128]{1,0:T(8,128)S(1)}) custom-call(s32[16]{0:T(128)S(1)} %copy-done.1, bf16[256,2048]{1,0:T(8,128)(2,1)S(1)} %get-tuple-element.52.q_ref, f32[16,256,128]{2,1,0:T(8,128)S(1)} %get-tuple-element.48.own_top_ref, ...), custom_call_target="tpu_custom_call" | custom-call | tf_op jit(solution)/shard_map/other/pallas_call | solution.py:295
  32.0 0.9 %collective-permute-done.7.vm_ref = bf16[64,2048]{1,0:T(8,128)(2,1)S(1)} collective-permute-done((bf16[64,2048]{1,0:T(8,128)(2,1)S(1)}, bf16[64,2048]{1,0:T(8,128)(2,1)S(1)}, u32[]{:S(2)}, u32[]{:S(2)}) %collective-permute-start.7) | collective-permute-done | bytes 262176 | tf_op jit(solution)/shard_map/ppermute | solution.py:22
  32.9 2.1 %collective-permute-start.8 = (bf16[64,2048]{1,0:T(8,128)(2,1)S(1)}, bf16[64,2048]{1,0:T(8,128)(2,1)S(1)}, u32[]{:S(2)}, u32[]{:S(2)}) collective-permute-start(bf16[64,2048]{1,0:T(8,128)(2,1)S(1)} %collective-permute-done.7.vm_ref), channel_id=1, source_target_pairs={{0,16},{8,24},{16,0},{24,8},{1,17},{9,25},{17,1},{25,9},{2,18},{10... | collective-permute-start | bytes 786440 | tf_op jit(solution)/shard_map/ppermute | solution.py:22
  35.1 2.0 %collective-permute-done.5.diagonal_k_ref = bf16[64,2048]{1,0:T(8,128)(2,1)S(1)} collective-permute-done((bf16[64,2048]{1,0:T(8,128)(2,1)S(1)}, bf16[64,2048]{1,0:T(8,128)(2,1)S(1)}, u32[]{:S(2)}, u32[]{:S(2)}) %collective-permute-start.5) | collective-permute-done | bytes 262176 | tf_op jit(solution)/shard_map/ppermute | solution.py:22
  37.1 1.3 %collective-permute-start.11 = (bf16[192,128]{1,0:T(8,128)(2,1)S(1)}, bf16[192,128]{1,0:T(8,128)(2,1)S(1)}, u32[]{:S(2)}, u32[]{:S(2)}) collective-permute-start(bf16[192,128]{1,0:T(8,128)(2,1)S(1)} %get-tuple-element.72), channel_id=1, source_target_pairs={{0,8},{8,0},{16,24},{24,16},{1,9},{9,1},{17,25},{25,17},{2,10},{10... | collective-permute-start | bytes 147464 | tf_op jit(solution)/shard_map/ppermute | solution.py:22
  38.5 1.7 %other.3 = (bf16[8,256,256]{2,1,0:T(8,128)(2,1)S(1)}, f32[8,256,128]{2,1,0:T(8,128)S(1)}, f32[256,128]{1,0:T(8,128)S(1)}) custom-call(s32[16]{0:T(128)S(1)} %copy-done.1, bf16[256,2048]{1,0:T(8,128)(2,1)S(1)} %get-tuple-element.52.q_ref, f32[16,256,128]{2,1,0:T(8,128)S(1)} %get-tuple-element.48.own_top_ref, ...), custom_call_target="tpu_custom_call" | custom-call | tf_op jit(solution)/shard_map/other/pallas_call | solution.py:295
  40.2 1.9 %own.1 = (f32[256,2048]{1,0:T(8,128)S(1)}, f32[256,128]{1,0:T(8,128)S(1)}) custom-call(s32[16]{0:T(128)S(1)} %copy-done.1, f32[16,256,256]{2,1,0:T(8,128)S(1)} %get-tuple-element.44.scores_ref, f32[8,256,128]{2,1,0:T(8,128)S(1)} %get-tuple-element.50.top_a_ref, f32[8,256,128]{2,1,0:T(8,128)S(1)} %get-tuple-element.53.top_b_ref, ...), custom_call_target="tpu_custom_call" | custom-call | tf_op jit(solution)/shard_map/own/pallas_call | solution.py:295
  42.0 3.5 %extra.1 = (f32[256,2048]{1,0:T(8,128)S(1)}, f32[256,128]{1,0:T(8,128)S(1)}) custom-call(s32[16]{0:T(128)S(1)} %copy-done.1, s32[16]{0:T(128)S(1)} %copy-done.3, bf16[256,2048]{1,0:T(8,128)(2,1)S(1)} %get-tuple-element.52.q_ref, f32[256,128]{1,0:T(8,128)S(1)} %get-tuple-element.55.own_total_ref, f32[256,128]{1,0:T(8,128)S(1)} %get-tuple-element.51.state_a_ref, ...), custom_call_target="tpu_custom_call" | custom-call | tf_op jit(solution)/shard_map/extra/pallas_call | solution.py:295
  45.8 0.6 %base.5 = (f32[256,1536]{1,0:T(8,128)S(1)}, f32[256,1536]{1,0:T(8,128)S(1)}) custom-call(f32[256,2048]{1,0:T(8,128)S(1)} %get-tuple-element.65.sum_ref, f32[256,128]{1,0:T(8,128)S(1)} %get-tuple-element.66.share_ref, f32[256,2048]{1,0:T(8,128)S(1)} %get-tuple-element.67.own_ref), custom_call_target="tpu_custom_call" | custom-call | tf_op jit(solution)/shard_map/base/pallas_call | solution.py:295
  46.4 1.4 %finish.3.rest_0_ = bf16[256,2048]{1,0:T(8,128)(2,1)} custom-call(f32[256,1536]{1,0:T(8,128)S(1)} %get-tuple-element.76.base_ref, f32[256,1536]{1,0:T(8,128)S(1)} %get-tuple-element.77.spread_ref, bf16[8,256,256]{2,1,0:T(8,128)(2,1)S(1)} %get-tuple-element.70.other_a_ref, bf16[8,256,256]{2,1,0:T(8,128)(2,1)S(1)} %get-tuple-element.71.other_b_ref, ...), custom_call_target="tpu_custom_call" | custom-call | tf_op jit(solution)/shard_map/finish/pallas_call | solution.py:295
  47.8 0.6 %collective-permute-done.12.vr_ref = bf16[192,384]{1,0:T(8,128)(2,1)S(1)} collective-permute-done((bf16[192,384]{1,0:T(8,128)(2,1)S(1)}, bf16[192,384]{1,0:T(8,128)(2,1)S(1)}, u32[]{:S(2)}, u32[]{:S(2)}) %collective-permute-start.12) | collective-permute-done | bytes 147488 | tf_op jit(solution)/shard_map/ppermute | solution.py:22
  48.4 0.9 %finish.4.rest_0_ = bf16[256,2048]{1,0:T(8,128)(2,1)} custom-call(f32[256,384]{1,0:T(8,128)S(1)} %get-tuple-element.73.base_ref, f32[256,384]{1,0:T(8,128)S(1)} %get-tuple-element.74.spread_ref, bf16[8,256,256]{2,1,0:T(8,128)(2,1)S(1)} %get-tuple-element.70.other_a_ref, ...), custom_call_target="tpu_custom_call", output_to_operand_aliasing={{}: (6, {})} | custom-call | tf_op jit(solution)/shard_map/finish/pallas_call | solution.py:295
  49.4 0.8 %finish.5 = bf16[256,2048]{1,0:T(8,128)(2,1)} custom-call(f32[256,128]{1,0:T(8,128)S(1)} %get-tuple-element.68.base_ref, f32[256,128]{1,0:T(8,128)S(1)} %get-tuple-element.69.spread_ref, bf16[8,256,256]{2,1,0:T(8,128)(2,1)S(1)} %get-tuple-element.70.other_a_ref, ...), custom_call_target="tpu_custom_call", output_to_operand_aliasing={{}: (6, {})} | custom-call | tf_op jit(solution)/shard_map/finish/pallas_call | solution.py:295
  (21 shorter events, 0.4 us)
Async XLA Ops:
  0.0 27.3 %collective-permute-start.4 = (bf16[256,2048]{1,0:T(8,128)(2,1)}, bf16[256,2048]{1,0:T(8,128)(2,1)S(1)}, u32[]{:S(2)}, u32[]{:S(2)}) collective-permute-start(bf16[256,2048]{1,0:T(8,128)(2,1)} %k_hbm.1), channel_id=1, source_target_pairs={{0,8},{8,0},{16,24},{24,16},{1,9},{9,1},{17,25},{25,17},{2,10},{10... | collective-permute-start | bytes 3145736 | tf_op jit(solution)/shard_map/ppermute | solution.py:22
  2.9 0.7 %copy-start = (s32[16]{0:T(128)S(1)}, s32[16]{0:T(128)}, u32[]{:S(2)}) copy-start(s32[16]{0:T(128)} %middle_ref.11) | copy-start | bytes 196
  3.6 0.7 %copy-start.2 = (s32[16]{0:T(128)S(1)}, s32[16]{0:T(128)}, u32[]{:S(2)}) copy-start(s32[16]{0:T(128)} %coarse_ref.3) | copy-start | bytes 196
  4.3 23.1 %copy-start.1 = (s32[16]{0:T(128)S(1)}, s32[16]{0:T(128)}, u32[]{:S(2)}) copy-start(s32[16]{0:T(128)} %middle_ref.11) | copy-start | bytes 196
  7.5 16.7 %collective-permute-start.6 = (bf16[128,2048]{1,0:T(8,128)(2,1)S(1)}, bf16[128,2048]{1,0:T(8,128)(2,1)S(1)}, u32[]{:S(2)}, u32[]{:S(2)}) collective-permute-start(bf16[128,2048]{1,0:T(8,128)(2,1)S(1)} %get-tuple-element.57), channel_id=1, source_target_pairs={{0,16},{8,24},{16,0},{24,8},{1,17},{9,25},{17,1},{25,9},{2,18},{10... | collective-permute-start | bytes 1572872 | tf_op jit(solution)/shard_map/ppermute | solution.py:22
  9.1 4.7 %collective-permute-start = (bf16[2,2048]{1,0:T(2,128)(2,1)S(1)}, bf16[2,2048]{1,0:T(2,128)(2,1)S(1)}, u32[]{:S(2)}, u32[]{:S(2)}) collective-permute-start(bf16[2,2048]{1,0:T(2,128)(2,1)S(1)} %get-tuple-element.45.refs_0_), channel_id=1, source_target_pairs={{0,10},{1,11},{2,8},{3,9},{4,14},{5,15},{6,12},{7,13},{8,2},{9,3},... | collective-permute-start | bytes 24584 | tf_op jit(solution)/shard_map/ppermute | solution.py:32
  13.8 5.3 %collective-permute-start.1 = (bf16[4,2048]{1,0:T(4,128)(2,1)S(1)}, bf16[4,2048]{1,0:T(4,128)(2,1)S(1)}, u32[]{:S(2)}, u32[]{:S(2)}) collective-permute-start(bf16[4,2048]{1,0:T(4,128)(2,1)S(1)} %stack.2.refs_0_), channel_id=1, source_target_pairs={{0,2},{1,3},{2,0},{3,1},{4,6},{5,7},{6,4},{7,5},{8,10},{9,11},{10,... | collective-permute-start | bytes 49160 | tf_op jit(solution)/shard_map/ppermute | solution.py:22
  15.4 4.9 %collective-permute-start.2 = (bf16[4,2048]{1,0:T(4,128)(2,1)S(1)}, bf16[4,2048]{1,0:T(4,128)(2,1)S(1)}, u32[]{:S(2)}, u32[]{:S(2)}) collective-permute-start(bf16[4,2048]{1,0:T(4,128)(2,1)S(1)} %stack.2.refs_0_), channel_id=1, source_target_pairs={{0,4},{1,5},{2,6},{3,7},{4,0},{5,1},{6,2},{7,3},{8,12},{9,13},{10,... | collective-permute-start | bytes 49160 | tf_op jit(solution)/shard_map/ppermute | solution.py:22
  18.0 5.5 %collective-permute-start.3 = (bf16[4,2048]{1,0:T(4,128)(2,1)S(1)}, bf16[4,2048]{1,0:T(4,128)(2,1)S(1)}, u32[]{:S(2)}, u32[]{:S(2)}) collective-permute-start(bf16[4,2048]{1,0:T(4,128)(2,1)S(1)} %stack.2.refs_0_), channel_id=1, source_target_pairs={{0,6},{1,7},{2,4},{3,5},{4,2},{5,3},{6,0},{7,1},{8,14},{9,15},{10,... | collective-permute-start | bytes 49160 | tf_op jit(solution)/shard_map/ppermute | solution.py:22
  23.6 9.4 %collective-permute-start.7 = (bf16[64,2048]{1,0:T(8,128)(2,1)S(1)}, bf16[64,2048]{1,0:T(8,128)(2,1)S(1)}, u32[]{:S(2)}, u32[]{:S(2)}) collective-permute-start(bf16[64,2048]{1,0:T(8,128)(2,1)S(1)} %get-tuple-element.62), channel_id=1, source_target_pairs={{0,8},{8,0},{16,24},{24,16},{1,9},{9,1},{17,25},{25,17},{2,10},{10... | collective-permute-start | bytes 786440 | tf_op jit(solution)/shard_map/ppermute | solution.py:22
  24.2 22.2 %collective-permute-start.13 = (bf16[192,1536]{1,0:T(8,128)(2,1)S(1)}, bf16[192,1536]{1,0:T(8,128)(2,1)S(1)}, u32[]{:S(2)}, u32[]{:S(2)}) collective-permute-start(bf16[192,1536]{1,0:T(8,128)(2,1)S(1)} %get-tuple-element.78), channel_id=1, source_target_pairs={{0,8},{8,0},{16,24},{24,16},{1,9},{9,1},{17,25},{25,17},{2,10},{10... | collective-permute-start | bytes 1769480 | tf_op jit(solution)/shard_map/ppermute | solution.py:22
  25.6 9.4 %collective-permute-start.9 = (bf16[16,2048]{1,0:T(8,128)(2,1)S(1)}, bf16[16,2048]{1,0:T(8,128)(2,1)S(1)}, u32[]{:S(2)}, u32[]{:S(2)}) collective-permute-start(bf16[16,2048]{1,0:T(8,128)(2,1)S(1)} %stack.3), channel_id=1, source_target_pairs={{0,18},{1,19},{2,16},{3,17},{4,22},{5,23},{6,20},{7,21},{8,26},{9,... | collective-permute-start | bytes 196616 | tf_op jit(solution)/shard_map/ppermute | solution.py:32
  25.7 22.8 %collective-permute-start.12 = (bf16[192,384]{1,0:T(8,128)(2,1)S(1)}, bf16[192,384]{1,0:T(8,128)(2,1)S(1)}, u32[]{:S(2)}, u32[]{:S(2)}) collective-permute-start(bf16[192,384]{1,0:T(8,128)(2,1)S(1)} %get-tuple-element.75), channel_id=1, source_target_pairs={{0,8},{8,0},{16,24},{24,16},{1,9},{9,1},{17,25},{25,17},{2,10},{10... | collective-permute-start | bytes 442376 | tf_op jit(solution)/shard_map/ppermute | solution.py:22
  28.2 9.0 %collective-permute-start.5 = (bf16[64,2048]{1,0:T(8,128)(2,1)S(1)}, bf16[64,2048]{1,0:T(8,128)(2,1)S(1)}, u32[]{:S(2)}, u32[]{:S(2)}) collective-permute-start(bf16[64,2048]{1,0:T(8,128)(2,1)S(1)} %pick.1), channel_id=1, source_target_pairs={{0,16},{8,24},{16,0},{24,8},{1,17},{9,25},{17,1},{25,9},{2,18},{10... | collective-permute-start | bytes 786440 | tf_op jit(solution)/shard_map/ppermute | solution.py:22
  32.9 9.1 %collective-permute-start.8 = (bf16[64,2048]{1,0:T(8,128)(2,1)S(1)}, bf16[64,2048]{1,0:T(8,128)(2,1)S(1)}, u32[]{:S(2)}, u32[]{:S(2)}) collective-permute-start(bf16[64,2048]{1,0:T(8,128)(2,1)S(1)} %collective-permute-done.7.vm_ref), channel_id=1, source_target_pairs={{0,16},{8,24},{16,0},{24,8},{1,17},{9,25},{17,1},{25,9},{2,18},{10... | collective-permute-start | bytes 786440 | tf_op jit(solution)/shard_map/ppermute | solution.py:22
  35.0 7.0 %collective-permute-start.10 = (bf16[32,2048]{1,0:T(8,128)(2,1)S(1)}, bf16[32,2048]{1,0:T(8,128)(2,1)S(1)}, u32[]{:S(2)}, u32[]{:S(2)}) collective-permute-start(bf16[32,2048]{1,0:T(8,128)(2,1)S(1)} %constant_dynamic-update-slice_fusion.mine_ref), channel_id=1, source_target_pairs={{0,1},{1,0},{2,3},{3,2},{4,5},{5,4},{6,7},{7,6},{8,9},{9,8},{10,11... | collective-permute-start | bytes 393224 | tf_op jit(solution)/shard_map/ppermute | solution.py:22
  37.1 12.2 %collective-permute-start.11 = (bf16[192,128]{1,0:T(8,128)(2,1)S(1)}, bf16[192,128]{1,0:T(8,128)(2,1)S(1)}, u32[]{:S(2)}, u32[]{:S(2)}) collective-permute-start(bf16[192,128]{1,0:T(8,128)(2,1)S(1)} %get-tuple-element.72), channel_id=1, source_target_pairs={{0,8},{8,0},{16,24},{24,16},{1,9},{9,1},{17,25},{25,17},{2,10},{10... | collective-permute-start | bytes 147464 | tf_op jit(solution)/shard_map/ppermute | solution.py:22
  40.1 1.9 %copy-start.3 = (s32[16]{0:T(128)S(1)}, s32[16]{0:T(128)}, u32[]{:S(2)}) copy-start(s32[16]{0:T(128)} %coarse_ref.3) | copy-start | bytes 196

commit v17 on v16

--- a/solution.py
+++ b/solution.py
@@ -10,7 +10,7 @@
 HEAD_COUNT = 16
 HEAD_FEATURES = 128
 MIDDLE_DILATION = 4
-CHUNKS = (12, 3, 1)
+CHUNKS = (12, 4)
 LANES = 128
 SUBLANES = 16
 EXP2_SCALE = HEAD_FEATURES ** (-0.5) * 1.4426950408889634

time: 50.3 us -> 50.1 us (level)
  waiting for transfers between devices: 12.3 us -> 14.1 us
  starting transfers between devices: 18.9 us -> 17.5 us
  Pallas kernels: 17.6 us -> 16.8 us
    ppermute x12 -> x11, waiting for transfers between devices: 9.15 us -> 11 us  [partner(): return lax.ppermute(value, axis, pairs)]
    ppermute x12 -> x11, starting transfers between devices: 17.3 us -> 16 us  [partner(): return lax.ppermute(value, axis, pairs)]
    pallas_call x13 -> x11, Pallas kernels: 17.5 us -> 16.8 us  [call(): pl.pallas_call(kernel, name=name, compiler_params=params, cost_estimate=c...]
  transfers between devices with their start and end apart: 14 -> 13, of which waited for: 7 -> 8; matrix products, arithmetic and copies ran while one was open for 0% -> 0% of each run, Pallas kernels for 33% -> 32%
where the time goes in v17:
time: 50.1 us; the launch traced here: 49.9 us
  starting transfers between devices  17.5 us (35%)
  Pallas kernels  16.8 us (34%)
  waiting for transfers between devices  14.1 us (28%)
  local copies, waits for them, and re-layouts  1.33 us (3%)
    pallas_call x11, Pallas kernels, call(): pl.pallas_call(kernel, name=name, compiler_params=params, cost_estimate=c...  16.8 us
    ppermute x11, starting transfers between devices, partner(): return lax.ppermute(value, axis, pairs)  16 us
    ppermute x11, waiting for transfers between devices, partner(): return lax.ppermute(value, axis, pairs)  11 us
    ppermute x2, waiting for transfers between devices, partner_elsewhere(): return lax.ppermute(value, ('inner', 'outer'), pairs)  3.11 us
    ppermute x2, starting transfers between devices, partner_elsewhere(): return lax.ppermute(value, ('inner', 'outer'), pairs)  1.55 us
    unnamed x9, local copies, waits for them, and re-layouts  1.32 us
  transfers between devices with their start and end apart: 13, of which 8 were waited for; matrix products, arithmetic and copies ran while one was open for 0% of the time, Pallas kernels for 32%

profile of v17, /device:TPU:0, one launch (start us, length us, event | category | flops | bytes accessed | tf_op | source)
XLA Modules:
  0.0 49.9 jit_solution(9131690600029481707)
XLA Ops:
  0.0 2.9 %collective-permute-start.4 = (bf16[256,2048]{1,0:T(8,128)(2,1)}, bf16[256,2048]{1,0:T(8,128)(2,1)S(1)}, u32[]{:S(2)}, u32[]{:S(2)}) collective-permute-start(bf16[256,2048]{1,0:T(8,128)(2,1)} %k_hbm.1), channel_id=1, source_target_pairs={{0,8},{8,0},{16,24},{24,16},{1,9},{9,1},{17,25},{25,17},{2,10},{10... | collective-permute-start | bytes 3145736 | tf_op jit(solution)/shard_map/ppermute | solution.py:22
  2.9 0.7 %copy-done = s32[16]{0:T(128)S(1)} copy-done((s32[16]{0:T(128)S(1)}, s32[16]{0:T(128)}, u32[]{:S(2)}) %copy-start) | copy-done | bytes 88
  3.6 0.7 %copy-done.2 = s32[16]{0:T(128)S(1)} copy-done((s32[16]{0:T(128)S(1)}, s32[16]{0:T(128)}, u32[]{:S(2)}) %copy-start.2) | copy-done | bytes 88
  4.3 3.2 %prepare.1 = (bf16[256,2048]{1,0:T(8,128)(2,1)S(1)}, bf16[256,2048]{1,0:T(8,128)(2,1)S(1)}, bf16[256,2048]{1,0:T(8,128)(2,1)S(1)}, bf16[128,2048]{1,0:T(8,128)(2...) custom-call(s32[16]{0:T(128)S(1)} %copy-done, ...), custom_call_target="tpu_custom_call" | custom-call | tf_op jit(solution)/shard_map/prepare/pallas_call | solution.py:295
  7.5 1.6 %collective-permute-start.6 = (bf16[128,2048]{1,0:T(8,128)(2,1)S(1)}, bf16[128,2048]{1,0:T(8,128)(2,1)S(1)}, u32[]{:S(2)}, u32[]{:S(2)}) collective-permute-start(bf16[128,2048]{1,0:T(8,128)(2,1)S(1)} %get-tuple-element.53), channel_id=1, source_target_pairs={{0,16},{8,24},{16,0},{24,8},{1,17},{9,25},{17,1},{25,9},{2,18},{10... | collective-permute-start | bytes 1572872 | tf_op jit(solution)/shard_map/ppermute | solution.py:22
  9.1 1.5 %collective-permute-start = (bf16[2,2048]{1,0:T(2,128)(2,1)S(1)}, bf16[2,2048]{1,0:T(2,128)(2,1)S(1)}, u32[]{:S(2)}, u32[]{:S(2)}) collective-permute-start(bf16[2,2048]{1,0:T(2,128)(2,1)S(1)} %get-tuple-element.41.refs_0_), channel_id=1, source_target_pairs={{0,10},{1,11},{2,8},{3,9},{4,14},{5,15},{6,12},{7,13},{8,2},{9,3},... | collective-permute-start | bytes 24584 | tf_op jit(solution)/shard_map/ppermute | solution.py:32
  10.6 3.1 %collective-permute-done.refs_1_ = bf16[2,2048]{1,0:T(2,128)(2,1)S(1)} collective-permute-done((bf16[2,2048]{1,0:T(2,128)(2,1)S(1)}, bf16[2,2048]{1,0:T(2,128)(2,1)S(1)}, u32[]{:S(2)}, u32[]{:S(2)}) %collective-permute-start) | collective-permute-done | bytes 8224 | tf_op jit(solution)/shard_map/ppermute | solution.py:32
  13.8 1.6 %collective-permute-start.1 = (bf16[4,2048]{1,0:T(4,128)(2,1)S(1)}, bf16[4,2048]{1,0:T(4,128)(2,1)S(1)}, u32[]{:S(2)}, u32[]{:S(2)}) collective-permute-start(bf16[4,2048]{1,0:T(4,128)(2,1)S(1)} %stack.2.refs_0_), channel_id=1, source_target_pairs={{0,2},{1,3},{2,0},{3,1},{4,6},{5,7},{6,4},{7,5},{8,10},{9,11},{10,... | collective-permute-start | bytes 49160 | tf_op jit(solution)/shard_map/ppermute | solution.py:22
  15.4 2.6 %collective-permute-start.2 = (bf16[4,2048]{1,0:T(4,128)(2,1)S(1)}, bf16[4,2048]{1,0:T(4,128)(2,1)S(1)}, u32[]{:S(2)}, u32[]{:S(2)}) collective-permute-start(bf16[4,2048]{1,0:T(4,128)(2,1)S(1)} %stack.2.refs_0_), channel_id=1, source_target_pairs={{0,4},{1,5},{2,6},{3,7},{4,0},{5,1},{6,2},{7,3},{8,12},{9,13},{10,... | collective-permute-start | bytes 49160 | tf_op jit(solution)/shard_map/ppermute | solution.py:22
  18.0 0.2 collective-permute-start.3
  18.2 0.8 %score.1 = (f32[16,256,256]{2,1,0:T(8,128)S(1)}, f32[16,256,128]{2,1,0:T(8,128)S(1)}) custom-call(bf16[256,2048]{1,0:T(8,128)(2,1)S(1)} %get-tuple-element.48.q_ref, bf16[256,2048]{1,0:T(8,128)(2,1)S(1)} %get-tuple-element.39.k_ref), custom_call_target="tpu_custom_call" | custom-call | tf_op jit(solution)/shard_map/score/pallas_call | solution.py:295
  19.0 1.2 %collective-permute-done.2.refs_2_ = bf16[4,2048]{1,0:T(4,128)(2,1)S(1)} collective-permute-done((bf16[4,2048]{1,0:T(4,128)(2,1)S(1)}, bf16[4,2048]{1,0:T(4,128)(2,1)S(1)}, u32[]{:S(2)}, u32[]{:S(2)}) %collective-permute-start.2) | collective-permute-done | bytes 16416 | tf_op jit(solution)/shard_map/ppermute | solution.py:22
  20.3 3.2 %collective-permute-done.3.refs_3_ = bf16[4,2048]{1,0:T(4,128)(2,1)S(1)} collective-permute-done((bf16[4,2048]{1,0:T(4,128)(2,1)S(1)}, bf16[4,2048]{1,0:T(4,128)(2,1)S(1)}, u32[]{:S(2)}, u32[]{:S(2)}) %collective-permute-start.3) | collective-permute-done | bytes 16416 | tf_op jit(solution)/shard_map/ppermute | solution.py:22
  23.5 0.6 %collective-permute-start.7 = (bf16[64,2048]{1,0:T(8,128)(2,1)S(1)}, bf16[64,2048]{1,0:T(8,128)(2,1)S(1)}, u32[]{:S(2)}, u32[]{:S(2)}) collective-permute-start(bf16[64,2048]{1,0:T(8,128)(2,1)S(1)} %get-tuple-element.57), channel_id=1, source_target_pairs={{0,8},{8,0},{16,24},{24,16},{1,9},{9,1},{17,25},{25,17},{2,10},{10... | collective-permute-start | bytes 786440 | tf_op jit(solution)/shard_map/ppermute | solution.py:22
  24.1 1.5 %collective-permute-start.12 = (bf16[192,1536]{1,0:T(8,128)(2,1)S(1)}, bf16[192,1536]{1,0:T(8,128)(2,1)S(1)}, u32[]{:S(2)}, u32[]{:S(2)}) collective-permute-start(bf16[192,1536]{1,0:T(8,128)(2,1)S(1)} %get-tuple-element.70), channel_id=1, source_target_pairs={{0,8},{8,0},{16,24},{24,16},{1,9},{9,1},{17,25},{25,17},{2,10},{10... | collective-permute-start | bytes 1769480 | tf_op jit(solution)/shard_map/ppermute | solution.py:22
  25.7 0.6 %collective-permute-start.11 = (bf16[192,512]{1,0:T(8,128)(2,1)S(1)}, bf16[192,512]{1,0:T(8,128)(2,1)S(1)}, u32[]{:S(2)}, u32[]{:S(2)}) collective-permute-start(bf16[192,512]{1,0:T(8,128)(2,1)S(1)} %get-tuple-element.67), channel_id=1, source_target_pairs={{0,8},{8,0},{16,24},{24,16},{1,9},{9,1},{17,25},{25,17},{2,10},{10... | collective-permute-start | bytes 589832 | tf_op jit(solution)/shard_map/ppermute | solution.py:22
  26.3 1.1 %collective-permute-done.4.k_ref.kp_ref = bf16[256,2048]{1,0:T(8,128)(2,1)S(1)} collective-permute-done((bf16[256,2048]{1,0:T(8,128)(2,1)}, bf16[256,2048]{1,0:T(8,128)(2,1)S(1)}, u32[]{:S(2)}, u32[]{:S(2)}) %collective-permute-start.4) | collective-permute-done | bytes 1048608 | tf_op jit(solution)/shard_map/ppermute | solution.py:22
  27.3 0.8 %pick.1 = bf16[64,2048]{1,0:T(8,128)(2,1)S(1)} custom-call(s32[16]{0:T(128)S(1)} %copy-done.1, bf16[256,2048]{1,0:T(8,128)(2,1)S(1)} %collective-permute-done.4.k_ref.kp_ref), custom_call_target="tpu_custom_call" | custom-call | tf_op jit(solution)/shard_map/pick/pallas_call | solution.py:295
  28.2 2.2 %collective-permute-start.5 = (bf16[64,2048]{1,0:T(8,128)(2,1)S(1)}, bf16[64,2048]{1,0:T(8,128)(2,1)S(1)}, u32[]{:S(2)}, u32[]{:S(2)}) collective-permute-start(bf16[64,2048]{1,0:T(8,128)(2,1)S(1)} %pick.1), channel_id=1, source_target_pairs={{0,16},{8,24},{16,0},{24,8},{1,17},{9,25},{17,1},{25,9},{2,18},{10... | collective-permute-start | bytes 786440 | tf_op jit(solution)/shard_map/ppermute | solution.py:22
  30.3 1.7 %other.2 = (bf16[8,256,256]{2,1,0:T(8,128)(2,1)S(1)}, f32[8,256,128]{2,1,0:T(8,128)S(1)}, f32[256,128]{1,0:T(8,128)S(1)}) custom-call(s32[16]{0:T(128)S(1)} %copy-done.1, bf16[256,2048]{1,0:T(8,128)(2,1)S(1)} %get-tuple-element.48.q_ref, f32[16,256,128]{2,1,0:T(8,128)S(1)} %get-tuple-element.44.own_top_ref, ...), custom_call_target="tpu_custom_call" | custom-call | tf_op jit(solution)/shard_map/other/pallas_call | solution.py:295
  32.0 0.9 %collective-permute-done.7.vm_ref = bf16[64,2048]{1,0:T(8,128)(2,1)S(1)} collective-permute-done((bf16[64,2048]{1,0:T(8,128)(2,1)S(1)}, bf16[64,2048]{1,0:T(8,128)(2,1)S(1)}, u32[]{:S(2)}, u32[]{:S(2)}) %collective-permute-start.7) | collective-permute-done | bytes 262176 | tf_op jit(solution)/shard_map/ppermute | solution.py:22
  32.9 2.1 %collective-permute-start.8 = (bf16[64,2048]{1,0:T(8,128)(2,1)S(1)}, bf16[64,2048]{1,0:T(8,128)(2,1)S(1)}, u32[]{:S(2)}, u32[]{:S(2)}) collective-permute-start(bf16[64,2048]{1,0:T(8,128)(2,1)S(1)} %collective-permute-done.7.vm_ref), channel_id=1, source_target_pairs={{0,16},{8,24},{16,0},{24,8},{1,17},{9,25},{17,1},{25,9},{2,18},{10... | collective-permute-start | bytes 786440 | tf_op jit(solution)/shard_map/ppermute | solution.py:22
  35.1 2.0 %collective-permute-done.5.diagonal_k_ref = bf16[64,2048]{1,0:T(8,128)(2,1)S(1)} collective-permute-done((bf16[64,2048]{1,0:T(8,128)(2,1)S(1)}, bf16[64,2048]{1,0:T(8,128)(2,1)S(1)}, u32[]{:S(2)}, u32[]{:S(2)}) %collective-permute-start.5) | collective-permute-done | bytes 262176 | tf_op jit(solution)/shard_map/ppermute | solution.py:22
  37.1 1.7 %other.3 = (bf16[8,256,256]{2,1,0:T(8,128)(2,1)S(1)}, f32[8,256,128]{2,1,0:T(8,128)S(1)}, f32[256,128]{1,0:T(8,128)S(1)}) custom-call(s32[16]{0:T(128)S(1)} %copy-done.1, bf16[256,2048]{1,0:T(8,128)(2,1)S(1)} %get-tuple-element.48.q_ref, f32[16,256,128]{2,1,0:T(8,128)S(1)} %get-tuple-element.44.own_top_ref, ...), custom_call_target="tpu_custom_call" | custom-call | tf_op jit(solution)/shard_map/other/pallas_call | solution.py:295
  38.9 1.9 %own.1 = (f32[256,2048]{1,0:T(8,128)S(1)}, f32[256,128]{1,0:T(8,128)S(1)}) custom-call(s32[16]{0:T(128)S(1)} %copy-done.1, f32[16,256,256]{2,1,0:T(8,128)S(1)} %get-tuple-element.40.scores_ref, f32[8,256,128]{2,1,0:T(8,128)S(1)} %get-tuple-element.46.top_a_ref, f32[8,256,128]{2,1,0:T(8,128)S(1)} %get-tuple-element.49.top_b_ref, ...), custom_call_target="tpu_custom_call" | custom-call | tf_op jit(solution)/shard_map/own/pallas_call | solution.py:295
  40.7 0.5 collective-permute-done.8.diagonal_v_ref
  41.2 3.5 %extra.1 = (f32[256,2048]{1,0:T(8,128)S(1)}, f32[256,128]{1,0:T(8,128)S(1)}) custom-call(s32[16]{0:T(128)S(1)} %copy-done.1, s32[16]{0:T(128)S(1)} %copy-done.3, bf16[256,2048]{1,0:T(8,128)(2,1)S(1)} %get-tuple-element.48.q_ref, f32[256,128]{1,0:T(8,128)S(1)} %get-tuple-element.51.own_total_ref, f32[256,128]{1,0:T(8,128)S(1)} %get-tuple-element.47.state_a_ref, ...), custom_call_target="tpu_custom_call" | custom-call | tf_op jit(solution)/shard_map/extra/pallas_call | solution.py:295
  44.7 0.2 base.2
  45.0 0.6 %base.3 = (f32[256,1536]{1,0:T(8,128)S(1)}, f32[256,1536]{1,0:T(8,128)S(1)}) custom-call(f32[256,2048]{1,0:T(8,128)S(1)} %get-tuple-element.60.sum_ref, f32[256,128]{1,0:T(8,128)S(1)} %get-tuple-element.61.share_ref, f32[256,2048]{1,0:T(8,128)S(1)} %get-tuple-element.62.own_ref), custom_call_target="tpu_custom_call" | custom-call | tf_op jit(solution)/shard_map/base/pallas_call | solution.py:295
  45.6 1.4 %finish.2.rest_0_ = bf16[256,2048]{1,0:T(8,128)(2,1)} custom-call(f32[256,1536]{1,0:T(8,128)S(1)} %get-tuple-element.68.base_ref, f32[256,1536]{1,0:T(8,128)S(1)} %get-tuple-element.69.spread_ref, bf16[8,256,256]{2,1,0:T(8,128)(2,1)S(1)} %get-tuple-element.65.other_a_ref, bf16[8,256,256]{2,1,0:T(8,128)(2,1)S(1)} %get-tuple-element.66.other_b_ref, ...), custom_call_target="tpu_custom_call" | custom-call | tf_op jit(solution)/shard_map/finish/pallas_call | solution.py:295
  46.9 2.0 %collective-permute-done.11.vr_ref = bf16[192,512]{1,0:T(8,128)(2,1)S(1)} collective-permute-done((bf16[192,512]{1,0:T(8,128)(2,1)S(1)}, bf16[192,512]{1,0:T(8,128)(2,1)S(1)}, u32[]{:S(2)}, u32[]{:S(2)}) %collective-permute-start.11) | collective-permute-done | bytes 196640 | tf_op jit(solution)/shard_map/ppermute | solution.py:22
  49.0 1.0 %finish.3 = bf16[256,2048]{1,0:T(8,128)(2,1)} custom-call(f32[256,512]{1,0:T(8,128)S(1)} %get-tuple-element.63.base_ref, f32[256,512]{1,0:T(8,128)S(1)} %get-tuple-element.64.spread_ref, bf16[8,256,256]{2,1,0:T(8,128)(2,1)S(1)} %get-tuple-element.65.other_a_ref, ...), custom_call_target="tpu_custom_call", output_to_operand_aliasing={{}: (6, {})} | custom-call | tf_op jit(solution)/shard_map/finish/pallas_call | solution.py:295
  (17 shorter events, 0.2 us)
Async XLA Ops:
  0.0 27.3 %collective-permute-start.4 = (bf16[256,2048]{1,0:T(8,128)(2,1)}, bf16[256,2048]{1,0:T(8,128)(2,1)S(1)}, u32[]{:S(2)}, u32[]{:S(2)}) collective-permute-start(bf16[256,2048]{1,0:T(8,128)(2,1)} %k_hbm.1), channel_id=1, source_target_pairs={{0,8},{8,0},{16,24},{24,16},{1,9},{9,1},{17,25},{25,17},{2,10},{10... | collective-permute-start | bytes 3145736 | tf_op jit(solution)/shard_map/ppermute | solution.py:22
  2.9 0.7 %copy-start = (s32[16]{0:T(128)S(1)}, s32[16]{0:T(128)}, u32[]{:S(2)}) copy-start(s32[16]{0:T(128)} %middle_ref.11) | copy-start | bytes 196
  3.6 0.7 %copy-start.2 = (s32[16]{0:T(128)S(1)}, s32[16]{0:T(128)}, u32[]{:S(2)}) copy-start(s32[16]{0:T(128)} %coarse_ref.3) | copy-start | bytes 196
  4.3 23.1 %copy-start.1 = (s32[16]{0:T(128)S(1)}, s32[16]{0:T(128)}, u32[]{:S(2)}) copy-start(s32[16]{0:T(128)} %middle_ref.11) | copy-start | bytes 196
  7.5 16.7 %collective-permute-start.6 = (bf16[128,2048]{1,0:T(8,128)(2,1)S(1)}, bf16[128,2048]{1,0:T(8,128)(2,1)S(1)}, u32[]{:S(2)}, u32[]{:S(2)}) collective-permute-start(bf16[128,2048]{1,0:T(8,128)(2,1)S(1)} %get-tuple-element.53), channel_id=1, source_target_pairs={{0,16},{8,24},{16,0},{24,8},{1,17},{9,25},{17,1},{25,9},{2,18},{10... | collective-permute-start | bytes 1572872 | tf_op jit(solution)/shard_map/ppermute | solution.py:22
  9.1 4.7 %collective-permute-start = (bf16[2,2048]{1,0:T(2,128)(2,1)S(1)}, bf16[2,2048]{1,0:T(2,128)(2,1)S(1)}, u32[]{:S(2)}, u32[]{:S(2)}) collective-permute-start(bf16[2,2048]{1,0:T(2,128)(2,1)S(1)} %get-tuple-element.41.refs_0_), channel_id=1, source_target_pairs={{0,10},{1,11},{2,8},{3,9},{4,14},{5,15},{6,12},{7,13},{8,2},{9,3},... | collective-permute-start | bytes 24584 | tf_op jit(solution)/shard_map/ppermute | solution.py:32
  13.8 5.3 %collective-permute-start.1 = (bf16[4,2048]{1,0:T(4,128)(2,1)S(1)}, bf16[4,2048]{1,0:T(4,128)(2,1)S(1)}, u32[]{:S(2)}, u32[]{:S(2)}) collective-permute-start(bf16[4,2048]{1,0:T(4,128)(2,1)S(1)} %stack.2.refs_0_), channel_id=1, source_target_pairs={{0,2},{1,3},{2,0},{3,1},{4,6},{5,7},{6,4},{7,5},{8,10},{9,11},{10,... | collective-permute-start | bytes 49160 | tf_op jit(solution)/shard_map/ppermute | solution.py:22
  15.4 4.9 %collective-permute-start.2 = (bf16[4,2048]{1,0:T(4,128)(2,1)S(1)}, bf16[4,2048]{1,0:T(4,128)(2,1)S(1)}, u32[]{:S(2)}, u32[]{:S(2)}) collective-permute-start(bf16[4,2048]{1,0:T(4,128)(2,1)S(1)} %stack.2.refs_0_), channel_id=1, source_target_pairs={{0,4},{1,5},{2,6},{3,7},{4,0},{5,1},{6,2},{7,3},{8,12},{9,13},{10,... | collective-permute-start | bytes 49160 | tf_op jit(solution)/shard_map/ppermute | solution.py:22
  18.0 5.5 %collective-permute-start.3 = (bf16[4,2048]{1,0:T(4,128)(2,1)S(1)}, bf16[4,2048]{1,0:T(4,128)(2,1)S(1)}, u32[]{:S(2)}, u32[]{:S(2)}) collective-permute-start(bf16[4,2048]{1,0:T(4,128)(2,1)S(1)} %stack.2.refs_0_), channel_id=1, source_target_pairs={{0,6},{1,7},{2,4},{3,5},{4,2},{5,3},{6,0},{7,1},{8,14},{9,15},{10,... | collective-permute-start | bytes 49160 | tf_op jit(solution)/shard_map/ppermute | solution.py:22
  23.5 9.4 %collective-permute-start.7 = (bf16[64,2048]{1,0:T(8,128)(2,1)S(1)}, bf16[64,2048]{1,0:T(8,128)(2,1)S(1)}, u32[]{:S(2)}, u32[]{:S(2)}) collective-permute-start(bf16[64,2048]{1,0:T(8,128)(2,1)S(1)} %get-tuple-element.57), channel_id=1, source_target_pairs={{0,8},{8,0},{16,24},{24,16},{1,9},{9,1},{17,25},{25,17},{2,10},{10... | collective-permute-start | bytes 786440 | tf_op jit(solution)/shard_map/ppermute | solution.py:22
  24.1 21.4 %collective-permute-start.12 = (bf16[192,1536]{1,0:T(8,128)(2,1)S(1)}, bf16[192,1536]{1,0:T(8,128)(2,1)S(1)}, u32[]{:S(2)}, u32[]{:S(2)}) collective-permute-start(bf16[192,1536]{1,0:T(8,128)(2,1)S(1)} %get-tuple-element.70), channel_id=1, source_target_pairs={{0,8},{8,0},{16,24},{24,16},{1,9},{9,1},{17,25},{25,17},{2,10},{10... | collective-permute-start | bytes 1769480 | tf_op jit(solution)/shard_map/ppermute | solution.py:22
  25.6 9.4 %collective-permute-start.9 = (bf16[16,2048]{1,0:T(8,128)(2,1)S(1)}, bf16[16,2048]{1,0:T(8,128)(2,1)S(1)}, u32[]{:S(2)}, u32[]{:S(2)}) collective-permute-start(bf16[16,2048]{1,0:T(8,128)(2,1)S(1)} %stack.3), channel_id=1, source_target_pairs={{0,18},{1,19},{2,16},{3,17},{4,22},{5,23},{6,20},{7,21},{8,26},{9,... | collective-permute-start | bytes 196616 | tf_op jit(solution)/shard_map/ppermute | solution.py:32
  25.7 23.3 %collective-permute-start.11 = (bf16[192,512]{1,0:T(8,128)(2,1)S(1)}, bf16[192,512]{1,0:T(8,128)(2,1)S(1)}, u32[]{:S(2)}, u32[]{:S(2)}) collective-permute-start(bf16[192,512]{1,0:T(8,128)(2,1)S(1)} %get-tuple-element.67), channel_id=1, source_target_pairs={{0,8},{8,0},{16,24},{24,16},{1,9},{9,1},{17,25},{25,17},{2,10},{10... | collective-permute-start | bytes 589832 | tf_op jit(solution)/shard_map/ppermute | solution.py:22
  28.2 9.0 %collective-permute-start.5 = (bf16[64,2048]{1,0:T(8,128)(2,1)S(1)}, bf16[64,2048]{1,0:T(8,128)(2,1)S(1)}, u32[]{:S(2)}, u32[]{:S(2)}) collective-permute-start(bf16[64,2048]{1,0:T(8,128)(2,1)S(1)} %pick.1), channel_id=1, source_target_pairs={{0,16},{8,24},{16,0},{24,8},{1,17},{9,25},{17,1},{25,9},{2,18},{10... | collective-permute-start | bytes 786440 | tf_op jit(solution)/shard_map/ppermute | solution.py:22
  32.9 8.3 %collective-permute-start.8 = (bf16[64,2048]{1,0:T(8,128)(2,1)S(1)}, bf16[64,2048]{1,0:T(8,128)(2,1)S(1)}, u32[]{:S(2)}, u32[]{:S(2)}) collective-permute-start(bf16[64,2048]{1,0:T(8,128)(2,1)S(1)} %collective-permute-done.7.vm_ref), channel_id=1, source_target_pairs={{0,16},{8,24},{16,0},{24,8},{1,17},{9,25},{17,1},{25,9},{2,18},{10... | collective-permute-start | bytes 786440 | tf_op jit(solution)/shard_map/ppermute | solution.py:22
  35.0 5.7 %collective-permute-start.10 = (bf16[32,2048]{1,0:T(8,128)(2,1)S(1)}, bf16[32,2048]{1,0:T(8,128)(2,1)S(1)}, u32[]{:S(2)}, u32[]{:S(2)}) collective-permute-start(bf16[32,2048]{1,0:T(8,128)(2,1)S(1)} %constant_dynamic-update-slice_fusion.mine_ref), channel_id=1, source_target_pairs={{0,1},{1,0},{2,3},{3,2},{4,5},{5,4},{6,7},{7,6},{8,9},{9,8},{10,11... | collective-permute-start | bytes 393224 | tf_op jit(solution)/shard_map/ppermute | solution.py:22
  38.8 2.4 %copy-start.3 = (s32[16]{0:T(128)S(1)}, s32[16]{0:T(128)}, u32[]{:S(2)}) copy-start(s32[16]{0:T(128)} %coarse_ref.3) | copy-start | bytes 196

commit v18 on v17

--- a/solution.py
+++ b/solution.py
@@ -10,7 +10,7 @@
 HEAD_COUNT = 16
 HEAD_FEATURES = 128
 MIDDLE_DILATION = 4
-CHUNKS = (12, 4)
+CHUNKS = (14, 2)
 LANES = 128
 SUBLANES = 16
 EXP2_SCALE = HEAD_FEATURES ** (-0.5) * 1.4426950408889634
@@ -376,14 +376,19 @@
     first = 0
     for chunk, vr in zip(CHUNKS, other_vr):
         heads = range(first, first + chunk)
-        base, spread = call(
-            functools.partial(base_kernel, heads),
-            "base",
-            extra_sum, share, own_sum,
-            out_shape=[pltpu.VMEM((rows, chunk * HEAD_FEATURES), f32)] * 2,
-            in_specs=[vmem] * 3,
-            out_specs=[vmem] * 2,
-        )
+        if not out:
+            base, spread = call(
+                functools.partial(base_kernel, heads),
+                "base",
+                extra_sum, share, own_sum,
+                out_shape=[pltpu.VMEM((rows, chunk * HEAD_FEATURES), f32)] * 2,
+                in_specs=[vmem] * 3,
+                out_specs=[vmem] * 2,
+            )
+        else:
+            chosen = slice(first * HEAD_FEATURES, None)
+            spread = jnp.repeat(share[:, first:HEAD_COUNT], HEAD_FEATURES, axis=1)
+            base = extra_sum[:, chosen] + spread * own_sum[:, chosen]
         args = [base, spread, weights_a, weights_b, other_vm, vr]
         out = [
             call(

time: 50.1 us -> 50.2 us (level)
  waiting for transfers between devices: 14.1 us -> 13 us
  starting transfers between devices: 17.5 us -> 18.5 us
    ppermute x11, waiting for transfers between devices: 11 us -> 9.86 us  [partner(): return lax.ppermute(value, axis, pairs)]
    ppermute x11, starting transfers between devices: 16 us -> 16.9 us  [partner(): return lax.ppermute(value, axis, pairs)]
    pallas_call x11 -> x10, Pallas kernels: 16.8 us -> 16.6 us  [call(): pl.pallas_call(kernel, name=name, compiler_params=params, cost_estimate=c...]
    unnamed x9 -> x10, local copies, waits for them, and re-layouts: 1.32 us -> 1.34 us
  transfers between devices with their start and end apart: 13 -> 13, of which waited for: 8 -> 7; matrix products, arithmetic and copies ran while one was open for 0% -> 1% of each run, Pallas kernels for 32% -> 31%
where the time goes in v18:
time: 50.2 us; the launch traced here: 50.1 us
  starting transfers between devices  18.5 us (37%)
  Pallas kernels  16.6 us (33%)
  waiting for transfers between devices  13 us (26%)
  local copies, waits for them, and re-layouts  1.78 us (4%)
    ppermute x11, starting transfers between devices, partner(): return lax.ppermute(value, axis, pairs)  16.9 us
    pallas_call x10, Pallas kernels, call(): pl.pallas_call(kernel, name=name, compiler_params=params, cost_estimate=c...  16.6 us
    ppermute x11, waiting for transfers between devices, partner(): return lax.ppermute(value, axis, pairs)  9.86 us
    ppermute x2, waiting for transfers between devices, partner_elsewhere(): return lax.ppermute(value, ('inner', 'outer'), pairs)  3.11 us
    ppermute x2, starting transfers between devices, partner_elsewhere(): return lax.ppermute(value, ('inner', 'outer'), pairs)  1.55 us
    unnamed x10, local copies, waits for them, and re-layouts  1.34 us
  transfers between devices with their start and end apart: 13, of which 7 were waited for; matrix products, arithmetic and copies ran while one was open for 1% of the time, Pallas kernels for 31%

profile of v18, /device:TPU:0, one launch (start us, length us, event | category | flops | bytes accessed | tf_op | source)
XLA Modules:
  0.0 50.1 jit_solution(2036407356864322328)
XLA Ops:
  0.0 2.9 %collective-permute-start.4 = (bf16[256,2048]{1,0:T(8,128)(2,1)}, bf16[256,2048]{1,0:T(8,128)(2,1)S(1)}, u32[]{:S(2)}, u32[]{:S(2)}) collective-permute-start(bf16[256,2048]{1,0:T(8,128)(2,1)} %k_hbm.1), channel_id=1, source_target_pairs={{0,8},{8,0},{16,24},{24,16},{1,9},{9,1},{17,25},{25,17},{2,10},{10... | collective-permute-start | bytes 3145736 | tf_op jit(solution)/shard_map/ppermute | solution.py:22
  2.9 0.7 %copy-done = s32[16]{0:T(128)S(1)} copy-done((s32[16]{0:T(128)S(1)}, s32[16]{0:T(128)}, u32[]{:S(2)}) %copy-start) | copy-done | bytes 88
  3.6 0.7 %copy-done.2 = s32[16]{0:T(128)S(1)} copy-done((s32[16]{0:T(128)S(1)}, s32[16]{0:T(128)}, u32[]{:S(2)}) %copy-start.2) | copy-done | bytes 88
  4.3 3.2 %prepare.1 = (bf16[256,2048]{1,0:T(8,128)(2,1)S(1)}, bf16[256,2048]{1,0:T(8,128)(2,1)S(1)}, bf16[256,2048]{1,0:T(8,128)(2,1)S(1)}, bf16[128,2048]{1,0:T(8,128)(2...) custom-call(s32[16]{0:T(128)S(1)} %copy-done, ...), custom_call_target="tpu_custom_call" | custom-call | tf_op jit(solution)/shard_map/prepare/pallas_call | solution.py:295
  7.5 1.6 %collective-permute-start.6 = (bf16[128,2048]{1,0:T(8,128)(2,1)S(1)}, bf16[128,2048]{1,0:T(8,128)(2,1)S(1)}, u32[]{:S(2)}, u32[]{:S(2)}) collective-permute-start(bf16[128,2048]{1,0:T(8,128)(2,1)S(1)} %get-tuple-element.51), channel_id=1, source_target_pairs={{0,16},{8,24},{16,0},{24,8},{1,17},{9,25},{17,1},{25,9},{2,18},{10... | collective-permute-start | bytes 1572872 | tf_op jit(solution)/shard_map/ppermute | solution.py:22
  9.1 1.5 %collective-permute-start = (bf16[2,2048]{1,0:T(2,128)(2,1)S(1)}, bf16[2,2048]{1,0:T(2,128)(2,1)S(1)}, u32[]{:S(2)}, u32[]{:S(2)}) collective-permute-start(bf16[2,2048]{1,0:T(2,128)(2,1)S(1)} %get-tuple-element.39.refs_0_), channel_id=1, source_target_pairs={{0,10},{1,11},{2,8},{3,9},{4,14},{5,15},{6,12},{7,13},{8,2},{9,3},... | collective-permute-start | bytes 24584 | tf_op jit(solution)/shard_map/ppermute | solution.py:32
  10.6 3.1 %collective-permute-done.refs_1_ = bf16[2,2048]{1,0:T(2,128)(2,1)S(1)} collective-permute-done((bf16[2,2048]{1,0:T(2,128)(2,1)S(1)}, bf16[2,2048]{1,0:T(2,128)(2,1)S(1)}, u32[]{:S(2)}, u32[]{:S(2)}) %collective-permute-start) | collective-permute-done | bytes 8224 | tf_op jit(solution)/shard_map/ppermute | solution.py:32
  13.8 1.6 %collective-permute-start.1 = (bf16[4,2048]{1,0:T(4,128)(2,1)S(1)}, bf16[4,2048]{1,0:T(4,128)(2,1)S(1)}, u32[]{:S(2)}, u32[]{:S(2)}) collective-permute-start(bf16[4,2048]{1,0:T(4,128)(2,1)S(1)} %stack.2.refs_0_), channel_id=1, source_target_pairs={{0,2},{1,3},{2,0},{3,1},{4,6},{5,7},{6,4},{7,5},{8,10},{9,11},{10,... | collective-permute-start | bytes 49160 | tf_op jit(solution)/shard_map/ppermute | solution.py:22
  15.4 2.6 %collective-permute-start.2 = (bf16[4,2048]{1,0:T(4,128)(2,1)S(1)}, bf16[4,2048]{1,0:T(4,128)(2,1)S(1)}, u32[]{:S(2)}, u32[]{:S(2)}) collective-permute-start(bf16[4,2048]{1,0:T(4,128)(2,1)S(1)} %stack.2.refs_0_), channel_id=1, source_target_pairs={{0,4},{1,5},{2,6},{3,7},{4,0},{5,1},{6,2},{7,3},{8,12},{9,13},{10,... | collective-permute-start | bytes 49160 | tf_op jit(solution)/shard_map/ppermute | solution.py:22
  18.0 0.2 collective-permute-start.3
  18.2 0.8 %score.1 = (f32[16,256,256]{2,1,0:T(8,128)S(1)}, f32[16,256,128]{2,1,0:T(8,128)S(1)}) custom-call(bf16[256,2048]{1,0:T(8,128)(2,1)S(1)} %get-tuple-element.46.q_ref, bf16[256,2048]{1,0:T(8,128)(2,1)S(1)} %get-tuple-element.37.k_ref), custom_call_target="tpu_custom_call" | custom-call | tf_op jit(solution)/shard_map/score/pallas_call | solution.py:295
  19.0 1.2 %collective-permute-done.2.refs_2_ = bf16[4,2048]{1,0:T(4,128)(2,1)S(1)} collective-permute-done((bf16[4,2048]{1,0:T(4,128)(2,1)S(1)}, bf16[4,2048]{1,0:T(4,128)(2,1)S(1)}, u32[]{:S(2)}, u32[]{:S(2)}) %collective-permute-start.2) | collective-permute-done | bytes 16416 | tf_op jit(solution)/shard_map/ppermute | solution.py:22
  20.3 3.4 %collective-permute-done.3.refs_3_ = bf16[4,2048]{1,0:T(4,128)(2,1)S(1)} collective-permute-done((bf16[4,2048]{1,0:T(4,128)(2,1)S(1)}, bf16[4,2048]{1,0:T(4,128)(2,1)S(1)}, u32[]{:S(2)}, u32[]{:S(2)}) %collective-permute-start.3) | collective-permute-done | bytes 16416 | tf_op jit(solution)/shard_map/ppermute | solution.py:22
  23.6 0.5 collective-permute-start.7
  24.2 1.6 %collective-permute-start.12 = (bf16[192,1792]{1,0:T(8,128)(2,1)S(1)}, bf16[192,1792]{1,0:T(8,128)(2,1)S(1)}, u32[]{:S(2)}, u32[]{:S(2)}) collective-permute-start(bf16[192,1792]{1,0:T(8,128)(2,1)S(1)} %get-tuple-element.66), channel_id=1, source_target_pairs={{0,8},{8,0},{16,24},{24,16},{1,9},{9,1},{17,25},{25,17},{2,10},{10... | collective-permute-start | bytes 2064392 | tf_op jit(solution)/shard_map/ppermute | solution.py:22
  25.8 1.6 %collective-permute-done.4.k_ref.kp_ref = bf16[256,2048]{1,0:T(8,128)(2,1)S(1)} collective-permute-done((bf16[256,2048]{1,0:T(8,128)(2,1)}, bf16[256,2048]{1,0:T(8,128)(2,1)S(1)}, u32[]{:S(2)}, u32[]{:S(2)}) %collective-permute-start.4) | collective-permute-done | bytes 1048608 | tf_op jit(solution)/shard_map/ppermute | solution.py:22
  27.3 0.8 %pick.1 = bf16[64,2048]{1,0:T(8,128)(2,1)S(1)} custom-call(s32[16]{0:T(128)S(1)} %copy-done.1, bf16[256,2048]{1,0:T(8,128)(2,1)S(1)} %collective-permute-done.4.k_ref.kp_ref), custom_call_target="tpu_custom_call" | custom-call | tf_op jit(solution)/shard_map/pick/pallas_call | solution.py:295
  28.2 2.2 %collective-permute-start.5 = (bf16[64,2048]{1,0:T(8,128)(2,1)S(1)}, bf16[64,2048]{1,0:T(8,128)(2,1)S(1)}, u32[]{:S(2)}, u32[]{:S(2)}) collective-permute-start(bf16[64,2048]{1,0:T(8,128)(2,1)S(1)} %pick.1), channel_id=1, source_target_pairs={{0,16},{8,24},{16,0},{24,8},{1,17},{9,25},{17,1},{25,9},{2,18},{10... | collective-permute-start | bytes 786440 | tf_op jit(solution)/shard_map/ppermute | solution.py:22
  30.3 1.7 %other.2 = (bf16[8,256,256]{2,1,0:T(8,128)(2,1)S(1)}, f32[8,256,128]{2,1,0:T(8,128)S(1)}, f32[256,128]{1,0:T(8,128)S(1)}) custom-call(s32[16]{0:T(128)S(1)} %copy-done.1, bf16[256,2048]{1,0:T(8,128)(2,1)S(1)} %get-tuple-element.46.q_ref, f32[16,256,128]{2,1,0:T(8,128)S(1)} %get-tuple-element.42.own_top_ref, ...), custom_call_target="tpu_custom_call" | custom-call | tf_op jit(solution)/shard_map/other/pallas_call | solution.py:295
  32.0 0.9 %collective-permute-done.7.vm_ref = bf16[64,2048]{1,0:T(8,128)(2,1)S(1)} collective-permute-done((bf16[64,2048]{1,0:T(8,128)(2,1)S(1)}, bf16[64,2048]{1,0:T(8,128)(2,1)S(1)}, u32[]{:S(2)}, u32[]{:S(2)}) %collective-permute-start.7) | collective-permute-done | bytes 262176 | tf_op jit(solution)/shard_map/ppermute | solution.py:22
  32.9 2.1 %collective-permute-start.8 = (bf16[64,2048]{1,0:T(8,128)(2,1)S(1)}, bf16[64,2048]{1,0:T(8,128)(2,1)S(1)}, u32[]{:S(2)}, u32[]{:S(2)}) collective-permute-start(bf16[64,2048]{1,0:T(8,128)(2,1)S(1)} %collective-permute-done.7.vm_ref), channel_id=1, source_target_pairs={{0,16},{8,24},{16,0},{24,8},{1,17},{9,25},{17,1},{25,9},{2,18},{10... | collective-permute-start | bytes 786440 | tf_op jit(solution)/shard_map/ppermute | solution.py:22
  35.1 1.6 %collective-permute-start.11 = (bf16[192,256]{1,0:T(8,128)(2,1)S(1)}, bf16[192,256]{1,0:T(8,128)(2,1)S(1)}, u32[]{:S(2)}, u32[]{:S(2)}) collective-permute-start(bf16[192,256]{1,0:T(8,128)(2,1)S(1)} %get-tuple-element.63), channel_id=1, source_target_pairs={{0,8},{8,0},{16,24},{24,16},{1,9},{9,1},{17,25},{25,17},{2,10},{10... | collective-permute-start | bytes 294920 | tf_op jit(solution)/shard_map/ppermute | solution.py:22
  36.7 1.7 %other.3 = (bf16[8,256,256]{2,1,0:T(8,128)(2,1)S(1)}, f32[8,256,128]{2,1,0:T(8,128)S(1)}, f32[256,128]{1,0:T(8,128)S(1)}) custom-call(s32[16]{0:T(128)S(1)} %copy-done.1, bf16[256,2048]{1,0:T(8,128)(2,1)S(1)} %get-tuple-element.46.q_ref, f32[16,256,128]{2,1,0:T(8,128)S(1)} %get-tuple-element.42.own_top_ref, ...), custom_call_target="tpu_custom_call" | custom-call | tf_op jit(solution)/shard_map/other/pallas_call | solution.py:295
  38.4 1.8 %own.1 = (f32[256,2048]{1,0:T(8,128)S(1)}, f32[256,128]{1,0:T(8,128)S(1)}) custom-call(s32[16]{0:T(128)S(1)} %copy-done.1, f32[16,256,256]{2,1,0:T(8,128)S(1)} %get-tuple-element.38.scores_ref, f32[8,256,128]{2,1,0:T(8,128)S(1)} %get-tuple-element.44.top_a_ref, f32[8,256,128]{2,1,0:T(8,128)S(1)} %get-tuple-element.47.top_b_ref, ...), custom_call_target="tpu_custom_call" | custom-call | tf_op jit(solution)/shard_map/own/pallas_call | solution.py:295
  40.2 0.3 collective-permute-done.8.diagonal_v_ref
  40.5 3.5 %extra.1 = (f32[256,2048]{1,0:T(8,128)S(1)}, f32[256,128]{1,0:T(8,128)S(1)}) custom-call(s32[16]{0:T(128)S(1)} %copy-done.1, s32[16]{0:T(128)S(1)} %copy-done.3, bf16[256,2048]{1,0:T(8,128)(2,1)S(1)} %get-tuple-element.46.q_ref, f32[256,128]{1,0:T(8,128)S(1)} %get-tuple-element.49.own_total_ref, f32[256,128]{1,0:T(8,128)S(1)} %get-tuple-element.45.state_a_ref, ...), custom_call_target="tpu_custom_call" | custom-call | tf_op jit(solution)/shard_map/extra/pallas_call | solution.py:295
  44.0 0.1 slice.10
  44.1 0.3 broadcast_in_dim.3
  44.6 0.6 %base.1 = (f32[256,1792]{1,0:T(8,128)S(1)}, f32[256,1792]{1,0:T(8,128)S(1)}) custom-call(f32[256,2048]{1,0:T(8,128)S(1)} %get-tuple-element.58.sum_ref, f32[256,128]{1,0:T(8,128)S(1)} %get-tuple-element.59.share_ref, f32[256,2048]{1,0:T(8,128)S(1)} %get-tuple-element.60.own_ref), custom_call_target="tpu_custom_call" | custom-call | tf_op jit(solution)/shard_map/base/pallas_call | solution.py:295
  45.2 2.5 %collective-permute-done.12.vr_ref = bf16[192,1792]{1,0:T(8,128)(2,1)S(1)} collective-permute-done((bf16[192,1792]{1,0:T(8,128)(2,1)S(1)}, bf16[192,1792]{1,0:T(8,128)(2,1)S(1)}, u32[]{:S(2)}, u32[]{:S(2)}) %collective-permute-start.12) | collective-permute-done | bytes 688160 | tf_op jit(solution)/shard_map/ppermute | solution.py:22
  47.7 1.5 %finish.2.rest_0_ = bf16[256,2048]{1,0:T(8,128)(2,1)} custom-call(f32[256,1792]{1,0:T(8,128)S(1)} %get-tuple-element.64.base_ref, f32[256,1792]{1,0:T(8,128)S(1)} %get-tuple-element.65.spread_ref, bf16[8,256,256]{2,1,0:T(8,128)(2,1)S(1)} %get-tuple-element.61.other_a_ref, bf16[8,256,256]{2,1,0:T(8,128)(2,1)S(1)} %get-tuple-element.62.other_b_ref, ...), custom_call_target="tpu_custom_call" | custom-call | tf_op jit(solution)/shard_map/finish/pallas_call | solution.py:295
  49.2 0.9 %finish.3 = bf16[256,2048]{1,0:T(8,128)(2,1)} custom-call(f32[256,256]{1,0:T(8,128)S(1)} %multiply_add_fusion.base_ref, f32[256,256]{1,0:T(8,128)S(1)} %bitcast.6, bf16[8,256,256]{2,1,0:T(8,128)(2,1)S(1)} %get-tuple-element.61.other_a_ref, bf16[8,256,256]{2,1,0:T(8,128)(2,1)S(1)} %get-tuple-element.62.other_b_ref, ...), custom_call_target="tpu_custom_call", output_to_operand_aliasing={{}: (6, {})} | custom-call | tf_op jit(solution)/shard_map/finish/pallas_call | solution.py:295
  (20 shorter events, 0.2 us)
Async XLA Ops:
  0.0 27.3 %collective-permute-start.4 = (bf16[256,2048]{1,0:T(8,128)(2,1)}, bf16[256,2048]{1,0:T(8,128)(2,1)S(1)}, u32[]{:S(2)}, u32[]{:S(2)}) collective-permute-start(bf16[256,2048]{1,0:T(8,128)(2,1)} %k_hbm.1), channel_id=1, source_target_pairs={{0,8},{8,0},{16,24},{24,16},{1,9},{9,1},{17,25},{25,17},{2,10},{10... | collective-permute-start | bytes 3145736 | tf_op jit(solution)/shard_map/ppermute | solution.py:22
  2.9 0.7 %copy-start = (s32[16]{0:T(128)S(1)}, s32[16]{0:T(128)}, u32[]{:S(2)}) copy-start(s32[16]{0:T(128)} %middle_ref.11) | copy-start | bytes 196
  3.6 0.7 %copy-start.2 = (s32[16]{0:T(128)S(1)}, s32[16]{0:T(128)}, u32[]{:S(2)}) copy-start(s32[16]{0:T(128)} %coarse_ref.3) | copy-start | bytes 196
  4.3 23.1 %copy-start.1 = (s32[16]{0:T(128)S(1)}, s32[16]{0:T(128)}, u32[]{:S(2)}) copy-start(s32[16]{0:T(128)} %middle_ref.11) | copy-start | bytes 196
  7.5 16.7 %collective-permute-start.6 = (bf16[128,2048]{1,0:T(8,128)(2,1)S(1)}, bf16[128,2048]{1,0:T(8,128)(2,1)S(1)}, u32[]{:S(2)}, u32[]{:S(2)}) collective-permute-start(bf16[128,2048]{1,0:T(8,128)(2,1)S(1)} %get-tuple-element.51), channel_id=1, source_target_pairs={{0,16},{8,24},{16,0},{24,8},{1,17},{9,25},{17,1},{25,9},{2,18},{10... | collective-permute-start | bytes 1572872 | tf_op jit(solution)/shard_map/ppermute | solution.py:22
  9.1 4.7 %collective-permute-start = (bf16[2,2048]{1,0:T(2,128)(2,1)S(1)}, bf16[2,2048]{1,0:T(2,128)(2,1)S(1)}, u32[]{:S(2)}, u32[]{:S(2)}) collective-permute-start(bf16[2,2048]{1,0:T(2,128)(2,1)S(1)} %get-tuple-element.39.refs_0_), channel_id=1, source_target_pairs={{0,10},{1,11},{2,8},{3,9},{4,14},{5,15},{6,12},{7,13},{8,2},{9,3},... | collective-permute-start | bytes 24584 | tf_op jit(solution)/shard_map/ppermute | solution.py:32
  13.8 5.3 %collective-permute-start.1 = (bf16[4,2048]{1,0:T(4,128)(2,1)S(1)}, bf16[4,2048]{1,0:T(4,128)(2,1)S(1)}, u32[]{:S(2)}, u32[]{:S(2)}) collective-permute-start(bf16[4,2048]{1,0:T(4,128)(2,1)S(1)} %stack.2.refs_0_), channel_id=1, source_target_pairs={{0,2},{1,3},{2,0},{3,1},{4,6},{5,7},{6,4},{7,5},{8,10},{9,11},{10,... | collective-permute-start | bytes 49160 | tf_op jit(solution)/shard_map/ppermute | solution.py:22
  15.4 4.9 %collective-permute-start.2 = (bf16[4,2048]{1,0:T(4,128)(2,1)S(1)}, bf16[4,2048]{1,0:T(4,128)(2,1)S(1)}, u32[]{:S(2)}, u32[]{:S(2)}) collective-permute-start(bf16[4,2048]{1,0:T(4,128)(2,1)S(1)} %stack.2.refs_0_), channel_id=1, source_target_pairs={{0,4},{1,5},{2,6},{3,7},{4,0},{5,1},{6,2},{7,3},{8,12},{9,13},{10,... | collective-permute-start | bytes 49160 | tf_op jit(solution)/shard_map/ppermute | solution.py:22
  18.0 5.6 %collective-permute-start.3 = (bf16[4,2048]{1,0:T(4,128)(2,1)S(1)}, bf16[4,2048]{1,0:T(4,128)(2,1)S(1)}, u32[]{:S(2)}, u32[]{:S(2)}) collective-permute-start(bf16[4,2048]{1,0:T(4,128)(2,1)S(1)} %stack.2.refs_0_), channel_id=1, source_target_pairs={{0,6},{1,7},{2,4},{3,5},{4,2},{5,3},{6,0},{7,1},{8,14},{9,15},{10,... | collective-permute-start | bytes 49160 | tf_op jit(solution)/shard_map/ppermute | solution.py:22
  23.6 9.3 %collective-permute-start.7 = (bf16[64,2048]{1,0:T(8,128)(2,1)S(1)}, bf16[64,2048]{1,0:T(8,128)(2,1)S(1)}, u32[]{:S(2)}, u32[]{:S(2)}) collective-permute-start(bf16[64,2048]{1,0:T(8,128)(2,1)S(1)} %get-tuple-element.55), channel_id=1, source_target_pairs={{0,8},{8,0},{16,24},{24,16},{1,9},{9,1},{17,25},{25,17},{2,10},{10... | collective-permute-start | bytes 786440 | tf_op jit(solution)/shard_map/ppermute | solution.py:22
  24.1 10.9 %collective-permute-start.9 = (bf16[16,2048]{1,0:T(8,128)(2,1)S(1)}, bf16[16,2048]{1,0:T(8,128)(2,1)S(1)}, u32[]{:S(2)}, u32[]{:S(2)}) collective-permute-start(bf16[16,2048]{1,0:T(8,128)(2,1)S(1)} %stack.3), channel_id=1, source_target_pairs={{0,18},{1,19},{2,16},{3,17},{4,22},{5,23},{6,20},{7,21},{8,26},{9,... | collective-permute-start | bytes 196616 | tf_op jit(solution)/shard_map/ppermute | solution.py:32
  24.2 23.5 %collective-permute-start.12 = (bf16[192,1792]{1,0:T(8,128)(2,1)S(1)}, bf16[192,1792]{1,0:T(8,128)(2,1)S(1)}, u32[]{:S(2)}, u32[]{:S(2)}) collective-permute-start(bf16[192,1792]{1,0:T(8,128)(2,1)S(1)} %get-tuple-element.66), channel_id=1, source_target_pairs={{0,8},{8,0},{16,24},{24,16},{1,9},{9,1},{17,25},{25,17},{2,10},{10... | collective-permute-start | bytes 2064392 | tf_op jit(solution)/shard_map/ppermute | solution.py:22
  28.2 8.5 %collective-permute-start.5 = (bf16[64,2048]{1,0:T(8,128)(2,1)S(1)}, bf16[64,2048]{1,0:T(8,128)(2,1)S(1)}, u32[]{:S(2)}, u32[]{:S(2)}) collective-permute-start(bf16[64,2048]{1,0:T(8,128)(2,1)S(1)} %pick.1), channel_id=1, source_target_pairs={{0,16},{8,24},{16,0},{24,8},{1,17},{9,25},{17,1},{25,9},{2,18},{10... | collective-permute-start | bytes 786440 | tf_op jit(solution)/shard_map/ppermute | solution.py:22
  32.9 7.6 %collective-permute-start.8 = (bf16[64,2048]{1,0:T(8,128)(2,1)S(1)}, bf16[64,2048]{1,0:T(8,128)(2,1)S(1)}, u32[]{:S(2)}, u32[]{:S(2)}) collective-permute-start(bf16[64,2048]{1,0:T(8,128)(2,1)S(1)} %collective-permute-done.7.vm_ref), channel_id=1, source_target_pairs={{0,16},{8,24},{16,0},{24,8},{1,17},{9,25},{17,1},{25,9},{2,18},{10... | collective-permute-start | bytes 786440 | tf_op jit(solution)/shard_map/ppermute | solution.py:22
  35.0 5.2 %collective-permute-start.10 = (bf16[32,2048]{1,0:T(8,128)(2,1)S(1)}, bf16[32,2048]{1,0:T(8,128)(2,1)S(1)}, u32[]{:S(2)}, u32[]{:S(2)}) collective-permute-start(bf16[32,2048]{1,0:T(8,128)(2,1)S(1)} %constant_dynamic-update-slice_fusion.mine_ref), channel_id=1, source_target_pairs={{0,1},{1,0},{2,3},{3,2},{4,5},{5,4},{6,7},{7,6},{8,9},{9,8},{10,11... | collective-permute-start | bytes 393224 | tf_op jit(solution)/shard_map/ppermute | solution.py:22
  35.1 14.1 %collective-permute-start.11 = (bf16[192,256]{1,0:T(8,128)(2,1)S(1)}, bf16[192,256]{1,0:T(8,128)(2,1)S(1)}, u32[]{:S(2)}, u32[]{:S(2)}) collective-permute-start(bf16[192,256]{1,0:T(8,128)(2,1)S(1)} %get-tuple-element.63), channel_id=1, source_target_pairs={{0,8},{8,0},{16,24},{24,16},{1,9},{9,1},{17,25},{25,17},{2,10},{10... | collective-permute-start | bytes 294920 | tf_op jit(solution)/shard_map/ppermute | solution.py:22
  38.4 2.2 %copy-start.3 = (s32[16]{0:T(128)S(1)}, s32[16]{0:T(128)}, u32[]{:S(2)}) copy-start(s32[16]{0:T(128)} %coarse_ref.3) | copy-start | bytes 196

commit v19 on v17

--- a/solution.py
+++ b/solution.py
@@ -10,7 +10,8 @@
 HEAD_COUNT = 16
 HEAD_FEATURES = 128
 MIDDLE_DILATION = 4
-CHUNKS = (12, 4)
+CHUNKS = (13, 3)
+LATE = 10
 LANES = 128
 SUBLANES = 16
 EXP2_SCALE = HEAD_FEATURES ** (-0.5) * 1.4426950408889634
@@ -226,7 +227,9 @@
         spread_ref[:, place_columns] = share
 
 
-def finish_kernel(heads, base_ref, spread_ref, other_a_ref, other_b_ref, vm_ref, vr_ref, *rest):
+def finish_kernel(
+    heads, base_ref, spread_ref, late_base_ref, late_spread_ref, other_a_ref, other_b_ref, vm_ref, vr_ref, *rest
+):
     out_ref, ready_ref, semaphores = rest[-3:]
     half = HEAD_COUNT // 2
     copies = []
@@ -234,7 +237,12 @@
         columns = head_columns(place)
         other_ref = (other_a_ref, other_b_ref)[head // half]
         values = jnp.concatenate([vm_ref[:, head_columns(head)], vr_ref[:, columns]], axis=0)
-        result = base_ref[:, columns] + spread_ref[:, columns] * dot(other_ref[head % half], values)
+        result = dot(other_ref[head % half], values)
+        if head < LATE:
+            result = base_ref[:, head_columns(head)] + spread_ref[:, head_columns(head)] * result
+        else:
+            late = head_columns(head - LATE)
+            result = late_base_ref[:, late] + late_spread_ref[:, late] * result
         ready_ref[place] = result.astype(jnp.bfloat16)
         target = out_ref.at[:, head_columns(head)]
         copies.append(pltpu.make_async_copy(ready_ref.at[place], target, semaphores.at[place]))
@@ -372,19 +380,22 @@
         out_specs=[vmem] * 2,
     )
 
+    base, spread = call(
+        functools.partial(base_kernel, range(LATE)),
+        "base",
+        extra_sum, share, own_sum,
+        out_shape=[pltpu.VMEM((rows, LATE * HEAD_FEATURES), f32)] * 2,
+        in_specs=[vmem] * 3,
+        out_specs=[vmem] * 2,
+    )
+    late = slice(LATE * HEAD_FEATURES, None)
+    late_spread = jnp.repeat(share[:, LATE:HEAD_COUNT], HEAD_FEATURES, axis=1)
+    late_base = extra_sum[:, late] + late_spread * own_sum[:, late]
     out = []
     first = 0
     for chunk, vr in zip(CHUNKS, other_vr):
         heads = range(first, first + chunk)
-        base, spread = call(
-            functools.partial(base_kernel, heads),
-            "base",
-            extra_sum, share, own_sum,
-            out_shape=[pltpu.VMEM((rows, chunk * HEAD_FEATURES), f32)] * 2,
-            in_specs=[vmem] * 3,
-            out_specs=[vmem] * 2,
-        )
-        args = [base, spread, weights_a, weights_b, other_vm, vr]
+        args = [base, spread, late_base, late_spread, weights_a, weights_b, other_vm, vr]
         out = [
             call(
                 functools.partial(finish_kernel, heads),

time: 50.1 us -> 56.3 us (1.12)
  local copies, waits for them, and re-layouts: 1.33 us -> 7.16 us
  waiting for transfers between devices: 14.1 us -> 11.1 us
  other arithmetic: 0 us -> 1.66 us
  Pallas kernels: 16.8 us -> 18.4 us
    unnamed x9 -> x17, local copies, waits for them, and re-layouts: 1.32 us -> 4.64 us
    ppermute x11, waiting for transfers between devices: 11 us -> 7.99 us  [partner(): return lax.ppermute(value, axis, pairs)]
    add x0 -> x1, other arithmetic: none -> 1.66 us  [on_device(): late_base = extra_sum[:, late] + late_spread * own_sum[:, late]]
    pallas_call x11 -> x10, Pallas kernels: 16.8 us -> 18.3 us  [call(): pl.pallas_call(kernel, name=name, compiler_params=params, cost_estimate=c...]
    reshape x0 -> x1, local copies, waits for them, and re-layouts: none -> 1.39 us  [on_device(): late_spread = jnp.repeat(share[:, LATE:HEAD_COUNT], HEAD_FEATURES, axis=1)]
    broadcast_in_dim x0 -> x1, local copies, waits for them, and re-layouts: none -> 0.95 us  [on_device(): late_spread = jnp.repeat(share[:, LATE:HEAD_COUNT], HEAD_FEATURES, axis=1)]
  transfers between devices with their start and end apart: 13 -> 13, of which waited for: 8 -> 7; matrix products, arithmetic and copies ran while one was open for 0% -> 7% of each run, Pallas kernels for 32% -> 31%
where the time goes in v19:
time: 56.3 us; the launch traced here: 56.1 us
  Pallas kernels  18.4 us (33%)
  starting transfers between devices  17.6 us (31%)
  waiting for transfers between devices  11.1 us (20%)
  local copies, waits for them, and re-layouts  7.16 us (13%)
  other arithmetic  1.66 us (3%)
    pallas_call x10, Pallas kernels, call(): pl.pallas_call(kernel, name=name, compiler_params=params, cost_estimate=c...  18.3 us
    ppermute x11, starting transfers between devices, partner(): return lax.ppermute(value, axis, pairs)  16.1 us
    ppermute x11, waiting for transfers between devices, partner(): return lax.ppermute(value, axis, pairs)  7.99 us
    unnamed x17, local copies, waits for them, and re-layouts  4.64 us
    ppermute x2, waiting for transfers between devices, partner_elsewhere(): return lax.ppermute(value, ('inner', 'outer'), pairs)  3.11 us
    add x1, other arithmetic, on_device(): late_base = extra_sum[:, late] + late_spread * own_sum[:, late]  1.66 us
    ppermute x2, starting transfers between devices, partner_elsewhere(): return lax.ppermute(value, ('inner', 'outer'), pairs)  1.55 us
    reshape x1, local copies, waits for them, and re-layouts, on_device(): late_spread = jnp.repeat(share[:, LATE:HEAD_COUNT], HEAD_FEATURES, axis=1)  1.39 us
  transfers between devices with their start and end apart: 13, of which 7 were waited for; matrix products, arithmetic and copies ran while one was open for 7% of the time, Pallas kernels for 31%

profile of v19, /device:TPU:0, one launch (start us, length us, event | category | flops | bytes accessed | tf_op | source)
XLA Modules:
  0.0 56.1 jit_solution(2025994507474574638)
XLA Ops:
  0.0 2.9 %collective-permute-start.4 = (bf16[256,2048]{1,0:T(8,128)(2,1)}, bf16[256,2048]{1,0:T(8,128)(2,1)S(1)}, u32[]{:S(2)}, u32[]{:S(2)}) collective-permute-start(bf16[256,2048]{1,0:T(8,128)(2,1)} %k_hbm.1), channel_id=1, source_target_pairs={{0,8},{8,0},{16,24},{24,16},{1,9},{9,1},{17,25},{25,17},{2,10},{10... | collective-permute-start | bytes 3145736 | tf_op jit(solution)/shard_map/ppermute | solution.py:23
  2.9 0.7 %copy-done.4 = s32[16]{0:T(128)S(1)} copy-done((s32[16]{0:T(128)S(1)}, s32[16]{0:T(128)}, u32[]{:S(2)}) %copy-start.4) | copy-done | bytes 88
  3.6 0.7 %copy-done.6 = s32[16]{0:T(128)S(1)} copy-done((s32[16]{0:T(128)S(1)}, s32[16]{0:T(128)}, u32[]{:S(2)}) %copy-start.6) | copy-done | bytes 88
  4.3 4.1 %prepare.1 = (bf16[256,2048]{1,0:T(8,128)(2,1)S(1)}, bf16[256,2048]{1,0:T(8,128)(2,1)S(1)}, bf16[256,2048]{1,0:T(8,128)(2,1)S(1)}, bf16[128,2048]{1,0:T(8,128)(2...) custom-call(s32[16]{0:T(128)S(1)} %copy-done.4, ...), custom_call_target="tpu_custom_call" | custom-call | tf_op jit(solution)/shard_map/prepare/pallas_call | solution.py:303
  8.4 1.6 %collective-permute-start.6 = (bf16[128,2048]{1,0:T(8,128)(2,1)S(1)}, bf16[128,2048]{1,0:T(8,128)(2,1)S(1)}, u32[]{:S(2)}, u32[]{:S(2)}) collective-permute-start(bf16[128,2048]{1,0:T(8,128)(2,1)S(1)} %get-tuple-element.51), channel_id=1, source_target_pairs={{0,16},{8,24},{16,0},{24,8},{1,17},{9,25},{17,1},{25,9},{2,18},{10... | collective-permute-start | bytes 1572872 | tf_op jit(solution)/shard_map/ppermute | solution.py:23
  10.0 1.5 %collective-permute-start = (bf16[2,2048]{1,0:T(2,128)(2,1)S(1)}, bf16[2,2048]{1,0:T(2,128)(2,1)S(1)}, u32[]{:S(2)}, u32[]{:S(2)}) collective-permute-start(bf16[2,2048]{1,0:T(2,128)(2,1)S(1)} %get-tuple-element.39.refs_0_), channel_id=1, source_target_pairs={{0,10},{1,11},{2,8},{3,9},{4,14},{5,15},{6,12},{7,13},{8,2},{9,3},... | collective-permute-start | bytes 24584 | tf_op jit(solution)/shard_map/ppermute | solution.py:33
  11.5 3.1 %collective-permute-done.refs_1_ = bf16[2,2048]{1,0:T(2,128)(2,1)S(1)} collective-permute-done((bf16[2,2048]{1,0:T(2,128)(2,1)S(1)}, bf16[2,2048]{1,0:T(2,128)(2,1)S(1)}, u32[]{:S(2)}, u32[]{:S(2)}) %collective-permute-start) | collective-permute-done | bytes 8224 | tf_op jit(solution)/shard_map/ppermute | solution.py:33
  14.7 1.6 %collective-permute-start.1 = (bf16[4,2048]{1,0:T(4,128)(2,1)S(1)}, bf16[4,2048]{1,0:T(4,128)(2,1)S(1)}, u32[]{:S(2)}, u32[]{:S(2)}) collective-permute-start(bf16[4,2048]{1,0:T(4,128)(2,1)S(1)} %stack.2.refs_0_), channel_id=1, source_target_pairs={{0,2},{1,3},{2,0},{3,1},{4,6},{5,7},{6,4},{7,5},{8,10},{9,11},{10,... | collective-permute-start | bytes 49160 | tf_op jit(solution)/shard_map/ppermute | solution.py:23
  16.3 2.6 %collective-permute-start.2 = (bf16[4,2048]{1,0:T(4,128)(2,1)S(1)}, bf16[4,2048]{1,0:T(4,128)(2,1)S(1)}, u32[]{:S(2)}, u32[]{:S(2)}) collective-permute-start(bf16[4,2048]{1,0:T(4,128)(2,1)S(1)} %stack.2.refs_0_), channel_id=1, source_target_pairs={{0,4},{1,5},{2,6},{3,7},{4,0},{5,1},{6,2},{7,3},{8,12},{9,13},{10,... | collective-permute-start | bytes 49160 | tf_op jit(solution)/shard_map/ppermute | solution.py:23
  19.1 0.8 %score.1 = (f32[16,256,256]{2,1,0:T(8,128)S(1)}, f32[16,256,128]{2,1,0:T(8,128)S(1)}) custom-call(bf16[256,2048]{1,0:T(8,128)(2,1)S(1)} %get-tuple-element.46.q_ref, bf16[256,2048]{1,0:T(8,128)(2,1)S(1)} %get-tuple-element.37.k_ref), custom_call_target="tpu_custom_call" | custom-call | tf_op jit(solution)/shard_map/score/pallas_call | solution.py:303
  19.9 1.2 %collective-permute-done.2.refs_2_ = bf16[4,2048]{1,0:T(4,128)(2,1)S(1)} collective-permute-done((bf16[4,2048]{1,0:T(4,128)(2,1)S(1)}, bf16[4,2048]{1,0:T(4,128)(2,1)S(1)}, u32[]{:S(2)}, u32[]{:S(2)}) %collective-permute-start.2) | collective-permute-done | bytes 16416 | tf_op jit(solution)/shard_map/ppermute | solution.py:23
  21.2 3.4 %collective-permute-done.3.refs_3_ = bf16[4,2048]{1,0:T(4,128)(2,1)S(1)} collective-permute-done((bf16[4,2048]{1,0:T(4,128)(2,1)S(1)}, bf16[4,2048]{1,0:T(4,128)(2,1)S(1)}, u32[]{:S(2)}, u32[]{:S(2)}) %collective-permute-start.3) | collective-permute-done | bytes 16416 | tf_op jit(solution)/shard_map/ppermute | solution.py:23
  24.6 0.5 collective-permute-start.7
  25.1 1.7 %collective-permute-start.12 = (bf16[192,1664]{1,0:T(8,128)(2,1)}, bf16[192,1664]{1,0:T(8,128)(2,1)}, u32[]{:S(2)}, u32[]{:S(2)}) collective-permute-start(bf16[192,1664]{1,0:T(8,128)(2,1)} %get-tuple-element.66), channel_id=1, source_target_pairs={{0,8},{8,0},{16,24},{24,16},{1,9},{9,1},{17,25},{25,17},{2,10},{10... | collective-permute-start | bytes 1916936 | tf_op jit(solution)/shard_map/ppermute | solution.py:23
  26.7 0.6 %collective-permute-done.4.k_ref.kp_ref = bf16[256,2048]{1,0:T(8,128)(2,1)S(1)} collective-permute-done((bf16[256,2048]{1,0:T(8,128)(2,1)}, bf16[256,2048]{1,0:T(8,128)(2,1)S(1)}, u32[]{:S(2)}, u32[]{:S(2)}) %collective-permute-start.4) | collective-permute-done | bytes 1048608 | tf_op jit(solution)/shard_map/ppermute | solution.py:23
  27.3 0.8 %pick.1 = bf16[64,2048]{1,0:T(8,128)(2,1)S(1)} custom-call(s32[16]{0:T(128)S(1)} %copy-done.5, bf16[256,2048]{1,0:T(8,128)(2,1)S(1)} %collective-permute-done.4.k_ref.kp_ref), custom_call_target="tpu_custom_call" | custom-call | tf_op jit(solution)/shard_map/pick/pallas_call | solution.py:303
  28.2 2.2 %collective-permute-start.5 = (bf16[64,2048]{1,0:T(8,128)(2,1)S(1)}, bf16[64,2048]{1,0:T(8,128)(2,1)S(1)}, u32[]{:S(2)}, u32[]{:S(2)}) collective-permute-start(bf16[64,2048]{1,0:T(8,128)(2,1)S(1)} %pick.1), channel_id=1, source_target_pairs={{0,16},{8,24},{16,0},{24,8},{1,17},{9,25},{17,1},{25,9},{2,18},{10... | collective-permute-start | bytes 786440 | tf_op jit(solution)/shard_map/ppermute | solution.py:23
  30.3 1.7 %other.2 = (bf16[8,256,256]{2,1,0:T(8,128)(2,1)S(1)}, f32[8,256,128]{2,1,0:T(8,128)S(1)}, f32[256,128]{1,0:T(8,128)S(1)}) custom-call(s32[16]{0:T(128)S(1)} %copy-done.5, bf16[256,2048]{1,0:T(8,128)(2,1)S(1)} %get-tuple-element.46.q_ref, f32[16,256,128]{2,1,0:T(8,128)S(1)} %get-tuple-element.42.own_top_ref, ...), custom_call_target="tpu_custom_call" | custom-call | tf_op jit(solution)/shard_map/other/pallas_call | solution.py:303
  32.0 1.9 %collective-permute-done.7.vm_ref = bf16[64,2048]{1,0:T(8,128)(2,1)S(1)} collective-permute-done((bf16[64,2048]{1,0:T(8,128)(2,1)S(1)}, bf16[64,2048]{1,0:T(8,128)(2,1)S(1)}, u32[]{:S(2)}, u32[]{:S(2)}) %collective-permute-start.7) | collective-permute-done | bytes 262176 | tf_op jit(solution)/shard_map/ppermute | solution.py:23
  33.9 1.1 %collective-permute-start.8 = (bf16[64,2048]{1,0:T(8,128)(2,1)S(1)}, bf16[64,2048]{1,0:T(8,128)(2,1)S(1)}, u32[]{:S(2)}, u32[]{:S(2)}) collective-permute-start(bf16[64,2048]{1,0:T(8,128)(2,1)S(1)} %collective-permute-done.7.vm_ref), channel_id=1, source_target_pairs={{0,16},{8,24},{16,0},{24,8},{1,17},{9,25},{17,1},{25,9},{2,18},{10... | collective-permute-start | bytes 786440 | tf_op jit(solution)/shard_map/ppermute | solution.py:23
  35.1 1.6 %collective-permute-start.11 = (bf16[192,384]{1,0:T(8,128)(2,1)}, bf16[192,384]{1,0:T(8,128)(2,1)S(1)}, u32[]{:S(2)}, u32[]{:S(2)}) collective-permute-start(bf16[192,384]{1,0:T(8,128)(2,1)} %get-tuple-element.65), channel_id=1, source_target_pairs={{0,8},{8,0},{16,24},{24,16},{1,9},{9,1},{17,25},{25,17},{2,10},{10... | collective-permute-start | bytes 442376 | tf_op jit(solution)/shard_map/ppermute | solution.py:23
  36.7 0.8 %collective-permute-done.5.diagonal_k_ref = bf16[64,2048]{1,0:T(8,128)(2,1)S(1)} collective-permute-done((bf16[64,2048]{1,0:T(8,128)(2,1)S(1)}, bf16[64,2048]{1,0:T(8,128)(2,1)S(1)}, u32[]{:S(2)}, u32[]{:S(2)}) %collective-permute-start.5) | collective-permute-done | bytes 262176 | tf_op jit(solution)/shard_map/ppermute | solution.py:23
  37.4 1.7 %other.3 = (bf16[8,256,256]{2,1,0:T(8,128)(2,1)S(1)}, f32[8,256,128]{2,1,0:T(8,128)S(1)}, f32[256,128]{1,0:T(8,128)S(1)}) custom-call(s32[16]{0:T(128)S(1)} %copy-done.5, bf16[256,2048]{1,0:T(8,128)(2,1)S(1)} %get-tuple-element.46.q_ref, f32[16,256,128]{2,1,0:T(8,128)S(1)} %get-tuple-element.42.own_top_ref, ...), custom_call_target="tpu_custom_call" | custom-call | tf_op jit(solution)/shard_map/other/pallas_call | solution.py:303
  39.1 1.9 %own.1 = (f32[256,2048]{1,0:T(8,128)S(1)}, f32[256,128]{1,0:T(8,128)S(1)}) custom-call(s32[16]{0:T(128)S(1)} %copy-done.5, f32[16,256,256]{2,1,0:T(8,128)S(1)} %get-tuple-element.38.scores_ref, f32[8,256,128]{2,1,0:T(8,128)S(1)} %get-tuple-element.44.top_a_ref, f32[8,256,128]{2,1,0:T(8,128)S(1)} %get-tuple-element.47.top_b_ref, ...), custom_call_target="tpu_custom_call" | custom-call | tf_op jit(solution)/shard_map/own/pallas_call | solution.py:303
  41.2 3.5 %extra.1 = (f32[256,2048]{1,0:T(8,128)S(1)}, f32[256,128]{1,0:T(8,128)S(1)}) custom-call(s32[16]{0:T(128)S(1)} %copy-done.5, s32[16]{0:T(128)S(1)} %copy-done.7, bf16[256,2048]{1,0:T(8,128)(2,1)S(1)} %get-tuple-element.46.q_ref, f32[256,128]{1,0:T(8,128)S(1)} %get-tuple-element.49.own_total_ref, f32[256,128]{1,0:T(8,128)S(1)} %get-tuple-element.45.state_a_ref, ...), custom_call_target="tpu_custom_call" | custom-call | tf_op jit(solution)/shard_map/extra/pallas_call | solution.py:303
  44.7 1.3 %copy-done.2 = f32[256,2048]{1,0:T(8,128)} copy-done((f32[256,2048]{1,0:T(8,128)}, f32[256,2048]{1,0:T(8,128)S(1)}, u32[]{:S(2)}) %copy-start.2) | copy-done | bytes 2097176
  46.2 1.0 %broadcast_in_dim.3 = f32[256,6,128]{0,2,1:T(8,128)} broadcast(f32[256,6]{0,1:T(8,128)S(1)} %copy.7), dimensions={0,1} | broadcast | bytes 792576 | tf_op jit(solution)/shard_map/broadcast_in_dim | solution.py:392
  47.2 1.4 %copy.8.late_spread_ref = f32[256,768]{1,0:T(8,128)S(1)} copy(f32[256,768]{0,1:T(8,128)} %bitcast.1) | data formatting | bytes 1572864 | tf_op jit(solution)/shard_map/reshape | solution.py:392
  48.6 1.7 %multiply_add_fusion.late_base_ref = f32[256,768]{1,0:T(8,128)S(1)} fusion(f32[256,768]{1,0:T(8,128)S(1)} %copy.8.late_spread_ref, f32[256,2048]{1,0:T(8,128)} %copy-done, f32[256,2048]{1,0:T(8,128)} %copy-done.2), kind=kLoop, calls=%fused_computation | loop fusion | flops 393216 | bytes 3145728 | tf_op jit(solution)/shard_map/add | solution.py:393
  50.7 1.6 %copy-done.3 = f32[256,2048]{1,0:T(8,128)S(1)} copy-done((f32[256,2048]{1,0:T(8,128)S(1)}, f32[256,2048]{1,0:T(8,128)}, u32[]{:S(2)}) %copy-start.3) | copy-done | bytes 2097176
  52.7 2.4 %finish.2.rest_0_ = bf16[256,2048]{1,0:T(8,128)(2,1)} custom-call(f32[256,1280]{1,0:T(8,128)S(1)} %get-tuple-element.61.base_ref, f32[256,1280]{1,0:T(8,128)S(1)} %get-tuple-element.62.spread_ref, f32[256,768]{1,0:T(8,128)S(1)} %multiply_add_fusion.late_base_ref, f32[256,768]{1,0:T(8,128)S(1)} %copy.8.late_spread_ref, ...), custom_call_target="tpu_custom_call" | custom-call | tf_op jit(solution)/shard_map/finish/pallas_call | solution.py:303
  55.1 0.9 %finish.3 = bf16[256,2048]{1,0:T(8,128)(2,1)} custom-call(f32[256,1280]{1,0:T(8,128)S(1)} %get-tuple-element.61.base_ref, f32[256,1280]{1,0:T(8,128)S(1)} %get-tuple-element.62.spread_ref, f32[256,768]{1,0:T(8,128)S(1)} %multiply_add_fusion.late_base_ref, f32[256,768]{1,0:T(8,128)S(1)} %copy.8.late_spread_ref, ...), custom_call_target="tpu_custom_call", output_to_operand_aliasing={{}: (8, {})} | custom-call | tf_op jit(solution)/shard_map/finish/pallas_call | solution.py:303
  (29 shorter events, 1.6 us)
Async XLA Ops:
  0.0 27.3 %collective-permute-start.4 = (bf16[256,2048]{1,0:T(8,128)(2,1)}, bf16[256,2048]{1,0:T(8,128)(2,1)S(1)}, u32[]{:S(2)}, u32[]{:S(2)}) collective-permute-start(bf16[256,2048]{1,0:T(8,128)(2,1)} %k_hbm.1), channel_id=1, source_target_pairs={{0,8},{8,0},{16,24},{24,16},{1,9},{9,1},{17,25},{25,17},{2,10},{10... | collective-permute-start | bytes 3145736 | tf_op jit(solution)/shard_map/ppermute | solution.py:23
  2.9 0.7 %copy-start.4 = (s32[16]{0:T(128)S(1)}, s32[16]{0:T(128)}, u32[]{:S(2)}) copy-start(s32[16]{0:T(128)} %middle_ref.11) | copy-start | bytes 196
  3.6 0.7 %copy-start.6 = (s32[16]{0:T(128)S(1)}, s32[16]{0:T(128)}, u32[]{:S(2)}) copy-start(s32[16]{0:T(128)} %coarse_ref.3) | copy-start | bytes 196
  4.3 23.1 %copy-start.5 = (s32[16]{0:T(128)S(1)}, s32[16]{0:T(128)}, u32[]{:S(2)}) copy-start(s32[16]{0:T(128)} %middle_ref.11) | copy-start | bytes 196
  8.4 16.7 %collective-permute-start.6 = (bf16[128,2048]{1,0:T(8,128)(2,1)S(1)}, bf16[128,2048]{1,0:T(8,128)(2,1)S(1)}, u32[]{:S(2)}, u32[]{:S(2)}) collective-permute-start(bf16[128,2048]{1,0:T(8,128)(2,1)S(1)} %get-tuple-element.51), channel_id=1, source_target_pairs={{0,16},{8,24},{16,0},{24,8},{1,17},{9,25},{17,1},{25,9},{2,18},{10... | collective-permute-start | bytes 1572872 | tf_op jit(solution)/shard_map/ppermute | solution.py:23
  10.0 4.7 %collective-permute-start = (bf16[2,2048]{1,0:T(2,128)(2,1)S(1)}, bf16[2,2048]{1,0:T(2,128)(2,1)S(1)}, u32[]{:S(2)}, u32[]{:S(2)}) collective-permute-start(bf16[2,2048]{1,0:T(2,128)(2,1)S(1)} %get-tuple-element.39.refs_0_), channel_id=1, source_target_pairs={{0,10},{1,11},{2,8},{3,9},{4,14},{5,15},{6,12},{7,13},{8,2},{9,3},... | collective-permute-start | bytes 24584 | tf_op jit(solution)/shard_map/ppermute | solution.py:33
  14.7 5.3 %collective-permute-start.1 = (bf16[4,2048]{1,0:T(4,128)(2,1)S(1)}, bf16[4,2048]{1,0:T(4,128)(2,1)S(1)}, u32[]{:S(2)}, u32[]{:S(2)}) collective-permute-start(bf16[4,2048]{1,0:T(4,128)(2,1)S(1)} %stack.2.refs_0_), channel_id=1, source_target_pairs={{0,2},{1,3},{2,0},{3,1},{4,6},{5,7},{6,4},{7,5},{8,10},{9,11},{10,... | collective-permute-start | bytes 49160 | tf_op jit(solution)/shard_map/ppermute | solution.py:23
  16.3 4.9 %collective-permute-start.2 = (bf16[4,2048]{1,0:T(4,128)(2,1)S(1)}, bf16[4,2048]{1,0:T(4,128)(2,1)S(1)}, u32[]{:S(2)}, u32[]{:S(2)}) collective-permute-start(bf16[4,2048]{1,0:T(4,128)(2,1)S(1)} %stack.2.refs_0_), channel_id=1, source_target_pairs={{0,4},{1,5},{2,6},{3,7},{4,0},{5,1},{6,2},{7,3},{8,12},{9,13},{10,... | collective-permute-start | bytes 49160 | tf_op jit(solution)/shard_map/ppermute | solution.py:23
  18.9 5.6 %collective-permute-start.3 = (bf16[4,2048]{1,0:T(4,128)(2,1)S(1)}, bf16[4,2048]{1,0:T(4,128)(2,1)S(1)}, u32[]{:S(2)}, u32[]{:S(2)}) collective-permute-start(bf16[4,2048]{1,0:T(4,128)(2,1)S(1)} %stack.2.refs_0_), channel_id=1, source_target_pairs={{0,6},{1,7},{2,4},{3,5},{4,2},{5,3},{6,0},{7,1},{8,14},{9,15},{10,... | collective-permute-start | bytes 49160 | tf_op jit(solution)/shard_map/ppermute | solution.py:23
  24.6 9.3 %collective-permute-start.7 = (bf16[64,2048]{1,0:T(8,128)(2,1)S(1)}, bf16[64,2048]{1,0:T(8,128)(2,1)S(1)}, u32[]{:S(2)}, u32[]{:S(2)}) collective-permute-start(bf16[64,2048]{1,0:T(8,128)(2,1)S(1)} %get-tuple-element.55), channel_id=1, source_target_pairs={{0,8},{8,0},{16,24},{24,16},{1,9},{9,1},{17,25},{25,17},{2,10},{10... | collective-permute-start | bytes 786440 | tf_op jit(solution)/shard_map/ppermute | solution.py:23
  25.1 10.0 %collective-permute-start.9 = (bf16[16,2048]{1,0:T(8,128)(2,1)S(1)}, bf16[16,2048]{1,0:T(8,128)(2,1)S(1)}, u32[]{:S(2)}, u32[]{:S(2)}) collective-permute-start(bf16[16,2048]{1,0:T(8,128)(2,1)S(1)} %stack.3), channel_id=1, source_target_pairs={{0,18},{1,19},{2,16},{3,17},{4,22},{5,23},{6,20},{7,21},{8,26},{9,... | collective-permute-start | bytes 196616 | tf_op jit(solution)/shard_map/ppermute | solution.py:33
  25.1 27.6 %collective-permute-start.12 = (bf16[192,1664]{1,0:T(8,128)(2,1)}, bf16[192,1664]{1,0:T(8,128)(2,1)}, u32[]{:S(2)}, u32[]{:S(2)}) collective-permute-start(bf16[192,1664]{1,0:T(8,128)(2,1)} %get-tuple-element.66), channel_id=1, source_target_pairs={{0,8},{8,0},{16,24},{24,16},{1,9},{9,1},{17,25},{25,17},{2,10},{10... | collective-permute-start | bytes 1916936 | tf_op jit(solution)/shard_map/ppermute | solution.py:23
  28.2 9.3 %collective-permute-start.5 = (bf16[64,2048]{1,0:T(8,128)(2,1)S(1)}, bf16[64,2048]{1,0:T(8,128)(2,1)S(1)}, u32[]{:S(2)}, u32[]{:S(2)}) collective-permute-start(bf16[64,2048]{1,0:T(8,128)(2,1)S(1)} %pick.1), channel_id=1, source_target_pairs={{0,16},{8,24},{16,0},{24,8},{1,17},{9,25},{17,1},{25,9},{2,18},{10... | collective-permute-start | bytes 786440 | tf_op jit(solution)/shard_map/ppermute | solution.py:23
  33.9 7.3 %collective-permute-start.8 = (bf16[64,2048]{1,0:T(8,128)(2,1)S(1)}, bf16[64,2048]{1,0:T(8,128)(2,1)S(1)}, u32[]{:S(2)}, u32[]{:S(2)}) collective-permute-start(bf16[64,2048]{1,0:T(8,128)(2,1)S(1)} %collective-permute-done.7.vm_ref), channel_id=1, source_target_pairs={{0,16},{8,24},{16,0},{24,8},{1,17},{9,25},{17,1},{25,9},{2,18},{10... | collective-permute-start | bytes 786440 | tf_op jit(solution)/shard_map/ppermute | solution.py:23
  35.0 6.0 %collective-permute-start.10 = (bf16[32,2048]{1,0:T(8,128)(2,1)S(1)}, bf16[32,2048]{1,0:T(8,128)(2,1)S(1)}, u32[]{:S(2)}, u32[]{:S(2)}) collective-permute-start(bf16[32,2048]{1,0:T(8,128)(2,1)S(1)} %constant_dynamic-update-slice_fusion.mine_ref), channel_id=1, source_target_pairs={{0,1},{1,0},{2,3},{3,2},{4,5},{5,4},{6,7},{7,6},{8,9},{9,8},{10,11... | collective-permute-start | bytes 393224 | tf_op jit(solution)/shard_map/ppermute | solution.py:23
  35.1 20.0 %collective-permute-start.11 = (bf16[192,384]{1,0:T(8,128)(2,1)}, bf16[192,384]{1,0:T(8,128)(2,1)S(1)}, u32[]{:S(2)}, u32[]{:S(2)}) collective-permute-start(bf16[192,384]{1,0:T(8,128)(2,1)} %get-tuple-element.65), channel_id=1, source_target_pairs={{0,8},{8,0},{16,24},{24,16},{1,9},{9,1},{17,25},{25,17},{2,10},{10... | collective-permute-start | bytes 442376 | tf_op jit(solution)/shard_map/ppermute | solution.py:23
  39.1 2.1 %copy-start.7 = (s32[16]{0:T(128)S(1)}, s32[16]{0:T(128)}, u32[]{:S(2)}) copy-start(s32[16]{0:T(128)} %coarse_ref.3) | copy-start | bytes 196
  41.0 3.7 %copy-start = (f32[256,2048]{1,0:T(8,128)}, f32[256,2048]{1,0:T(8,128)S(1)}, u32[]{:S(2)}) copy-start(f32[256,2048]{1,0:T(8,128)S(1)} %get-tuple-element.60.own_ref) | copy-start | bytes 6291460
  44.7 1.3 %copy-start.2 = (f32[256,2048]{1,0:T(8,128)}, f32[256,2048]{1,0:T(8,128)S(1)}, u32[]{:S(2)}) copy-start(f32[256,2048]{1,0:T(8,128)S(1)} %get-tuple-element.58.sum_ref) | copy-start | bytes 6291460
  48.6 2.1 %copy-start.1 = (f32[256,2048]{1,0:T(8,128)S(1)}, f32[256,2048]{1,0:T(8,128)}, u32[]{:S(2)}) copy-start(f32[256,2048]{1,0:T(8,128)} %copy-done) | copy-start | bytes 6291460
  50.7 1.6 %copy-start.3 = (f32[256,2048]{1,0:T(8,128)S(1)}, f32[256,2048]{1,0:T(8,128)}, u32[]{:S(2)}) copy-start(f32[256,2048]{1,0:T(8,128)} %copy-done.2) | copy-start | bytes 6291460

commit v20 on v18

--- a/solution.py
+++ b/solution.py
@@ -235,9 +235,9 @@
         other_ref = (other_a_ref, other_b_ref)[head // half]
         values = jnp.concatenate([vm_ref[:, head_columns(head)], vr_ref[:, columns]], axis=0)
         result = base_ref[:, columns] + spread_ref[:, columns] * dot(other_ref[head % half], values)
-        ready_ref[place] = result.astype(jnp.bfloat16)
+        ready_ref[:, columns] = result.astype(jnp.bfloat16)
         target = out_ref.at[:, head_columns(head)]
-        copies.append(pltpu.make_async_copy(ready_ref.at[place], target, semaphores.at[place]))
+        copies.append(pltpu.make_async_copy(ready_ref.at[:, columns], target, semaphores.at[place]))
         copies[-1].start()
     for copy in copies:
         copy.wait()
@@ -399,7 +399,7 @@
                 in_specs=[vmem] * len(args) + [anywhere] * len(out),
                 out_specs=anywhere,
                 input_output_aliases={len(args): 0} if out else {},
-                scratch_shapes=[pltpu.VMEM((chunk, rows, HEAD_FEATURES), bf16), pltpu.SemaphoreType.DMA((chunk,))],
+                scratch_shapes=[pltpu.VMEM((rows, chunk * HEAD_FEATURES), bf16), pltpu.SemaphoreType.DMA((chunk,))],
             )
         ]
         first += chunk

time: 50.2 us -> 50.2 us (level)
  no operation moved by 1% of the time
where the time goes in v20:
time: 50.2 us; the launch traced here: 50.1 us
  starting transfers between devices  18.5 us (37%)
  Pallas kernels  16.6 us (33%)
  waiting for transfers between devices  13 us (26%)
  local copies, waits for them, and re-layouts  1.78 us (4%)
    ppermute x11, starting transfers between devices, partner(): return lax.ppermute(value, axis, pairs)  16.9 us
    pallas_call x10, Pallas kernels, call(): pl.pallas_call(kernel, name=name, compiler_params=params, cost_estimate=c...  16.6 us
    ppermute x11, waiting for transfers between devices, partner(): return lax.ppermute(value, axis, pairs)  9.86 us
    ppermute x2, waiting for transfers between devices, partner_elsewhere(): return lax.ppermute(value, ('inner', 'outer'), pairs)  3.11 us
    ppermute x2, starting transfers between devices, partner_elsewhere(): return lax.ppermute(value, ('inner', 'outer'), pairs)  1.55 us
    unnamed x10, local copies, waits for them, and re-layouts  1.34 us
  transfers between devices with their start and end apart: 13, of which 7 were waited for; matrix products, arithmetic and copies ran while one was open for 1% of the time, Pallas kernels for 31%

profile of v20, /device:TPU:0, one launch (start us, length us, event | category | flops | bytes accessed | tf_op | source)
XLA Modules:
  0.0 50.1 jit_solution(4479619318585032247)
XLA Ops:
  0.0 2.9 %collective-permute-start.4 = (bf16[256,2048]{1,0:T(8,128)(2,1)}, bf16[256,2048]{1,0:T(8,128)(2,1)S(1)}, u32[]{:S(2)}, u32[]{:S(2)}) collective-permute-start(bf16[256,2048]{1,0:T(8,128)(2,1)} %k_hbm.1), channel_id=1, source_target_pairs={{0,8},{8,0},{16,24},{24,16},{1,9},{9,1},{17,25},{25,17},{2,10},{10... | collective-permute-start | bytes 3145736 | tf_op jit(solution)/shard_map/ppermute | solution.py:22
  2.9 0.7 %copy-done = s32[16]{0:T(128)S(1)} copy-done((s32[16]{0:T(128)S(1)}, s32[16]{0:T(128)}, u32[]{:S(2)}) %copy-start) | copy-done | bytes 88
  3.6 0.7 %copy-done.2 = s32[16]{0:T(128)S(1)} copy-done((s32[16]{0:T(128)S(1)}, s32[16]{0:T(128)}, u32[]{:S(2)}) %copy-start.2) | copy-done | bytes 88
  4.3 3.2 %prepare.1 = (bf16[256,2048]{1,0:T(8,128)(2,1)S(1)}, bf16[256,2048]{1,0:T(8,128)(2,1)S(1)}, bf16[256,2048]{1,0:T(8,128)(2,1)S(1)}, bf16[128,2048]{1,0:T(8,128)(2...) custom-call(s32[16]{0:T(128)S(1)} %copy-done, ...), custom_call_target="tpu_custom_call" | custom-call | tf_op jit(solution)/shard_map/prepare/pallas_call | solution.py:295
  7.5 1.6 %collective-permute-start.6 = (bf16[128,2048]{1,0:T(8,128)(2,1)S(1)}, bf16[128,2048]{1,0:T(8,128)(2,1)S(1)}, u32[]{:S(2)}, u32[]{:S(2)}) collective-permute-start(bf16[128,2048]{1,0:T(8,128)(2,1)S(1)} %get-tuple-element.51), channel_id=1, source_target_pairs={{0,16},{8,24},{16,0},{24,8},{1,17},{9,25},{17,1},{25,9},{2,18},{10... | collective-permute-start | bytes 1572872 | tf_op jit(solution)/shard_map/ppermute | solution.py:22
  9.1 1.5 %collective-permute-start = (bf16[2,2048]{1,0:T(2,128)(2,1)S(1)}, bf16[2,2048]{1,0:T(2,128)(2,1)S(1)}, u32[]{:S(2)}, u32[]{:S(2)}) collective-permute-start(bf16[2,2048]{1,0:T(2,128)(2,1)S(1)} %get-tuple-element.39.refs_0_), channel_id=1, source_target_pairs={{0,10},{1,11},{2,8},{3,9},{4,14},{5,15},{6,12},{7,13},{8,2},{9,3},... | collective-permute-start | bytes 24584 | tf_op jit(solution)/shard_map/ppermute | solution.py:32
  10.6 3.1 %collective-permute-done.refs_1_ = bf16[2,2048]{1,0:T(2,128)(2,1)S(1)} collective-permute-done((bf16[2,2048]{1,0:T(2,128)(2,1)S(1)}, bf16[2,2048]{1,0:T(2,128)(2,1)S(1)}, u32[]{:S(2)}, u32[]{:S(2)}) %collective-permute-start) | collective-permute-done | bytes 8224 | tf_op jit(solution)/shard_map/ppermute | solution.py:32
  13.8 1.6 %collective-permute-start.1 = (bf16[4,2048]{1,0:T(4,128)(2,1)S(1)}, bf16[4,2048]{1,0:T(4,128)(2,1)S(1)}, u32[]{:S(2)}, u32[]{:S(2)}) collective-permute-start(bf16[4,2048]{1,0:T(4,128)(2,1)S(1)} %stack.2.refs_0_), channel_id=1, source_target_pairs={{0,2},{1,3},{2,0},{3,1},{4,6},{5,7},{6,4},{7,5},{8,10},{9,11},{10,... | collective-permute-start | bytes 49160 | tf_op jit(solution)/shard_map/ppermute | solution.py:22
  15.4 2.6 %collective-permute-start.2 = (bf16[4,2048]{1,0:T(4,128)(2,1)S(1)}, bf16[4,2048]{1,0:T(4,128)(2,1)S(1)}, u32[]{:S(2)}, u32[]{:S(2)}) collective-permute-start(bf16[4,2048]{1,0:T(4,128)(2,1)S(1)} %stack.2.refs_0_), channel_id=1, source_target_pairs={{0,4},{1,5},{2,6},{3,7},{4,0},{5,1},{6,2},{7,3},{8,12},{9,13},{10,... | collective-permute-start | bytes 49160 | tf_op jit(solution)/shard_map/ppermute | solution.py:22
  18.0 0.2 collective-permute-start.3
  18.2 0.8 %score.1 = (f32[16,256,256]{2,1,0:T(8,128)S(1)}, f32[16,256,128]{2,1,0:T(8,128)S(1)}) custom-call(bf16[256,2048]{1,0:T(8,128)(2,1)S(1)} %get-tuple-element.46.q_ref, bf16[256,2048]{1,0:T(8,128)(2,1)S(1)} %get-tuple-element.37.k_ref), custom_call_target="tpu_custom_call" | custom-call | tf_op jit(solution)/shard_map/score/pallas_call | solution.py:295
  19.0 1.2 %collective-permute-done.2.refs_2_ = bf16[4,2048]{1,0:T(4,128)(2,1)S(1)} collective-permute-done((bf16[4,2048]{1,0:T(4,128)(2,1)S(1)}, bf16[4,2048]{1,0:T(4,128)(2,1)S(1)}, u32[]{:S(2)}, u32[]{:S(2)}) %collective-permute-start.2) | collective-permute-done | bytes 16416 | tf_op jit(solution)/shard_map/ppermute | solution.py:22
  20.3 3.4 %collective-permute-done.3.refs_3_ = bf16[4,2048]{1,0:T(4,128)(2,1)S(1)} collective-permute-done((bf16[4,2048]{1,0:T(4,128)(2,1)S(1)}, bf16[4,2048]{1,0:T(4,128)(2,1)S(1)}, u32[]{:S(2)}, u32[]{:S(2)}) %collective-permute-start.3) | collective-permute-done | bytes 16416 | tf_op jit(solution)/shard_map/ppermute | solution.py:22
  23.6 0.5 collective-permute-start.7
  24.2 1.6 %collective-permute-start.12 = (bf16[192,1792]{1,0:T(8,128)(2,1)S(1)}, bf16[192,1792]{1,0:T(8,128)(2,1)S(1)}, u32[]{:S(2)}, u32[]{:S(2)}) collective-permute-start(bf16[192,1792]{1,0:T(8,128)(2,1)S(1)} %get-tuple-element.66), channel_id=1, source_target_pairs={{0,8},{8,0},{16,24},{24,16},{1,9},{9,1},{17,25},{25,17},{2,10},{10... | collective-permute-start | bytes 2064392 | tf_op jit(solution)/shard_map/ppermute | solution.py:22
  25.8 1.6 %collective-permute-done.4.k_ref.kp_ref = bf16[256,2048]{1,0:T(8,128)(2,1)S(1)} collective-permute-done((bf16[256,2048]{1,0:T(8,128)(2,1)}, bf16[256,2048]{1,0:T(8,128)(2,1)S(1)}, u32[]{:S(2)}, u32[]{:S(2)}) %collective-permute-start.4) | collective-permute-done | bytes 1048608 | tf_op jit(solution)/shard_map/ppermute | solution.py:22
  27.3 0.8 %pick.1 = bf16[64,2048]{1,0:T(8,128)(2,1)S(1)} custom-call(s32[16]{0:T(128)S(1)} %copy-done.1, bf16[256,2048]{1,0:T(8,128)(2,1)S(1)} %collective-permute-done.4.k_ref.kp_ref), custom_call_target="tpu_custom_call" | custom-call | tf_op jit(solution)/shard_map/pick/pallas_call | solution.py:295
  28.2 2.2 %collective-permute-start.5 = (bf16[64,2048]{1,0:T(8,128)(2,1)S(1)}, bf16[64,2048]{1,0:T(8,128)(2,1)S(1)}, u32[]{:S(2)}, u32[]{:S(2)}) collective-permute-start(bf16[64,2048]{1,0:T(8,128)(2,1)S(1)} %pick.1), channel_id=1, source_target_pairs={{0,16},{8,24},{16,0},{24,8},{1,17},{9,25},{17,1},{25,9},{2,18},{10... | collective-permute-start | bytes 786440 | tf_op jit(solution)/shard_map/ppermute | solution.py:22
  30.3 1.7 %other.2 = (bf16[8,256,256]{2,1,0:T(8,128)(2,1)S(1)}, f32[8,256,128]{2,1,0:T(8,128)S(1)}, f32[256,128]{1,0:T(8,128)S(1)}) custom-call(s32[16]{0:T(128)S(1)} %copy-done.1, bf16[256,2048]{1,0:T(8,128)(2,1)S(1)} %get-tuple-element.46.q_ref, f32[16,256,128]{2,1,0:T(8,128)S(1)} %get-tuple-element.42.own_top_ref, ...), custom_call_target="tpu_custom_call" | custom-call | tf_op jit(solution)/shard_map/other/pallas_call | solution.py:295
  32.0 0.9 %collective-permute-done.7.vm_ref = bf16[64,2048]{1,0:T(8,128)(2,1)S(1)} collective-permute-done((bf16[64,2048]{1,0:T(8,128)(2,1)S(1)}, bf16[64,2048]{1,0:T(8,128)(2,1)S(1)}, u32[]{:S(2)}, u32[]{:S(2)}) %collective-permute-start.7) | collective-permute-done | bytes 262176 | tf_op jit(solution)/shard_map/ppermute | solution.py:22
  32.9 2.1 %collective-permute-start.8 = (bf16[64,2048]{1,0:T(8,128)(2,1)S(1)}, bf16[64,2048]{1,0:T(8,128)(2,1)S(1)}, u32[]{:S(2)}, u32[]{:S(2)}) collective-permute-start(bf16[64,2048]{1,0:T(8,128)(2,1)S(1)} %collective-permute-done.7.vm_ref), channel_id=1, source_target_pairs={{0,16},{8,24},{16,0},{24,8},{1,17},{9,25},{17,1},{25,9},{2,18},{10... | collective-permute-start | bytes 786440 | tf_op jit(solution)/shard_map/ppermute | solution.py:22
  35.1 1.6 %collective-permute-start.11 = (bf16[192,256]{1,0:T(8,128)(2,1)S(1)}, bf16[192,256]{1,0:T(8,128)(2,1)S(1)}, u32[]{:S(2)}, u32[]{:S(2)}) collective-permute-start(bf16[192,256]{1,0:T(8,128)(2,1)S(1)} %get-tuple-element.63), channel_id=1, source_target_pairs={{0,8},{8,0},{16,24},{24,16},{1,9},{9,1},{17,25},{25,17},{2,10},{10... | collective-permute-start | bytes 294920 | tf_op jit(solution)/shard_map/ppermute | solution.py:22
  36.7 1.7 %other.3 = (bf16[8,256,256]{2,1,0:T(8,128)(2,1)S(1)}, f32[8,256,128]{2,1,0:T(8,128)S(1)}, f32[256,128]{1,0:T(8,128)S(1)}) custom-call(s32[16]{0:T(128)S(1)} %copy-done.1, bf16[256,2048]{1,0:T(8,128)(2,1)S(1)} %get-tuple-element.46.q_ref, f32[16,256,128]{2,1,0:T(8,128)S(1)} %get-tuple-element.42.own_top_ref, ...), custom_call_target="tpu_custom_call" | custom-call | tf_op jit(solution)/shard_map/other/pallas_call | solution.py:295
  38.4 1.8 %own.1 = (f32[256,2048]{1,0:T(8,128)S(1)}, f32[256,128]{1,0:T(8,128)S(1)}) custom-call(s32[16]{0:T(128)S(1)} %copy-done.1, f32[16,256,256]{2,1,0:T(8,128)S(1)} %get-tuple-element.38.scores_ref, f32[8,256,128]{2,1,0:T(8,128)S(1)} %get-tuple-element.44.top_a_ref, f32[8,256,128]{2,1,0:T(8,128)S(1)} %get-tuple-element.47.top_b_ref, ...), custom_call_target="tpu_custom_call" | custom-call | tf_op jit(solution)/shard_map/own/pallas_call | solution.py:295
  40.2 0.3 collective-permute-done.8.diagonal_v_ref
  40.5 3.5 %extra.1 = (f32[256,2048]{1,0:T(8,128)S(1)}, f32[256,128]{1,0:T(8,128)S(1)}) custom-call(s32[16]{0:T(128)S(1)} %copy-done.1, s32[16]{0:T(128)S(1)} %copy-done.3, bf16[256,2048]{1,0:T(8,128)(2,1)S(1)} %get-tuple-element.46.q_ref, f32[256,128]{1,0:T(8,128)S(1)} %get-tuple-element.49.own_total_ref, f32[256,128]{1,0:T(8,128)S(1)} %get-tuple-element.45.state_a_ref, ...), custom_call_target="tpu_custom_call" | custom-call | tf_op jit(solution)/shard_map/extra/pallas_call | solution.py:295
  44.0 0.1 slice.10
  44.1 0.3 broadcast_in_dim.3
  44.6 0.6 %base.1 = (f32[256,1792]{1,0:T(8,128)S(1)}, f32[256,1792]{1,0:T(8,128)S(1)}) custom-call(f32[256,2048]{1,0:T(8,128)S(1)} %get-tuple-element.58.sum_ref, f32[256,128]{1,0:T(8,128)S(1)} %get-tuple-element.59.share_ref, f32[256,2048]{1,0:T(8,128)S(1)} %get-tuple-element.60.own_ref), custom_call_target="tpu_custom_call" | custom-call | tf_op jit(solution)/shard_map/base/pallas_call | solution.py:295
  45.2 2.5 %collective-permute-done.12.vr_ref = bf16[192,1792]{1,0:T(8,128)(2,1)S(1)} collective-permute-done((bf16[192,1792]{1,0:T(8,128)(2,1)S(1)}, bf16[192,1792]{1,0:T(8,128)(2,1)S(1)}, u32[]{:S(2)}, u32[]{:S(2)}) %collective-permute-start.12) | collective-permute-done | bytes 688160 | tf_op jit(solution)/shard_map/ppermute | solution.py:22
  47.7 1.5 %finish.2.rest_0_ = bf16[256,2048]{1,0:T(8,128)(2,1)} custom-call(f32[256,1792]{1,0:T(8,128)S(1)} %get-tuple-element.64.base_ref, f32[256,1792]{1,0:T(8,128)S(1)} %get-tuple-element.65.spread_ref, bf16[8,256,256]{2,1,0:T(8,128)(2,1)S(1)} %get-tuple-element.61.other_a_ref, bf16[8,256,256]{2,1,0:T(8,128)(2,1)S(1)} %get-tuple-element.62.other_b_ref, ...), custom_call_target="tpu_custom_call" | custom-call | tf_op jit(solution)/shard_map/finish/pallas_call | solution.py:295
  49.2 0.9 %finish.3 = bf16[256,2048]{1,0:T(8,128)(2,1)} custom-call(f32[256,256]{1,0:T(8,128)S(1)} %multiply_add_fusion.base_ref, f32[256,256]{1,0:T(8,128)S(1)} %bitcast.6, bf16[8,256,256]{2,1,0:T(8,128)(2,1)S(1)} %get-tuple-element.61.other_a_ref, bf16[8,256,256]{2,1,0:T(8,128)(2,1)S(1)} %get-tuple-element.62.other_b_ref, ...), custom_call_target="tpu_custom_call", output_to_operand_aliasing={{}: (6, {})} | custom-call | tf_op jit(solution)/shard_map/finish/pallas_call | solution.py:295
  (20 shorter events, 0.2 us)
Async XLA Ops:
  0.0 27.3 %collective-permute-start.4 = (bf16[256,2048]{1,0:T(8,128)(2,1)}, bf16[256,2048]{1,0:T(8,128)(2,1)S(1)}, u32[]{:S(2)}, u32[]{:S(2)}) collective-permute-start(bf16[256,2048]{1,0:T(8,128)(2,1)} %k_hbm.1), channel_id=1, source_target_pairs={{0,8},{8,0},{16,24},{24,16},{1,9},{9,1},{17,25},{25,17},{2,10},{10... | collective-permute-start | bytes 3145736 | tf_op jit(solution)/shard_map/ppermute | solution.py:22
  2.9 0.7 %copy-start = (s32[16]{0:T(128)S(1)}, s32[16]{0:T(128)}, u32[]{:S(2)}) copy-start(s32[16]{0:T(128)} %middle_ref.11) | copy-start | bytes 196
  3.6 0.7 %copy-start.2 = (s32[16]{0:T(128)S(1)}, s32[16]{0:T(128)}, u32[]{:S(2)}) copy-start(s32[16]{0:T(128)} %coarse_ref.3) | copy-start | bytes 196
  4.3 23.1 %copy-start.1 = (s32[16]{0:T(128)S(1)}, s32[16]{0:T(128)}, u32[]{:S(2)}) copy-start(s32[16]{0:T(128)} %middle_ref.11) | copy-start | bytes 196
  7.5 16.7 %collective-permute-start.6 = (bf16[128,2048]{1,0:T(8,128)(2,1)S(1)}, bf16[128,2048]{1,0:T(8,128)(2,1)S(1)}, u32[]{:S(2)}, u32[]{:S(2)}) collective-permute-start(bf16[128,2048]{1,0:T(8,128)(2,1)S(1)} %get-tuple-element.51), channel_id=1, source_target_pairs={{0,16},{8,24},{16,0},{24,8},{1,17},{9,25},{17,1},{25,9},{2,18},{10... | collective-permute-start | bytes 1572872 | tf_op jit(solution)/shard_map/ppermute | solution.py:22
  9.1 4.7 %collective-permute-start = (bf16[2,2048]{1,0:T(2,128)(2,1)S(1)}, bf16[2,2048]{1,0:T(2,128)(2,1)S(1)}, u32[]{:S(2)}, u32[]{:S(2)}) collective-permute-start(bf16[2,2048]{1,0:T(2,128)(2,1)S(1)} %get-tuple-element.39.refs_0_), channel_id=1, source_target_pairs={{0,10},{1,11},{2,8},{3,9},{4,14},{5,15},{6,12},{7,13},{8,2},{9,3},... | collective-permute-start | bytes 24584 | tf_op jit(solution)/shard_map/ppermute | solution.py:32
  13.8 5.3 %collective-permute-start.1 = (bf16[4,2048]{1,0:T(4,128)(2,1)S(1)}, bf16[4,2048]{1,0:T(4,128)(2,1)S(1)}, u32[]{:S(2)}, u32[]{:S(2)}) collective-permute-start(bf16[4,2048]{1,0:T(4,128)(2,1)S(1)} %stack.2.refs_0_), channel_id=1, source_target_pairs={{0,2},{1,3},{2,0},{3,1},{4,6},{5,7},{6,4},{7,5},{8,10},{9,11},{10,... | collective-permute-start | bytes 49160 | tf_op jit(solution)/shard_map/ppermute | solution.py:22
  15.4 4.9 %collective-permute-start.2 = (bf16[4,2048]{1,0:T(4,128)(2,1)S(1)}, bf16[4,2048]{1,0:T(4,128)(2,1)S(1)}, u32[]{:S(2)}, u32[]{:S(2)}) collective-permute-start(bf16[4,2048]{1,0:T(4,128)(2,1)S(1)} %stack.2.refs_0_), channel_id=1, source_target_pairs={{0,4},{1,5},{2,6},{3,7},{4,0},{5,1},{6,2},{7,3},{8,12},{9,13},{10,... | collective-permute-start | bytes 49160 | tf_op jit(solution)/shard_map/ppermute | solution.py:22
  18.0 5.6 %collective-permute-start.3 = (bf16[4,2048]{1,0:T(4,128)(2,1)S(1)}, bf16[4,2048]{1,0:T(4,128)(2,1)S(1)}, u32[]{:S(2)}, u32[]{:S(2)}) collective-permute-start(bf16[4,2048]{1,0:T(4,128)(2,1)S(1)} %stack.2.refs_0_), channel_id=1, source_target_pairs={{0,6},{1,7},{2,4},{3,5},{4,2},{5,3},{6,0},{7,1},{8,14},{9,15},{10,... | collective-permute-start | bytes 49160 | tf_op jit(solution)/shard_map/ppermute | solution.py:22
  23.6 9.3 %collective-permute-start.7 = (bf16[64,2048]{1,0:T(8,128)(2,1)S(1)}, bf16[64,2048]{1,0:T(8,128)(2,1)S(1)}, u32[]{:S(2)}, u32[]{:S(2)}) collective-permute-start(bf16[64,2048]{1,0:T(8,128)(2,1)S(1)} %get-tuple-element.55), channel_id=1, source_target_pairs={{0,8},{8,0},{16,24},{24,16},{1,9},{9,1},{17,25},{25,17},{2,10},{10... | collective-permute-start | bytes 786440 | tf_op jit(solution)/shard_map/ppermute | solution.py:22
  24.1 10.9 %collective-permute-start.9 = (bf16[16,2048]{1,0:T(8,128)(2,1)S(1)}, bf16[16,2048]{1,0:T(8,128)(2,1)S(1)}, u32[]{:S(2)}, u32[]{:S(2)}) collective-permute-start(bf16[16,2048]{1,0:T(8,128)(2,1)S(1)} %stack.3), channel_id=1, source_target_pairs={{0,18},{1,19},{2,16},{3,17},{4,22},{5,23},{6,20},{7,21},{8,26},{9,... | collective-permute-start | bytes 196616 | tf_op jit(solution)/shard_map/ppermute | solution.py:32
  24.2 23.5 %collective-permute-start.12 = (bf16[192,1792]{1,0:T(8,128)(2,1)S(1)}, bf16[192,1792]{1,0:T(8,128)(2,1)S(1)}, u32[]{:S(2)}, u32[]{:S(2)}) collective-permute-start(bf16[192,1792]{1,0:T(8,128)(2,1)S(1)} %get-tuple-element.66), channel_id=1, source_target_pairs={{0,8},{8,0},{16,24},{24,16},{1,9},{9,1},{17,25},{25,17},{2,10},{10... | collective-permute-start | bytes 2064392 | tf_op jit(solution)/shard_map/ppermute | solution.py:22
  28.2 8.5 %collective-permute-start.5 = (bf16[64,2048]{1,0:T(8,128)(2,1)S(1)}, bf16[64,2048]{1,0:T(8,128)(2,1)S(1)}, u32[]{:S(2)}, u32[]{:S(2)}) collective-permute-start(bf16[64,2048]{1,0:T(8,128)(2,1)S(1)} %pick.1), channel_id=1, source_target_pairs={{0,16},{8,24},{16,0},{24,8},{1,17},{9,25},{17,1},{25,9},{2,18},{10... | collective-permute-start | bytes 786440 | tf_op jit(solution)/shard_map/ppermute | solution.py:22
  32.9 7.6 %collective-permute-start.8 = (bf16[64,2048]{1,0:T(8,128)(2,1)S(1)}, bf16[64,2048]{1,0:T(8,128)(2,1)S(1)}, u32[]{:S(2)}, u32[]{:S(2)}) collective-permute-start(bf16[64,2048]{1,0:T(8,128)(2,1)S(1)} %collective-permute-done.7.vm_ref), channel_id=1, source_target_pairs={{0,16},{8,24},{16,0},{24,8},{1,17},{9,25},{17,1},{25,9},{2,18},{10... | collective-permute-start | bytes 786440 | tf_op jit(solution)/shard_map/ppermute | solution.py:22
  35.0 5.2 %collective-permute-start.10 = (bf16[32,2048]{1,0:T(8,128)(2,1)S(1)}, bf16[32,2048]{1,0:T(8,128)(2,1)S(1)}, u32[]{:S(2)}, u32[]{:S(2)}) collective-permute-start(bf16[32,2048]{1,0:T(8,128)(2,1)S(1)} %constant_dynamic-update-slice_fusion.mine_ref), channel_id=1, source_target_pairs={{0,1},{1,0},{2,3},{3,2},{4,5},{5,4},{6,7},{7,6},{8,9},{9,8},{10,11... | collective-permute-start | bytes 393224 | tf_op jit(solution)/shard_map/ppermute | solution.py:22
  35.1 14.1 %collective-permute-start.11 = (bf16[192,256]{1,0:T(8,128)(2,1)S(1)}, bf16[192,256]{1,0:T(8,128)(2,1)S(1)}, u32[]{:S(2)}, u32[]{:S(2)}) collective-permute-start(bf16[192,256]{1,0:T(8,128)(2,1)S(1)} %get-tuple-element.63), channel_id=1, source_target_pairs={{0,8},{8,0},{16,24},{24,16},{1,9},{9,1},{17,25},{25,17},{2,10},{10... | collective-permute-start | bytes 294920 | tf_op jit(solution)/shard_map/ppermute | solution.py:22
  38.4 2.2 %copy-start.3 = (s32[16]{0:T(128)S(1)}, s32[16]{0:T(128)}, u32[]{:S(2)}) copy-start(s32[16]{0:T(128)} %coarse_ref.3) | copy-start | bytes 196

commit v21 on v19

--- a/solution.py
+++ b/solution.py
@@ -11,7 +11,7 @@
 HEAD_FEATURES = 128
 MIDDLE_DILATION = 4
 CHUNKS = (13, 3)
-LATE = 10
+LATE = 14
 LANES = 128
 SUBLANES = 16
 EXP2_SCALE = HEAD_FEATURES ** (-0.5) * 1.4426950408889634
@@ -243,9 +243,9 @@
         else:
             late = head_columns(head - LATE)
             result = late_base_ref[:, late] + late_spread_ref[:, late] * result
-        ready_ref[place] = result.astype(jnp.bfloat16)
+        ready_ref[:, columns] = result.astype(jnp.bfloat16)
         target = out_ref.at[:, head_columns(head)]
-        copies.append(pltpu.make_async_copy(ready_ref.at[place], target, semaphores.at[place]))
+        copies.append(pltpu.make_async_copy(ready_ref.at[:, columns], target, semaphores.at[place]))
         copies[-1].start()
     for copy in copies:
         copy.wait()
@@ -405,7 +405,7 @@
                 in_specs=[vmem] * len(args) + [anywhere] * len(out),
                 out_specs=anywhere,
                 input_output_aliases={len(args): 0} if out else {},
-                scratch_shapes=[pltpu.VMEM((chunk, rows, HEAD_FEATURES), bf16), pltpu.SemaphoreType.DMA((chunk,))],
+                scratch_shapes=[pltpu.VMEM((rows, chunk * HEAD_FEATURES), bf16), pltpu.SemaphoreType.DMA((chunk,))],
             )
         ]
         first += chunk

time: 56.3 us -> 50 us (0.89)
  local copies, waits for them, and re-layouts: 7.16 us -> 1.78 us
  Pallas kernels: 18.4 us -> 16.6 us
  waiting for transfers between devices: 11.1 us -> 12.8 us
  other arithmetic: 1.66 us -> 0.08 us
  starting transfers between devices: 17.6 us -> 18.5 us
    unnamed x17 -> x10, local copies, waits for them, and re-layouts: 4.64 us -> 1.34 us
    pallas_call x10, Pallas kernels: 18.3 us -> 16.5 us  [call(): pl.pallas_call(kernel, name=name, compiler_params=params, cost_estimate=c...]
    ppermute x11, waiting for transfers between devices: 7.99 us -> 9.72 us  [partner(): return lax.ppermute(value, axis, pairs)]
    add x1, other arithmetic: 1.66 us -> 0.08 us  [on_device(): late_base = extra_sum[:, late] + late_spread * own_sum[:, late]]
    reshape x1 -> x0, local copies, waits for them, and re-layouts: 1.39 us -> none  [on_device(): late_spread = jnp.repeat(share[:, LATE:HEAD_COUNT], HEAD_FEATURES, axis=1)]
    ppermute x11, starting transfers between devices: 16.1 us -> 16.9 us  [partner(): return lax.ppermute(value, axis, pairs)]
    broadcast_in_dim x1, local copies, waits for them, and re-layouts: 0.95 us -> 0.34 us  [on_device(): late_spread = jnp.repeat(share[:, LATE:HEAD_COUNT], HEAD_FEATURES, axis=1)]
  transfers between devices with their start and end apart: 13 -> 13, of which waited for: 7 -> 8; matrix products, arithmetic and copies ran while one was open for 7% -> 1% of each run, Pallas kernels for 31% -> 31%
where the time goes in v21:
time: 50 us; the launch traced here: 49.9 us
  starting transfers between devices  18.5 us (37%)
  Pallas kernels  16.6 us (33%)
  waiting for transfers between devices  12.8 us (26%)
  local copies, waits for them, and re-layouts  1.78 us (4%)
    ppermute x11, starting transfers between devices, partner(): return lax.ppermute(value, axis, pairs)  16.9 us
    pallas_call x10, Pallas kernels, call(): pl.pallas_call(kernel, name=name, compiler_params=params, cost_estimate=c...  16.5 us
    ppermute x11, waiting for transfers between devices, partner(): return lax.ppermute(value, axis, pairs)  9.72 us
    ppermute x2, waiting for transfers between devices, partner_elsewhere(): return lax.ppermute(value, ('inner', 'outer'), pairs)  3.11 us
    ppermute x2, starting transfers between devices, partner_elsewhere(): return lax.ppermute(value, ('inner', 'outer'), pairs)  1.55 us
    unnamed x10, local copies, waits for them, and re-layouts  1.34 us
  transfers between devices with their start and end apart: 13, of which 8 were waited for; matrix products, arithmetic and copies ran while one was open for 1% of the time, Pallas kernels for 31%

profile of v21, /device:TPU:0, one launch (start us, length us, event | category | flops | bytes accessed | tf_op | source)
XLA Modules:
  0.0 49.9 jit_solution(10905839116311814669)
XLA Ops:
  0.0 2.9 %collective-permute-start.4 = (bf16[256,2048]{1,0:T(8,128)(2,1)}, bf16[256,2048]{1,0:T(8,128)(2,1)S(1)}, u32[]{:S(2)}, u32[]{:S(2)}) collective-permute-start(bf16[256,2048]{1,0:T(8,128)(2,1)} %k_hbm.1), channel_id=1, source_target_pairs={{0,8},{8,0},{16,24},{24,16},{1,9},{9,1},{17,25},{25,17},{2,10},{10... | collective-permute-start | bytes 3145736 | tf_op jit(solution)/shard_map/ppermute | solution.py:23
  2.9 0.7 %copy-done = s32[16]{0:T(128)S(1)} copy-done((s32[16]{0:T(128)S(1)}, s32[16]{0:T(128)}, u32[]{:S(2)}) %copy-start) | copy-done | bytes 88
  3.6 0.7 %copy-done.2 = s32[16]{0:T(128)S(1)} copy-done((s32[16]{0:T(128)S(1)}, s32[16]{0:T(128)}, u32[]{:S(2)}) %copy-start.2) | copy-done | bytes 88
  4.3 3.2 %prepare.1 = (bf16[256,2048]{1,0:T(8,128)(2,1)S(1)}, bf16[256,2048]{1,0:T(8,128)(2,1)S(1)}, bf16[256,2048]{1,0:T(8,128)(2,1)S(1)}, bf16[128,2048]{1,0:T(8,128)(2...) custom-call(s32[16]{0:T(128)S(1)} %copy-done, ...), custom_call_target="tpu_custom_call" | custom-call | tf_op jit(solution)/shard_map/prepare/pallas_call | solution.py:303
  7.5 1.6 %collective-permute-start.6 = (bf16[128,2048]{1,0:T(8,128)(2,1)S(1)}, bf16[128,2048]{1,0:T(8,128)(2,1)S(1)}, u32[]{:S(2)}, u32[]{:S(2)}) collective-permute-start(bf16[128,2048]{1,0:T(8,128)(2,1)S(1)} %get-tuple-element.51), channel_id=1, source_target_pairs={{0,16},{8,24},{16,0},{24,8},{1,17},{9,25},{17,1},{25,9},{2,18},{10... | collective-permute-start | bytes 1572872 | tf_op jit(solution)/shard_map/ppermute | solution.py:23
  9.1 1.5 %collective-permute-start = (bf16[2,2048]{1,0:T(2,128)(2,1)S(1)}, bf16[2,2048]{1,0:T(2,128)(2,1)S(1)}, u32[]{:S(2)}, u32[]{:S(2)}) collective-permute-start(bf16[2,2048]{1,0:T(2,128)(2,1)S(1)} %get-tuple-element.39.refs_0_), channel_id=1, source_target_pairs={{0,10},{1,11},{2,8},{3,9},{4,14},{5,15},{6,12},{7,13},{8,2},{9,3},... | collective-permute-start | bytes 24584 | tf_op jit(solution)/shard_map/ppermute | solution.py:33
  10.6 3.1 %collective-permute-done.refs_1_ = bf16[2,2048]{1,0:T(2,128)(2,1)S(1)} collective-permute-done((bf16[2,2048]{1,0:T(2,128)(2,1)S(1)}, bf16[2,2048]{1,0:T(2,128)(2,1)S(1)}, u32[]{:S(2)}, u32[]{:S(2)}) %collective-permute-start) | collective-permute-done | bytes 8224 | tf_op jit(solution)/shard_map/ppermute | solution.py:33
  13.8 1.6 %collective-permute-start.1 = (bf16[4,2048]{1,0:T(4,128)(2,1)S(1)}, bf16[4,2048]{1,0:T(4,128)(2,1)S(1)}, u32[]{:S(2)}, u32[]{:S(2)}) collective-permute-start(bf16[4,2048]{1,0:T(4,128)(2,1)S(1)} %stack.2.refs_0_), channel_id=1, source_target_pairs={{0,2},{1,3},{2,0},{3,1},{4,6},{5,7},{6,4},{7,5},{8,10},{9,11},{10,... | collective-permute-start | bytes 49160 | tf_op jit(solution)/shard_map/ppermute | solution.py:23
  15.4 2.6 %collective-permute-start.2 = (bf16[4,2048]{1,0:T(4,128)(2,1)S(1)}, bf16[4,2048]{1,0:T(4,128)(2,1)S(1)}, u32[]{:S(2)}, u32[]{:S(2)}) collective-permute-start(bf16[4,2048]{1,0:T(4,128)(2,1)S(1)} %stack.2.refs_0_), channel_id=1, source_target_pairs={{0,4},{1,5},{2,6},{3,7},{4,0},{5,1},{6,2},{7,3},{8,12},{9,13},{10,... | collective-permute-start | bytes 49160 | tf_op jit(solution)/shard_map/ppermute | solution.py:23
  18.0 0.2 collective-permute-start.3
  18.2 0.8 %score.1 = (f32[16,256,256]{2,1,0:T(8,128)S(1)}, f32[16,256,128]{2,1,0:T(8,128)S(1)}) custom-call(bf16[256,2048]{1,0:T(8,128)(2,1)S(1)} %get-tuple-element.46.q_ref, bf16[256,2048]{1,0:T(8,128)(2,1)S(1)} %get-tuple-element.37.k_ref), custom_call_target="tpu_custom_call" | custom-call | tf_op jit(solution)/shard_map/score/pallas_call | solution.py:303
  19.0 1.2 %collective-permute-done.2.refs_2_ = bf16[4,2048]{1,0:T(4,128)(2,1)S(1)} collective-permute-done((bf16[4,2048]{1,0:T(4,128)(2,1)S(1)}, bf16[4,2048]{1,0:T(4,128)(2,1)S(1)}, u32[]{:S(2)}, u32[]{:S(2)}) %collective-permute-start.2) | collective-permute-done | bytes 16416 | tf_op jit(solution)/shard_map/ppermute | solution.py:23
  20.3 3.4 %collective-permute-done.3.refs_3_ = bf16[4,2048]{1,0:T(4,128)(2,1)S(1)} collective-permute-done((bf16[4,2048]{1,0:T(4,128)(2,1)S(1)}, bf16[4,2048]{1,0:T(4,128)(2,1)S(1)}, u32[]{:S(2)}, u32[]{:S(2)}) %collective-permute-start.3) | collective-permute-done | bytes 16416 | tf_op jit(solution)/shard_map/ppermute | solution.py:23
  23.6 0.5 collective-permute-start.7
  24.2 1.6 %collective-permute-start.12 = (bf16[192,1664]{1,0:T(8,128)(2,1)S(1)}, bf16[192,1664]{1,0:T(8,128)(2,1)S(1)}, u32[]{:S(2)}, u32[]{:S(2)}) collective-permute-start(bf16[192,1664]{1,0:T(8,128)(2,1)S(1)} %get-tuple-element.66), channel_id=1, source_target_pairs={{0,8},{8,0},{16,24},{24,16},{1,9},{9,1},{17,25},{25,17},{2,10},{10... | collective-permute-start | bytes 1916936 | tf_op jit(solution)/shard_map/ppermute | solution.py:23
  25.8 1.6 %collective-permute-done.4.k_ref.kp_ref = bf16[256,2048]{1,0:T(8,128)(2,1)S(1)} collective-permute-done((bf16[256,2048]{1,0:T(8,128)(2,1)}, bf16[256,2048]{1,0:T(8,128)(2,1)S(1)}, u32[]{:S(2)}, u32[]{:S(2)}) %collective-permute-start.4) | collective-permute-done | bytes 1048608 | tf_op jit(solution)/shard_map/ppermute | solution.py:23
  27.3 0.8 %pick.1 = bf16[64,2048]{1,0:T(8,128)(2,1)S(1)} custom-call(s32[16]{0:T(128)S(1)} %copy-done.1, bf16[256,2048]{1,0:T(8,128)(2,1)S(1)} %collective-permute-done.4.k_ref.kp_ref), custom_call_target="tpu_custom_call" | custom-call | tf_op jit(solution)/shard_map/pick/pallas_call | solution.py:303
  28.2 2.2 %collective-permute-start.5 = (bf16[64,2048]{1,0:T(8,128)(2,1)S(1)}, bf16[64,2048]{1,0:T(8,128)(2,1)S(1)}, u32[]{:S(2)}, u32[]{:S(2)}) collective-permute-start(bf16[64,2048]{1,0:T(8,128)(2,1)S(1)} %pick.1), channel_id=1, source_target_pairs={{0,16},{8,24},{16,0},{24,8},{1,17},{9,25},{17,1},{25,9},{2,18},{10... | collective-permute-start | bytes 786440 | tf_op jit(solution)/shard_map/ppermute | solution.py:23
  30.3 1.7 %other.2 = (bf16[8,256,256]{2,1,0:T(8,128)(2,1)S(1)}, f32[8,256,128]{2,1,0:T(8,128)S(1)}, f32[256,128]{1,0:T(8,128)S(1)}) custom-call(s32[16]{0:T(128)S(1)} %copy-done.1, bf16[256,2048]{1,0:T(8,128)(2,1)S(1)} %get-tuple-element.46.q_ref, f32[16,256,128]{2,1,0:T(8,128)S(1)} %get-tuple-element.42.own_top_ref, ...), custom_call_target="tpu_custom_call" | custom-call | tf_op jit(solution)/shard_map/other/pallas_call | solution.py:303
  32.0 0.9 %collective-permute-done.7.vm_ref = bf16[64,2048]{1,0:T(8,128)(2,1)S(1)} collective-permute-done((bf16[64,2048]{1,0:T(8,128)(2,1)S(1)}, bf16[64,2048]{1,0:T(8,128)(2,1)S(1)}, u32[]{:S(2)}, u32[]{:S(2)}) %collective-permute-start.7) | collective-permute-done | bytes 262176 | tf_op jit(solution)/shard_map/ppermute | solution.py:23
  32.9 2.1 %collective-permute-start.8 = (bf16[64,2048]{1,0:T(8,128)(2,1)S(1)}, bf16[64,2048]{1,0:T(8,128)(2,1)S(1)}, u32[]{:S(2)}, u32[]{:S(2)}) collective-permute-start(bf16[64,2048]{1,0:T(8,128)(2,1)S(1)} %collective-permute-done.7.vm_ref), channel_id=1, source_target_pairs={{0,16},{8,24},{16,0},{24,8},{1,17},{9,25},{17,1},{25,9},{2,18},{10... | collective-permute-start | bytes 786440 | tf_op jit(solution)/shard_map/ppermute | solution.py:23
  35.1 1.6 %collective-permute-start.11 = (bf16[192,384]{1,0:T(8,128)(2,1)S(1)}, bf16[192,384]{1,0:T(8,128)(2,1)S(1)}, u32[]{:S(2)}, u32[]{:S(2)}) collective-permute-start(bf16[192,384]{1,0:T(8,128)(2,1)S(1)} %get-tuple-element.65), channel_id=1, source_target_pairs={{0,8},{8,0},{16,24},{24,16},{1,9},{9,1},{17,25},{25,17},{2,10},{10... | collective-permute-start | bytes 442376 | tf_op jit(solution)/shard_map/ppermute | solution.py:23
  36.7 1.7 %other.3 = (bf16[8,256,256]{2,1,0:T(8,128)(2,1)S(1)}, f32[8,256,128]{2,1,0:T(8,128)S(1)}, f32[256,128]{1,0:T(8,128)S(1)}) custom-call(s32[16]{0:T(128)S(1)} %copy-done.1, bf16[256,2048]{1,0:T(8,128)(2,1)S(1)} %get-tuple-element.46.q_ref, f32[16,256,128]{2,1,0:T(8,128)S(1)} %get-tuple-element.42.own_top_ref, ...), custom_call_target="tpu_custom_call" | custom-call | tf_op jit(solution)/shard_map/other/pallas_call | solution.py:303
  38.4 1.8 %own.1 = (f32[256,2048]{1,0:T(8,128)S(1)}, f32[256,128]{1,0:T(8,128)S(1)}) custom-call(s32[16]{0:T(128)S(1)} %copy-done.1, f32[16,256,256]{2,1,0:T(8,128)S(1)} %get-tuple-element.38.scores_ref, f32[8,256,128]{2,1,0:T(8,128)S(1)} %get-tuple-element.44.top_a_ref, f32[8,256,128]{2,1,0:T(8,128)S(1)} %get-tuple-element.47.top_b_ref, ...), custom_call_target="tpu_custom_call" | custom-call | tf_op jit(solution)/shard_map/own/pallas_call | solution.py:303
  40.2 0.3 collective-permute-done.8.diagonal_v_ref
  40.5 3.5 %extra.1 = (f32[256,2048]{1,0:T(8,128)S(1)}, f32[256,128]{1,0:T(8,128)S(1)}) custom-call(s32[16]{0:T(128)S(1)} %copy-done.1, s32[16]{0:T(128)S(1)} %copy-done.3, bf16[256,2048]{1,0:T(8,128)(2,1)S(1)} %get-tuple-element.46.q_ref, f32[256,128]{1,0:T(8,128)S(1)} %get-tuple-element.49.own_total_ref, f32[256,128]{1,0:T(8,128)S(1)} %get-tuple-element.45.state_a_ref, ...), custom_call_target="tpu_custom_call" | custom-call | tf_op jit(solution)/shard_map/extra/pallas_call | solution.py:303
  44.2 0.3 broadcast_in_dim.3
  44.5 0.6 %base.1 = (f32[256,1792]{1,0:T(8,128)S(1)}, f32[256,1792]{1,0:T(8,128)S(1)}) custom-call(f32[256,2048]{1,0:T(8,128)S(1)} %get-tuple-element.58.sum_ref, f32[256,128]{1,0:T(8,128)S(1)} %get-tuple-element.59.share_ref, f32[256,2048]{1,0:T(8,128)S(1)} %get-tuple-element.60.own_ref), custom_call_target="tpu_custom_call" | custom-call | tf_op jit(solution)/shard_map/base/pallas_call | solution.py:303
  45.2 1.4 %collective-permute-done.12.vr_ref = bf16[192,1664]{1,0:T(8,128)(2,1)S(1)} collective-permute-done((bf16[192,1664]{1,0:T(8,128)(2,1)S(1)}, bf16[192,1664]{1,0:T(8,128)(2,1)S(1)}, u32[]{:S(2)}, u32[]{:S(2)}) %collective-permute-start.12) | collective-permute-done | bytes 639008 | tf_op jit(solution)/shard_map/ppermute | solution.py:23
  46.6 1.4 %finish.2.rest_0_ = bf16[256,2048]{1,0:T(8,128)(2,1)} custom-call(f32[256,1792]{1,0:T(8,128)S(1)} %get-tuple-element.61.base_ref, f32[256,1792]{1,0:T(8,128)S(1)} %get-tuple-element.62.spread_ref, f32[256,256]{1,0:T(8,128)S(1)} %multiply_add_fusion.late_base_ref, f32[256,256]{1,0:T(8,128)S(1)} %bitcast.6, ...), custom_call_target="tpu_custom_call" | custom-call | tf_op jit(solution)/shard_map/finish/pallas_call | solution.py:303
  48.0 0.9 %collective-permute-done.11.vr_ref = bf16[192,384]{1,0:T(8,128)(2,1)S(1)} collective-permute-done((bf16[192,384]{1,0:T(8,128)(2,1)S(1)}, bf16[192,384]{1,0:T(8,128)(2,1)S(1)}, u32[]{:S(2)}, u32[]{:S(2)}) %collective-permute-start.11) | collective-permute-done | bytes 147488 | tf_op jit(solution)/shard_map/ppermute | solution.py:23
  49.0 0.9 %finish.3 = bf16[256,2048]{1,0:T(8,128)(2,1)} custom-call(f32[256,1792]{1,0:T(8,128)S(1)} %get-tuple-element.61.base_ref, f32[256,1792]{1,0:T(8,128)S(1)} %get-tuple-element.62.spread_ref, f32[256,256]{1,0:T(8,128)S(1)} %multiply_add_fusion.late_base_ref, f32[256,256]{1,0:T(8,128)S(1)} %bitcast.7, ...), custom_call_target="tpu_custom_call", output_to_operand_aliasing={{}: (8, {})} | custom-call | tf_op jit(solution)/shard_map/finish/pallas_call | solution.py:303
  (20 shorter events, 0.3 us)
Async XLA Ops:
  0.0 27.3 %collective-permute-start.4 = (bf16[256,2048]{1,0:T(8,128)(2,1)}, bf16[256,2048]{1,0:T(8,128)(2,1)S(1)}, u32[]{:S(2)}, u32[]{:S(2)}) collective-permute-start(bf16[256,2048]{1,0:T(8,128)(2,1)} %k_hbm.1), channel_id=1, source_target_pairs={{0,8},{8,0},{16,24},{24,16},{1,9},{9,1},{17,25},{25,17},{2,10},{10... | collective-permute-start | bytes 3145736 | tf_op jit(solution)/shard_map/ppermute | solution.py:23
  2.9 0.7 %copy-start = (s32[16]{0:T(128)S(1)}, s32[16]{0:T(128)}, u32[]{:S(2)}) copy-start(s32[16]{0:T(128)} %middle_ref.11) | copy-start | bytes 196
  3.6 0.7 %copy-start.2 = (s32[16]{0:T(128)S(1)}, s32[16]{0:T(128)}, u32[]{:S(2)}) copy-start(s32[16]{0:T(128)} %coarse_ref.3) | copy-start | bytes 196
  4.3 23.1 %copy-start.1 = (s32[16]{0:T(128)S(1)}, s32[16]{0:T(128)}, u32[]{:S(2)}) copy-start(s32[16]{0:T(128)} %middle_ref.11) | copy-start | bytes 196
  7.5 16.7 %collective-permute-start.6 = (bf16[128,2048]{1,0:T(8,128)(2,1)S(1)}, bf16[128,2048]{1,0:T(8,128)(2,1)S(1)}, u32[]{:S(2)}, u32[]{:S(2)}) collective-permute-start(bf16[128,2048]{1,0:T(8,128)(2,1)S(1)} %get-tuple-element.51), channel_id=1, source_target_pairs={{0,16},{8,24},{16,0},{24,8},{1,17},{9,25},{17,1},{25,9},{2,18},{10... | collective-permute-start | bytes 1572872 | tf_op jit(solution)/shard_map/ppermute | solution.py:23
  9.1 4.7 %collective-permute-start = (bf16[2,2048]{1,0:T(2,128)(2,1)S(1)}, bf16[2,2048]{1,0:T(2,128)(2,1)S(1)}, u32[]{:S(2)}, u32[]{:S(2)}) collective-permute-start(bf16[2,2048]{1,0:T(2,128)(2,1)S(1)} %get-tuple-element.39.refs_0_), channel_id=1, source_target_pairs={{0,10},{1,11},{2,8},{3,9},{4,14},{5,15},{6,12},{7,13},{8,2},{9,3},... | collective-permute-start | bytes 24584 | tf_op jit(solution)/shard_map/ppermute | solution.py:33
  13.8 5.3 %collective-permute-start.1 = (bf16[4,2048]{1,0:T(4,128)(2,1)S(1)}, bf16[4,2048]{1,0:T(4,128)(2,1)S(1)}, u32[]{:S(2)}, u32[]{:S(2)}) collective-permute-start(bf16[4,2048]{1,0:T(4,128)(2,1)S(1)} %stack.2.refs_0_), channel_id=1, source_target_pairs={{0,2},{1,3},{2,0},{3,1},{4,6},{5,7},{6,4},{7,5},{8,10},{9,11},{10,... | collective-permute-start | bytes 49160 | tf_op jit(solution)/shard_map/ppermute | solution.py:23
  15.4 4.9 %collective-permute-start.2 = (bf16[4,2048]{1,0:T(4,128)(2,1)S(1)}, bf16[4,2048]{1,0:T(4,128)(2,1)S(1)}, u32[]{:S(2)}, u32[]{:S(2)}) collective-permute-start(bf16[4,2048]{1,0:T(4,128)(2,1)S(1)} %stack.2.refs_0_), channel_id=1, source_target_pairs={{0,4},{1,5},{2,6},{3,7},{4,0},{5,1},{6,2},{7,3},{8,12},{9,13},{10,... | collective-permute-start | bytes 49160 | tf_op jit(solution)/shard_map/ppermute | solution.py:23
  18.0 5.6 %collective-permute-start.3 = (bf16[4,2048]{1,0:T(4,128)(2,1)S(1)}, bf16[4,2048]{1,0:T(4,128)(2,1)S(1)}, u32[]{:S(2)}, u32[]{:S(2)}) collective-permute-start(bf16[4,2048]{1,0:T(4,128)(2,1)S(1)} %stack.2.refs_0_), channel_id=1, source_target_pairs={{0,6},{1,7},{2,4},{3,5},{4,2},{5,3},{6,0},{7,1},{8,14},{9,15},{10,... | collective-permute-start | bytes 49160 | tf_op jit(solution)/shard_map/ppermute | solution.py:23
  23.6 9.3 %collective-permute-start.7 = (bf16[64,2048]{1,0:T(8,128)(2,1)S(1)}, bf16[64,2048]{1,0:T(8,128)(2,1)S(1)}, u32[]{:S(2)}, u32[]{:S(2)}) collective-permute-start(bf16[64,2048]{1,0:T(8,128)(2,1)S(1)} %get-tuple-element.55), channel_id=1, source_target_pairs={{0,8},{8,0},{16,24},{24,16},{1,9},{9,1},{17,25},{25,17},{2,10},{10... | collective-permute-start | bytes 786440 | tf_op jit(solution)/shard_map/ppermute | solution.py:23
  24.1 10.9 %collective-permute-start.9 = (bf16[16,2048]{1,0:T(8,128)(2,1)S(1)}, bf16[16,2048]{1,0:T(8,128)(2,1)S(1)}, u32[]{:S(2)}, u32[]{:S(2)}) collective-permute-start(bf16[16,2048]{1,0:T(8,128)(2,1)S(1)} %stack.3), channel_id=1, source_target_pairs={{0,18},{1,19},{2,16},{3,17},{4,22},{5,23},{6,20},{7,21},{8,26},{9,... | collective-permute-start | bytes 196616 | tf_op jit(solution)/shard_map/ppermute | solution.py:33
  24.2 22.5 %collective-permute-start.12 = (bf16[192,1664]{1,0:T(8,128)(2,1)S(1)}, bf16[192,1664]{1,0:T(8,128)(2,1)S(1)}, u32[]{:S(2)}, u32[]{:S(2)}) collective-permute-start(bf16[192,1664]{1,0:T(8,128)(2,1)S(1)} %get-tuple-element.66), channel_id=1, source_target_pairs={{0,8},{8,0},{16,24},{24,16},{1,9},{9,1},{17,25},{25,17},{2,10},{10... | collective-permute-start | bytes 1916936 | tf_op jit(solution)/shard_map/ppermute | solution.py:23
  28.2 8.5 %collective-permute-start.5 = (bf16[64,2048]{1,0:T(8,128)(2,1)S(1)}, bf16[64,2048]{1,0:T(8,128)(2,1)S(1)}, u32[]{:S(2)}, u32[]{:S(2)}) collective-permute-start(bf16[64,2048]{1,0:T(8,128)(2,1)S(1)} %pick.1), channel_id=1, source_target_pairs={{0,16},{8,24},{16,0},{24,8},{1,17},{9,25},{17,1},{25,9},{2,18},{10... | collective-permute-start | bytes 786440 | tf_op jit(solution)/shard_map/ppermute | solution.py:23
  32.9 7.6 %collective-permute-start.8 = (bf16[64,2048]{1,0:T(8,128)(2,1)S(1)}, bf16[64,2048]{1,0:T(8,128)(2,1)S(1)}, u32[]{:S(2)}, u32[]{:S(2)}) collective-permute-start(bf16[64,2048]{1,0:T(8,128)(2,1)S(1)} %collective-permute-done.7.vm_ref), channel_id=1, source_target_pairs={{0,16},{8,24},{16,0},{24,8},{1,17},{9,25},{17,1},{25,9},{2,18},{10... | collective-permute-start | bytes 786440 | tf_op jit(solution)/shard_map/ppermute | solution.py:23
  35.0 5.2 %collective-permute-start.10 = (bf16[32,2048]{1,0:T(8,128)(2,1)S(1)}, bf16[32,2048]{1,0:T(8,128)(2,1)S(1)}, u32[]{:S(2)}, u32[]{:S(2)}) collective-permute-start(bf16[32,2048]{1,0:T(8,128)(2,1)S(1)} %constant_dynamic-update-slice_fusion.mine_ref), channel_id=1, source_target_pairs={{0,1},{1,0},{2,3},{3,2},{4,5},{5,4},{6,7},{7,6},{8,9},{9,8},{10,11... | collective-permute-start | bytes 393224 | tf_op jit(solution)/shard_map/ppermute | solution.py:23
  35.1 13.8 %collective-permute-start.11 = (bf16[192,384]{1,0:T(8,128)(2,1)S(1)}, bf16[192,384]{1,0:T(8,128)(2,1)S(1)}, u32[]{:S(2)}, u32[]{:S(2)}) collective-permute-start(bf16[192,384]{1,0:T(8,128)(2,1)S(1)} %get-tuple-element.65), channel_id=1, source_target_pairs={{0,8},{8,0},{16,24},{24,16},{1,9},{9,1},{17,25},{25,17},{2,10},{10... | collective-permute-start | bytes 442376 | tf_op jit(solution)/shard_map/ppermute | solution.py:23
  38.4 2.2 %copy-start.3 = (s32[16]{0:T(128)S(1)}, s32[16]{0:T(128)}, u32[]{:S(2)}) copy-start(s32[16]{0:T(128)} %coarse_ref.3) | copy-start | bytes 196

commit v22 on v20

--- a/solution.py
+++ b/solution.py
@@ -236,9 +236,11 @@
         values = jnp.concatenate([vm_ref[:, head_columns(head)], vr_ref[:, columns]], axis=0)
         result = base_ref[:, columns] + spread_ref[:, columns] * dot(other_ref[head % half], values)
         ready_ref[:, columns] = result.astype(jnp.bfloat16)
-        target = out_ref.at[:, head_columns(head)]
-        copies.append(pltpu.make_async_copy(ready_ref.at[:, columns], target, semaphores.at[place]))
-        copies[-1].start()
+        if (place + 1) % 2 == 0 or place + 1 == len(heads):
+            pair = slice(place // 2 * 2 * HEAD_FEATURES, (place + 1) * HEAD_FEATURES)
+            target = out_ref.at[:, heads[0] * HEAD_FEATURES + pair.start : heads[0] * HEAD_FEATURES + pair.stop]
+            copies.append(pltpu.make_async_copy(ready_ref.at[:, pair], target, semaphores.at[place]))
+            copies[-1].start()
     for copy in copies:
         copy.wait()
 

time: 50.2 us -> 50.2 us (level)
  no operation moved by 1% of the time
where the time goes in v22:
time: 50.2 us; the launch traced here: 50.1 us
  starting transfers between devices  18.5 us (37%)
  Pallas kernels  16.6 us (33%)
  waiting for transfers between devices  13 us (26%)
  local copies, waits for them, and re-layouts  1.78 us (4%)
    ppermute x11, starting transfers between devices, partner(): return lax.ppermute(value, axis, pairs)  16.9 us
    pallas_call x10, Pallas kernels, call(): pl.pallas_call(kernel, name=name, compiler_params=params, cost_estimate=c...  16.6 us
    ppermute x11, waiting for transfers between devices, partner(): return lax.ppermute(value, axis, pairs)  9.86 us
    ppermute x2, waiting for transfers between devices, partner_elsewhere(): return lax.ppermute(value, ('inner', 'outer'), pairs)  3.11 us
    ppermute x2, starting transfers between devices, partner_elsewhere(): return lax.ppermute(value, ('inner', 'outer'), pairs)  1.55 us
    unnamed x10, local copies, waits for them, and re-layouts  1.34 us
  transfers between devices with their start and end apart: 13, of which 7 were waited for; matrix products, arithmetic and copies ran while one was open for 1% of the time, Pallas kernels for 31%

profile of v22, /device:TPU:0, one launch (start us, length us, event | category | flops | bytes accessed | tf_op | source)
XLA Modules:
  0.0 50.1 jit_solution(13215499102957422179)
XLA Ops:
  0.0 2.9 %collective-permute-start.4 = (bf16[256,2048]{1,0:T(8,128)(2,1)}, bf16[256,2048]{1,0:T(8,128)(2,1)S(1)}, u32[]{:S(2)}, u32[]{:S(2)}) collective-permute-start(bf16[256,2048]{1,0:T(8,128)(2,1)} %k_hbm.1), channel_id=1, source_target_pairs={{0,8},{8,0},{16,24},{24,16},{1,9},{9,1},{17,25},{25,17},{2,10},{10... | collective-permute-start | bytes 3145736 | tf_op jit(solution)/shard_map/ppermute | solution.py:22
  2.9 0.7 %copy-done = s32[16]{0:T(128)S(1)} copy-done((s32[16]{0:T(128)S(1)}, s32[16]{0:T(128)}, u32[]{:S(2)}) %copy-start) | copy-done | bytes 88
  3.6 0.7 %copy-done.2 = s32[16]{0:T(128)S(1)} copy-done((s32[16]{0:T(128)S(1)}, s32[16]{0:T(128)}, u32[]{:S(2)}) %copy-start.2) | copy-done | bytes 88
  4.3 3.2 %prepare.1 = (bf16[256,2048]{1,0:T(8,128)(2,1)S(1)}, bf16[256,2048]{1,0:T(8,128)(2,1)S(1)}, bf16[256,2048]{1,0:T(8,128)(2,1)S(1)}, bf16[128,2048]{1,0:T(8,128)(2...) custom-call(s32[16]{0:T(128)S(1)} %copy-done, ...), custom_call_target="tpu_custom_call" | custom-call | tf_op jit(solution)/shard_map/prepare/pallas_call | solution.py:297
  7.5 1.6 %collective-permute-start.6 = (bf16[128,2048]{1,0:T(8,128)(2,1)S(1)}, bf16[128,2048]{1,0:T(8,128)(2,1)S(1)}, u32[]{:S(2)}, u32[]{:S(2)}) collective-permute-start(bf16[128,2048]{1,0:T(8,128)(2,1)S(1)} %get-tuple-element.51), channel_id=1, source_target_pairs={{0,16},{8,24},{16,0},{24,8},{1,17},{9,25},{17,1},{25,9},{2,18},{10... | collective-permute-start | bytes 1572872 | tf_op jit(solution)/shard_map/ppermute | solution.py:22
  9.1 1.5 %collective-permute-start = (bf16[2,2048]{1,0:T(2,128)(2,1)S(1)}, bf16[2,2048]{1,0:T(2,128)(2,1)S(1)}, u32[]{:S(2)}, u32[]{:S(2)}) collective-permute-start(bf16[2,2048]{1,0:T(2,128)(2,1)S(1)} %get-tuple-element.39.refs_0_), channel_id=1, source_target_pairs={{0,10},{1,11},{2,8},{3,9},{4,14},{5,15},{6,12},{7,13},{8,2},{9,3},... | collective-permute-start | bytes 24584 | tf_op jit(solution)/shard_map/ppermute | solution.py:32
  10.6 3.1 %collective-permute-done.refs_1_ = bf16[2,2048]{1,0:T(2,128)(2,1)S(1)} collective-permute-done((bf16[2,2048]{1,0:T(2,128)(2,1)S(1)}, bf16[2,2048]{1,0:T(2,128)(2,1)S(1)}, u32[]{:S(2)}, u32[]{:S(2)}) %collective-permute-start) | collective-permute-done | bytes 8224 | tf_op jit(solution)/shard_map/ppermute | solution.py:32
  13.8 1.6 %collective-permute-start.1 = (bf16[4,2048]{1,0:T(4,128)(2,1)S(1)}, bf16[4,2048]{1,0:T(4,128)(2,1)S(1)}, u32[]{:S(2)}, u32[]{:S(2)}) collective-permute-start(bf16[4,2048]{1,0:T(4,128)(2,1)S(1)} %stack.2.refs_0_), channel_id=1, source_target_pairs={{0,2},{1,3},{2,0},{3,1},{4,6},{5,7},{6,4},{7,5},{8,10},{9,11},{10,... | collective-permute-start | bytes 49160 | tf_op jit(solution)/shard_map/ppermute | solution.py:22
  15.4 2.6 %collective-permute-start.2 = (bf16[4,2048]{1,0:T(4,128)(2,1)S(1)}, bf16[4,2048]{1,0:T(4,128)(2,1)S(1)}, u32[]{:S(2)}, u32[]{:S(2)}) collective-permute-start(bf16[4,2048]{1,0:T(4,128)(2,1)S(1)} %stack.2.refs_0_), channel_id=1, source_target_pairs={{0,4},{1,5},{2,6},{3,7},{4,0},{5,1},{6,2},{7,3},{8,12},{9,13},{10,... | collective-permute-start | bytes 49160 | tf_op jit(solution)/shard_map/ppermute | solution.py:22
  18.0 0.2 collective-permute-start.3
  18.2 0.8 %score.1 = (f32[16,256,256]{2,1,0:T(8,128)S(1)}, f32[16,256,128]{2,1,0:T(8,128)S(1)}) custom-call(bf16[256,2048]{1,0:T(8,128)(2,1)S(1)} %get-tuple-element.46.q_ref, bf16[256,2048]{1,0:T(8,128)(2,1)S(1)} %get-tuple-element.37.k_ref), custom_call_target="tpu_custom_call" | custom-call | tf_op jit(solution)/shard_map/score/pallas_call | solution.py:297
  19.0 1.2 %collective-permute-done.2.refs_2_ = bf16[4,2048]{1,0:T(4,128)(2,1)S(1)} collective-permute-done((bf16[4,2048]{1,0:T(4,128)(2,1)S(1)}, bf16[4,2048]{1,0:T(4,128)(2,1)S(1)}, u32[]{:S(2)}, u32[]{:S(2)}) %collective-permute-start.2) | collective-permute-done | bytes 16416 | tf_op jit(solution)/shard_map/ppermute | solution.py:22
  20.3 3.4 %collective-permute-done.3.refs_3_ = bf16[4,2048]{1,0:T(4,128)(2,1)S(1)} collective-permute-done((bf16[4,2048]{1,0:T(4,128)(2,1)S(1)}, bf16[4,2048]{1,0:T(4,128)(2,1)S(1)}, u32[]{:S(2)}, u32[]{:S(2)}) %collective-permute-start.3) | collective-permute-done | bytes 16416 | tf_op jit(solution)/shard_map/ppermute | solution.py:22
  23.6 0.5 collective-permute-start.7
  24.2 1.6 %collective-permute-start.12 = (bf16[192,1792]{1,0:T(8,128)(2,1)S(1)}, bf16[192,1792]{1,0:T(8,128)(2,1)S(1)}, u32[]{:S(2)}, u32[]{:S(2)}) collective-permute-start(bf16[192,1792]{1,0:T(8,128)(2,1)S(1)} %get-tuple-element.66), channel_id=1, source_target_pairs={{0,8},{8,0},{16,24},{24,16},{1,9},{9,1},{17,25},{25,17},{2,10},{10... | collective-permute-start | bytes 2064392 | tf_op jit(solution)/shard_map/ppermute | solution.py:22
  25.8 1.6 %collective-permute-done.4.k_ref.kp_ref = bf16[256,2048]{1,0:T(8,128)(2,1)S(1)} collective-permute-done((bf16[256,2048]{1,0:T(8,128)(2,1)}, bf16[256,2048]{1,0:T(8,128)(2,1)S(1)}, u32[]{:S(2)}, u32[]{:S(2)}) %collective-permute-start.4) | collective-permute-done | bytes 1048608 | tf_op jit(solution)/shard_map/ppermute | solution.py:22
  27.3 0.8 %pick.1 = bf16[64,2048]{1,0:T(8,128)(2,1)S(1)} custom-call(s32[16]{0:T(128)S(1)} %copy-done.1, bf16[256,2048]{1,0:T(8,128)(2,1)S(1)} %collective-permute-done.4.k_ref.kp_ref), custom_call_target="tpu_custom_call" | custom-call | tf_op jit(solution)/shard_map/pick/pallas_call | solution.py:297
  28.2 2.2 %collective-permute-start.5 = (bf16[64,2048]{1,0:T(8,128)(2,1)S(1)}, bf16[64,2048]{1,0:T(8,128)(2,1)S(1)}, u32[]{:S(2)}, u32[]{:S(2)}) collective-permute-start(bf16[64,2048]{1,0:T(8,128)(2,1)S(1)} %pick.1), channel_id=1, source_target_pairs={{0,16},{8,24},{16,0},{24,8},{1,17},{9,25},{17,1},{25,9},{2,18},{10... | collective-permute-start | bytes 786440 | tf_op jit(solution)/shard_map/ppermute | solution.py:22
  30.3 1.7 %other.2 = (bf16[8,256,256]{2,1,0:T(8,128)(2,1)S(1)}, f32[8,256,128]{2,1,0:T(8,128)S(1)}, f32[256,128]{1,0:T(8,128)S(1)}) custom-call(s32[16]{0:T(128)S(1)} %copy-done.1, bf16[256,2048]{1,0:T(8,128)(2,1)S(1)} %get-tuple-element.46.q_ref, f32[16,256,128]{2,1,0:T(8,128)S(1)} %get-tuple-element.42.own_top_ref, ...), custom_call_target="tpu_custom_call" | custom-call | tf_op jit(solution)/shard_map/other/pallas_call | solution.py:297
  32.0 0.9 %collective-permute-done.7.vm_ref = bf16[64,2048]{1,0:T(8,128)(2,1)S(1)} collective-permute-done((bf16[64,2048]{1,0:T(8,128)(2,1)S(1)}, bf16[64,2048]{1,0:T(8,128)(2,1)S(1)}, u32[]{:S(2)}, u32[]{:S(2)}) %collective-permute-start.7) | collective-permute-done | bytes 262176 | tf_op jit(solution)/shard_map/ppermute | solution.py:22
  32.9 2.1 %collective-permute-start.8 = (bf16[64,2048]{1,0:T(8,128)(2,1)S(1)}, bf16[64,2048]{1,0:T(8,128)(2,1)S(1)}, u32[]{:S(2)}, u32[]{:S(2)}) collective-permute-start(bf16[64,2048]{1,0:T(8,128)(2,1)S(1)} %collective-permute-done.7.vm_ref), channel_id=1, source_target_pairs={{0,16},{8,24},{16,0},{24,8},{1,17},{9,25},{17,1},{25,9},{2,18},{10... | collective-permute-start | bytes 786440 | tf_op jit(solution)/shard_map/ppermute | solution.py:22
  35.1 1.6 %collective-permute-start.11 = (bf16[192,256]{1,0:T(8,128)(2,1)S(1)}, bf16[192,256]{1,0:T(8,128)(2,1)S(1)}, u32[]{:S(2)}, u32[]{:S(2)}) collective-permute-start(bf16[192,256]{1,0:T(8,128)(2,1)S(1)} %get-tuple-element.63), channel_id=1, source_target_pairs={{0,8},{8,0},{16,24},{24,16},{1,9},{9,1},{17,25},{25,17},{2,10},{10... | collective-permute-start | bytes 294920 | tf_op jit(solution)/shard_map/ppermute | solution.py:22
  36.7 1.7 %other.3 = (bf16[8,256,256]{2,1,0:T(8,128)(2,1)S(1)}, f32[8,256,128]{2,1,0:T(8,128)S(1)}, f32[256,128]{1,0:T(8,128)S(1)}) custom-call(s32[16]{0:T(128)S(1)} %copy-done.1, bf16[256,2048]{1,0:T(8,128)(2,1)S(1)} %get-tuple-element.46.q_ref, f32[16,256,128]{2,1,0:T(8,128)S(1)} %get-tuple-element.42.own_top_ref, ...), custom_call_target="tpu_custom_call" | custom-call | tf_op jit(solution)/shard_map/other/pallas_call | solution.py:297
  38.4 1.8 %own.1 = (f32[256,2048]{1,0:T(8,128)S(1)}, f32[256,128]{1,0:T(8,128)S(1)}) custom-call(s32[16]{0:T(128)S(1)} %copy-done.1, f32[16,256,256]{2,1,0:T(8,128)S(1)} %get-tuple-element.38.scores_ref, f32[8,256,128]{2,1,0:T(8,128)S(1)} %get-tuple-element.44.top_a_ref, f32[8,256,128]{2,1,0:T(8,128)S(1)} %get-tuple-element.47.top_b_ref, ...), custom_call_target="tpu_custom_call" | custom-call | tf_op jit(solution)/shard_map/own/pallas_call | solution.py:297
  40.2 0.3 collective-permute-done.8.diagonal_v_ref
  40.5 3.5 %extra.1 = (f32[256,2048]{1,0:T(8,128)S(1)}, f32[256,128]{1,0:T(8,128)S(1)}) custom-call(s32[16]{0:T(128)S(1)} %copy-done.1, s32[16]{0:T(128)S(1)} %copy-done.3, bf16[256,2048]{1,0:T(8,128)(2,1)S(1)} %get-tuple-element.46.q_ref, f32[256,128]{1,0:T(8,128)S(1)} %get-tuple-element.49.own_total_ref, f32[256,128]{1,0:T(8,128)S(1)} %get-tuple-element.45.state_a_ref, ...), custom_call_target="tpu_custom_call" | custom-call | tf_op jit(solution)/shard_map/extra/pallas_call | solution.py:297
  44.0 0.1 slice.10
  44.1 0.3 broadcast_in_dim.3
  44.6 0.6 %base.1 = (f32[256,1792]{1,0:T(8,128)S(1)}, f32[256,1792]{1,0:T(8,128)S(1)}) custom-call(f32[256,2048]{1,0:T(8,128)S(1)} %get-tuple-element.58.sum_ref, f32[256,128]{1,0:T(8,128)S(1)} %get-tuple-element.59.share_ref, f32[256,2048]{1,0:T(8,128)S(1)} %get-tuple-element.60.own_ref), custom_call_target="tpu_custom_call" | custom-call | tf_op jit(solution)/shard_map/base/pallas_call | solution.py:297
  45.2 2.5 %collective-permute-done.12.vr_ref = bf16[192,1792]{1,0:T(8,128)(2,1)S(1)} collective-permute-done((bf16[192,1792]{1,0:T(8,128)(2,1)S(1)}, bf16[192,1792]{1,0:T(8,128)(2,1)S(1)}, u32[]{:S(2)}, u32[]{:S(2)}) %collective-permute-start.12) | collective-permute-done | bytes 688160 | tf_op jit(solution)/shard_map/ppermute | solution.py:22
  47.7 1.5 %finish.2.rest_0_ = bf16[256,2048]{1,0:T(8,128)(2,1)} custom-call(f32[256,1792]{1,0:T(8,128)S(1)} %get-tuple-element.64.base_ref, f32[256,1792]{1,0:T(8,128)S(1)} %get-tuple-element.65.spread_ref, bf16[8,256,256]{2,1,0:T(8,128)(2,1)S(1)} %get-tuple-element.61.other_a_ref, bf16[8,256,256]{2,1,0:T(8,128)(2,1)S(1)} %get-tuple-element.62.other_b_ref, ...), custom_call_target="tpu_custom_call" | custom-call | tf_op jit(solution)/shard_map/finish/pallas_call | solution.py:297
  49.2 0.9 %finish.3 = bf16[256,2048]{1,0:T(8,128)(2,1)} custom-call(f32[256,256]{1,0:T(8,128)S(1)} %multiply_add_fusion.base_ref, f32[256,256]{1,0:T(8,128)S(1)} %bitcast.6, bf16[8,256,256]{2,1,0:T(8,128)(2,1)S(1)} %get-tuple-element.61.other_a_ref, bf16[8,256,256]{2,1,0:T(8,128)(2,1)S(1)} %get-tuple-element.62.other_b_ref, ...), custom_call_target="tpu_custom_call", output_to_operand_aliasing={{}: (6, {})} | custom-call | tf_op jit(solution)/shard_map/finish/pallas_call | solution.py:297
  (20 shorter events, 0.2 us)
Async XLA Ops:
  0.0 27.3 %collective-permute-start.4 = (bf16[256,2048]{1,0:T(8,128)(2,1)}, bf16[256,2048]{1,0:T(8,128)(2,1)S(1)}, u32[]{:S(2)}, u32[]{:S(2)}) collective-permute-start(bf16[256,2048]{1,0:T(8,128)(2,1)} %k_hbm.1), channel_id=1, source_target_pairs={{0,8},{8,0},{16,24},{24,16},{1,9},{9,1},{17,25},{25,17},{2,10},{10... | collective-permute-start | bytes 3145736 | tf_op jit(solution)/shard_map/ppermute | solution.py:22
  2.9 0.7 %copy-start = (s32[16]{0:T(128)S(1)}, s32[16]{0:T(128)}, u32[]{:S(2)}) copy-start(s32[16]{0:T(128)} %middle_ref.11) | copy-start | bytes 196
  3.6 0.7 %copy-start.2 = (s32[16]{0:T(128)S(1)}, s32[16]{0:T(128)}, u32[]{:S(2)}) copy-start(s32[16]{0:T(128)} %coarse_ref.3) | copy-start | bytes 196
  4.3 23.1 %copy-start.1 = (s32[16]{0:T(128)S(1)}, s32[16]{0:T(128)}, u32[]{:S(2)}) copy-start(s32[16]{0:T(128)} %middle_ref.11) | copy-start | bytes 196
  7.5 16.7 %collective-permute-start.6 = (bf16[128,2048]{1,0:T(8,128)(2,1)S(1)}, bf16[128,2048]{1,0:T(8,128)(2,1)S(1)}, u32[]{:S(2)}, u32[]{:S(2)}) collective-permute-start(bf16[128,2048]{1,0:T(8,128)(2,1)S(1)} %get-tuple-element.51), channel_id=1, source_target_pairs={{0,16},{8,24},{16,0},{24,8},{1,17},{9,25},{17,1},{25,9},{2,18},{10... | collective-permute-start | bytes 1572872 | tf_op jit(solution)/shard_map/ppermute | solution.py:22
  9.1 4.7 %collective-permute-start = (bf16[2,2048]{1,0:T(2,128)(2,1)S(1)}, bf16[2,2048]{1,0:T(2,128)(2,1)S(1)}, u32[]{:S(2)}, u32[]{:S(2)}) collective-permute-start(bf16[2,2048]{1,0:T(2,128)(2,1)S(1)} %get-tuple-element.39.refs_0_), channel_id=1, source_target_pairs={{0,10},{1,11},{2,8},{3,9},{4,14},{5,15},{6,12},{7,13},{8,2},{9,3},... | collective-permute-start | bytes 24584 | tf_op jit(solution)/shard_map/ppermute | solution.py:32
  13.8 5.3 %collective-permute-start.1 = (bf16[4,2048]{1,0:T(4,128)(2,1)S(1)}, bf16[4,2048]{1,0:T(4,128)(2,1)S(1)}, u32[]{:S(2)}, u32[]{:S(2)}) collective-permute-start(bf16[4,2048]{1,0:T(4,128)(2,1)S(1)} %stack.2.refs_0_), channel_id=1, source_target_pairs={{0,2},{1,3},{2,0},{3,1},{4,6},{5,7},{6,4},{7,5},{8,10},{9,11},{10,... | collective-permute-start | bytes 49160 | tf_op jit(solution)/shard_map/ppermute | solution.py:22
  15.4 4.9 %collective-permute-start.2 = (bf16[4,2048]{1,0:T(4,128)(2,1)S(1)}, bf16[4,2048]{1,0:T(4,128)(2,1)S(1)}, u32[]{:S(2)}, u32[]{:S(2)}) collective-permute-start(bf16[4,2048]{1,0:T(4,128)(2,1)S(1)} %stack.2.refs_0_), channel_id=1, source_target_pairs={{0,4},{1,5},{2,6},{3,7},{4,0},{5,1},{6,2},{7,3},{8,12},{9,13},{10,... | collective-permute-start | bytes 49160 | tf_op jit(solution)/shard_map/ppermute | solution.py:22
  18.0 5.6 %collective-permute-start.3 = (bf16[4,2048]{1,0:T(4,128)(2,1)S(1)}, bf16[4,2048]{1,0:T(4,128)(2,1)S(1)}, u32[]{:S(2)}, u32[]{:S(2)}) collective-permute-start(bf16[4,2048]{1,0:T(4,128)(2,1)S(1)} %stack.2.refs_0_), channel_id=1, source_target_pairs={{0,6},{1,7},{2,4},{3,5},{4,2},{5,3},{6,0},{7,1},{8,14},{9,15},{10,... | collective-permute-start | bytes 49160 | tf_op jit(solution)/shard_map/ppermute | solution.py:22
  23.6 9.3 %collective-permute-start.7 = (bf16[64,2048]{1,0:T(8,128)(2,1)S(1)}, bf16[64,2048]{1,0:T(8,128)(2,1)S(1)}, u32[]{:S(2)}, u32[]{:S(2)}) collective-permute-start(bf16[64,2048]{1,0:T(8,128)(2,1)S(1)} %get-tuple-element.55), channel_id=1, source_target_pairs={{0,8},{8,0},{16,24},{24,16},{1,9},{9,1},{17,25},{25,17},{2,10},{10... | collective-permute-start | bytes 786440 | tf_op jit(solution)/shard_map/ppermute | solution.py:22
  24.1 10.9 %collective-permute-start.9 = (bf16[16,2048]{1,0:T(8,128)(2,1)S(1)}, bf16[16,2048]{1,0:T(8,128)(2,1)S(1)}, u32[]{:S(2)}, u32[]{:S(2)}) collective-permute-start(bf16[16,2048]{1,0:T(8,128)(2,1)S(1)} %stack.3), channel_id=1, source_target_pairs={{0,18},{1,19},{2,16},{3,17},{4,22},{5,23},{6,20},{7,21},{8,26},{9,... | collective-permute-start | bytes 196616 | tf_op jit(solution)/shard_map/ppermute | solution.py:32
  24.2 23.5 %collective-permute-start.12 = (bf16[192,1792]{1,0:T(8,128)(2,1)S(1)}, bf16[192,1792]{1,0:T(8,128)(2,1)S(1)}, u32[]{:S(2)}, u32[]{:S(2)}) collective-permute-start(bf16[192,1792]{1,0:T(8,128)(2,1)S(1)} %get-tuple-element.66), channel_id=1, source_target_pairs={{0,8},{8,0},{16,24},{24,16},{1,9},{9,1},{17,25},{25,17},{2,10},{10... | collective-permute-start | bytes 2064392 | tf_op jit(solution)/shard_map/ppermute | solution.py:22
  28.2 8.5 %collective-permute-start.5 = (bf16[64,2048]{1,0:T(8,128)(2,1)S(1)}, bf16[64,2048]{1,0:T(8,128)(2,1)S(1)}, u32[]{:S(2)}, u32[]{:S(2)}) collective-permute-start(bf16[64,2048]{1,0:T(8,128)(2,1)S(1)} %pick.1), channel_id=1, source_target_pairs={{0,16},{8,24},{16,0},{24,8},{1,17},{9,25},{17,1},{25,9},{2,18},{10... | collective-permute-start | bytes 786440 | tf_op jit(solution)/shard_map/ppermute | solution.py:22
  32.9 7.6 %collective-permute-start.8 = (bf16[64,2048]{1,0:T(8,128)(2,1)S(1)}, bf16[64,2048]{1,0:T(8,128)(2,1)S(1)}, u32[]{:S(2)}, u32[]{:S(2)}) collective-permute-start(bf16[64,2048]{1,0:T(8,128)(2,1)S(1)} %collective-permute-done.7.vm_ref), channel_id=1, source_target_pairs={{0,16},{8,24},{16,0},{24,8},{1,17},{9,25},{17,1},{25,9},{2,18},{10... | collective-permute-start | bytes 786440 | tf_op jit(solution)/shard_map/ppermute | solution.py:22
  35.0 5.2 %collective-permute-start.10 = (bf16[32,2048]{1,0:T(8,128)(2,1)S(1)}, bf16[32,2048]{1,0:T(8,128)(2,1)S(1)}, u32[]{:S(2)}, u32[]{:S(2)}) collective-permute-start(bf16[32,2048]{1,0:T(8,128)(2,1)S(1)} %constant_dynamic-update-slice_fusion.mine_ref), channel_id=1, source_target_pairs={{0,1},{1,0},{2,3},{3,2},{4,5},{5,4},{6,7},{7,6},{8,9},{9,8},{10,11... | collective-permute-start | bytes 393224 | tf_op jit(solution)/shard_map/ppermute | solution.py:22
  35.1 14.1 %collective-permute-start.11 = (bf16[192,256]{1,0:T(8,128)(2,1)S(1)}, bf16[192,256]{1,0:T(8,128)(2,1)S(1)}, u32[]{:S(2)}, u32[]{:S(2)}) collective-permute-start(bf16[192,256]{1,0:T(8,128)(2,1)S(1)} %get-tuple-element.63), channel_id=1, source_target_pairs={{0,8},{8,0},{16,24},{24,16},{1,9},{9,1},{17,25},{25,17},{2,10},{10... | collective-permute-start | bytes 294920 | tf_op jit(solution)/shard_map/ppermute | solution.py:22
  38.4 2.2 %copy-start.3 = (s32[16]{0:T(128)S(1)}, s32[16]{0:T(128)}, u32[]{:S(2)}) copy-start(s32[16]{0:T(128)} %coarse_ref.3) | copy-start | bytes 196

commit v23 on v21

--- a/solution.py
+++ b/solution.py
@@ -244,9 +244,11 @@
             late = head_columns(head - LATE)
             result = late_base_ref[:, late] + late_spread_ref[:, late] * result
         ready_ref[:, columns] = result.astype(jnp.bfloat16)
-        target = out_ref.at[:, head_columns(head)]
-        copies.append(pltpu.make_async_copy(ready_ref.at[:, columns], target, semaphores.at[place]))
-        copies[-1].start()
+        if (place + 1) % 2 == 0 or place + 1 == len(heads):
+            pair = slice(place // 2 * 2 * HEAD_FEATURES, (place + 1) * HEAD_FEATURES)
+            target = out_ref.at[:, heads[0] * HEAD_FEATURES + pair.start : heads[0] * HEAD_FEATURES + pair.stop]
+            copies.append(pltpu.make_async_copy(ready_ref.at[:, pair], target, semaphores.at[place]))
+            copies[-1].start()
     for copy in copies:
         copy.wait()
 

time: 50 us -> 50.1 us (level)
  no operation moved by 1% of the time
where the time goes in v23:
time: 50.1 us; the launch traced here: 49.9 us
  starting transfers between devices  18.5 us (37%)
  Pallas kernels  16.6 us (33%)
  waiting for transfers between devices  12.8 us (26%)
  local copies, waits for them, and re-layouts  1.78 us (4%)
    ppermute x11, starting transfers between devices, partner(): return lax.ppermute(value, axis, pairs)  16.9 us
    pallas_call x10, Pallas kernels, call(): pl.pallas_call(kernel, name=name, compiler_params=params, cost_estimate=c...  16.6 us
    ppermute x11, waiting for transfers between devices, partner(): return lax.ppermute(value, axis, pairs)  9.7 us
    ppermute x2, waiting for transfers between devices, partner_elsewhere(): return lax.ppermute(value, ('inner', 'outer'), pairs)  3.11 us
    ppermute x2, starting transfers between devices, partner_elsewhere(): return lax.ppermute(value, ('inner', 'outer'), pairs)  1.55 us
    unnamed x10, local copies, waits for them, and re-layouts  1.34 us
  transfers between devices with their start and end apart: 13, of which 8 were waited for; matrix products, arithmetic and copies ran while one was open for 1% of the time, Pallas kernels for 31%

profile of v23, /device:TPU:0, one launch (start us, length us, event | category | flops | bytes accessed | tf_op | source)
XLA Modules:
  0.0 49.9 jit_solution(17454024519082871902)
XLA Ops:
  0.0 2.9 %collective-permute-start.4 = (bf16[256,2048]{1,0:T(8,128)(2,1)}, bf16[256,2048]{1,0:T(8,128)(2,1)S(1)}, u32[]{:S(2)}, u32[]{:S(2)}) collective-permute-start(bf16[256,2048]{1,0:T(8,128)(2,1)} %k_hbm.1), channel_id=1, source_target_pairs={{0,8},{8,0},{16,24},{24,16},{1,9},{9,1},{17,25},{25,17},{2,10},{10... | collective-permute-start | bytes 3145736 | tf_op jit(solution)/shard_map/ppermute | solution.py:23
  2.9 0.7 %copy-done = s32[16]{0:T(128)S(1)} copy-done((s32[16]{0:T(128)S(1)}, s32[16]{0:T(128)}, u32[]{:S(2)}) %copy-start) | copy-done | bytes 88
  3.6 0.7 %copy-done.2 = s32[16]{0:T(128)S(1)} copy-done((s32[16]{0:T(128)S(1)}, s32[16]{0:T(128)}, u32[]{:S(2)}) %copy-start.2) | copy-done | bytes 88
  4.3 3.2 %prepare.1 = (bf16[256,2048]{1,0:T(8,128)(2,1)S(1)}, bf16[256,2048]{1,0:T(8,128)(2,1)S(1)}, bf16[256,2048]{1,0:T(8,128)(2,1)S(1)}, bf16[128,2048]{1,0:T(8,128)(2...) custom-call(s32[16]{0:T(128)S(1)} %copy-done, ...), custom_call_target="tpu_custom_call" | custom-call | tf_op jit(solution)/shard_map/prepare/pallas_call | solution.py:305
  7.5 1.6 %collective-permute-start.6 = (bf16[128,2048]{1,0:T(8,128)(2,1)S(1)}, bf16[128,2048]{1,0:T(8,128)(2,1)S(1)}, u32[]{:S(2)}, u32[]{:S(2)}) collective-permute-start(bf16[128,2048]{1,0:T(8,128)(2,1)S(1)} %get-tuple-element.51), channel_id=1, source_target_pairs={{0,16},{8,24},{16,0},{24,8},{1,17},{9,25},{17,1},{25,9},{2,18},{10... | collective-permute-start | bytes 1572872 | tf_op jit(solution)/shard_map/ppermute | solution.py:23
  9.1 1.5 %collective-permute-start = (bf16[2,2048]{1,0:T(2,128)(2,1)S(1)}, bf16[2,2048]{1,0:T(2,128)(2,1)S(1)}, u32[]{:S(2)}, u32[]{:S(2)}) collective-permute-start(bf16[2,2048]{1,0:T(2,128)(2,1)S(1)} %get-tuple-element.39.refs_0_), channel_id=1, source_target_pairs={{0,10},{1,11},{2,8},{3,9},{4,14},{5,15},{6,12},{7,13},{8,2},{9,3},... | collective-permute-start | bytes 24584 | tf_op jit(solution)/shard_map/ppermute | solution.py:33
  10.6 3.1 %collective-permute-done.refs_1_ = bf16[2,2048]{1,0:T(2,128)(2,1)S(1)} collective-permute-done((bf16[2,2048]{1,0:T(2,128)(2,1)S(1)}, bf16[2,2048]{1,0:T(2,128)(2,1)S(1)}, u32[]{:S(2)}, u32[]{:S(2)}) %collective-permute-start) | collective-permute-done | bytes 8224 | tf_op jit(solution)/shard_map/ppermute | solution.py:33
  13.8 1.6 %collective-permute-start.1 = (bf16[4,2048]{1,0:T(4,128)(2,1)S(1)}, bf16[4,2048]{1,0:T(4,128)(2,1)S(1)}, u32[]{:S(2)}, u32[]{:S(2)}) collective-permute-start(bf16[4,2048]{1,0:T(4,128)(2,1)S(1)} %stack.2.refs_0_), channel_id=1, source_target_pairs={{0,2},{1,3},{2,0},{3,1},{4,6},{5,7},{6,4},{7,5},{8,10},{9,11},{10,... | collective-permute-start | bytes 49160 | tf_op jit(solution)/shard_map/ppermute | solution.py:23
  15.4 2.6 %collective-permute-start.2 = (bf16[4,2048]{1,0:T(4,128)(2,1)S(1)}, bf16[4,2048]{1,0:T(4,128)(2,1)S(1)}, u32[]{:S(2)}, u32[]{:S(2)}) collective-permute-start(bf16[4,2048]{1,0:T(4,128)(2,1)S(1)} %stack.2.refs_0_), channel_id=1, source_target_pairs={{0,4},{1,5},{2,6},{3,7},{4,0},{5,1},{6,2},{7,3},{8,12},{9,13},{10,... | collective-permute-start | bytes 49160 | tf_op jit(solution)/shard_map/ppermute | solution.py:23
  18.0 0.2 collective-permute-start.3
  18.2 0.8 %score.1 = (f32[16,256,256]{2,1,0:T(8,128)S(1)}, f32[16,256,128]{2,1,0:T(8,128)S(1)}) custom-call(bf16[256,2048]{1,0:T(8,128)(2,1)S(1)} %get-tuple-element.46.q_ref, bf16[256,2048]{1,0:T(8,128)(2,1)S(1)} %get-tuple-element.37.k_ref), custom_call_target="tpu_custom_call" | custom-call | tf_op jit(solution)/shard_map/score/pallas_call | solution.py:305
  19.0 1.2 %collective-permute-done.2.refs_2_ = bf16[4,2048]{1,0:T(4,128)(2,1)S(1)} collective-permute-done((bf16[4,2048]{1,0:T(4,128)(2,1)S(1)}, bf16[4,2048]{1,0:T(4,128)(2,1)S(1)}, u32[]{:S(2)}, u32[]{:S(2)}) %collective-permute-start.2) | collective-permute-done | bytes 16416 | tf_op jit(solution)/shard_map/ppermute | solution.py:23
  20.3 3.4 %collective-permute-done.3.refs_3_ = bf16[4,2048]{1,0:T(4,128)(2,1)S(1)} collective-permute-done((bf16[4,2048]{1,0:T(4,128)(2,1)S(1)}, bf16[4,2048]{1,0:T(4,128)(2,1)S(1)}, u32[]{:S(2)}, u32[]{:S(2)}) %collective-permute-start.3) | collective-permute-done | bytes 16416 | tf_op jit(solution)/shard_map/ppermute | solution.py:23
  23.6 0.5 collective-permute-start.7
  24.2 1.6 %collective-permute-start.12 = (bf16[192,1664]{1,0:T(8,128)(2,1)S(1)}, bf16[192,1664]{1,0:T(8,128)(2,1)S(1)}, u32[]{:S(2)}, u32[]{:S(2)}) collective-permute-start(bf16[192,1664]{1,0:T(8,128)(2,1)S(1)} %get-tuple-element.66), channel_id=1, source_target_pairs={{0,8},{8,0},{16,24},{24,16},{1,9},{9,1},{17,25},{25,17},{2,10},{10... | collective-permute-start | bytes 1916936 | tf_op jit(solution)/shard_map/ppermute | solution.py:23
  25.8 1.6 %collective-permute-done.4.k_ref.kp_ref = bf16[256,2048]{1,0:T(8,128)(2,1)S(1)} collective-permute-done((bf16[256,2048]{1,0:T(8,128)(2,1)}, bf16[256,2048]{1,0:T(8,128)(2,1)S(1)}, u32[]{:S(2)}, u32[]{:S(2)}) %collective-permute-start.4) | collective-permute-done | bytes 1048608 | tf_op jit(solution)/shard_map/ppermute | solution.py:23
  27.3 0.8 %pick.1 = bf16[64,2048]{1,0:T(8,128)(2,1)S(1)} custom-call(s32[16]{0:T(128)S(1)} %copy-done.1, bf16[256,2048]{1,0:T(8,128)(2,1)S(1)} %collective-permute-done.4.k_ref.kp_ref), custom_call_target="tpu_custom_call" | custom-call | tf_op jit(solution)/shard_map/pick/pallas_call | solution.py:305
  28.2 2.2 %collective-permute-start.5 = (bf16[64,2048]{1,0:T(8,128)(2,1)S(1)}, bf16[64,2048]{1,0:T(8,128)(2,1)S(1)}, u32[]{:S(2)}, u32[]{:S(2)}) collective-permute-start(bf16[64,2048]{1,0:T(8,128)(2,1)S(1)} %pick.1), channel_id=1, source_target_pairs={{0,16},{8,24},{16,0},{24,8},{1,17},{9,25},{17,1},{25,9},{2,18},{10... | collective-permute-start | bytes 786440 | tf_op jit(solution)/shard_map/ppermute | solution.py:23
  30.3 1.7 %other.2 = (bf16[8,256,256]{2,1,0:T(8,128)(2,1)S(1)}, f32[8,256,128]{2,1,0:T(8,128)S(1)}, f32[256,128]{1,0:T(8,128)S(1)}) custom-call(s32[16]{0:T(128)S(1)} %copy-done.1, bf16[256,2048]{1,0:T(8,128)(2,1)S(1)} %get-tuple-element.46.q_ref, f32[16,256,128]{2,1,0:T(8,128)S(1)} %get-tuple-element.42.own_top_ref, ...), custom_call_target="tpu_custom_call" | custom-call | tf_op jit(solution)/shard_map/other/pallas_call | solution.py:305
  32.0 0.9 %collective-permute-done.7.vm_ref = bf16[64,2048]{1,0:T(8,128)(2,1)S(1)} collective-permute-done((bf16[64,2048]{1,0:T(8,128)(2,1)S(1)}, bf16[64,2048]{1,0:T(8,128)(2,1)S(1)}, u32[]{:S(2)}, u32[]{:S(2)}) %collective-permute-start.7) | collective-permute-done | bytes 262176 | tf_op jit(solution)/shard_map/ppermute | solution.py:23
  32.9 2.1 %collective-permute-start.8 = (bf16[64,2048]{1,0:T(8,128)(2,1)S(1)}, bf16[64,2048]{1,0:T(8,128)(2,1)S(1)}, u32[]{:S(2)}, u32[]{:S(2)}) collective-permute-start(bf16[64,2048]{1,0:T(8,128)(2,1)S(1)} %collective-permute-done.7.vm_ref), channel_id=1, source_target_pairs={{0,16},{8,24},{16,0},{24,8},{1,17},{9,25},{17,1},{25,9},{2,18},{10... | collective-permute-start | bytes 786440 | tf_op jit(solution)/shard_map/ppermute | solution.py:23
  35.1 1.6 %collective-permute-start.11 = (bf16[192,384]{1,0:T(8,128)(2,1)S(1)}, bf16[192,384]{1,0:T(8,128)(2,1)S(1)}, u32[]{:S(2)}, u32[]{:S(2)}) collective-permute-start(bf16[192,384]{1,0:T(8,128)(2,1)S(1)} %get-tuple-element.65), channel_id=1, source_target_pairs={{0,8},{8,0},{16,24},{24,16},{1,9},{9,1},{17,25},{25,17},{2,10},{10... | collective-permute-start | bytes 442376 | tf_op jit(solution)/shard_map/ppermute | solution.py:23
  36.7 1.7 %other.3 = (bf16[8,256,256]{2,1,0:T(8,128)(2,1)S(1)}, f32[8,256,128]{2,1,0:T(8,128)S(1)}, f32[256,128]{1,0:T(8,128)S(1)}) custom-call(s32[16]{0:T(128)S(1)} %copy-done.1, bf16[256,2048]{1,0:T(8,128)(2,1)S(1)} %get-tuple-element.46.q_ref, f32[16,256,128]{2,1,0:T(8,128)S(1)} %get-tuple-element.42.own_top_ref, ...), custom_call_target="tpu_custom_call" | custom-call | tf_op jit(solution)/shard_map/other/pallas_call | solution.py:305
  38.4 1.8 %own.1 = (f32[256,2048]{1,0:T(8,128)S(1)}, f32[256,128]{1,0:T(8,128)S(1)}) custom-call(s32[16]{0:T(128)S(1)} %copy-done.1, f32[16,256,256]{2,1,0:T(8,128)S(1)} %get-tuple-element.38.scores_ref, f32[8,256,128]{2,1,0:T(8,128)S(1)} %get-tuple-element.44.top_a_ref, f32[8,256,128]{2,1,0:T(8,128)S(1)} %get-tuple-element.47.top_b_ref, ...), custom_call_target="tpu_custom_call" | custom-call | tf_op jit(solution)/shard_map/own/pallas_call | solution.py:305
  40.2 0.3 collective-permute-done.8.diagonal_v_ref
  40.5 3.5 %extra.1 = (f32[256,2048]{1,0:T(8,128)S(1)}, f32[256,128]{1,0:T(8,128)S(1)}) custom-call(s32[16]{0:T(128)S(1)} %copy-done.1, s32[16]{0:T(128)S(1)} %copy-done.3, bf16[256,2048]{1,0:T(8,128)(2,1)S(1)} %get-tuple-element.46.q_ref, f32[256,128]{1,0:T(8,128)S(1)} %get-tuple-element.49.own_total_ref, f32[256,128]{1,0:T(8,128)S(1)} %get-tuple-element.45.state_a_ref, ...), custom_call_target="tpu_custom_call" | custom-call | tf_op jit(solution)/shard_map/extra/pallas_call | solution.py:305
  44.2 0.3 broadcast_in_dim.3
  44.5 0.6 %base.1 = (f32[256,1792]{1,0:T(8,128)S(1)}, f32[256,1792]{1,0:T(8,128)S(1)}) custom-call(f32[256,2048]{1,0:T(8,128)S(1)} %get-tuple-element.58.sum_ref, f32[256,128]{1,0:T(8,128)S(1)} %get-tuple-element.59.share_ref, f32[256,2048]{1,0:T(8,128)S(1)} %get-tuple-element.60.own_ref), custom_call_target="tpu_custom_call" | custom-call | tf_op jit(solution)/shard_map/base/pallas_call | solution.py:305
  45.2 1.4 %collective-permute-done.12.vr_ref = bf16[192,1664]{1,0:T(8,128)(2,1)S(1)} collective-permute-done((bf16[192,1664]{1,0:T(8,128)(2,1)S(1)}, bf16[192,1664]{1,0:T(8,128)(2,1)S(1)}, u32[]{:S(2)}, u32[]{:S(2)}) %collective-permute-start.12) | collective-permute-done | bytes 639008 | tf_op jit(solution)/shard_map/ppermute | solution.py:23
  46.6 1.4 %finish.2.rest_0_ = bf16[256,2048]{1,0:T(8,128)(2,1)} custom-call(f32[256,1792]{1,0:T(8,128)S(1)} %get-tuple-element.61.base_ref, f32[256,1792]{1,0:T(8,128)S(1)} %get-tuple-element.62.spread_ref, f32[256,256]{1,0:T(8,128)S(1)} %multiply_add_fusion.late_base_ref, f32[256,256]{1,0:T(8,128)S(1)} %bitcast.6, ...), custom_call_target="tpu_custom_call" | custom-call | tf_op jit(solution)/shard_map/finish/pallas_call | solution.py:305
  48.1 0.9 %collective-permute-done.11.vr_ref = bf16[192,384]{1,0:T(8,128)(2,1)S(1)} collective-permute-done((bf16[192,384]{1,0:T(8,128)(2,1)S(1)}, bf16[192,384]{1,0:T(8,128)(2,1)S(1)}, u32[]{:S(2)}, u32[]{:S(2)}) %collective-permute-start.11) | collective-permute-done | bytes 147488 | tf_op jit(solution)/shard_map/ppermute | solution.py:23
  49.0 0.9 %finish.3 = bf16[256,2048]{1,0:T(8,128)(2,1)} custom-call(f32[256,1792]{1,0:T(8,128)S(1)} %get-tuple-element.61.base_ref, f32[256,1792]{1,0:T(8,128)S(1)} %get-tuple-element.62.spread_ref, f32[256,256]{1,0:T(8,128)S(1)} %multiply_add_fusion.late_base_ref, f32[256,256]{1,0:T(8,128)S(1)} %bitcast.7, ...), custom_call_target="tpu_custom_call", output_to_operand_aliasing={{}: (8, {})} | custom-call | tf_op jit(solution)/shard_map/finish/pallas_call | solution.py:305
  (20 shorter events, 0.3 us)
Async XLA Ops:
  0.0 27.3 %collective-permute-start.4 = (bf16[256,2048]{1,0:T(8,128)(2,1)}, bf16[256,2048]{1,0:T(8,128)(2,1)S(1)}, u32[]{:S(2)}, u32[]{:S(2)}) collective-permute-start(bf16[256,2048]{1,0:T(8,128)(2,1)} %k_hbm.1), channel_id=1, source_target_pairs={{0,8},{8,0},{16,24},{24,16},{1,9},{9,1},{17,25},{25,17},{2,10},{10... | collective-permute-start | bytes 3145736 | tf_op jit(solution)/shard_map/ppermute | solution.py:23
  2.9 0.7 %copy-start = (s32[16]{0:T(128)S(1)}, s32[16]{0:T(128)}, u32[]{:S(2)}) copy-start(s32[16]{0:T(128)} %middle_ref.11) | copy-start | bytes 196
  3.6 0.7 %copy-start.2 = (s32[16]{0:T(128)S(1)}, s32[16]{0:T(128)}, u32[]{:S(2)}) copy-start(s32[16]{0:T(128)} %coarse_ref.3) | copy-start | bytes 196
  4.3 23.1 %copy-start.1 = (s32[16]{0:T(128)S(1)}, s32[16]{0:T(128)}, u32[]{:S(2)}) copy-start(s32[16]{0:T(128)} %middle_ref.11) | copy-start | bytes 196
  7.5 16.7 %collective-permute-start.6 = (bf16[128,2048]{1,0:T(8,128)(2,1)S(1)}, bf16[128,2048]{1,0:T(8,128)(2,1)S(1)}, u32[]{:S(2)}, u32[]{:S(2)}) collective-permute-start(bf16[128,2048]{1,0:T(8,128)(2,1)S(1)} %get-tuple-element.51), channel_id=1, source_target_pairs={{0,16},{8,24},{16,0},{24,8},{1,17},{9,25},{17,1},{25,9},{2,18},{10... | collective-permute-start | bytes 1572872 | tf_op jit(solution)/shard_map/ppermute | solution.py:23
  9.1 4.7 %collective-permute-start = (bf16[2,2048]{1,0:T(2,128)(2,1)S(1)}, bf16[2,2048]{1,0:T(2,128)(2,1)S(1)}, u32[]{:S(2)}, u32[]{:S(2)}) collective-permute-start(bf16[2,2048]{1,0:T(2,128)(2,1)S(1)} %get-tuple-element.39.refs_0_), channel_id=1, source_target_pairs={{0,10},{1,11},{2,8},{3,9},{4,14},{5,15},{6,12},{7,13},{8,2},{9,3},... | collective-permute-start | bytes 24584 | tf_op jit(solution)/shard_map/ppermute | solution.py:33
  13.8 5.3 %collective-permute-start.1 = (bf16[4,2048]{1,0:T(4,128)(2,1)S(1)}, bf16[4,2048]{1,0:T(4,128)(2,1)S(1)}, u32[]{:S(2)}, u32[]{:S(2)}) collective-permute-start(bf16[4,2048]{1,0:T(4,128)(2,1)S(1)} %stack.2.refs_0_), channel_id=1, source_target_pairs={{0,2},{1,3},{2,0},{3,1},{4,6},{5,7},{6,4},{7,5},{8,10},{9,11},{10,... | collective-permute-start | bytes 49160 | tf_op jit(solution)/shard_map/ppermute | solution.py:23
  15.4 4.9 %collective-permute-start.2 = (bf16[4,2048]{1,0:T(4,128)(2,1)S(1)}, bf16[4,2048]{1,0:T(4,128)(2,1)S(1)}, u32[]{:S(2)}, u32[]{:S(2)}) collective-permute-start(bf16[4,2048]{1,0:T(4,128)(2,1)S(1)} %stack.2.refs_0_), channel_id=1, source_target_pairs={{0,4},{1,5},{2,6},{3,7},{4,0},{5,1},{6,2},{7,3},{8,12},{9,13},{10,... | collective-permute-start | bytes 49160 | tf_op jit(solution)/shard_map/ppermute | solution.py:23
  18.0 5.6 %collective-permute-start.3 = (bf16[4,2048]{1,0:T(4,128)(2,1)S(1)}, bf16[4,2048]{1,0:T(4,128)(2,1)S(1)}, u32[]{:S(2)}, u32[]{:S(2)}) collective-permute-start(bf16[4,2048]{1,0:T(4,128)(2,1)S(1)} %stack.2.refs_0_), channel_id=1, source_target_pairs={{0,6},{1,7},{2,4},{3,5},{4,2},{5,3},{6,0},{7,1},{8,14},{9,15},{10,... | collective-permute-start | bytes 49160 | tf_op jit(solution)/shard_map/ppermute | solution.py:23
  23.6 9.3 %collective-permute-start.7 = (bf16[64,2048]{1,0:T(8,128)(2,1)S(1)}, bf16[64,2048]{1,0:T(8,128)(2,1)S(1)}, u32[]{:S(2)}, u32[]{:S(2)}) collective-permute-start(bf16[64,2048]{1,0:T(8,128)(2,1)S(1)} %get-tuple-element.55), channel_id=1, source_target_pairs={{0,8},{8,0},{16,24},{24,16},{1,9},{9,1},{17,25},{25,17},{2,10},{10... | collective-permute-start | bytes 786440 | tf_op jit(solution)/shard_map/ppermute | solution.py:23
  24.1 10.9 %collective-permute-start.9 = (bf16[16,2048]{1,0:T(8,128)(2,1)S(1)}, bf16[16,2048]{1,0:T(8,128)(2,1)S(1)}, u32[]{:S(2)}, u32[]{:S(2)}) collective-permute-start(bf16[16,2048]{1,0:T(8,128)(2,1)S(1)} %stack.3), channel_id=1, source_target_pairs={{0,18},{1,19},{2,16},{3,17},{4,22},{5,23},{6,20},{7,21},{8,26},{9,... | collective-permute-start | bytes 196616 | tf_op jit(solution)/shard_map/ppermute | solution.py:33
  24.2 22.5 %collective-permute-start.12 = (bf16[192,1664]{1,0:T(8,128)(2,1)S(1)}, bf16[192,1664]{1,0:T(8,128)(2,1)S(1)}, u32[]{:S(2)}, u32[]{:S(2)}) collective-permute-start(bf16[192,1664]{1,0:T(8,128)(2,1)S(1)} %get-tuple-element.66), channel_id=1, source_target_pairs={{0,8},{8,0},{16,24},{24,16},{1,9},{9,1},{17,25},{25,17},{2,10},{10... | collective-permute-start | bytes 1916936 | tf_op jit(solution)/shard_map/ppermute | solution.py:23
  28.2 8.5 %collective-permute-start.5 = (bf16[64,2048]{1,0:T(8,128)(2,1)S(1)}, bf16[64,2048]{1,0:T(8,128)(2,1)S(1)}, u32[]{:S(2)}, u32[]{:S(2)}) collective-permute-start(bf16[64,2048]{1,0:T(8,128)(2,1)S(1)} %pick.1), channel_id=1, source_target_pairs={{0,16},{8,24},{16,0},{24,8},{1,17},{9,25},{17,1},{25,9},{2,18},{10... | collective-permute-start | bytes 786440 | tf_op jit(solution)/shard_map/ppermute | solution.py:23
  32.9 7.6 %collective-permute-start.8 = (bf16[64,2048]{1,0:T(8,128)(2,1)S(1)}, bf16[64,2048]{1,0:T(8,128)(2,1)S(1)}, u32[]{:S(2)}, u32[]{:S(2)}) collective-permute-start(bf16[64,2048]{1,0:T(8,128)(2,1)S(1)} %collective-permute-done.7.vm_ref), channel_id=1, source_target_pairs={{0,16},{8,24},{16,0},{24,8},{1,17},{9,25},{17,1},{25,9},{2,18},{10... | collective-permute-start | bytes 786440 | tf_op jit(solution)/shard_map/ppermute | solution.py:23
  35.0 5.2 %collective-permute-start.10 = (bf16[32,2048]{1,0:T(8,128)(2,1)S(1)}, bf16[32,2048]{1,0:T(8,128)(2,1)S(1)}, u32[]{:S(2)}, u32[]{:S(2)}) collective-permute-start(bf16[32,2048]{1,0:T(8,128)(2,1)S(1)} %constant_dynamic-update-slice_fusion.mine_ref), channel_id=1, source_target_pairs={{0,1},{1,0},{2,3},{3,2},{4,5},{5,4},{6,7},{7,6},{8,9},{9,8},{10,11... | collective-permute-start | bytes 393224 | tf_op jit(solution)/shard_map/ppermute | solution.py:23
  35.1 13.8 %collective-permute-start.11 = (bf16[192,384]{1,0:T(8,128)(2,1)S(1)}, bf16[192,384]{1,0:T(8,128)(2,1)S(1)}, u32[]{:S(2)}, u32[]{:S(2)}) collective-permute-start(bf16[192,384]{1,0:T(8,128)(2,1)S(1)} %get-tuple-element.65), channel_id=1, source_target_pairs={{0,8},{8,0},{16,24},{24,16},{1,9},{9,1},{17,25},{25,17},{2,10},{10... | collective-permute-start | bytes 442376 | tf_op jit(solution)/shard_map/ppermute | solution.py:23
  38.4 2.2 %copy-start.3 = (s32[16]{0:T(128)S(1)}, s32[16]{0:T(128)}, u32[]{:S(2)}) copy-start(s32[16]{0:T(128)} %coarse_ref.3) | copy-start | bytes 196
